TPU v7x, 32 devices: a whole 2x2x4 slice. The times are simulated.
32 devices in a mesh: dp: 8 (over z, y), ctx: 4 (over x, core).
Axes of the slice: x: 2, y: 2, z: 4, core: 2. Of those that a mesh axis runs over, the one named last changes fastest.
Arguments:
- frame_input: bfloat16 [16, 256, 1536], P('dp', 'ctx'), may hold values from -6 to 6
- queries: bfloat16 [16, 256, 768], P('dp', 'ctx'), may hold values from -18 to 18
- key_proj: bfloat16 [16, 256, 768], P('dp', 'ctx'), may hold values from -18 to 18
- value_proj: bfloat16 [16, 256, 768], P('dp', 'ctx'), may hold values from -6 to 6
- out_weight: bfloat16 [1536, 768], P('ctx', 'dp'), may hold values from -0.21875 to 0.21875
- conv_weight: bfloat16 [31, 1536], P(None, 'dp'), may hold values from -1 to 1
- lengths: int32 [16], P('dp'), may hold values from 64 to 256, as said below
- grad_output: bfloat16 [16, 256, 1536], P('dp', 'ctx'), may hold values from -6 to 6
Outputs:
- block_output: bfloat16 [16, 256, 1536], P('dp', 'ctx')
- grad_input: bfloat16 [16, 256, 1536], P('dp', 'ctx')
- grad_queries: bfloat16 [16, 256, 768], P('dp', 'ctx')
- grad_keys: bfloat16 [16, 256, 768], P('dp', 'ctx')
- grad_values: bfloat16 [16, 256, 768], P('dp', 'ctx')
- grad_out_weight: float32 [1536, 768], P('ctx', 'dp')
- grad_conv_weight: float32 [31, 1536], P(None, 'dp')
Inputs may be any that keep to these rules, and one draw needn't show every extreme that they name: `lengths`: at least one utterance of every draw fills all 256 frame slots.
All inputs are finite; a program needn't handle non-finite values.
Results may differ from a plain program's by a relative error of at most 0.035.
Values may be sent and summed in bfloat16 or wider, within the bound.
No kernel may reach another device: no remote copies, remote signals or barrier semaphores. Data moves between devices by JAX's collectives and lax.ppermute only.
A program may use at most 128 MiB of HBM per device.

v0:
```python
import jax
import jax.numpy as jnp
from jax import lax
from jax.sharding import PartitionSpec as P

HEAD_DIM = 64


masked_score = -1e30


def padded_2(array, sides, width):
    for axis, dim in sides:
        size, length = (lax.axis_size(axis), array.shape[dim])
        up = [(i, (i + 1) % size) for i in range(size - 1)]
        down = [(j, i) for i, j in up]
        last = lax.slice_in_dim(array, length - width, length, axis=dim)
        leading = lax.slice_in_dim(array, 0, width, axis=dim)
        before = lax.ppermute(last, axis, up)
        after = lax.ppermute(leading, axis, down)
        array = jnp.concatenate([before, array, after], axis=dim)
    return array


def depthwise(lhs, rhs):
    return lax.conv_general_dilated(
        lhs,
        rhs,
        (1,),
        "VALID",
        dimension_numbers=("NWC", "WIO", "NWC"),
        feature_group_count=lhs.shape[2],
        precision=lax.Precision.HIGHEST,
    )


def per_device(
    frame_input, queries, key_proj, value_proj, out_weight, conv_weight, lengths, grad_output
):
    utt_count = frame_input.shape[0]
    frame_count = frame_input.shape[1]
    inner_width = queries.shape[2]
    head_count = inner_width // HEAD_DIM
    group_heads = max((g for g in range(1, 7) if head_count % g == 0))
    group_count = head_count // group_heads
    group_width = group_heads * HEAD_DIM
    tap_count = conv_weight.shape[0]
    half_span = (tap_count - 1) // 2
    score_scale = HEAD_DIM ** (-0.5)
    total_frames = frame_count * lax.axis_size("ctx")
    offset = lax.axis_index("ctx") * frame_count
    own_valid = (offset + jnp.arange(frame_count, dtype=jnp.int32))[None, :] < lengths[:, None]
    all_valid = jnp.arange(total_frames, dtype=jnp.int32)[None, :] < lengths[:, None]

    def grouped(values):
        row_count = values.shape[1]
        return values.reshape(utt_count, row_count, group_count, group_width).transpose(2, 0, 1, 3)

    def ungrouped(values):
        row_count = values.shape[2]
        return values.transpose(1, 2, 0, 3).reshape(utt_count, row_count, group_count * group_width)

    def split_heads(values):
        return values.reshape(utt_count, values.shape[1], group_heads, HEAD_DIM)

    def stats_grouped(values):
        row_count = values.shape[1]
        return values.reshape(utt_count, row_count, group_count, group_heads).transpose(2, 0, 3, 1)

    def masked_scores(query_block, key_block, key_mask):
        scores = (
            jnp.einsum(
                "uqgd,ukgd->ugqk", query_block, key_block, preferred_element_type=jnp.float32
            )
            * score_scale
        )
        return jnp.where(key_mask[:, None, None, :], scores, masked_score)

    taps = lax.all_gather(conv_weight, "dp", axis=1, tiled=True).astype(jnp.float32)
    panel_rows = lax.all_gather(out_weight, "dp", axis=1, tiled=True)
    weight_full = lax.all_gather(panel_rows, "ctx", axis=0, tiled=True)
    all_keys, all_values = (
        lax.all_gather(key_proj, "ctx", axis=1, tiled=True),
        lax.all_gather(value_proj, "ctx", axis=1, tiled=True),
    )
    query_groups = grouped(queries)
    key_groups = grouped(all_keys)
    value_groups = grouped(all_values)

    def forward_group(unused, items):
        query_group, key_group, value_group = items
        query_block = split_heads(query_group)
        scores = masked_scores(query_block, split_heads(key_group), all_valid)
        largest = jnp.max(scores, axis=-1)
        log_group = largest + jnp.log(jnp.sum(jnp.exp(scores - largest[..., None]), axis=-1))
        weights_low = jnp.exp(scores - log_group[..., None]).astype(jnp.bfloat16)
        attended_group = jnp.einsum(
            "ugqk,ukgd->uqgd",
            weights_low,
            split_heads(value_group),
            preferred_element_type=jnp.float32,
        )
        return (None, (log_group, attended_group.reshape(utt_count, frame_count, group_width)))

    _, (log_groups, attended_groups) = lax.scan(
        forward_group, None, (query_groups, key_groups, value_groups)
    )
    attended = ungrouped(attended_groups).astype(jnp.bfloat16)
    log_total = log_groups.transpose(1, 3, 0, 2).reshape(utt_count, frame_count, head_count)
    projected = jnp.einsum("ufe,de->ufd", attended, weight_full, preferred_element_type=jnp.float32)
    hidden = (frame_input.astype(jnp.float32) + projected).astype(jnp.bfloat16)
    masked_hidden = jnp.where(own_valid[:, :, None], hidden, jnp.zeros_like(hidden))
    padded = padded_2(masked_hidden, (("ctx", 1),), half_span).astype(jnp.float32)
    conv_sum = depthwise(padded, taps[:, None, :])
    sigmoid = jax.nn.sigmoid(conv_sum)
    block_output = (hidden.astype(jnp.float32) + conv_sum * sigmoid).astype(jnp.bfloat16)
    grad_local = grad_output.astype(jnp.float32)
    swish_slope = sigmoid * (1.0 + conv_sum * (1.0 - sigmoid))
    grad_conv = (grad_local * swish_slope).astype(jnp.bfloat16)
    grad_padded = padded_2(grad_conv, (("ctx", 1),), half_span).astype(jnp.float32)
    back_sum = depthwise(grad_padded, taps[::-1][:, None, :])
    grad_hidden = (grad_local + jnp.where(own_valid[:, :, None], back_sum, 0.0)).astype(
        jnp.bfloat16
    )
    grad_conv_wide = grad_conv.astype(jnp.float32)
    kernel_term = jnp.zeros((tap_count, conv_sum.shape[2]), jnp.float32)
    for utt_index in range(utt_count):
        kernel_term = (
            kernel_term
            + depthwise(padded[utt_index : utt_index + 1], grad_conv_wide[utt_index][:, None, :])[0]
        )
    kernel_whole = lax.psum(kernel_term.astype(jnp.bfloat16), "ctx")
    grad_conv_weight = lax.psum_scatter(kernel_whole, "dp", scatter_dimension=1, tiled=True).astype(
        jnp.float32
    )
    grad_attended = jnp.einsum(
        "ufd,de->ufe", grad_hidden, weight_full, preferred_element_type=jnp.float32
    ).astype(jnp.bfloat16)
    row_delta = jnp.sum(
        grad_attended.astype(jnp.float32).reshape(utt_count, frame_count, head_count, HEAD_DIM)
        * attended.astype(jnp.float32).reshape(utt_count, frame_count, head_count, HEAD_DIM),
        axis=-1,
    )
    grad_groups = grouped(grad_attended)

    def query_group_step(unused, items):
        query_group, key_group, value_group, grad_group, log_group, delta_group = items
        key_block = split_heads(key_group)
        weights = jnp.exp(
            masked_scores(split_heads(query_group), key_block, all_valid) - log_group[..., None]
        )
        grad_weights = jnp.einsum(
            "uqgd,ukgd->ugqk",
            split_heads(grad_group),
            split_heads(value_group),
            preferred_element_type=jnp.float32,
        )
        grad_scores = (weights * (grad_weights - delta_group[..., None])).astype(jnp.bfloat16)
        query_sum = jnp.einsum(
            "ugqk,ukgd->uqgd", grad_scores, key_block, preferred_element_type=jnp.float32
        )
        return (None, query_sum.reshape(utt_count, frame_count, group_width))

    _, query_sums = lax.scan(
        query_group_step,
        None,
        (
            query_groups,
            key_groups,
            value_groups,
            grad_groups,
            stats_grouped(log_total),
            stats_grouped(row_delta),
        ),
    )
    grad_queries = (ungrouped(query_sums) * score_scale).astype(jnp.bfloat16)
    total_log, total_delta = (
        lax.all_gather(log_total, "ctx", axis=1, tiled=True),
        lax.all_gather(row_delta, "ctx", axis=1, tiled=True),
    )
    own_key_groups = grouped(key_proj)
    own_value_groups = grouped(value_proj)
    group_zeros = jnp.zeros((group_count, utt_count, frame_count, group_width), jnp.float32)
    start_sums = (group_zeros, group_zeros)
    query_all, grad_all = (
        lax.all_gather(queries, "ctx", axis=1, tiled=True),
        lax.all_gather(grad_attended, "ctx", axis=1, tiled=True),
    )
    log_piece = stats_grouped(total_log)
    delta_piece = stats_grouped(total_delta)

    def key_group_step(unused, items):
        (
            query_group,
            grad_group,
            log_group,
            delta_group,
            key_group,
            value_group,
            key_sum,
            value_sum,
        ) = items
        query_block = split_heads(query_group)
        grad_block = split_heads(grad_group)
        weights = jnp.exp(
            masked_scores(query_block, split_heads(key_group), own_valid) - log_group[..., None]
        )
        grad_weights = jnp.einsum(
            "uqgd,ukgd->ugqk",
            grad_block,
            split_heads(value_group),
            preferred_element_type=jnp.float32,
        )
        grad_scores = (weights * (grad_weights - delta_group[..., None])).astype(jnp.bfloat16)
        key_next = key_sum + jnp.einsum(
            "ugqk,uqgd->ukgd", grad_scores, query_block, preferred_element_type=jnp.float32
        ).reshape(utt_count, frame_count, group_width)
        value_next = value_sum + jnp.einsum(
            "ugqk,uqgd->ukgd",
            weights.astype(jnp.bfloat16),
            grad_block,
            preferred_element_type=jnp.float32,
        ).reshape(utt_count, frame_count, group_width)
        return (None, (key_next, value_next))

    _, result_sums = lax.scan(
        key_group_step,
        None,
        (
            grouped(query_all),
            grouped(grad_all),
            log_piece,
            delta_piece,
            own_key_groups,
            own_value_groups,
            start_sums[0],
            start_sums[1],
        ),
    )
    key_sum, value_sum = result_sums
    grad_keys = (ungrouped(key_sum) * score_scale).astype(jnp.bfloat16)
    grad_values = ungrouped(value_sum).astype(jnp.bfloat16)
    hidden_cols = lax.slice_in_dim(
        grad_hidden, 0, weight_full.shape[0] // lax.axis_size("ctx") * lax.axis_size("ctx"), axis=2
    )
    panel_share = lax.psum_scatter(
        jnp.einsum("ufd,ufe->de", hidden_cols, attended, preferred_element_type=jnp.float32).astype(
            jnp.bfloat16
        ),
        "ctx",
        scatter_dimension=0,
        tiled=True,
    )
    grad_out_weight = lax.psum_scatter(panel_share, "dp", scatter_dimension=1, tiled=True).astype(
        jnp.float32
    )
    return (
        block_output,
        grad_hidden,
        grad_queries,
        grad_keys,
        grad_values,
        grad_out_weight,
        grad_conv_weight,
    )


def solution(mesh):
    placed = (
        P("dp", "ctx", None),
        P("dp", "ctx", None),
        P("dp", "ctx", None),
        P("dp", "ctx", None),
        P("ctx", "dp"),
        P(None, "dp"),
        P("dp"),
        P("dp", "ctx", None),
    )
    return jax.shard_map(
        per_device,
        mesh=mesh,
        in_specs=placed,
        out_specs=(
            P("dp", "ctx", None),
            P("dp", "ctx", None),
            P("dp", "ctx", None),
            P("dp", "ctx", None),
            P("dp", "ctx", None),
            P("ctx", "dp"),
            P(None, "dp"),
        ),
        check_vma=False,
    )
```

profile of v0, /device:TPU:0, one launch (start us, length us, event | category | flops | bytes accessed | tf_op | source)
XLA Modules:
  0.0 300.7 jit_solution(744322589899727858)
XLA Ops:
  7.2 33.6 %all_gather.29 = bf16[384,768]{0,1:T(8,128)(2,1)S(1)} all-gather(bf16[384,96]{0,1:T(8,128)(2,1)} %param.18), channel_id=1, replica_groups=mesh['dp'=8,'ctx'=4] {'dp'}, dimensions={1}, use_global_device_ids=true | all-gather | bytes 663552 | tf_op jit(solution)/shard_map/all_gather | solution.py:80
  42.3 8.6 %all_gather.27 = bf16[2,256,768]{2,0,1:T(2,128)(2,1)S(1)} all-gather(bf16[2,64,768]{2,0,1:T(2,128)(2,1)S(1)} %copy.131), channel_id=1, replica_groups=mesh['dp'=8,'ctx'=4] {'ctx'}, dimensions={1}, use_global_device_ids=true | all-gather | bytes 983040 | tf_op jit(solution)/shard_map/all_gather | solution.py:83
  52.0 13.3 %all_gather.28 = bf16[2,256,768]{2,0,1:T(2,128)(2,1)S(1)} all-gather(bf16[2,64,768]{2,0,1:T(2,128)(2,1)S(1)} %copy.133), channel_id=1, replica_groups=mesh['dp'=8,'ctx'=4] {'ctx'}, dimensions={1}, use_global_device_ids=true | all-gather | bytes 983040 | tf_op jit(solution)/shard_map/all_gather | solution.py:84
  66.2 4.4 %while.37 = (s32[]{:T(128)}, f32[2,2,6,64]{3,2,1,0:T(8,128)S(1)}, bf16[2,2,64,384]{3,2,0,1:T(8,128)(2,1)S(1)}, bf16[2,2,64,384]{3,2,1,0:T(8,128)(2,1)S(1)}, bf16...) while((s32[]{:T(128)}, f32[2,2,6,64]{3,2,1,0:T(8,128)S(1)}, ...), condition=%wide.region_3.4_spmd.clone, body=%wide.region_0.3_spmd.clone.sunk | while | flops 51707648 | bytes 5747829 | solution.py:105
  72.0 2.6 broadcast_select_fusion
  76.0 3.0 %collective-permute-start = (bf16[2,15,1536]{2,1,0:T(8,128)(2,1)S(1)}, bf16[2,15,1536]{2,1,0:T(8,128)(2,1)S(1)}, u32[]{:S(2)}, u32[]{:S(2)}) collective-permute-start(bf16[2,15,1536]{2,1,0:T(8,128)(2,1)S(1)} %get-tuple-element.406), channel_id=1, source_target_pairs={{0,1},{1,2},{2,3},{4,5},{5,6},{6,7},{8,9},{9,10},{10,11},{12,13},{... | collective-permute-start | bytes 276488 | tf_op jit(solution)/shard_map/ppermute | solution.py:19
  79.0 30.5 %all-gather = bf16[8,192,31]{1,2,0:T(8,128)(2,1)S(1)} all-gather(bf16[1,192,31]{1,2,0:T(8,128)(2,1)S(1)} %bitcast.216), channel_id=1, replica_groups=mesh['dp'=8,'ctx'=4] {'dp'}, dimensions={0}, use_global_device_ids=true | all-gather | bytes 107136 | tf_op jit(solution)/shard_map/all_gather | solution.py:79
  110.0 2.7 fusion.47
  115.1 3.0 %collective-permute-start.2 = (bf16[2,15,1536]{2,1,0:T(8,128)(2,1)S(1)}, bf16[2,15,1536]{2,1,0:T(8,128)(2,1)S(1)}, u32[]{:S(2)}, u32[]{:S(2)}) collective-permute-start(bf16[2,15,1536]{2,1,0:T(8,128)(2,1)S(1)} %get-tuple-element.404), channel_id=1, source_target_pairs={{0,1},{1,2},{2,3},{4,5},{5,6},{6,7},{8,9},{9,10},{10,11},{12,13},{... | collective-permute-start | bytes 276488 | tf_op jit(solution)/shard_map/ppermute | solution.py:19
  119.2 2.3 fusion.45
  121.9 2.2 bitcast_convert_fusion
  129.1 12.4 %all_gather.32 = bf16[2,256,768]{2,0,1:T(2,128)(2,1)} all-gather(bf16[2,64,768]{2,0,1:T(2,128)(2,1)} %copy.158), channel_id=1, replica_groups=mesh['dp'=8,'ctx'=4] {'ctx'}, dimensions={1}, use_global_device_ids=true | all-gather | bytes 983040 | tf_op jit(solution)/shard_map/all_gather | solution.py:186
  141.5 3.0 %copy.159 = bf16[2,256,768]{1,2,0:T(8,128)(2,1)} copy(bf16[2,256,768]{2,0,1:T(2,128)(2,1)} %all_gather.32) | data formatting | bytes 1572864 | tf_op jit(solution)/shard_map/all_gather | solution.py:186
  146.3 8.1 %all_gather.33 = f32[2,256,12]{2,0,1:T(2,128)} all-gather(f32[2,64,12]{2,0,1:T(2,128)S(1)} %copy.161), channel_id=1, replica_groups=mesh['dp'=8,'ctx'=4] {'ctx'}, dimensions={1}, use_global_device_ids=true | all-gather | bytes 30720 | tf_op jit(solution)/shard_map/all_gather | solution.py:178
  164.5 2.1 fusion.37
  167.9 9.3 %all_gather.34 = bf16[2,256,768]{2,1,0:T(8,128)(2,1)} all-gather(bf16[2,64,768]{2,1,0:T(8,128)(2,1)S(1)} %fusion.37), channel_id=1, replica_groups=mesh['dp'=8,'ctx'=4] {'ctx'}, dimensions={1}, use_global_device_ids=true | all-gather | bytes 983040 | tf_op jit(solution)/shard_map/all_gather | solution.py:187
  177.2 2.8 reshape.203
  180.0 3.1 %copy.163 = bf16[2,256,2,384]{1,3,0,2:T(8,128)(2,1)} copy(bf16[2,256,2,384]{3,2,1,0:T(2,128)(2,1)} %reshape.203) | data formatting | bytes 1572864 | tf_op jit(solution)/shard_map/reshape | solution.py:57
  185.3 5.9 %all_gather.35 = f32[2,256,12]{2,0,1:T(2,128)S(1)} all-gather(f32[2,64,12]{2,0,1:T(2,128)S(1)} %copy.164), channel_id=1, replica_groups=mesh['dp'=8,'ctx'=4] {'ctx'}, dimensions={1}, use_global_device_ids=true | all-gather | bytes 30720 | tf_op jit(solution)/shard_map/all_gather | solution.py:179
  192.9 17.9 %while.39 = (s32[]{:T(128)}, f32[2,2,64,384]{2,3,1,0:T(8,128)}, bf16[2,2,64,384]{2,3,1,0:T(8,128)(2,1)}, bf16[2,2,256,384]{2,3,0,1:T(8,128)(2,1)}, bf16[2,2,64,3...) while((s32[]{:T(128)}, f32[2,2,64,384]{2,3,1,0:T(8,128)}, ...), condition=%wide.region_8.9_spmd.clone, body=%wide.region_7.8_spmd.clone.sunk | while | flops 102039680 | bytes 7791261 | solution.py:226
  212.7 2.1 copy.178
  215.8 9.4 %while.38 = (s32[]{:T(128)}, f32[2,2,64,384]{2,3,1,0:T(8,128)}, bf16[2,2,256,384]{2,3,1,0:T(8,128)(2,1)S(1)}, bf16[2,2,64,384]{3,2,1,0:T(8,128)(2,1)S(1)}, f32[2...) while((s32[]{:T(128)}, f32[2,2,64,384]{2,3,1,0:T(8,128)}, ...), condition=%wide.region_6.7_spmd.clone, body=%wide.region_5.6_spmd.clone.sunk | while | flops 76677632 | bytes 6120585 | solution.py:164
  230.5 11.0 %psum.8 = bf16[31,192]{1,0:T(8,128)(2,1)S(1)} all-reduce(bf16[31,192]{1,0:T(8,128)(2,1)S(1)} %copy.181), channel_id=1, replica_groups=mesh['dp'=8,'ctx'=4] {'ctx'}, use_global_device_ids=true, to_apply=%region_11.12 | all-reduce | flops 5952 | bytes 23808 | tf_op jit(solution)/shard_map/psum | solution.py:132
  242.2 50.2 %reduce-scatter.10.cloned.1.call-done = bf16[96,384]{1,0:T(8,128)(2,1)} async-done(((bf16[768,384]{1,0:T(8,128)(2,1)}), bf16[96,384]{1,0:T(8,128)(2,1)}) %reduce-scatter.10.cloned.1.call-update) | async-done | bytes 73744
  (188 shorter events, 74.2 us)
Async XLA Ops:
  7.2 34.8 %copy-start.8 = (bf16[2,64,768]{2,1,0:T(8,128)(2,1)S(1)}, bf16[2,64,768]{2,1,0:T(8,128)(2,1)}, u32[]{:S(2)}) copy-start(bf16[2,64,768]{2,1,0:T(8,128)(2,1)} %param.15) | copy-start | bytes 589828
  7.2 34.9 %copy-start.10 = (bf16[2,64,768]{2,1,0:T(8,128)(2,1)S(1)}, bf16[2,64,768]{2,1,0:T(8,128)(2,1)}, u32[]{:S(2)}) copy-start(bf16[2,64,768]{2,1,0:T(8,128)(2,1)} %param.16) | copy-start | bytes 589828
  7.2 64.8 %all-gather.3.cloned.1.call-start = ((), (), s32[]{:S(2)}) async-start(), calls=%async_computation.3 | async-start | bytes 2949120 | tf_op jit(solution)/shard_map/all_gather | solution.py:81
  41.9 170.8 %reduce-scatter.8.cloned.1.call-start = ((), (), s32[]{:S(2)}) async-start(), calls=%async_computation.4 | async-start | bytes 2949120 | tf_op jit(solution)/shard_map/reduce_scatter | solution.py:246
  42.1 9.7 %copy-start.12 = (bf16[2,64,768]{2,1,0:T(8,128)(2,1)S(1)}, bf16[2,64,768]{2,1,0:T(8,128)(2,1)}, u32[]{:S(2)}) copy-start(bf16[2,64,768]{2,1,0:T(8,128)(2,1)} %param.17) | copy-start | bytes 589828
  70.6 39.0 %copy-start = (bf16[2,2,64,384]{3,2,1,0:T(8,128)(2,1)}, bf16[2,2,64,384]{3,2,1,0:T(8,128)(2,1)S(1)}, u32[]{:S(2)}) copy-start(bf16[2,2,64,384]{3,2,1,0:T(8,128)(2,1)S(1)} %get-tuple-element.702) | copy-start | bytes 589828
  70.6 75.5 %copy-start.17 = (f32[2,2,6,64]{3,2,1,0:T(8,128)}, f32[2,2,6,64]{3,2,1,0:T(8,128)S(1)}, u32[]{:S(2)}) copy-start(f32[2,2,6,64]{3,2,1,0:T(8,128)S(1)} %get-tuple-element.631) | copy-start | bytes 18436
  70.6 8.4 %copy-start.19 = (bf16[31,192]{1,0:T(8,128)(2,1)S(1)}, bf16[31,192]{1,0:T(8,128)(2,1)}, u32[]{:S(2)}) copy-start(bf16[31,192]{1,0:T(8,128)(2,1)} %param.19) | copy-start | bytes 35716
  74.7 35.1 %collective-permute-start.1 = (bf16[2,15,1536]{2,1,0:T(8,128)(2,1)S(1)}, bf16[2,15,1536]{2,1,0:T(8,128)(2,1)S(1)}, u32[]{:S(2)}, u32[]{:S(2)}) collective-permute-start(bf16[2,15,1536]{2,1,0:T(8,128)(2,1)S(1)} %get-tuple-element.407), channel_id=1, source_target_pairs={{1,0},{2,1},{3,2},{5,4},{6,5},{7,6},{9,8},{10,9},{11,10},{13,12},{... | collective-permute-start | bytes 276488 | tf_op jit(solution)/shard_map/ppermute | solution.py:20
  76.0 33.8 %collective-permute-start = (bf16[2,15,1536]{2,1,0:T(8,128)(2,1)S(1)}, bf16[2,15,1536]{2,1,0:T(8,128)(2,1)S(1)}, u32[]{:S(2)}, u32[]{:S(2)}) collective-permute-start(bf16[2,15,1536]{2,1,0:T(8,128)(2,1)S(1)} %get-tuple-element.406), channel_id=1, source_target_pairs={{0,1},{1,2},{2,3},{4,5},{5,6},{6,7},{8,9},{9,10},{10,11},{12,13},{... | collective-permute-start | bytes 276488 | tf_op jit(solution)/shard_map/ppermute | solution.py:19
  109.9 2.7 copy-start.5
  110.0 2.7 copy-start.6
  113.8 4.7 %collective-permute-start.3 = (bf16[2,15,1536]{2,1,0:T(8,128)(2,1)S(1)}, bf16[2,15,1536]{2,1,0:T(8,128)(2,1)S(1)}, u32[]{:S(2)}, u32[]{:S(2)}) collective-permute-start(bf16[2,15,1536]{2,1,0:T(8,128)(2,1)S(1)} %get-tuple-element.405), channel_id=1, source_target_pairs={{1,0},{2,1},{3,2},{5,4},{6,5},{7,6},{9,8},{10,9},{11,10},{13,12},{... | collective-permute-start | bytes 276488 | tf_op jit(solution)/shard_map/ppermute | solution.py:20
  115.1 4.0 %collective-permute-start.2 = (bf16[2,15,1536]{2,1,0:T(8,128)(2,1)S(1)}, bf16[2,15,1536]{2,1,0:T(8,128)(2,1)S(1)}, u32[]{:S(2)}, u32[]{:S(2)}) collective-permute-start(bf16[2,15,1536]{2,1,0:T(8,128)(2,1)S(1)} %get-tuple-element.404), channel_id=1, source_target_pairs={{0,1},{1,2},{2,3},{4,5},{5,6},{6,7},{8,9},{9,10},{10,11},{12,13},{... | collective-permute-start | bytes 276488 | tf_op jit(solution)/shard_map/ppermute | solution.py:19
  121.8 42.7 %copy-start.2 = (bf16[2,64,1536]{2,1,0:T(8,128)(2,1)}, bf16[2,64,1536]{2,1,0:T(8,128)(2,1)S(1)}, u32[]{:S(2)}) copy-start(bf16[2,64,1536]{2,1,0:T(8,128)(2,1)S(1)} %fusion.41) | copy-start | bytes 1179652
  121.8 3.2 %copy-start.11 = (bf16[2,64,768]{2,1,0:T(8,128)(2,1)S(1)}, bf16[2,64,768]{2,1,0:T(8,128)(2,1)}, u32[]{:S(2)}) copy-start(bf16[2,64,768]{2,1,0:T(8,128)(2,1)} %param.16) | copy-start | bytes 589828
  121.9 3.9 %copy-start.13 = (bf16[2,64,768]{2,1,0:T(8,128)(2,1)S(1)}, bf16[2,64,768]{2,1,0:T(8,128)(2,1)}, u32[]{:S(2)}) copy-start(bf16[2,64,768]{2,1,0:T(8,128)(2,1)} %param.17) | copy-start | bytes 589828
  124.0 2.4 copy-start.15
  124.1 105.6 %reduce-scatter.12.cloned.1.call-start = ((), (), s32[]{:S(2)}) async-start(), calls=%async_computation.6 | async-start | bytes 442368
  164.4 127.9 %reduce-scatter.10.cloned.1.call-start = ((), (), s32[]{:S(2)}) async-start(), calls=%async_computation.5 | async-start | bytes 663552
  166.7 16.4 %copy-start.4 = (bf16[2,64,768]{2,1,0:T(8,128)(2,1)}, bf16[2,64,768]{2,1,0:T(8,128)(2,1)S(1)}, u32[]{:S(2)}) copy-start(bf16[2,64,768]{2,1,0:T(8,128)(2,1)S(1)} %fusion.37) | copy-start | bytes 589828
  210.8 5.0 %copy-start.1 = (bf16[2,2,64,384]{3,2,1,0:T(8,128)(2,1)S(1)}, bf16[2,2,64,384]{3,2,1,0:T(8,128)(2,1)}, u32[]{:S(2)}) copy-start(bf16[2,2,64,384]{3,2,1,0:T(8,128)(2,1)} %copy-done) | copy-start | bytes 589828
  210.8 5.0 %copy-start.18 = (f32[2,2,6,64]{3,2,1,0:T(8,128)S(1)}, f32[2,2,6,64]{3,2,1,0:T(8,128)}, u32[]{:S(2)}) copy-start(f32[2,2,6,64]{3,2,1,0:T(8,128)} %copy-done.17) | copy-start | bytes 18436
  225.2 3.4 %copy-start.7 = (bf16[2,2,64,384]{2,3,1,0:T(8,128)(2,1)S(1)}, bf16[2,2,64,384]{2,3,1,0:T(8,128)(2,1)}, u32[]{:S(2)}) copy-start(bf16[2,2,64,384]{2,3,1,0:T(8,128)(2,1)} %get-tuple-element.149) | copy-start | bytes 589828
  (4 other events, 6.7 us)
Sparse Core Ops, SparseCore 0:
  42.0 29.3 all-gather.2
  124.2 38.3 reduce-scatter.7
  166.3 61.4 reduce-scatter.11
  231.3 61.0 reduce-scatter.9
where the time goes:
time: 302 us; the launch traced here: 301 us
  blocking collectives  133 us (44%)
  local copies, waits for them, and re-layouts  55 us (18%)
  waiting for transfers between devices  50.8 us (17%)
  matrix products  26.3 us (9%)
  between operations  14.3 us (5%)
  other arithmetic  12.5 us (4%)
  starting transfers between devices  8.82 us (3%)
    unnamed x6, waiting for transfers between devices  50.3 us
    all_gather x1, blocking collectives, per_device(): panel_rows = lax.all_gather(out_weight, 'dp', axis=1, tiled=True)  33.6 us
    all_gather x1, blocking collectives, per_device(): lax.all_gather(conv_weight, 'dp', axis=1, tiled=True).astype(jnp.float32)  30.5 us
    all_gather x1, blocking collectives, per_device(): lax.all_gather(value_proj, 'ctx', axis=1, tiled=True)  13.3 us
    all_gather x1, blocking collectives, per_device(): lax.all_gather(queries, 'ctx', axis=1, tiled=True)  12.4 us
    unnamed x54, local copies, waits for them, and re-layouts  11.3 us
    psum x1, blocking collectives, per_device(): kernel_whole = lax.psum(kernel_term.astype(jnp.bfloat16), 'ctx')  11 us
    all_gather x1, blocking collectives, per_device(): lax.all_gather(grad_attended, 'ctx', axis=1, tiled=True)  9.34 us
  transfers between devices with their start and end apart: 8, of which 2 were waited for; matrix products, arithmetic and copies ran while one was open for 26% of the time, Pallas kernels for 0%

commit v1 on v0

--- a/solution.py
+++ b/solution.py
@@ -1,6 +1,10 @@
+import functools
+
 import jax
 import jax.numpy as jnp
 from jax import lax
+from jax.experimental import pallas as pl
+from jax.experimental.pallas import tpu as pltpu
 from jax.sharding import PartitionSpec as P
 
 HEAD_DIM = 64
@@ -34,7 +38,7 @@
     )
 
 
-def per_device(
+def general_device(
     frame_input, queries, key_proj, value_proj, out_weight, conv_weight, lengths, grad_output
 ):
     utt_count = frame_input.shape[0]
@@ -265,6 +269,381 @@
     )
 
 
+LANES = 128
+N_CTX = 4
+N_DP = 8
+DP_BITS = (4, 2, 1)
+TAP_PAD = 32
+
+
+def slot_of(index, me):
+    apart = jnp.bitwise_xor(index, me)
+    return ((apart & 1) << 2) | (apart & 2) | ((apart >> 2) & 1)
+
+
+def dot_tt(lhs, rhs, lhs_dim, rhs_dim):
+    return lax.dot_general(
+        lhs, rhs, (((lhs_dim,), (rhs_dim,)), ((), ())), preferred_element_type=jnp.float32
+    )
+
+
+def call_kernel(body, out_shape, scratch=(), smem_first=False, count=1, cost=None):
+    vmem = pl.BlockSpec(memory_space=pltpu.VMEM)
+    specs = [vmem] * count
+    if smem_first:
+        specs[0] = pl.BlockSpec(memory_space=pltpu.SMEM)
+    return pl.pallas_call(
+        body,
+        out_shape=out_shape,
+        in_specs=specs,
+        out_specs=jax.tree.map(lambda unused: vmem, out_shape),
+        scratch_shapes=list(scratch),
+        compiler_params=pltpu.CompilerParams(vmem_limit_bytes=48 * 1024 * 1024),
+        cost_estimate=cost,
+    )
+
+
+def pack_heads(query_ref, key_ref, value_ref, out_ref):
+    half = query_ref.shape[2] // 2
+    for utt in range(2):
+        for side in range(2):
+            for slot, ref in enumerate((query_ref, key_ref, value_ref)):
+                out_ref[2 * utt + side, :, slot * half : (slot + 1) * half] = ref[
+                    utt, :, side * half : (side + 1) * half
+                ]
+
+
+def pack_channels(frame_ref, grad_ref, out_ref):
+    width = frame_ref.shape[2] // N_CTX
+    for dest in range(N_CTX):
+        for slot, ref in enumerate((frame_ref, grad_ref)):
+            out_ref[dest, slot] = ref[:, :, dest * width : (dest + 1) * width]
+
+
+def unpack_channels(in_ref, output_ref, grad_ref):
+    width = in_ref.shape[4]
+    for source in range(N_CTX):
+        for slot, ref in enumerate((output_ref, grad_ref)):
+            ref[:, :, source * width : (source + 1) * width] = in_ref[source, slot]
+
+
+def unpack_heads(in_ref, query_ref, key_ref, value_ref):
+    half = in_ref.shape[2] // 3
+    for utt in range(2):
+        for side in range(2):
+            for slot, ref in enumerate((query_ref, key_ref, value_ref)):
+                ref[utt, :, side * half : (side + 1) * half] = in_ref[
+                    2 * utt + side, :, slot * half : (slot + 1) * half
+                ]
+
+
+def head_parts(ref, slot, half):
+    rows = ref.shape[0] * ref.shape[1]
+    return ref[:, :, slot * half : (slot + 1) * half].reshape(rows, half)
+
+
+def half_masks(rows):
+    lane = lax.broadcasted_iota(jnp.int32, (rows, LANES), 1)
+    low = jnp.where(lane < HEAD_DIM, 1.0, 0.0)
+    return low.astype(jnp.bfloat16), (1.0 - low).astype(jnp.bfloat16)
+
+
+def attend(length_ref, packed_ref, attended_ref, weight_ref):
+    half = packed_ref.shape[2] // 3
+    rows = packed_ref.shape[0] * packed_ref.shape[1]
+    length = length_ref[lax.axis_index("ctx") // 2]
+    query, key, value = (head_parts(packed_ref, slot, half) for slot in range(3))
+    masks = half_masks(rows)
+    real = lax.broadcasted_iota(jnp.int32, (rows, rows), 0) < length
+    for pair in range(half // LANES):
+        cols = slice(pair * LANES, (pair + 1) * LANES)
+        key_pair, value_pair = key[:, cols], value[:, cols]
+        parts = []
+        for side in range(2):
+            scores = dot_tt(key_pair, query[:, cols] * masks[side], 1, 1) * HEAD_DIM ** (-0.5)
+            scores = jnp.where(real, scores, masked_score)
+            largest = jnp.max(scores, axis=0, keepdims=True)
+            powers = jnp.exp(scores - largest)
+            total = jnp.sum(powers, axis=0, keepdims=True)
+            low = (powers * (1.0 / total)).astype(jnp.bfloat16)
+            weight_ref[2 * pair + side] = low
+            mixed = dot_tt(value_pair, low, 0, 0)
+            parts.append(mixed[side * HEAD_DIM : (side + 1) * HEAD_DIM])
+        joined = jnp.concatenate(parts, axis=0).T.astype(jnp.bfloat16)
+        for dest in range(N_CTX):
+            attended_ref[dest, :, cols] = joined
+
+
+def middle(
+    length_ref,
+    attended_ref,
+    weight_ref,
+    side_ref,
+    result_ref,
+    back_ref,
+    panel_ref,
+    taps_ref,
+    tap_sum_ref,
+    rows_ref,
+    hidden_ref,
+    masked_ref,
+    cotangent_ref,
+    grad_ref,
+):
+    rows, half = attended_ref.shape[1], attended_ref.shape[2]
+    frames, width = side_ref.shape[3], side_ref.shape[4]
+    chunks = width // LANES
+    entries = 2 * half // N_DP
+    tap_count, reach = 31, 15
+    own = width // 2
+    group, place = lax.axis_index("dp"), lax.axis_index("ctx")
+    for part in range(N_DP):
+        rows_ref[part * entries : (part + 1) * entries] = weight_ref[
+            slot_of(part, group), 0:entries
+        ]
+    pieces = []
+    for part in range(2):
+        block = weight_ref[slot_of(2 * place + part, group), entries:].astype(jnp.float32)
+        pieces.append(jnp.concatenate([block[:, :own], block[:, own:]], axis=0))
+    taps = jnp.concatenate(pieces, axis=1)
+    for chunk in range(chunks):
+        for tap in range(tap_count):
+            taps_ref[chunk, tap] = jnp.broadcast_to(
+                taps[tap : tap + 1, chunk * LANES : (chunk + 1) * LANES], (8, LANES)
+            )
+    tap_sum_ref[...] = jnp.zeros_like(tap_sum_ref)
+    edge = jnp.zeros((2 * chunks, 16, LANES), jnp.float32)
+    for ref in (masked_ref, cotangent_ref):
+        ref[:, 0:16, :] = edge
+        ref[:, 16 + rows : 32 + rows, :] = edge
+    for utt in range(2):
+        real = lax.broadcasted_iota(jnp.int32, (rows, LANES), 0) < length_ref[utt]
+        projected = dot_tt(attended_ref[2 * utt], rows_ref[0:half], 1, 0)
+        projected += dot_tt(attended_ref[2 * utt + 1], rows_ref[half:], 1, 0)
+        hidden = side_ref[:, 0, utt].reshape(rows, width).astype(jnp.float32) + projected
+        hidden = hidden.astype(jnp.bfloat16).astype(jnp.float32)
+        for chunk in range(chunks):
+            piece = hidden[:, chunk * LANES : (chunk + 1) * LANES]
+            hidden_ref[utt * chunks + chunk] = piece
+            masked_ref[utt * chunks + chunk, 16 : 16 + rows, :] = jnp.where(real, piece, 0.0)
+
+    def convolve(step, carry):
+        utt, chunk = step // chunks, step % chunks
+        cols = pl.ds(pl.multiple_of(chunk * LANES, LANES), LANES)
+        length = length_ref[utt]
+        shape = (frames // 8, 8, LANES)
+        for block in range(N_CTX):
+            base = block * frames
+            total = jnp.zeros(shape, jnp.float32)
+            for tap in range(tap_count):
+                piece = masked_ref[step, base + tap + 16 - reach : base + tap + 16 - reach + frames, :]
+                total += taps_ref[chunk, tap][None] * piece.reshape(shape)
+            total = total.reshape(frames, LANES)
+            gate = jax.nn.sigmoid(total)
+            outer = hidden_ref[step, base : base + frames, :] + total * gate
+            result_ref[block, 0, utt, :, cols] = outer.astype(jnp.bfloat16)
+            incoming = side_ref[block, 1, utt, :, cols].astype(jnp.float32)
+            slope = gate * (1.0 + total * (1.0 - gate))
+            low = (incoming * slope).astype(jnp.bfloat16)
+            cotangent_ref[step, 16 + base : 16 + base + frames, :] = low.astype(jnp.float32)
+        for block in range(N_CTX):
+            base = block * frames
+            total = jnp.zeros(shape, jnp.float32)
+            held = masked_ref[step, 16 + base : 16 + base + frames, :].reshape(shape)
+            for tap in range(tap_count):
+                first = base + 16 + reach - tap
+                piece = cotangent_ref[step, first : first + frames, :].reshape(shape)
+                total += taps_ref[chunk, tap][None] * piece
+                tap_sum_ref[chunk, tap] += jnp.sum(held * piece, axis=0)
+            place_of = base + lax.broadcasted_iota(jnp.int32, (frames, LANES), 0)
+            total = jnp.where(place_of < length, total.reshape(frames, LANES), 0.0)
+            incoming = side_ref[block, 1, utt, :, cols].astype(jnp.float32)
+            low = (incoming + total).astype(jnp.bfloat16)
+            result_ref[block, 1, utt, :, cols] = low
+            grad_ref[utt, base : base + frames, cols] = low
+        return carry
+
+    lax.fori_loop(0, 2 * chunks, convolve, 0)
+    sums = [
+        jnp.concatenate([jnp.sum(tap_sum_ref[chunk, tap], axis=0, keepdims=True) for tap in range(TAP_PAD)], axis=0)
+        for chunk in range(chunks)
+    ]
+    sums = jnp.concatenate(sums, axis=1).astype(jnp.bfloat16)
+    for utt in range(2):
+        for side in range(2):
+            back_ref[2 * utt + side, 0:rows, :] = dot_tt(
+                grad_ref[utt], rows_ref[side * half : (side + 1) * half], 1, 1
+            ).astype(jnp.bfloat16)
+            back_ref[2 * utt + side, rows:, :] = sums
+    for side in range(2):
+        panel = dot_tt(attended_ref[side], grad_ref[0], 0, 0)
+        panel += dot_tt(attended_ref[2 + side], grad_ref[1], 0, 0)
+        panel = panel.astype(jnp.bfloat16)
+        for part in range(N_DP // 2):
+            panel_ref[slot_of(side * N_DP // 2 + part, group)] = panel[
+                part * entries : (part + 1) * entries
+            ]
+
+
+def attend_back(packed_ref, weight_ref, back_ref, out_ref, taps_ref):
+    half = packed_ref.shape[2] // 3
+    sources, frames = packed_ref.shape[0], packed_ref.shape[1]
+    rows = sources * frames
+    own = half // 2
+    group = lax.axis_index("dp")
+    query, key, value = (head_parts(packed_ref, slot, half) for slot in range(3))
+    masks = half_masks(rows)
+    scale = HEAD_DIM ** (-0.5)
+    arriving = back_ref[0, 0:rows, :].astype(jnp.float32)
+    for source in range(1, sources):
+        arriving += back_ref[source, 0:rows, :].astype(jnp.float32)
+    arriving = arriving.astype(jnp.bfloat16)
+    low_lanes = lax.broadcasted_iota(jnp.int32, (rows, LANES), 1) < HEAD_DIM
+    for pair in range(half // LANES):
+        cols = slice(pair * LANES, (pair + 1) * LANES)
+        key_pair, value_pair = key[:, cols], value[:, cols]
+        query_pair, grad_pair = query[:, cols], arriving[:, cols]
+        query_parts, key_parts, value_parts = [], [], []
+        for side in range(2):
+            low = weight_ref[2 * pair + side]
+            weights = low.astype(jnp.float32)
+            moved = weights * dot_tt(value_pair, grad_pair * masks[side], 1, 1)
+            delta = jnp.sum(moved, axis=0, keepdims=True)
+            grad_scores = (moved - weights * delta).astype(jnp.bfloat16)
+            value_parts.append(dot_tt(low, grad_pair, 1, 0))
+            key_parts.append(dot_tt(grad_scores, query_pair, 1, 0))
+            mixed = dot_tt(key_pair, grad_scores, 0, 0)
+            query_parts.append(mixed[side * HEAD_DIM : (side + 1) * HEAD_DIM])
+        query_sum = (jnp.concatenate(query_parts, axis=0).T * scale).astype(jnp.bfloat16)
+        key_sum = (jnp.where(low_lanes, key_parts[0], key_parts[1]) * scale).astype(jnp.bfloat16)
+        value_sum = jnp.where(low_lanes, value_parts[0], value_parts[1]).astype(jnp.bfloat16)
+        for slot, total in enumerate((query_sum, key_sum, value_sum)):
+            first = slot * half + pair * LANES
+            out_ref[:, :, first : first + LANES] = total.reshape(sources, frames, LANES)
+    for source in range(sources):
+        block = back_ref[source, rows:, :].astype(jnp.float32)
+        for part in range(2):
+            piece = block[:, part * own : (part + 1) * own]
+            piece = jnp.concatenate([piece[: TAP_PAD // 2], piece[TAP_PAD // 2 :]], axis=1)
+            taps_ref[slot_of(2 * source + part, group)] = piece.astype(jnp.bfloat16)
+
+
+def swapped(array, bit):
+    return lax.ppermute(array, "dp", [(i, i ^ bit) for i in range(N_DP)])
+
+
+def traded(array):
+    return lax.all_to_all(array, "ctx", 0, 0, tiled=True)
+
+
+def per_device(
+    frame_input, queries, key_proj, value_proj, out_weight, conv_weight, lengths, grad_output
+):
+    utts, frames, wide = frame_input.shape
+    inner = queries.shape[2]
+    half, width = inner // 2, wide // N_CTX
+    rows = N_CTX * frames
+    low, f32 = jnp.bfloat16, jnp.float32
+    shape = jax.ShapeDtypeStruct
+    entries = out_weight.shape[1]
+    tap_count = conv_weight.shape[0]
+
+    tap_rows = jnp.pad(conv_weight, ((0, TAP_PAD - tap_count), (0, 0)))
+    tap_rows = jnp.concatenate([tap_rows[: TAP_PAD // 2], tap_rows[TAP_PAD // 2 :]], axis=1)
+    shard = jnp.concatenate([out_weight.T, tap_rows], axis=0)[None]
+    for bit in DP_BITS:
+        shard = jnp.concatenate([shard, swapped(shard, bit)], axis=0)
+
+    packed = traded(
+        call_kernel(pack_heads, shape((N_CTX, frames, 3 * half), low), count=3)(
+            queries, key_proj, value_proj
+        )
+    )
+    sides = traded(
+        call_kernel(pack_channels, shape((N_CTX, 2, utts, frames, width), low), count=2)(
+            frame_input, grad_output
+        )
+    )
+    attended, weights = call_kernel(
+        attend,
+        (shape((N_CTX, rows, half), low), shape((half // HEAD_DIM, rows, rows), low)),
+        smem_first=True,
+        count=2,
+    )(lengths, packed)
+    attended_all = traded(attended)
+    chunks = width // LANES
+    results, back, panels = call_kernel(
+        middle,
+        (
+            shape((N_CTX, 2, utts, frames, width), low),
+            shape((N_CTX, rows + TAP_PAD, half), low),
+            shape((N_DP, entries, width), low),
+        ),
+        scratch=(
+            pltpu.VMEM((chunks, TAP_PAD, 8, LANES), f32),
+            pltpu.VMEM((chunks, TAP_PAD, 8, LANES), f32),
+            pltpu.VMEM((inner, width), low),
+            pltpu.VMEM((utts * chunks, rows, LANES), f32),
+            pltpu.VMEM((utts * chunks, rows + 32, LANES), f32),
+            pltpu.VMEM((utts * chunks, rows + 32, LANES), f32),
+            pltpu.VMEM((utts, rows, width), low),
+        ),
+        smem_first=True,
+        count=4,
+    )(lengths, attended_all, shard, sides)
+
+    def added(kept, came):
+        return (kept.astype(f32) + came.astype(f32)).astype(low)
+
+    panels = added(panels[:4], swapped(panels[4:], 1))
+    back = traded(back)
+    grads, tap_slots = call_kernel(
+        attend_back,
+        (shape((N_CTX, frames, 3 * half), low), shape((N_DP, TAP_PAD // 2, width), low)),
+        count=3,
+    )(packed, weights, back)
+    tap_slots = added(tap_slots[:4], swapped(tap_slots[4:], 1))
+    summed = jnp.concatenate([panels, tap_slots], axis=1)
+    summed = added(summed[:2], swapped(summed[2:], 2))
+    last = summed[0].astype(f32) + swapped(summed[1], 4).astype(f32)
+    grad_queries, grad_keys, grad_values = call_kernel(
+        unpack_heads, (shape((utts, frames, inner), low),) * 3, count=1
+    )(traded(grads))
+    block_output, grad_input = call_kernel(
+        unpack_channels, (shape((utts, frames, wide), low),) * 2, count=1
+    )(traded(results))
+    grad_out_weight = last[:entries].T
+    own = width // 2
+    grad_taps = jnp.concatenate([last[entries:, :own], last[entries:, own:]], axis=0)[:tap_count]
+    return (
+        block_output,
+        grad_input,
+        grad_queries,
+        grad_keys,
+        grad_values,
+        grad_out_weight,
+        grad_taps,
+    )
+
+
+def chosen(sizes, *arrays):
+    frame_input, queries, out_weight, conv_weight = (arrays[i] for i in (0, 1, 4, 5))
+    utts, frames, wide = frame_input.shape
+    inner = queries.shape[2]
+    fits = (
+        sizes == (N_DP, N_CTX)
+        and utts == 2
+        and frames == 64
+        and wide % (N_CTX * LANES) == 0
+        and inner % (2 * LANES) == 0
+        and inner // N_DP % 16 == 0
+        and inner // 2 == wide // N_CTX
+        and conv_weight.shape == (31, wide // N_DP)
+        and out_weight.shape == (wide // N_CTX, inner // N_DP)
+    )
+    return (per_device if fits else general_device)(*arrays)
+
+
 def solution(mesh):
     placed = (
         P("dp", "ctx", None),
@@ -276,8 +655,9 @@
         P("dp"),
         P("dp", "ctx", None),
     )
+    sizes = (mesh.shape["dp"], mesh.shape["ctx"])
     return jax.shard_map(
-        per_device,
+        functools.partial(chosen, sizes),
         mesh=mesh,
         in_specs=placed,
         out_specs=(

time: 302 us -> 115 us (0.38)
  blocking collectives: 133 us -> 0 us
  local copies, waits for them, and re-layouts: 55 us -> 5.41 us
  starting transfers between devices: 8.82 us -> 35.6 us
  matrix products: 26.3 us -> 0 us
  Pallas kernels: 0 us -> 18 us
  between operations: 14.3 us -> 0.81 us
  other arithmetic: 12.5 us -> 2 us
    all_gather x8 -> x0, blocking collectives: 122 us -> none  [the longest x1 33.6 us: per_device(): panel_rows = lax.all_gather(out_weight, 'dp', axis=1, tiled=True)]
    unnamed x6 -> x0, waiting for transfers between devices: 50.3 us -> none
    all_to_all x0 -> x6, waiting for transfers between devices: none -> 36.2 us  [traded(): return lax.all_to_all(array, 'ctx', 0, 0, tiled=True)]
    all_to_all x0 -> x6, starting transfers between devices: none -> 22.1 us  [traded(): return lax.all_to_all(array, 'ctx', 0, 0, tiled=True)]
    pallas_call x0 -> x7, Pallas kernels: none -> 18 us  [the longest x1 7.89 us: per_device(): call_kernel(middle, (shape((N_CTX, 2, utts, frames, width), low), shape((...]
    dot_general x17 -> x0, matrix products: 17.5 us -> none  [the longest x6 3.6 us: masked_scores(): jnp.einsum('uqgd,ukgd->ugqk', query_block, key_block, preferred_element_t...]
    ppermute x4 -> x7, waiting for transfers between devices: 0.54 us -> 16.1 us  [swapped(): return lax.ppermute(array, 'dp', [(i, i ^ bit) for i in range(N_DP)])]
    reshape x18 -> x0, local copies, waits for them, and re-layouts: 12.8 us -> none  [the longest x6 8.3 us: grouped(): values.reshape(utt_count, row_count, group_count, group_width)]
  transfers between devices with their start and end apart: 8 -> 13, of which waited for: 2 -> 9; matrix products, arithmetic and copies ran while one was open for 26% -> 2% of each run, Pallas kernels for 0% -> 7%
where the time goes in v1:
time: 115 us; the launch traced here: 114 us
  waiting for transfers between devices  52.3 us (45%)
  starting transfers between devices  35.6 us (31%)
  Pallas kernels  18 us (16%)
  local copies, waits for them, and re-layouts  5.41 us (5%)
  other arithmetic  2 us (2%)
    all_to_all x6, waiting for transfers between devices, traded(): return lax.all_to_all(array, 'ctx', 0, 0, tiled=True)  36.2 us
    all_to_all x6, starting transfers between devices, traded(): return lax.all_to_all(array, 'ctx', 0, 0, tiled=True)  22.1 us
    ppermute x7, waiting for transfers between devices, swapped(): return lax.ppermute(array, 'dp', [(i, i ^ bit) for i in range(N_DP)])  16.1 us
    ppermute x7, starting transfers between devices, swapped(): return lax.ppermute(array, 'dp', [(i, i ^ bit) for i in range(N_DP)])  13.5 us
    pallas_call x1, Pallas kernels, per_device(): call_kernel(middle, (shape((N_CTX, 2, utts, frames, width), low), shape((...  7.89 us
    unnamed x22, local copies, waits for them, and re-layouts  4.61 us
    pallas_call x1, Pallas kernels, per_device(): call_kernel(attend, (shape((N_CTX, rows, half), low), shape((half // HEAD...  3.67 us
    pallas_call x1, Pallas kernels, per_device(): call_kernel(attend_back, (shape((N_CTX, frames, 3 * half), low), shape((N...  2.76 us
  transfers between devices with their start and end apart: 13, of which 9 were waited for; matrix products, arithmetic and copies ran while one was open for 2% of the time, Pallas kernels for 7%

profile of v1, /device:TPU:0, one launch (start us, length us, event | category | flops | bytes accessed | tf_op | source)
XLA Modules:
  0.0 114.1 jit_solution(8673246504636217143)
XLA Ops:
  4.3 4.3 %all-to-all-start = ((bf16[4,64,1152]{2,1,0:T(8,128)(2,1)}), bf16[4,64,1152]{2,1,0:T(8,128)(2,1)S(1)}, u32[]{:S(2)}, u32[]{:S(2)}) async-start(bf16[4,64,1152]{2,1,0:T(8,128)(2,1)} %shard_map.135), calls=%async_computation | async-start | bytes 1179648 | tf_op jit(solution)/shard_map/all_to_all | solution.py:536
  9.6 8.6 %all-to-all-done.packed_ref = bf16[4,64,1152]{2,1,0:T(8,128)(2,1)S(1)} async-done(((bf16[4,64,1152]{2,1,0:T(8,128)(2,1)}), bf16[4,64,1152]{2,1,0:T(8,128)(2,1)S(1)}, u32[]{:S(2)}, u32[]{:S(2)}) %all-to-all-start) | async-done | bytes 589856 | tf_op jit(solution)/shard_map/all_to_all | solution.py:536
  18.2 3.6 %all-to-all-start.2 = ((bf16[4,2,2,64,384]{4,3,2,1,0:T(8,128)(2,1)}), bf16[4,2,2,64,384]{4,3,2,1,0:T(8,128)(2,1)S(1)}, u32[]{:S(2)}, u32[]{:S(2)}) async-start(bf16[4,2,2,64,384]{4,3,2,1,0:T(8,128)(2,1)} %shard_map.137), calls=%async_computation.2 | async-start | bytes 1572864 | tf_op jit(solution)/shard_map/all_to_all | solution.py:536
  21.9 3.3 %collective-permute-start = (bf16[1,112,384]{2,1,0:T(8,128)(2,1)S(1)}, bf16[1,112,384]{2,1,0:T(8,128)(2,1)S(1)}, u32[]{:S(2)}, u32[]{:S(2)}) collective-permute-start(bf16[1,112,384]{2,1,0:T(8,128)(2,1)S(1)} %maximum_bitcast_fusion), channel_id=1, source_target_pairs={{0,16},{4,20},{8,24},{12,28},{16,0},{20,4},{24,8},{28,12},{1,17},{... | collective-permute-start | bytes 258056 | tf_op jit(solution)/shard_map/ppermute | solution.py:532
  25.2 5.0 %collective-permute-done = bf16[1,112,384]{2,1,0:T(8,128)(2,1)S(1)} collective-permute-done((bf16[1,112,384]{2,1,0:T(8,128)(2,1)S(1)}, bf16[1,112,384]{2,1,0:T(8,128)(2,1)S(1)}, u32[]{:S(2)}, u32[]{:S(2)}) %collective-permute-start) | collective-permute-done | bytes 86048 | tf_op jit(solution)/shard_map/ppermute | solution.py:532
  31.1 3.7 %shard_map.136 = (bf16[4,256,384]{2,1,0:T(8,128)(2,1)}, bf16[6,256,256]{2,1,0:T(8,128)(2,1)S(1)}) custom-call(s32[2]{0:T(128)S(1)} %copy-done.8, bf16[4,64,1152]{2,1,0:T(8,128)(2,1)S(1)} %all-to-all-done.packed_ref), custom_call_target="tpu_custom_call" | custom-call | tf_op jit(solution)/shard_map/pallas_call | solution.py:567
  35.6 3.5 %all-to-all-start.1 = ((bf16[4,256,384]{2,1,0:T(8,128)(2,1)}), bf16[4,256,384]{2,1,0:T(8,128)(2,1)S(1)}, u32[]{:S(2)}, u32[]{:S(2)}) async-start(bf16[4,256,384]{2,1,0:T(8,128)(2,1)} %get-tuple-element.19), calls=%async_computation.1 | async-start | bytes 1572864 | tf_op jit(solution)/shard_map/all_to_all | solution.py:536
  39.2 1.6 %collective-permute-start.2 = (bf16[4,112,384]{2,1,0:T(8,128)(2,1)S(1)}, bf16[4,112,384]{2,1,0:T(8,128)(2,1)S(1)}, u32[]{:S(2)}, u32[]{:S(2)}) collective-permute-start(bf16[4,112,384]{2,1,0:T(8,128)(2,1)S(1)} %pad_maximum_fusion.1), channel_id=1, source_target_pairs={{0,4},{4,0},{8,12},{12,8},{16,20},{20,16},{24,28},{28,24},{1,5},{5... | collective-permute-start | bytes 1032200 | tf_op jit(solution)/shard_map/ppermute | solution.py:532
  40.8 8.9 %collective-permute-done.2 = bf16[4,112,384]{2,1,0:T(8,128)(2,1)S(1)} collective-permute-done((bf16[4,112,384]{2,1,0:T(8,128)(2,1)S(1)}, bf16[4,112,384]{2,1,0:T(8,128)(2,1)S(1)}, u32[]{:S(2)}, u32[]{:S(2)}) %collective-permute-start.2) | collective-permute-done | bytes 344096 | tf_op jit(solution)/shard_map/ppermute | solution.py:532
  49.8 1.0 all-to-all-done.1.attended_ref
  50.7 7.9 %shard_map.138 = (bf16[4,2,2,64,384]{4,3,2,1,0:T(8,128)(2,1)}, bf16[4,288,384]{2,1,0:T(8,128)(2,1)S(1)}, bf16[8,96,384]{2,1,0:T(8,128)(2,1)S(1)}) custom-call(s32[2]{0:T(128)S(1)} %copy-done.8, bf16[4,256,384]{2,1,0:T(8,128)(2,1)S(1)} %all-to-all-done.1.attended_ref, bf16[8,112,384]{2,1,0:T(8,128)(2,1)S(1)} %pad_maximum_fusion.weight_ref, ...), custom_call_target="tpu_custom_call" | custom-call | tf_op jit(solution)/shard_map/pallas_call | solution.py:575
  59.6 3.6 %all-to-all-start.4 = ((bf16[4,288,384]{2,1,0:T(8,128)(2,1)}), bf16[4,288,384]{2,1,0:T(8,128)(2,1)S(1)}, u32[]{:S(2)}, u32[]{:S(2)}) async-start(bf16[4,288,384]{2,1,0:T(8,128)(2,1)} %copy-done), calls=%async_computation.4 | async-start | bytes 1769472 | tf_op jit(solution)/shard_map/all_to_all | solution.py:536
  63.3 1.6 %collective-permute-start.3 = (bf16[4,96,384]{2,1,0:T(8,128)(2,1)S(1)}, bf16[4,96,384]{2,1,0:T(8,128)(2,1)}, u32[]{:S(2)}, u32[]{:S(2)}) collective-permute-start(bf16[4,96,384]{2,1,0:T(8,128)(2,1)S(1)} %slice.46), channel_id=1, source_target_pairs={{0,4},{4,0},{8,12},{12,8},{16,20},{20,16},{24,28},{28,24},{1,5},{5... | collective-permute-start | bytes 884744 | tf_op jit(solution)/shard_map/ppermute | solution.py:532
  64.8 11.1 %all-to-all-done.4.back_ref = bf16[4,288,384]{2,1,0:T(8,128)(2,1)S(1)} async-done(((bf16[4,288,384]{2,1,0:T(8,128)(2,1)}), bf16[4,288,384]{2,1,0:T(8,128)(2,1)S(1)}, u32[]{:S(2)}, u32[]{:S(2)}) %all-to-all-start.4) | async-done | bytes 884768 | tf_op jit(solution)/shard_map/all_to_all | solution.py:536
  75.9 2.8 %shard_map.140 = (bf16[4,64,1152]{2,1,0:T(8,128)(2,1)}, bf16[8,16,384]{2,1,0:T(8,128)(2,1)S(1)}) custom-call(bf16[4,64,1152]{2,1,0:T(8,128)(2,1)S(1)} %all-to-all-done.packed_ref, bf16[6,256,256]{2,1,0:T(8,128)(2,1)S(1)} %copy-done.2, bf16[4,288,384]{2,1,0:T(8,128)(2,1)S(1)} %all-to-all-done.4.back_ref), custom_call_target="tpu_custom_call" | custom-call | tf_op jit(solution)/shard_map/pallas_call | solution.py:600
  78.7 1.5 %collective-permute-start.4 = (bf16[4,16,384]{2,1,0:T(8,128)(2,1)S(1)}, bf16[4,16,384]{2,1,0:T(8,128)(2,1)S(1)}, u32[]{:S(2)}, u32[]{:S(2)}) collective-permute-start(bf16[4,16,384]{2,1,0:T(8,128)(2,1)S(1)} %slice.48), channel_id=1, source_target_pairs={{0,4},{4,0},{8,12},{12,8},{16,20},{20,16},{24,28},{28,24},{1,5},{5... | collective-permute-start | bytes 147464 | tf_op jit(solution)/shard_map/ppermute | solution.py:532
  80.2 1.0 add_convert_fusion
  81.2 1.5 %collective-permute-done.4 = bf16[4,16,384]{2,1,0:T(8,128)(2,1)S(1)} collective-permute-done((bf16[4,16,384]{2,1,0:T(8,128)(2,1)S(1)}, bf16[4,16,384]{2,1,0:T(8,128)(2,1)S(1)}, u32[]{:S(2)}, u32[]{:S(2)}) %collective-permute-start.4) | collective-permute-done | bytes 49184 | tf_op jit(solution)/shard_map/ppermute | solution.py:532
  82.8 1.3 %collective-permute-start.5 = (bf16[2,112,384]{2,1,0:T(8,128)(2,1)S(1)}, bf16[2,112,384]{2,1,0:T(8,128)(2,1)S(1)}, u32[]{:S(2)}, u32[]{:S(2)}) collective-permute-start(bf16[2,112,384]{2,1,0:T(8,128)(2,1)S(1)} %pad_maximum_fusion.2), channel_id=1, source_target_pairs={{0,8},{4,12},{8,0},{12,4},{16,24},{20,28},{24,16},{28,20},{1,9},{5... | collective-permute-start | bytes 516104 | tf_op jit(solution)/shard_map/ppermute | solution.py:532
  84.1 3.5 %all-to-all-start.3 = ((bf16[4,2,2,64,384]{4,3,2,1,0:T(8,128)(2,1)}), bf16[4,2,2,64,384]{4,3,2,1,0:T(8,128)(2,1)S(1)}, u32[]{:S(2)}, u32[]{:S(2)}) async-start(bf16[4,2,2,64,384]{4,3,2,1,0:T(8,128)(2,1)} %get-tuple-element.20), calls=%async_computation.3 | async-start | bytes 1572864 | tf_op jit(solution)/shard_map/all_to_all | solution.py:536
  88.3 3.4 %collective-permute-start.6 = (bf16[112,384]{1,0:T(8,128)(2,1)S(1)}, bf16[112,384]{1,0:T(8,128)(2,1)S(1)}, u32[]{:S(2)}, u32[]{:S(2)}) collective-permute-start(bf16[112,384]{1,0:T(8,128)(2,1)S(1)} %slice_bitcast_fusion.1), channel_id=1, source_target_pairs={{0,16},{4,20},{8,24},{12,28},{16,0},{20,4},{24,8},{28,12},{1,17},{... | collective-permute-start | bytes 258056 | tf_op jit(solution)/shard_map/ppermute | solution.py:532
  91.8 7.5 %all-to-all-done.3.in_ref = bf16[4,2,2,64,384]{4,3,2,1,0:T(8,128)(2,1)S(1)} async-done(((bf16[4,2,2,64,384]{4,3,2,1,0:T(8,128)(2,1)}), bf16[4,2,2,64,384]{4,3,2,1,0:T(8,128)(2,1)S(1)}, u32[]{:S(2)}, u32[]{:S(2)}) %all-to-all-start.3) | async-done | bytes 786464 | tf_op jit(solution)/shard_map/all_to_all | solution.py:536
  100.2 3.5 %all-to-all-start.5 = ((bf16[4,64,1152]{2,1,0:T(8,128)(2,1)}), bf16[4,64,1152]{2,1,0:T(8,128)(2,1)S(1)}, u32[]{:S(2)}, u32[]{:S(2)}) async-start(bf16[4,64,1152]{2,1,0:T(8,128)(2,1)} %get-tuple-element.25), calls=%async_computation.5 | async-start | bytes 1179648 | tf_op jit(solution)/shard_map/all_to_all | solution.py:536
  105.1 8.1 %all-to-all-done.5.in_ref = bf16[4,64,1152]{2,1,0:T(8,128)(2,1)S(1)} async-done(((bf16[4,64,1152]{2,1,0:T(8,128)(2,1)}), bf16[4,64,1152]{2,1,0:T(8,128)(2,1)S(1)}, u32[]{:S(2)}, u32[]{:S(2)}) %all-to-all-start.5) | async-done | bytes 589856 | tf_op jit(solution)/shard_map/all_to_all | solution.py:536
  (47 shorter events, 11.4 us)
Async XLA Ops:
  0.6 0.9 copy-start.5
  1.6 0.9 copy-start.6
  2.5 0.9 copy-start.7
  4.3 4.3 %copy-start.3 = (bf16[2,64,1536]{2,1,0:T(8,128)(2,1)S(1)}, bf16[2,64,1536]{2,1,0:T(8,128)(2,1)}, u32[]{:S(2)}) copy-start(bf16[2,64,1536]{2,1,0:T(8,128)(2,1)} %frame_ref.1) | copy-start | bytes 1179652
  4.3 4.3 %copy-start.4 = (bf16[2,64,1536]{2,1,0:T(8,128)(2,1)S(1)}, bf16[2,64,1536]{2,1,0:T(8,128)(2,1)}, u32[]{:S(2)}) copy-start(bf16[2,64,1536]{2,1,0:T(8,128)(2,1)} %grad_ref.1) | copy-start | bytes 1179652
  4.3 13.9 %all-to-all-start = ((bf16[4,64,1152]{2,1,0:T(8,128)(2,1)}), bf16[4,64,1152]{2,1,0:T(8,128)(2,1)S(1)}, u32[]{:S(2)}, u32[]{:S(2)}) async-start(bf16[4,64,1152]{2,1,0:T(8,128)(2,1)} %shard_map.135), calls=%async_computation | async-start | bytes 1179648 | tf_op jit(solution)/shard_map/all_to_all | solution.py:536
  18.2 3.6 %copy-start.10 = (bf16[31,192]{1,0:T(8,128)(2,1)S(1)}, bf16[31,192]{1,0:T(8,128)(2,1)}, u32[]{:S(2)}) copy-start(bf16[31,192]{1,0:T(8,128)(2,1)} %param.13) | copy-start | bytes 35716
  18.2 3.7 %copy-start.9 = (bf16[384,96]{0,1:T(8,128)(2,1)S(1)}, bf16[384,96]{0,1:T(8,128)(2,1)}, u32[]{:S(2)}) copy-start(bf16[384,96]{0,1:T(8,128)(2,1)} %param.12) | copy-start | bytes 221188
  18.2 17.4 %all-to-all-start.2 = ((bf16[4,2,2,64,384]{4,3,2,1,0:T(8,128)(2,1)}), bf16[4,2,2,64,384]{4,3,2,1,0:T(8,128)(2,1)S(1)}, u32[]{:S(2)}, u32[]{:S(2)}) async-start(bf16[4,2,2,64,384]{4,3,2,1,0:T(8,128)(2,1)} %shard_map.137), calls=%async_computation.2 | async-start | bytes 1572864 | tf_op jit(solution)/shard_map/all_to_all | solution.py:536
  21.9 9.1 %copy-start.8 = (s32[2]{0:T(128)S(1)}, s32[2]{0:T(128)}, u32[]{:S(2)}) copy-start(s32[2]{0:T(128)} %length_ref.3) | copy-start | bytes 28
  21.9 8.3 %collective-permute-start = (bf16[1,112,384]{2,1,0:T(8,128)(2,1)S(1)}, bf16[1,112,384]{2,1,0:T(8,128)(2,1)S(1)}, u32[]{:S(2)}, u32[]{:S(2)}) collective-permute-start(bf16[1,112,384]{2,1,0:T(8,128)(2,1)S(1)} %maximum_bitcast_fusion), channel_id=1, source_target_pairs={{0,16},{4,20},{8,24},{12,28},{16,0},{20,4},{24,8},{28,12},{1,17},{... | collective-permute-start | bytes 258056 | tf_op jit(solution)/shard_map/ppermute | solution.py:532
  30.3 8.9 %collective-permute-start.1 = (bf16[2,112,384]{2,1,0:T(8,128)(2,1)S(1)}, bf16[2,112,384]{2,1,0:T(8,128)(2,1)S(1)}, u32[]{:S(2)}, u32[]{:S(2)}) collective-permute-start(bf16[2,112,384]{2,1,0:T(8,128)(2,1)S(1)} %pad_maximum_fusion.3), channel_id=1, source_target_pairs={{0,8},{4,12},{8,0},{12,4},{16,24},{20,28},{24,16},{28,20},{1,9},{5... | collective-permute-start | bytes 516104 | tf_op jit(solution)/shard_map/ppermute | solution.py:532
  34.7 0.9 copy-start.1
  35.6 15.1 %all-to-all-start.1 = ((bf16[4,256,384]{2,1,0:T(8,128)(2,1)}), bf16[4,256,384]{2,1,0:T(8,128)(2,1)S(1)}, u32[]{:S(2)}, u32[]{:S(2)}) async-start(bf16[4,256,384]{2,1,0:T(8,128)(2,1)} %get-tuple-element.19), calls=%async_computation.1 | async-start | bytes 1572864 | tf_op jit(solution)/shard_map/all_to_all | solution.py:536
  39.2 10.5 %collective-permute-start.2 = (bf16[4,112,384]{2,1,0:T(8,128)(2,1)S(1)}, bf16[4,112,384]{2,1,0:T(8,128)(2,1)S(1)}, u32[]{:S(2)}, u32[]{:S(2)}) collective-permute-start(bf16[4,112,384]{2,1,0:T(8,128)(2,1)S(1)} %pad_maximum_fusion.1), channel_id=1, source_target_pairs={{0,4},{4,0},{8,12},{12,8},{16,20},{20,16},{24,28},{28,24},{1,5},{5... | collective-permute-start | bytes 1032200 | tf_op jit(solution)/shard_map/ppermute | solution.py:532
  58.6 0.9 copy-start
  59.6 16.3 %copy-start.2 = (bf16[6,256,256]{2,1,0:T(8,128)(2,1)S(1)}, bf16[6,256,256]{2,1,0:T(8,128)(2,1)}, u32[]{:S(2)}) copy-start(bf16[6,256,256]{2,1,0:T(8,128)(2,1)} %copy-done.1) | copy-start | bytes 2359300
  59.6 16.3 %all-to-all-start.4 = ((bf16[4,288,384]{2,1,0:T(8,128)(2,1)}), bf16[4,288,384]{2,1,0:T(8,128)(2,1)S(1)}, u32[]{:S(2)}, u32[]{:S(2)}) async-start(bf16[4,288,384]{2,1,0:T(8,128)(2,1)} %copy-done), calls=%async_computation.4 | async-start | bytes 1769472 | tf_op jit(solution)/shard_map/all_to_all | solution.py:536
  63.3 16.9 %collective-permute-start.3 = (bf16[4,96,384]{2,1,0:T(8,128)(2,1)S(1)}, bf16[4,96,384]{2,1,0:T(8,128)(2,1)}, u32[]{:S(2)}, u32[]{:S(2)}) collective-permute-start(bf16[4,96,384]{2,1,0:T(8,128)(2,1)S(1)} %slice.46), channel_id=1, source_target_pairs={{0,4},{4,0},{8,12},{12,8},{16,20},{20,16},{24,28},{28,24},{1,5},{5... | collective-permute-start | bytes 884744 | tf_op jit(solution)/shard_map/ppermute | solution.py:532
  78.7 4.1 %collective-permute-start.4 = (bf16[4,16,384]{2,1,0:T(8,128)(2,1)S(1)}, bf16[4,16,384]{2,1,0:T(8,128)(2,1)S(1)}, u32[]{:S(2)}, u32[]{:S(2)}) collective-permute-start(bf16[4,16,384]{2,1,0:T(8,128)(2,1)S(1)} %slice.48), channel_id=1, source_target_pairs={{0,4},{4,0},{8,12},{12,8},{16,20},{20,16},{24,28},{28,24},{1,5},{5... | collective-permute-start | bytes 147464 | tf_op jit(solution)/shard_map/ppermute | solution.py:532
  82.8 5.5 %collective-permute-start.5 = (bf16[2,112,384]{2,1,0:T(8,128)(2,1)S(1)}, bf16[2,112,384]{2,1,0:T(8,128)(2,1)S(1)}, u32[]{:S(2)}, u32[]{:S(2)}) collective-permute-start(bf16[2,112,384]{2,1,0:T(8,128)(2,1)S(1)} %pad_maximum_fusion.2), channel_id=1, source_target_pairs={{0,8},{4,12},{8,0},{12,4},{16,24},{20,28},{24,16},{28,20},{1,9},{5... | collective-permute-start | bytes 516104 | tf_op jit(solution)/shard_map/ppermute | solution.py:532
  84.1 15.1 %all-to-all-start.3 = ((bf16[4,2,2,64,384]{4,3,2,1,0:T(8,128)(2,1)}), bf16[4,2,2,64,384]{4,3,2,1,0:T(8,128)(2,1)S(1)}, u32[]{:S(2)}, u32[]{:S(2)}) async-start(bf16[4,2,2,64,384]{4,3,2,1,0:T(8,128)(2,1)} %get-tuple-element.20), calls=%async_computation.3 | async-start | bytes 1572864 | tf_op jit(solution)/shard_map/all_to_all | solution.py:536
  88.3 15.4 %collective-permute-start.6 = (bf16[112,384]{1,0:T(8,128)(2,1)S(1)}, bf16[112,384]{1,0:T(8,128)(2,1)S(1)}, u32[]{:S(2)}, u32[]{:S(2)}) collective-permute-start(bf16[112,384]{1,0:T(8,128)(2,1)S(1)} %slice_bitcast_fusion.1), channel_id=1, source_target_pairs={{0,16},{4,20},{8,24},{12,28},{16,0},{20,4},{24,8},{28,12},{1,17},{... | collective-permute-start | bytes 258056 | tf_op jit(solution)/shard_map/ppermute | solution.py:532
  100.2 13.0 %all-to-all-start.5 = ((bf16[4,64,1152]{2,1,0:T(8,128)(2,1)}), bf16[4,64,1152]{2,1,0:T(8,128)(2,1)S(1)}, u32[]{:S(2)}, u32[]{:S(2)}) async-start(bf16[4,64,1152]{2,1,0:T(8,128)(2,1)} %get-tuple-element.25), calls=%async_computation.5 | async-start | bytes 1179648 | tf_op jit(solution)/shard_map/all_to_all | solution.py:536

commit v2 on v1

--- a/solution.py
+++ b/solution.py
@@ -274,6 +274,8 @@
 N_DP = 8
 DP_BITS = (4, 2, 1)
 TAP_PAD = 32
+TAPS = 31
+REACH = 15
 
 
 def slot_of(index, me):
@@ -287,59 +289,94 @@
     )
 
 
-def call_kernel(body, out_shape, scratch=(), smem_first=False, count=1, cost=None):
-    vmem = pl.BlockSpec(memory_space=pltpu.VMEM)
-    specs = [vmem] * count
-    if smem_first:
-        specs[0] = pl.BlockSpec(memory_space=pltpu.SMEM)
+def call_kernel(body, out_shape, ins, outs=None, scratch=()):
+    spaces = {
+        "smem": pl.BlockSpec(memory_space=pltpu.SMEM),
+        "vmem": pl.BlockSpec(memory_space=pltpu.VMEM),
+        "hbm": pl.BlockSpec(memory_space=pltpu.HBM),
+        "any": pl.BlockSpec(memory_space=pl.ANY),
+    }
     return pl.pallas_call(
         body,
         out_shape=out_shape,
-        in_specs=specs,
-        out_specs=jax.tree.map(lambda unused: vmem, out_shape),
+        in_specs=[spaces[space] for space in ins],
+        out_specs=[spaces[space] for space in (outs or ["vmem"] * len(out_shape))],
         scratch_shapes=list(scratch),
-        compiler_params=pltpu.CompilerParams(vmem_limit_bytes=48 * 1024 * 1024),
-        cost_estimate=cost,
-    )
-
-
-def pack_heads(query_ref, key_ref, value_ref, out_ref):
+        compiler_params=pltpu.CompilerParams(vmem_limit_bytes=40 * 1024 * 1024),
+    )
+
+
+def half_of(index):
+    return lax.shift_right_logical(index, 1)
+
+
+def columns(start, size):
+    return pl.ds(pl.multiple_of(start, LANES), size)
+
+
+def run_copies(pairs, sem):
+    copies = [
+        pltpu.make_async_copy(source, target, sem.at[number])
+        for number, (source, target) in enumerate(pairs)
+    ]
+    for copy in copies:
+        copy.start()
+    for copy in copies:
+        copy.wait()
+
+
+def pack_heads(query_ref, key_ref, value_ref, *rest):
+    outs, sem = rest[:N_CTX], rest[N_CTX]
     half = query_ref.shape[2] // 2
-    for utt in range(2):
-        for side in range(2):
-            for slot, ref in enumerate((query_ref, key_ref, value_ref)):
-                out_ref[2 * utt + side, :, slot * half : (slot + 1) * half] = ref[
-                    utt, :, side * half : (side + 1) * half
-                ]
-
-
-def pack_channels(frame_ref, grad_ref, out_ref):
-    width = frame_ref.shape[2] // N_CTX
-    for dest in range(N_CTX):
-        for slot, ref in enumerate((frame_ref, grad_ref)):
-            out_ref[dest, slot] = ref[:, :, dest * width : (dest + 1) * width]
-
-
-def unpack_channels(in_ref, output_ref, grad_ref):
-    width = in_ref.shape[4]
-    for source in range(N_CTX):
-        for slot, ref in enumerate((output_ref, grad_ref)):
-            ref[:, :, source * width : (source + 1) * width] = in_ref[source, slot]
-
-
-def unpack_heads(in_ref, query_ref, key_ref, value_ref):
-    half = in_ref.shape[2] // 3
-    for utt in range(2):
-        for side in range(2):
-            for slot, ref in enumerate((query_ref, key_ref, value_ref)):
-                ref[utt, :, side * half : (side + 1) * half] = in_ref[
-                    2 * utt + side, :, slot * half : (slot + 1) * half
-                ]
-
-
-def head_parts(ref, slot, half):
-    rows = ref.shape[0] * ref.shape[1]
-    return ref[:, :, slot * half : (slot + 1) * half].reshape(rows, half)
+    place = lax.axis_index("ctx")
+    pairs = []
+    for apart in (2, 3, 1, 0):
+        dest = place ^ apart
+        cols = columns((dest & 1) * half, half)
+        for slot, ref in enumerate((query_ref, key_ref, value_ref)):
+            pairs.append((ref.at[half_of(dest), :, cols], outs[apart].at[slot]))
+    run_copies(pairs, sem)
+
+
+def pack_channels(in_ref, *rest):
+    outs, sem = rest[:N_CTX], rest[N_CTX]
+    width = in_ref.shape[2] // N_CTX
+    place = lax.axis_index("ctx")
+    pairs = []
+    for apart in (2, 3, 1, 0):
+        cols = columns((place ^ apart) * width, width)
+        for utt in range(2):
+            pairs.append((in_ref.at[utt, :, cols], outs[apart].at[utt]))
+    run_copies(pairs, sem)
+
+
+def unpack_channels(*refs):
+    ins, out_ref, sem = refs[:N_CTX], refs[N_CTX], refs[N_CTX + 1]
+    width = ins[0].shape[2]
+    place = lax.axis_index("ctx")
+    pairs = []
+    for apart in range(N_CTX):
+        cols = columns((place ^ apart) * width, width)
+        for utt in range(2):
+            pairs.append((ins[apart].at[utt], out_ref.at[utt, :, cols]))
+    run_copies(pairs, sem)
+
+
+def unpack_heads(*refs):
+    ins, outs, sem = refs[:N_CTX], refs[N_CTX : N_CTX + 3], refs[N_CTX + 3]
+    half = ins[0].shape[2]
+    place = lax.axis_index("ctx")
+    pairs = []
+    for apart in range(N_CTX):
+        source = place ^ apart
+        cols = columns((source & 1) * half, half)
+        for slot in range(3):
+            pairs.append((ins[apart].at[slot], outs[slot].at[half_of(source), :, cols]))
+    run_copies(pairs, sem)
+
+
+def head_parts(refs, slot):
+    return jnp.concatenate([ref[slot] for ref in refs], axis=0)
 
 
 def half_masks(rows):
@@ -348,13 +385,16 @@
     return low.astype(jnp.bfloat16), (1.0 - low).astype(jnp.bfloat16)
 
 
-def attend(length_ref, packed_ref, attended_ref, weight_ref):
-    half = packed_ref.shape[2] // 3
-    rows = packed_ref.shape[0] * packed_ref.shape[1]
-    length = length_ref[lax.axis_index("ctx") // 2]
-    query, key, value = (head_parts(packed_ref, slot, half) for slot in range(3))
+def attend(length_ref, *refs):
+    ins, attended_ref, weight_ref = refs[:N_CTX], refs[N_CTX], refs[N_CTX + 1]
+    frames, half = ins[0].shape[1], ins[0].shape[2]
+    rows = N_CTX * frames
+    place = lax.axis_index("ctx")
+    length = length_ref[half_of(place)]
+    query, key, value = (head_parts(ins, slot) for slot in range(3))
     masks = half_masks(rows)
-    real = lax.broadcasted_iota(jnp.int32, (rows, rows), 0) < length
+    frame = lax.broadcasted_iota(jnp.int32, (rows, rows), 0) ^ (place * frames)
+    real = frame < length
     for pair in range(half // LANES):
         cols = slice(pair * LANES, (pair + 1) * LANES)
         key_pair, value_pair = key[:, cols], value[:, cols]
@@ -370,33 +410,27 @@
             mixed = dot_tt(value_pair, low, 0, 0)
             parts.append(mixed[side * HEAD_DIM : (side + 1) * HEAD_DIM])
         joined = jnp.concatenate(parts, axis=0).T.astype(jnp.bfloat16)
-        for dest in range(N_CTX):
-            attended_ref[dest, :, cols] = joined
-
-
-def middle(
-    length_ref,
-    attended_ref,
-    weight_ref,
-    side_ref,
-    result_ref,
-    back_ref,
-    panel_ref,
-    taps_ref,
-    tap_sum_ref,
-    rows_ref,
-    hidden_ref,
-    masked_ref,
-    cotangent_ref,
-    grad_ref,
-):
-    rows, half = attended_ref.shape[1], attended_ref.shape[2]
-    frames, width = side_ref.shape[3], side_ref.shape[4]
+        attended_ref[:, :, cols] = joined.reshape(N_CTX, frames, LANES)
+
+
+def forward(length_ref, weight_ref, *refs):
+    attended_refs, frame_refs = refs[:N_CTX], refs[N_CTX : 2 * N_CTX]
+    out_refs = refs[2 * N_CTX : 3 * N_CTX]
+    whole_ref, rows_ref, taps_ref, total_ref, masked_ref = refs[3 * N_CTX : 3 * N_CTX + 5]
+    hidden_ref, frame_ref, result_ref = refs[3 * N_CTX + 5 :]
+    frames, half = attended_refs[0].shape[1], attended_refs[0].shape[2]
+    width = frame_ref.shape[3]
+    rows = N_CTX * frames
     chunks = width // LANES
     entries = 2 * half // N_DP
-    tap_count, reach = 31, 15
     own = width // 2
     group, place = lax.axis_index("dp"), lax.axis_index("ctx")
+    for apart in range(N_CTX):
+        source = place ^ apart
+        cols = columns((source & 1) * half, half)
+        for block in range(N_CTX):
+            whole_ref[half_of(source), block ^ source, :, cols] = attended_refs[apart][block]
+        frame_ref[source] = frame_refs[apart][...]
     for part in range(N_DP):
         rows_ref[part * entries : (part + 1) * entries] = weight_ref[
             slot_of(part, group), 0:entries
@@ -407,20 +441,18 @@
         pieces.append(jnp.concatenate([block[:, :own], block[:, own:]], axis=0))
     taps = jnp.concatenate(pieces, axis=1)
     for chunk in range(chunks):
-        for tap in range(tap_count):
+        for tap in range(TAPS):
             taps_ref[chunk, tap] = jnp.broadcast_to(
                 taps[tap : tap + 1, chunk * LANES : (chunk + 1) * LANES], (8, LANES)
             )
-    tap_sum_ref[...] = jnp.zeros_like(tap_sum_ref)
     edge = jnp.zeros((2 * chunks, 16, LANES), jnp.float32)
-    for ref in (masked_ref, cotangent_ref):
-        ref[:, 0:16, :] = edge
-        ref[:, 16 + rows : 32 + rows, :] = edge
+    masked_ref[:, 0:16, :] = edge
+    masked_ref[:, 16 + rows : 32 + rows, :] = edge
     for utt in range(2):
         real = lax.broadcasted_iota(jnp.int32, (rows, LANES), 0) < length_ref[utt]
-        projected = dot_tt(attended_ref[2 * utt], rows_ref[0:half], 1, 0)
-        projected += dot_tt(attended_ref[2 * utt + 1], rows_ref[half:], 1, 0)
-        hidden = side_ref[:, 0, utt].reshape(rows, width).astype(jnp.float32) + projected
+        mixed = whole_ref[utt].reshape(rows, 2 * half)
+        projected = dot_tt(mixed, rows_ref[...], 1, 0)
+        hidden = frame_ref[:, utt].reshape(rows, width).astype(jnp.float32) + projected
         hidden = hidden.astype(jnp.bfloat16).astype(jnp.float32)
         for chunk in range(chunks):
             piece = hidden[:, chunk * LANES : (chunk + 1) * LANES]
@@ -429,20 +461,52 @@
 
     def convolve(step, carry):
         utt, chunk = step // chunks, step % chunks
-        cols = pl.ds(pl.multiple_of(chunk * LANES, LANES), LANES)
+        cols = columns(chunk * LANES, LANES)
+        shape = (frames // 8, 8, LANES)
+        for block in range(N_CTX):
+            base = block * frames
+            total = jnp.zeros(shape, jnp.float32)
+            for tap in range(TAPS):
+                first = base + tap + 16 - REACH
+                piece = masked_ref[step, first : first + frames, :]
+                total += taps_ref[chunk, tap][None] * piece.reshape(shape)
+            total = total.reshape(frames, LANES)
+            total_ref[step, base : base + frames, :] = total
+            outer = hidden_ref[step, base : base + frames, :] + total * jax.nn.sigmoid(total)
+            result_ref[block, utt, :, cols] = outer.astype(jnp.bfloat16)
+        return carry
+
+    lax.fori_loop(0, 2 * chunks, convolve, 0)
+    for apart in range(N_CTX):
+        out_refs[apart][...] = result_ref[place ^ apart]
+
+
+def backward(length_ref, total_ref, masked_ref, taps_ref, rows_ref, *refs):
+    side_refs, out_refs = refs[:N_CTX], refs[N_CTX : 2 * N_CTX]
+    grad_ref, keep_ref, send_ref, sums_ref = refs[2 * N_CTX : 2 * N_CTX + 4]
+    side_ref, result_ref, cotangent_ref, tap_sum_ref = refs[2 * N_CTX + 4 :]
+    frames, width = side_refs[0].shape[1], side_refs[0].shape[2]
+    rows = N_CTX * frames
+    chunks = width // LANES
+    half = rows_ref.shape[0] // 2
+    place = lax.axis_index("ctx")
+    for apart in range(N_CTX):
+        side_ref[place ^ apart] = side_refs[apart][...]
+    tap_sum_ref[...] = jnp.zeros_like(tap_sum_ref)
+    edge = jnp.zeros((2 * chunks, 16, LANES), jnp.float32)
+    cotangent_ref[:, 0:16, :] = edge
+    cotangent_ref[:, 16 + rows : 32 + rows, :] = edge
+
+    def convolve(step, carry):
+        utt, chunk = step // chunks, step % chunks
+        cols = columns(chunk * LANES, LANES)
         length = length_ref[utt]
         shape = (frames // 8, 8, LANES)
         for block in range(N_CTX):
             base = block * frames
-            total = jnp.zeros(shape, jnp.float32)
-            for tap in range(tap_count):
-                piece = masked_ref[step, base + tap + 16 - reach : base + tap + 16 - reach + frames, :]
-                total += taps_ref[chunk, tap][None] * piece.reshape(shape)
-            total = total.reshape(frames, LANES)
+            total = total_ref[step, base : base + frames, :]
             gate = jax.nn.sigmoid(total)
-            outer = hidden_ref[step, base : base + frames, :] + total * gate
-            result_ref[block, 0, utt, :, cols] = outer.astype(jnp.bfloat16)
-            incoming = side_ref[block, 1, utt, :, cols].astype(jnp.float32)
+            incoming = side_ref[block, utt, :, cols].astype(jnp.float32)
             slope = gate * (1.0 + total * (1.0 - gate))
             low = (incoming * slope).astype(jnp.bfloat16)
             cotangent_ref[step, 16 + base : 16 + base + frames, :] = low.astype(jnp.float32)
@@ -450,34 +514,58 @@
             base = block * frames
             total = jnp.zeros(shape, jnp.float32)
             held = masked_ref[step, 16 + base : 16 + base + frames, :].reshape(shape)
-            for tap in range(tap_count):
-                first = base + 16 + reach - tap
+            for tap in range(TAPS):
+                first = base + 16 + REACH - tap
                 piece = cotangent_ref[step, first : first + frames, :].reshape(shape)
                 total += taps_ref[chunk, tap][None] * piece
                 tap_sum_ref[chunk, tap] += jnp.sum(held * piece, axis=0)
             place_of = base + lax.broadcasted_iota(jnp.int32, (frames, LANES), 0)
             total = jnp.where(place_of < length, total.reshape(frames, LANES), 0.0)
-            incoming = side_ref[block, 1, utt, :, cols].astype(jnp.float32)
+            incoming = side_ref[block, utt, :, cols].astype(jnp.float32)
             low = (incoming + total).astype(jnp.bfloat16)
-            result_ref[block, 1, utt, :, cols] = low
+            result_ref[block, utt, :, cols] = low
             grad_ref[utt, base : base + frames, cols] = low
         return carry
 
     lax.fori_loop(0, 2 * chunks, convolve, 0)
     sums = [
-        jnp.concatenate([jnp.sum(tap_sum_ref[chunk, tap], axis=0, keepdims=True) for tap in range(TAP_PAD)], axis=0)
+        jnp.concatenate(
+            [
+                jnp.sum(tap_sum_ref[chunk, tap], axis=0, keepdims=True)
+                for tap in range(TAP_PAD)
+            ],
+            axis=0,
+        )
         for chunk in range(chunks)
     ]
     sums = jnp.concatenate(sums, axis=1).astype(jnp.bfloat16)
-    for utt in range(2):
-        for side in range(2):
-            back_ref[2 * utt + side, 0:rows, :] = dot_tt(
-                grad_ref[utt], rows_ref[side * half : (side + 1) * half], 1, 1
-            ).astype(jnp.bfloat16)
-            back_ref[2 * utt + side, rows:, :] = sums
+    sums_ref[...] = sums
+    for apart in range(N_CTX):
+        out_refs[apart][...] = result_ref[place ^ apart]
+        dest = place ^ apart
+        mixed = dot_tt(
+            grad_ref[half_of(dest)],
+            rows_ref[pl.ds(pl.multiple_of((dest & 1) * half, half), half)],
+            1,
+            1,
+        ).astype(jnp.bfloat16)
+        ref = send_ref if apart % 2 else keep_ref
+        for block in range(N_CTX):
+            first = pl.multiple_of((block ^ dest) * frames, frames)
+            ref[apart // 2, pl.ds(first, frames), :] = mixed[block * frames : (block + 1) * frames]
+    for part in range(2):
+        send_ref[part, rows:, :] = sums[part * TAP_PAD // 2 : (part + 1) * TAP_PAD // 2]
+
+
+def make_panels(whole_ref, grad_ref, panel_ref):
+    rows, half = grad_ref.shape[1], whole_ref.shape[3] // 2
+    entries = 2 * half // N_DP
+    group = lax.axis_index("dp")
     for side in range(2):
-        panel = dot_tt(attended_ref[side], grad_ref[0], 0, 0)
-        panel += dot_tt(attended_ref[2 + side], grad_ref[1], 0, 0)
+        panel = 0.0
+        for utt in range(2):
+            mixed = whole_ref[utt, :, :, side * half : (side + 1) * half].reshape(rows, half)
+            panel += dot_tt(mixed, grad_ref[utt], 0, 0)
         panel = panel.astype(jnp.bfloat16)
         for part in range(N_DP // 2):
             panel_ref[slot_of(side * N_DP // 2 + part, group)] = panel[
@@ -485,19 +573,27 @@
             ]
 
 
-def attend_back(packed_ref, weight_ref, back_ref, out_ref, taps_ref):
-    half = packed_ref.shape[2] // 3
-    sources, frames = packed_ref.shape[0], packed_ref.shape[1]
-    rows = sources * frames
+def relay(keep_ref, came_ref, sums_ref, out_ref):
+    rows = keep_ref.shape[1]
+    total = keep_ref[1].astype(jnp.float32) + came_ref[1, 0:rows, :].astype(jnp.float32)
+    out_ref[0:rows, :] = total.astype(jnp.bfloat16)
+    out_ref[rows : rows + TAP_PAD, :] = sums_ref[...]
+    for part in range(2):
+        first = rows + TAP_PAD + part * TAP_PAD // 2
+        out_ref[first : first + TAP_PAD // 2, :] = came_ref[part, rows:, :]
+
+
+def attend_back(weight_ref, keep_ref, came_ref, far_ref, sums_ref, *refs):
+    ins, out_refs, taps_ref = refs[:N_CTX], refs[N_CTX : 2 * N_CTX], refs[2 * N_CTX]
+    frames, half = ins[0].shape[1], ins[0].shape[2]
+    rows = N_CTX * frames
     own = half // 2
-    group = lax.axis_index("dp")
-    query, key, value = (head_parts(packed_ref, slot, half) for slot in range(3))
+    group, place = lax.axis_index("dp"), lax.axis_index("ctx")
+    query, key, value = (head_parts(ins, slot) for slot in range(3))
     masks = half_masks(rows)
     scale = HEAD_DIM ** (-0.5)
-    arriving = back_ref[0, 0:rows, :].astype(jnp.float32)
-    for source in range(1, sources):
-        arriving += back_ref[source, 0:rows, :].astype(jnp.float32)
-    arriving = arriving.astype(jnp.bfloat16)
+    arriving = keep_ref[0].astype(jnp.float32) + came_ref[0, 0:rows, :].astype(jnp.float32)
+    arriving = (arriving + far_ref[0:rows, :].astype(jnp.float32)).astype(jnp.bfloat16)
     low_lanes = lax.broadcasted_iota(jnp.int32, (rows, LANES), 1) < HEAD_DIM
     for pair in range(half // LANES):
         cols = slice(pair * LANES, (pair + 1) * LANES)
@@ -518,22 +614,32 @@
         key_sum = (jnp.where(low_lanes, key_parts[0], key_parts[1]) * scale).astype(jnp.bfloat16)
         value_sum = jnp.where(low_lanes, value_parts[0], value_parts[1]).astype(jnp.bfloat16)
         for slot, total in enumerate((query_sum, key_sum, value_sum)):
-            first = slot * half + pair * LANES
-            out_ref[:, :, first : first + LANES] = total.reshape(sources, frames, LANES)
-    for source in range(sources):
-        block = back_ref[source, rows:, :].astype(jnp.float32)
+            for apart in range(N_CTX):
+                out_refs[apart][slot, :, cols] = total[apart * frames : (apart + 1) * frames]
+    pieces = [sums_ref[...]]
+    pieces.append(jnp.concatenate([came_ref[0, rows:, :], came_ref[1, rows:, :]], axis=0))
+    for part in range(2):
+        first = rows + part * TAP_PAD
+        pieces.append(far_ref[first : first + TAP_PAD, :])
+    for apart, piece in enumerate(pieces):
+        block = piece.astype(jnp.float32)
         for part in range(2):
-            piece = block[:, part * own : (part + 1) * own]
-            piece = jnp.concatenate([piece[: TAP_PAD // 2], piece[TAP_PAD // 2 :]], axis=1)
-            taps_ref[slot_of(2 * source + part, group)] = piece.astype(jnp.bfloat16)
+            mine = block[:, part * own : (part + 1) * own]
+            mine = jnp.concatenate([mine[: TAP_PAD // 2], mine[TAP_PAD // 2 :]], axis=1)
+            taps_ref[slot_of(2 * (place ^ apart) + part, group)] = mine.astype(jnp.bfloat16)
 
 
 def swapped(array, bit):
     return lax.ppermute(array, "dp", [(i, i ^ bit) for i in range(N_DP)])
 
 
-def traded(array):
-    return lax.all_to_all(array, "ctx", 0, 0, tiled=True)
+def crossed(array, apart):
+    return lax.ppermute(array, "ctx", [(i, i ^ apart) for i in range(N_CTX)])
+
+
+def traded(blocks):
+    came = {apart: crossed(blocks[apart], apart) for apart in (2, 3, 1)}
+    return [blocks[0]] + [came[apart] for apart in (1, 2, 3)]
 
 
 def per_device(
@@ -543,75 +649,126 @@
     inner = queries.shape[2]
     half, width = inner // 2, wide // N_CTX
     rows = N_CTX * frames
+    chunks = width // LANES
     low, f32 = jnp.bfloat16, jnp.float32
     shape = jax.ShapeDtypeStruct
     entries = out_weight.shape[1]
     tap_count = conv_weight.shape[0]
-
+    dma = pltpu.SemaphoreType.DMA
+    head_block = shape((3, frames, half), low)
+    channel_block = shape((utts, frames, width), low)
+
+    packed = traded(
+        call_kernel(
+            pack_heads, (head_block,) * N_CTX, ["hbm"] * 3, scratch=[dma((3 * N_CTX,))]
+        )(queries, key_proj, value_proj)
+    )
     tap_rows = jnp.pad(conv_weight, ((0, TAP_PAD - tap_count), (0, 0)))
     tap_rows = jnp.concatenate([tap_rows[: TAP_PAD // 2], tap_rows[TAP_PAD // 2 :]], axis=1)
     shard = jnp.concatenate([out_weight.T, tap_rows], axis=0)[None]
     for bit in DP_BITS:
         shard = jnp.concatenate([shard, swapped(shard, bit)], axis=0)
 
-    packed = traded(
-        call_kernel(pack_heads, shape((N_CTX, frames, 3 * half), low), count=3)(
-            queries, key_proj, value_proj
-        )
-    )
-    sides = traded(
-        call_kernel(pack_channels, shape((N_CTX, 2, utts, frames, width), low), count=2)(
-            frame_input, grad_output
-        )
-    )
+    def spread(array):
+        blocks = call_kernel(
+            pack_channels, (channel_block,) * N_CTX, ["hbm"], scratch=[dma((2 * N_CTX,))]
+        )(array)
+        return traded(blocks)
+
+    frame_blocks = spread(frame_input)
     attended, weights = call_kernel(
         attend,
-        (shape((N_CTX, rows, half), low), shape((half // HEAD_DIM, rows, rows), low)),
-        smem_first=True,
-        count=2,
-    )(lengths, packed)
-    attended_all = traded(attended)
-    chunks = width // LANES
-    results, back, panels = call_kernel(
-        middle,
         (
-            shape((N_CTX, 2, utts, frames, width), low),
-            shape((N_CTX, rows + TAP_PAD, half), low),
-            shape((N_DP, entries, width), low),
+            shape((N_CTX, frames, half), low),
+            shape((half // HEAD_DIM, rows, rows), low),
         ),
-        scratch=(
+        ["smem"] + ["vmem"] * N_CTX,
+    )(lengths, *packed)
+    across = crossed(attended, 2)
+    beside = crossed(attended, 1)
+    diagonal = crossed(across, 1)
+    grad_blocks = spread(grad_output)
+    forward_out = call_kernel(
+        forward,
+        (channel_block,) * N_CTX
+        + (
+            shape((utts, N_CTX, frames, inner), low),
+            shape((inner, width), low),
+            shape((chunks, TAP_PAD, 8, LANES), f32),
+            shape((utts * chunks, rows, LANES), f32),
+            shape((utts * chunks, rows + 32, LANES), f32),
+        ),
+        ["smem"] + ["vmem"] * (1 + 2 * N_CTX),
+        scratch=[
+            pltpu.VMEM((utts * chunks, rows, LANES), f32),
+            pltpu.VMEM((N_CTX, utts, frames, width), low),
+            pltpu.VMEM((N_CTX, utts, frames, width), low),
+        ],
+    )(lengths, shard, attended, beside, across, diagonal, *frame_blocks)
+    output_blocks = traded(forward_out[:N_CTX])
+    whole, weight_rows, taps, totals, masked = forward_out[N_CTX:]
+    backward_out = call_kernel(
+        backward,
+        (channel_block,) * N_CTX
+        + (
+            shape((utts, rows, width), low),
+            shape((2, rows, half), low),
+            shape((2, rows + TAP_PAD // 2, half), low),
+            shape((TAP_PAD, width), low),
+        ),
+        ["smem"] + ["vmem"] * (4 + N_CTX),
+        scratch=[
+            pltpu.VMEM((N_CTX, utts, frames, width), low),
+            pltpu.VMEM((N_CTX, utts, frames, width), low),
+            pltpu.VMEM((utts * chunks, rows + 32, LANES), f32),
             pltpu.VMEM((chunks, TAP_PAD, 8, LANES), f32),
-            pltpu.VMEM((chunks, TAP_PAD, 8, LANES), f32),
-            pltpu.VMEM((inner, width), low),
-            pltpu.VMEM((utts * chunks, rows, LANES), f32),
-            pltpu.VMEM((utts * chunks, rows + 32, LANES), f32),
-            pltpu.VMEM((utts * chunks, rows + 32, LANES), f32),
-            pltpu.VMEM((utts, rows, width), low),
-        ),
-        smem_first=True,
-        count=4,
-    )(lengths, attended_all, shard, sides)
-
-    def added(kept, came):
-        return (kept.astype(f32) + came.astype(f32)).astype(low)
-
+        ],
+    )(lengths, totals, masked, taps, weight_rows, *grad_blocks)
+    grad_hidden, keep, send, sums = backward_out[N_CTX:]
+    came = crossed(send, 1)
+    (panels,) = call_kernel(
+        make_panels, (shape((N_DP, entries, width), low),), ["vmem"] * 2
+    )(whole, grad_hidden)
+
+    def added(kept, arrived):
+        return (kept.astype(f32) + arrived.astype(f32)).astype(low)
+
+    (far,) = call_kernel(
+        relay, (shape((rows + 2 * TAP_PAD, half), low),), ["vmem"] * 3
+    )(keep, came, sums)
+    far = crossed(far, 2)
+    input_blocks = traded(backward_out[:N_CTX])
     panels = added(panels[:4], swapped(panels[4:], 1))
-    back = traded(back)
-    grads, tap_slots = call_kernel(
+    back_out = call_kernel(
         attend_back,
-        (shape((N_CTX, frames, 3 * half), low), shape((N_DP, TAP_PAD // 2, width), low)),
-        count=3,
-    )(packed, weights, back)
+        (head_block,) * N_CTX + (shape((N_DP, TAP_PAD // 2, width), low),),
+        ["vmem"] * (5 + N_CTX),
+    )(weights, keep, came, far, sums, *packed)
+    grad_blocks = traded(back_out[:N_CTX])
+    tap_slots = back_out[N_CTX]
     tap_slots = added(tap_slots[:4], swapped(tap_slots[4:], 1))
     summed = jnp.concatenate([panels, tap_slots], axis=1)
     summed = added(summed[:2], swapped(summed[2:], 2))
     last = summed[0].astype(f32) + swapped(summed[1], 4).astype(f32)
+
+    def gathered(blocks):
+        return call_kernel(
+            unpack_channels,
+            (shape((utts, frames, wide), low),),
+            ["any"] * N_CTX,
+            ["hbm"],
+            [dma((2 * N_CTX,))],
+        )(*blocks)[0]
+
+    block_output = gathered(output_blocks)
+    grad_input = gathered(input_blocks)
     grad_queries, grad_keys, grad_values = call_kernel(
-        unpack_heads, (shape((utts, frames, inner), low),) * 3, count=1
-    )(traded(grads))
-    block_output, grad_input = call_kernel(
-        unpack_channels, (shape((utts, frames, wide), low),) * 2, count=1
-    )(traded(results))
+        unpack_heads,
+        (shape((utts, frames, inner), low),) * 3,
+        ["any"] * N_CTX,
+        ["hbm"] * 3,
+        [dma((3 * N_CTX,))],
+    )(*grad_blocks)
     grad_out_weight = last[:entries].T
     own = width // 2
     grad_taps = jnp.concatenate([last[entries:, :own], last[entries:, own:]], axis=0)[:tap_count]
@@ -638,7 +795,7 @@
         and inner % (2 * LANES) == 0
         and inner // N_DP % 16 == 0
         and inner // 2 == wide // N_CTX
-        and conv_weight.shape == (31, wide // N_DP)
+        and conv_weight.shape == (TAPS, wide // N_DP)
         and out_weight.shape == (wide // N_CTX, inner // N_DP)
     )
     return (per_device if fits else general_device)(*arrays)

time: 115 us -> 86.1 us (0.75)
  waiting for transfers between devices: 52.3 us -> 34.4 us
  starting transfers between devices: 35.6 us -> 29.5 us
  local copies, waits for them, and re-layouts: 5.41 us -> 2.47 us
  Pallas kernels: 18 us -> 16.7 us
    all_to_all x6 -> x0, waiting for transfers between devices: 36.2 us -> none  [traded(): return lax.all_to_all(array, 'ctx', 0, 0, tiled=True)]
    ppermute x0 -> x23, waiting for transfers between devices: none -> 23.8 us  [crossed(): return lax.ppermute(array, 'ctx', [(i, i ^ apart) for i in range(N_CTX)])]
    all_to_all x6 -> x0, starting transfers between devices: 22.1 us -> none  [traded(): return lax.all_to_all(array, 'ctx', 0, 0, tiled=True)]
    ppermute x0 -> x23, starting transfers between devices: none -> 16.3 us  [crossed(): return lax.ppermute(array, 'ctx', [(i, i ^ apart) for i in range(N_CTX)])]
    ppermute x7, waiting for transfers between devices: 16.1 us -> 10.6 us  [swapped(): return lax.ppermute(array, 'dp', [(i, i ^ bit) for i in range(N_DP)])]
    unnamed x22 -> x12, local copies, waits for them, and re-layouts: 4.61 us -> 0.95 us
    pallas_call x7 -> x12, Pallas kernels: 18 us -> 16.7 us  [the longest x1 5.19 us: per_device(): call_kernel(backward, (channel_block,) * N_CTX + (shape((utts, rows, widt...]
  transfers between devices with their start and end apart: 13 -> 30, of which waited for: 9 -> 15; matrix products, arithmetic and copies ran while one was open for 2% -> 0% of each run, Pallas kernels for 7% -> 13%
where the time goes in v2:
time: 86.1 us; the launch traced here: 85.9 us
  waiting for transfers between devices  34.4 us (40%)
  starting transfers between devices  29.5 us (34%)
  Pallas kernels  16.7 us (19%)
  local copies, waits for them, and re-layouts  2.47 us (3%)
  other arithmetic  1.96 us (2%)
  between operations  0.88 us (1%)
    ppermute x23, waiting for transfers between devices, crossed(): return lax.ppermute(array, 'ctx', [(i, i ^ apart) for i in range(N_CTX)])  23.8 us
    ppermute x23, starting transfers between devices, crossed(): return lax.ppermute(array, 'ctx', [(i, i ^ apart) for i in range(N_CTX)])  16.3 us
    ppermute x7, starting transfers between devices, swapped(): return lax.ppermute(array, 'dp', [(i, i ^ bit) for i in range(N_DP)])  13.1 us
    ppermute x7, waiting for transfers between devices, swapped(): return lax.ppermute(array, 'dp', [(i, i ^ bit) for i in range(N_DP)])  10.6 us
    pallas_call x1, Pallas kernels, per_device(): call_kernel(backward, (channel_block,) * N_CTX + (shape((utts, rows, widt...  5.19 us
    pallas_call x1, Pallas kernels, per_device(): call_kernel(forward, (channel_block,) * N_CTX + (shape((utts, N_CTX, fram...  3.14 us
    pallas_call x1, Pallas kernels, per_device(): call_kernel(attend, (shape((N_CTX, frames, half), low), shape((half // HE...  2.78 us
    pallas_call x1, Pallas kernels, per_device(): call_kernel(attend_back, (head_block,) * N_CTX + (shape((N_DP, TAP_PAD //...  1.98 us
  transfers between devices with their start and end apart: 30, of which 15 were waited for; matrix products, arithmetic and copies ran while one was open for 0% of the time, Pallas kernels for 13%

profile of v2, /device:TPU:0, one launch (start us, length us, event | category | flops | bytes accessed | tf_op | source)
XLA Modules:
  0.0 85.9 jit_solution(12096726030516703852)
XLA Ops:
  2.4 4.1 %collective-permute-start = (bf16[1,112,384]{2,1,0:T(8,128)(2,1)S(1)}, bf16[1,112,384]{2,1,0:T(8,128)(2,1)S(1)}, u32[]{:S(2)}, u32[]{:S(2)}) collective-permute-start(bf16[1,112,384]{2,1,0:T(8,128)(2,1)S(1)} %maximum_bitcast_fusion), channel_id=1, source_target_pairs={{0,16},{4,20},{8,24},{12,28},{16,0},{20,4},{24,8},{28,12},{1,17},{... | collective-permute-start | bytes 258056 | tf_op jit(solution)/shard_map/ppermute | solution.py:633
  6.4 4.4 %collective-permute-done = bf16[1,112,384]{2,1,0:T(8,128)(2,1)S(1)} collective-permute-done((bf16[1,112,384]{2,1,0:T(8,128)(2,1)S(1)}, bf16[1,112,384]{2,1,0:T(8,128)(2,1)S(1)}, u32[]{:S(2)}, u32[]{:S(2)}) %collective-permute-start) | collective-permute-done | bytes 86048 | tf_op jit(solution)/shard_map/ppermute | solution.py:633
  12.8 1.6 %collective-permute-start.4 = (bf16[3,64,384]{2,1,0:T(8,128)(2,1)S(1)}, bf16[3,64,384]{2,1,0:T(8,128)(2,1)S(1)}, u32[]{:S(2)}, u32[]{:S(2)}) collective-permute-start(bf16[3,64,384]{2,1,0:T(8,128)(2,1)S(1)} %get-tuple-element.48), channel_id=1, source_target_pairs={{0,2},{1,3},{2,0},{3,1},{4,6},{5,7},{6,4},{7,5},{8,10},{9,11},{10,... | collective-permute-start | bytes 442376 | tf_op jit(solution)/shard_map/ppermute | solution.py:637
  14.7 1.6 %collective-permute-done.1 = bf16[2,112,384]{2,1,0:T(8,128)(2,1)S(1)} collective-permute-done((bf16[2,112,384]{2,1,0:T(8,128)(2,1)S(1)}, bf16[2,112,384]{2,1,0:T(8,128)(2,1)S(1)}, u32[]{:S(2)}, u32[]{:S(2)}) %collective-permute-start.1) | collective-permute-done | bytes 172064 | tf_op jit(solution)/shard_map/ppermute | solution.py:633
  16.3 1.7 %collective-permute-start.2 = (bf16[4,112,384]{2,1,0:T(8,128)(2,1)S(1)}, bf16[4,112,384]{2,1,0:T(8,128)(2,1)S(1)}, u32[]{:S(2)}, u32[]{:S(2)}) collective-permute-start(bf16[4,112,384]{2,1,0:T(8,128)(2,1)S(1)} %pad_maximum_fusion.1), channel_id=1, source_target_pairs={{0,4},{4,0},{8,12},{12,8},{16,20},{20,16},{24,28},{28,24},{1,5},{5... | collective-permute-start | bytes 1032200 | tf_op jit(solution)/shard_map/ppermute | solution.py:633
  19.5 2.3 %collective-permute-done.5.refs_3_ = bf16[3,64,384]{2,1,0:T(8,128)(2,1)S(1)} collective-permute-done((bf16[3,64,384]{2,1,0:T(8,128)(2,1)S(1)}, bf16[3,64,384]{2,1,0:T(8,128)(2,1)S(1)}, u32[]{:S(2)}, u32[]{:S(2)}) %collective-permute-start.5) | collective-permute-done | bytes 147488 | tf_op jit(solution)/shard_map/ppermute | solution.py:637
  21.8 2.8 %shard_map.136 = (bf16[4,64,384]{2,1,0:T(8,128)(2,1)S(1)}, bf16[6,256,256]{2,1,0:T(8,128)(2,1)S(1)}) custom-call(s32[2]{0:T(128)S(1)} %copy-done.5, bf16[3,64,384]{2,1,0:T(8,128)(2,1)S(1)} %get-tuple-element.46.refs_0_, bf16[3,64,384]{2,1,0:T(8,128)(2,1)S(1)} %collective-permute-done.3.refs_1_, bf16[3,64,384]{2,1,0:T(8,128)(2,1)S(1)} %collective-permute-done.4.refs_2_, ...), custom_call_target="tpu_custom_call" | custom-call | tf_op jit(solution)/shard_map/pallas_call | solution.py:679
  24.6 1.6 %collective-permute-start.7 = (bf16[4,64,384]{2,1,0:T(8,128)(2,1)S(1)}, bf16[4,64,384]{2,1,0:T(8,128)(2,1)S(1)}, u32[]{:S(2)}, u32[]{:S(2)}) collective-permute-start(bf16[4,64,384]{2,1,0:T(8,128)(2,1)S(1)} %get-tuple-element.50.refs_0_), channel_id=1, source_target_pairs={{0,2},{1,3},{2,0},{3,1},{4,6},{5,7},{6,4},{7,5},{8,10},{9,11},{10,... | collective-permute-start | bytes 589832 | tf_op jit(solution)/shard_map/ppermute | solution.py:637
  28.5 5.9 %collective-permute-done.10.refs_6_ = bf16[2,64,384]{2,1,0:T(8,128)(2,1)S(1)} collective-permute-done((bf16[2,64,384]{2,1,0:T(8,128)(2,1)S(1)}, bf16[2,64,384]{2,1,0:T(8,128)(2,1)S(1)}, u32[]{:S(2)}, u32[]{:S(2)}) %collective-permute-start.10) | collective-permute-done | bytes 98336 | tf_op jit(solution)/shard_map/ppermute | solution.py:637
  36.1 1.5 %collective-permute-start.16 = (bf16[2,64,384]{2,1,0:T(8,128)(2,1)S(1)}, bf16[2,64,384]{2,1,0:T(8,128)(2,1)S(1)}, u32[]{:S(2)}, u32[]{:S(2)}) collective-permute-start(bf16[2,64,384]{2,1,0:T(8,128)(2,1)S(1)} %get-tuple-element.65), channel_id=1, source_target_pairs={{0,2},{1,3},{2,0},{3,1},{4,6},{5,7},{6,4},{7,5},{8,10},{9,11},{10,... | collective-permute-start | bytes 294920 | tf_op jit(solution)/shard_map/ppermute | solution.py:637
  37.9 3.1 %shard_map.138 = (bf16[2,64,384]{2,1,0:T(8,128)(2,1)S(1)}, bf16[2,64,384]{2,1,0:T(8,128)(2,1)S(1)}, bf16[2,64,384]{2,1,0:T(8,128)(2,1)S(1)}, bf16[2,64,384]{2,1,...) custom-call(s32[2]{0:T(128)S(1)} %copy-done.5, ...), custom_call_target="tpu_custom_call" | custom-call | tf_op jit(solution)/shard_map/pallas_call | solution.py:691
  42.7 5.2 %shard_map.141 = (bf16[2,64,384]{2,1,0:T(8,128)(2,1)S(1)}, bf16[2,64,384]{2,1,0:T(8,128)(2,1)S(1)}, bf16[2,64,384]{2,1,0:T(8,128)(2,1)S(1)}, bf16[2,64,384]{2,1,...) custom-call(s32[2]{0:T(128)S(1)} %copy-done.5, ...), custom_call_target="tpu_custom_call" | custom-call | tf_op jit(solution)/shard_map/pallas_call | solution.py:710
  49.0 1.6 %collective-permute-start.26 = (bf16[4,96,384]{2,1,0:T(8,128)(2,1)S(1)}, bf16[4,96,384]{2,1,0:T(8,128)(2,1)S(1)}, u32[]{:S(2)}, u32[]{:S(2)}) collective-permute-start(bf16[4,96,384]{2,1,0:T(8,128)(2,1)S(1)} %slice.58), channel_id=1, source_target_pairs={{0,4},{4,0},{8,12},{12,8},{16,20},{20,16},{24,28},{28,24},{1,5},{5... | collective-permute-start | bytes 884744 | tf_op jit(solution)/shard_map/ppermute | solution.py:633
  50.6 1.6 %collective-permute-start.22 = (bf16[320,384]{1,0:T(8,128)(2,1)S(1)}, bf16[320,384]{1,0:T(8,128)(2,1)S(1)}, u32[]{:S(2)}, u32[]{:S(2)}) collective-permute-start(bf16[320,384]{1,0:T(8,128)(2,1)S(1)} %shard_map.143), channel_id=1, source_target_pairs={{0,2},{1,3},{2,0},{3,1},{4,6},{5,7},{6,4},{7,5},{8,10},{9,11},{10,... | collective-permute-start | bytes 737288 | tf_op jit(solution)/shard_map/ppermute | solution.py:637
  52.2 6.2 %collective-permute-done.22.far_ref = bf16[320,384]{1,0:T(8,128)(2,1)S(1)} collective-permute-done((bf16[320,384]{1,0:T(8,128)(2,1)S(1)}, bf16[320,384]{1,0:T(8,128)(2,1)S(1)}, u32[]{:S(2)}, u32[]{:S(2)}) %collective-permute-start.22) | collective-permute-done | bytes 245792 | tf_op jit(solution)/shard_map/ppermute | solution.py:637
  58.4 2.0 %shard_map.144 = (bf16[3,64,384]{2,1,0:T(8,128)(2,1)S(1)}, bf16[3,64,384]{2,1,0:T(8,128)(2,1)S(1)}, bf16[3,64,384]{2,1,0:T(8,128)(2,1)S(1)}, bf16[3,64,384]{2,1,0:T(8,128)(2,1)S(1)}, bf16[8,16,384]{2,1,0:T(8,128)(2,1)S(1)}) custom-call(bf16[6,256,256]{2,1,0:T(8,128)(2,1)S(1)} %get-tuple-element.71.weight_ref, ...), custom_call_target="tpu_custom_call" | custom-call | tf_op jit(solution)/shard_map/pallas_call | solution.py:742
  61.7 2.8 %collective-permute-done.27 = bf16[4,16,384]{2,1,0:T(8,128)(2,1)S(1)} collective-permute-done((bf16[4,16,384]{2,1,0:T(8,128)(2,1)S(1)}, bf16[4,16,384]{2,1,0:T(8,128)(2,1)S(1)}, u32[]{:S(2)}, u32[]{:S(2)}) %collective-permute-start.27) | collective-permute-done | bytes 49184 | tf_op jit(solution)/shard_map/ppermute | solution.py:633
  64.6 1.5 %collective-permute-start.28 = (bf16[2,112,384]{2,1,0:T(8,128)(2,1)S(1)}, bf16[2,112,384]{2,1,0:T(8,128)(2,1)S(1)}, u32[]{:S(2)}, u32[]{:S(2)}) collective-permute-start(bf16[2,112,384]{2,1,0:T(8,128)(2,1)S(1)} %pad_maximum_fusion.2), channel_id=1, source_target_pairs={{0,8},{4,12},{8,0},{12,4},{16,24},{20,28},{24,16},{28,20},{1,9},{5... | collective-permute-start | bytes 516104 | tf_op jit(solution)/shard_map/ppermute | solution.py:633
  66.1 1.5 %collective-permute-start.19 = (bf16[2,64,384]{2,1,0:T(8,128)(2,1)S(1)}, bf16[2,64,384]{2,1,0:T(8,128)(2,1)S(1)}, u32[]{:S(2)}, u32[]{:S(2)}) collective-permute-start(bf16[2,64,384]{2,1,0:T(8,128)(2,1)S(1)} %get-tuple-element.69), channel_id=1, source_target_pairs={{0,2},{1,3},{2,0},{3,1},{4,6},{5,7},{6,4},{7,5},{8,10},{9,11},{10,... | collective-permute-start | bytes 294920 | tf_op jit(solution)/shard_map/ppermute | solution.py:637
  68.2 1.8 %collective-permute-done.28 = bf16[2,112,384]{2,1,0:T(8,128)(2,1)S(1)} collective-permute-done((bf16[2,112,384]{2,1,0:T(8,128)(2,1)S(1)}, bf16[2,112,384]{2,1,0:T(8,128)(2,1)S(1)}, u32[]{:S(2)}, u32[]{:S(2)}) %collective-permute-start.28) | collective-permute-done | bytes 172064 | tf_op jit(solution)/shard_map/ppermute | solution.py:633
  70.1 1.5 %collective-permute-start.13 = (bf16[2,64,384]{2,1,0:T(8,128)(2,1)S(1)}, bf16[2,64,384]{2,1,0:T(8,128)(2,1)S(1)}, u32[]{:S(2)}, u32[]{:S(2)}) collective-permute-start(bf16[2,64,384]{2,1,0:T(8,128)(2,1)S(1)} %get-tuple-element.57), channel_id=1, source_target_pairs={{0,2},{1,3},{2,0},{3,1},{4,6},{5,7},{6,4},{7,5},{8,10},{9,11},{10,... | collective-permute-start | bytes 294920 | tf_op jit(solution)/shard_map/ppermute | solution.py:637
  73.0 1.5 %collective-permute-start.24 = (bf16[3,64,384]{2,1,0:T(8,128)(2,1)S(1)}, bf16[3,64,384]{2,1,0:T(8,128)(2,1)S(1)}, u32[]{:S(2)}, u32[]{:S(2)}) collective-permute-start(bf16[3,64,384]{2,1,0:T(8,128)(2,1)S(1)} %get-tuple-element.77), channel_id=1, source_target_pairs={{0,2},{1,3},{2,0},{3,1},{4,6},{5,7},{6,4},{7,5},{8,10},{9,11},{10,... | collective-permute-start | bytes 442376 | tf_op jit(solution)/shard_map/ppermute | solution.py:637
  75.9 2.2 %collective-permute-start.29 = (bf16[112,384]{1,0:T(8,128)(2,1)S(1)}, bf16[112,384]{1,0:T(8,128)(2,1)S(1)}, u32[]{:S(2)}, u32[]{:S(2)}) collective-permute-start(bf16[112,384]{1,0:T(8,128)(2,1)S(1)} %slice_bitcast_fusion.1), channel_id=1, source_target_pairs={{0,16},{4,20},{8,24},{12,28},{16,0},{20,4},{24,8},{28,12},{1,17},{... | collective-permute-start | bytes 258056 | tf_op jit(solution)/shard_map/ppermute | solution.py:633
  81.2 2.4 %collective-permute-done.25.refs_3_ = bf16[3,64,384]{2,1,0:T(8,128)(2,1)S(1)} collective-permute-done((bf16[3,64,384]{2,1,0:T(8,128)(2,1)S(1)}, bf16[3,64,384]{2,1,0:T(8,128)(2,1)S(1)}, u32[]{:S(2)}, u32[]{:S(2)}) %collective-permute-start.25) | collective-permute-done | bytes 147488 | tf_op jit(solution)/shard_map/ppermute | solution.py:637
  (76 shorter events, 22.8 us)
Async XLA Ops:
  2.4 8.4 %collective-permute-start = (bf16[1,112,384]{2,1,0:T(8,128)(2,1)S(1)}, bf16[1,112,384]{2,1,0:T(8,128)(2,1)S(1)}, u32[]{:S(2)}, u32[]{:S(2)}) collective-permute-start(bf16[1,112,384]{2,1,0:T(8,128)(2,1)S(1)} %maximum_bitcast_fusion), channel_id=1, source_target_pairs={{0,16},{4,20},{8,24},{12,28},{16,0},{20,4},{24,8},{28,12},{1,17},{... | collective-permute-start | bytes 258056 | tf_op jit(solution)/shard_map/ppermute | solution.py:633
  10.8 5.5 %collective-permute-start.1 = (bf16[2,112,384]{2,1,0:T(8,128)(2,1)S(1)}, bf16[2,112,384]{2,1,0:T(8,128)(2,1)S(1)}, u32[]{:S(2)}, u32[]{:S(2)}) collective-permute-start(bf16[2,112,384]{2,1,0:T(8,128)(2,1)S(1)} %pad_maximum_fusion.3), channel_id=1, source_target_pairs={{0,8},{4,12},{8,0},{12,4},{16,24},{20,28},{24,16},{28,20},{1,9},{5... | collective-permute-start | bytes 516104 | tf_op jit(solution)/shard_map/ppermute | solution.py:633
  12.8 5.3 %collective-permute-start.3 = (bf16[3,64,384]{2,1,0:T(8,128)(2,1)S(1)}, bf16[3,64,384]{2,1,0:T(8,128)(2,1)S(1)}, u32[]{:S(2)}, u32[]{:S(2)}) collective-permute-start(bf16[3,64,384]{2,1,0:T(8,128)(2,1)S(1)} %get-tuple-element.47), channel_id=1, source_target_pairs={{0,1},{1,0},{2,3},{3,2},{4,5},{5,4},{6,7},{7,6},{8,9},{9,8},{10,11... | collective-permute-start | bytes 442376 | tf_op jit(solution)/shard_map/ppermute | solution.py:637
  12.8 6.7 %collective-permute-start.4 = (bf16[3,64,384]{2,1,0:T(8,128)(2,1)S(1)}, bf16[3,64,384]{2,1,0:T(8,128)(2,1)S(1)}, u32[]{:S(2)}, u32[]{:S(2)}) collective-permute-start(bf16[3,64,384]{2,1,0:T(8,128)(2,1)S(1)} %get-tuple-element.48), channel_id=1, source_target_pairs={{0,2},{1,3},{2,0},{3,1},{4,6},{5,7},{6,4},{7,5},{8,10},{9,11},{10,... | collective-permute-start | bytes 442376 | tf_op jit(solution)/shard_map/ppermute | solution.py:637
  14.4 7.4 %collective-permute-start.5 = (bf16[3,64,384]{2,1,0:T(8,128)(2,1)S(1)}, bf16[3,64,384]{2,1,0:T(8,128)(2,1)S(1)}, u32[]{:S(2)}, u32[]{:S(2)}) collective-permute-start(bf16[3,64,384]{2,1,0:T(8,128)(2,1)S(1)} %get-tuple-element.49), channel_id=1, source_target_pairs={{0,3},{1,2},{2,1},{3,0},{4,7},{5,6},{6,5},{7,4},{8,11},{9,10},{10,... | collective-permute-start | bytes 442376 | tf_op jit(solution)/shard_map/ppermute | solution.py:637
  16.3 21.2 %collective-permute-start.2 = (bf16[4,112,384]{2,1,0:T(8,128)(2,1)S(1)}, bf16[4,112,384]{2,1,0:T(8,128)(2,1)S(1)}, u32[]{:S(2)}, u32[]{:S(2)}) collective-permute-start(bf16[4,112,384]{2,1,0:T(8,128)(2,1)S(1)} %pad_maximum_fusion.1), channel_id=1, source_target_pairs={{0,4},{4,0},{8,12},{12,8},{16,20},{20,16},{24,28},{28,24},{1,5},{5... | collective-permute-start | bytes 1032200 | tf_op jit(solution)/shard_map/ppermute | solution.py:633
  24.6 9.9 %collective-permute-start.7 = (bf16[4,64,384]{2,1,0:T(8,128)(2,1)S(1)}, bf16[4,64,384]{2,1,0:T(8,128)(2,1)S(1)}, u32[]{:S(2)}, u32[]{:S(2)}) collective-permute-start(bf16[4,64,384]{2,1,0:T(8,128)(2,1)S(1)} %get-tuple-element.50.refs_0_), channel_id=1, source_target_pairs={{0,2},{1,3},{2,0},{3,1},{4,6},{5,7},{6,4},{7,5},{8,10},{9,11},{10,... | collective-permute-start | bytes 589832 | tf_op jit(solution)/shard_map/ppermute | solution.py:637
  26.3 8.2 %collective-permute-start.10 = (bf16[2,64,384]{2,1,0:T(8,128)(2,1)S(1)}, bf16[2,64,384]{2,1,0:T(8,128)(2,1)S(1)}, u32[]{:S(2)}, u32[]{:S(2)}) collective-permute-start(bf16[2,64,384]{2,1,0:T(8,128)(2,1)S(1)} %get-tuple-element.53), channel_id=1, source_target_pairs={{0,2},{1,3},{2,0},{3,1},{4,6},{5,7},{6,4},{7,5},{8,10},{9,11},{10,... | collective-permute-start | bytes 294920 | tf_op jit(solution)/shard_map/ppermute | solution.py:637
  26.9 9.0 %collective-permute-start.11 = (bf16[2,64,384]{2,1,0:T(8,128)(2,1)S(1)}, bf16[2,64,384]{2,1,0:T(8,128)(2,1)S(1)}, u32[]{:S(2)}, u32[]{:S(2)}) collective-permute-start(bf16[2,64,384]{2,1,0:T(8,128)(2,1)S(1)} %get-tuple-element.54), channel_id=1, source_target_pairs={{0,3},{1,2},{2,1},{3,0},{4,7},{5,6},{6,5},{7,4},{8,11},{9,10},{10,... | collective-permute-start | bytes 294920 | tf_op jit(solution)/shard_map/ppermute | solution.py:637
  28.0 8.1 %collective-permute-start.9 = (bf16[2,64,384]{2,1,0:T(8,128)(2,1)S(1)}, bf16[2,64,384]{2,1,0:T(8,128)(2,1)S(1)}, u32[]{:S(2)}, u32[]{:S(2)}) collective-permute-start(bf16[2,64,384]{2,1,0:T(8,128)(2,1)S(1)} %get-tuple-element.52), channel_id=1, source_target_pairs={{0,1},{1,0},{2,3},{3,2},{4,5},{5,4},{6,7},{7,6},{8,9},{9,8},{10,11... | collective-permute-start | bytes 294920 | tf_op jit(solution)/shard_map/ppermute | solution.py:637
  36.1 5.6 %collective-permute-start.16 = (bf16[2,64,384]{2,1,0:T(8,128)(2,1)S(1)}, bf16[2,64,384]{2,1,0:T(8,128)(2,1)S(1)}, u32[]{:S(2)}, u32[]{:S(2)}) collective-permute-start(bf16[2,64,384]{2,1,0:T(8,128)(2,1)S(1)} %get-tuple-element.65), channel_id=1, source_target_pairs={{0,2},{1,3},{2,0},{3,1},{4,6},{5,7},{6,4},{7,5},{8,10},{9,11},{10,... | collective-permute-start | bytes 294920 | tf_op jit(solution)/shard_map/ppermute | solution.py:637
  49.0 12.7 %collective-permute-start.26 = (bf16[4,96,384]{2,1,0:T(8,128)(2,1)S(1)}, bf16[4,96,384]{2,1,0:T(8,128)(2,1)S(1)}, u32[]{:S(2)}, u32[]{:S(2)}) collective-permute-start(bf16[4,96,384]{2,1,0:T(8,128)(2,1)S(1)} %slice.58), channel_id=1, source_target_pairs={{0,4},{4,0},{8,12},{12,8},{16,20},{20,16},{24,28},{28,24},{1,5},{5... | collective-permute-start | bytes 884744 | tf_op jit(solution)/shard_map/ppermute | solution.py:633
  50.6 7.8 %collective-permute-start.22 = (bf16[320,384]{1,0:T(8,128)(2,1)S(1)}, bf16[320,384]{1,0:T(8,128)(2,1)S(1)}, u32[]{:S(2)}, u32[]{:S(2)}) collective-permute-start(bf16[320,384]{1,0:T(8,128)(2,1)S(1)} %shard_map.143), channel_id=1, source_target_pairs={{0,2},{1,3},{2,0},{3,1},{4,6},{5,7},{6,4},{7,5},{8,10},{9,11},{10,... | collective-permute-start | bytes 737288 | tf_op jit(solution)/shard_map/ppermute | solution.py:637
  64.6 5.5 %collective-permute-start.28 = (bf16[2,112,384]{2,1,0:T(8,128)(2,1)S(1)}, bf16[2,112,384]{2,1,0:T(8,128)(2,1)S(1)}, u32[]{:S(2)}, u32[]{:S(2)}) collective-permute-start(bf16[2,112,384]{2,1,0:T(8,128)(2,1)S(1)} %pad_maximum_fusion.2), channel_id=1, source_target_pairs={{0,8},{4,12},{8,0},{12,4},{16,24},{20,28},{24,16},{28,20},{1,9},{5... | collective-permute-start | bytes 516104 | tf_op jit(solution)/shard_map/ppermute | solution.py:633
  66.1 5.5 %collective-permute-start.18 = (bf16[2,64,384]{2,1,0:T(8,128)(2,1)S(1)}, bf16[2,64,384]{2,1,0:T(8,128)(2,1)S(1)}, u32[]{:S(2)}, u32[]{:S(2)}) collective-permute-start(bf16[2,64,384]{2,1,0:T(8,128)(2,1)S(1)} %get-tuple-element.68), channel_id=1, source_target_pairs={{0,1},{1,0},{2,3},{3,2},{4,5},{5,4},{6,7},{7,6},{8,9},{9,8},{10,11... | collective-permute-start | bytes 294920 | tf_op jit(solution)/shard_map/ppermute | solution.py:637
  66.1 5.6 %collective-permute-start.19 = (bf16[2,64,384]{2,1,0:T(8,128)(2,1)S(1)}, bf16[2,64,384]{2,1,0:T(8,128)(2,1)S(1)}, u32[]{:S(2)}, u32[]{:S(2)}) collective-permute-start(bf16[2,64,384]{2,1,0:T(8,128)(2,1)S(1)} %get-tuple-element.69), channel_id=1, source_target_pairs={{0,2},{1,3},{2,0},{3,1},{4,6},{5,7},{6,4},{7,5},{8,10},{9,11},{10,... | collective-permute-start | bytes 294920 | tf_op jit(solution)/shard_map/ppermute | solution.py:637
  67.6 5.4 %collective-permute-start.20 = (bf16[2,64,384]{2,1,0:T(8,128)(2,1)S(1)}, bf16[2,64,384]{2,1,0:T(8,128)(2,1)S(1)}, u32[]{:S(2)}, u32[]{:S(2)}) collective-permute-start(bf16[2,64,384]{2,1,0:T(8,128)(2,1)S(1)} %get-tuple-element.70), channel_id=1, source_target_pairs={{0,3},{1,2},{2,1},{3,0},{4,7},{5,6},{6,5},{7,4},{8,11},{9,10},{10,... | collective-permute-start | bytes 294920 | tf_op jit(solution)/shard_map/ppermute | solution.py:637
  68.0 6.6 %collective-permute-start.12 = (bf16[2,64,384]{2,1,0:T(8,128)(2,1)S(1)}, bf16[2,64,384]{2,1,0:T(8,128)(2,1)S(1)}, u32[]{:S(2)}, u32[]{:S(2)}) collective-permute-start(bf16[2,64,384]{2,1,0:T(8,128)(2,1)S(1)} %get-tuple-element.56), channel_id=1, source_target_pairs={{0,1},{1,0},{2,3},{3,2},{4,5},{5,4},{6,7},{7,6},{8,9},{9,8},{10,11... | collective-permute-start | bytes 294920 | tf_op jit(solution)/shard_map/ppermute | solution.py:637
  70.1 5.8 %collective-permute-start.13 = (bf16[2,64,384]{2,1,0:T(8,128)(2,1)S(1)}, bf16[2,64,384]{2,1,0:T(8,128)(2,1)S(1)}, u32[]{:S(2)}, u32[]{:S(2)}) collective-permute-start(bf16[2,64,384]{2,1,0:T(8,128)(2,1)S(1)} %get-tuple-element.57), channel_id=1, source_target_pairs={{0,2},{1,3},{2,0},{3,1},{4,6},{5,7},{6,4},{7,5},{8,10},{9,11},{10,... | collective-permute-start | bytes 294920 | tf_op jit(solution)/shard_map/ppermute | solution.py:637
  71.6 7.3 %collective-permute-start.14 = (bf16[2,64,384]{2,1,0:T(8,128)(2,1)S(1)}, bf16[2,64,384]{2,1,0:T(8,128)(2,1)S(1)}, u32[]{:S(2)}, u32[]{:S(2)}) collective-permute-start(bf16[2,64,384]{2,1,0:T(8,128)(2,1)S(1)} %get-tuple-element.58), channel_id=1, source_target_pairs={{0,3},{1,2},{2,1},{3,0},{4,7},{5,6},{6,5},{7,4},{8,11},{9,10},{10,... | collective-permute-start | bytes 294920 | tf_op jit(solution)/shard_map/ppermute | solution.py:637
  71.7 8.0 %collective-permute-start.23 = (bf16[3,64,384]{2,1,0:T(8,128)(2,1)S(1)}, bf16[3,64,384]{2,1,0:T(8,128)(2,1)S(1)}, u32[]{:S(2)}, u32[]{:S(2)}) collective-permute-start(bf16[3,64,384]{2,1,0:T(8,128)(2,1)S(1)} %get-tuple-element.76), channel_id=1, source_target_pairs={{0,1},{1,0},{2,3},{3,2},{4,5},{5,4},{6,7},{7,6},{8,9},{9,8},{10,11... | collective-permute-start | bytes 442376 | tf_op jit(solution)/shard_map/ppermute | solution.py:637
  73.0 8.1 %collective-permute-start.24 = (bf16[3,64,384]{2,1,0:T(8,128)(2,1)S(1)}, bf16[3,64,384]{2,1,0:T(8,128)(2,1)S(1)}, u32[]{:S(2)}, u32[]{:S(2)}) collective-permute-start(bf16[3,64,384]{2,1,0:T(8,128)(2,1)S(1)} %get-tuple-element.77), channel_id=1, source_target_pairs={{0,2},{1,3},{2,0},{3,1},{4,6},{5,7},{6,4},{7,5},{8,10},{9,11},{10,... | collective-permute-start | bytes 442376 | tf_op jit(solution)/shard_map/ppermute | solution.py:637
  74.5 9.0 %collective-permute-start.25 = (bf16[3,64,384]{2,1,0:T(8,128)(2,1)S(1)}, bf16[3,64,384]{2,1,0:T(8,128)(2,1)S(1)}, u32[]{:S(2)}, u32[]{:S(2)}) collective-permute-start(bf16[3,64,384]{2,1,0:T(8,128)(2,1)S(1)} %get-tuple-element.78), channel_id=1, source_target_pairs={{0,3},{1,2},{2,1},{3,0},{4,7},{5,6},{6,5},{7,4},{8,11},{9,10},{10,... | collective-permute-start | bytes 442376 | tf_op jit(solution)/shard_map/ppermute | solution.py:637
  75.9 8.6 %collective-permute-start.29 = (bf16[112,384]{1,0:T(8,128)(2,1)S(1)}, bf16[112,384]{1,0:T(8,128)(2,1)S(1)}, u32[]{:S(2)}, u32[]{:S(2)}) collective-permute-start(bf16[112,384]{1,0:T(8,128)(2,1)S(1)} %slice_bitcast_fusion.1), channel_id=1, source_target_pairs={{0,16},{4,20},{8,24},{12,28},{16,0},{20,4},{24,8},{28,12},{1,17},{... | collective-permute-start | bytes 258056 | tf_op jit(solution)/shard_map/ppermute | solution.py:633
  (12 other events, 72.9 us)

commit v3 on v2

--- a/solution.py
+++ b/solution.py
@@ -272,15 +272,19 @@
 LANES = 128
 N_CTX = 4
 N_DP = 8
-DP_BITS = (4, 2, 1)
+Z_FIRST = (4, 2, 1)
+Y_FIRST = (1, 4, 2)
 TAP_PAD = 32
 TAPS = 31
 REACH = 15
 
 
-def slot_of(index, me):
+def slot_of(index, me, bits=Z_FIRST):
     apart = jnp.bitwise_xor(index, me)
-    return ((apart & 1) << 2) | (apart & 2) | ((apart >> 2) & 1)
+    place = 0
+    for order, bit in enumerate(bits):
+        place += jnp.where((apart & bit) != 0, 1 << order, 0)
+    return place
 
 
 def dot_tt(lhs, rhs, lhs_dim, rhs_dim):
@@ -289,7 +293,7 @@
     )
 
 
-def call_kernel(body, out_shape, ins, outs=None, scratch=()):
+def call_kernel(body, out_shape, ins, outs=None, scratch=(), room=40):
     spaces = {
         "smem": pl.BlockSpec(memory_space=pltpu.SMEM),
         "vmem": pl.BlockSpec(memory_space=pltpu.VMEM),
@@ -302,7 +306,7 @@
         in_specs=[spaces[space] for space in ins],
         out_specs=[spaces[space] for space in (outs or ["vmem"] * len(out_shape))],
         scratch_shapes=list(scratch),
-        compiler_params=pltpu.CompilerParams(vmem_limit_bytes=40 * 1024 * 1024),
+        compiler_params=pltpu.CompilerParams(vmem_limit_bytes=room * 1024 * 1024),
     )
 
 
@@ -314,19 +318,39 @@
     return pl.ds(pl.multiple_of(start, LANES), size)
 
 
+def start_copies(pairs, sem):
+    for number, (source, target) in enumerate(pairs):
+        pltpu.make_async_copy(source, target, sem.at[number]).start()
+
+
+def wait_copies(pairs, sem):
+    for number, (source, target) in enumerate(pairs):
+        pltpu.make_async_copy(source, target, sem.at[number]).wait()
+
+
 def run_copies(pairs, sem):
-    copies = [
-        pltpu.make_async_copy(source, target, sem.at[number])
-        for number, (source, target) in enumerate(pairs)
-    ]
-    for copy in copies:
-        copy.start()
-    for copy in copies:
-        copy.wait()
-
-
-def pack_heads(query_ref, key_ref, value_ref, *rest):
-    outs, sem = rest[:N_CTX], rest[N_CTX]
+    start_copies(pairs, sem)
+    wait_copies(pairs, sem)
+
+
+def untouched(*refs):
+    pass
+
+
+def gate(arrays, *awaited):
+    count = len(arrays)
+    spec = pl.BlockSpec(memory_space=pl.ANY)
+    return pl.pallas_call(
+        untouched,
+        out_shape=tuple(jax.ShapeDtypeStruct(array.shape, array.dtype) for array in arrays),
+        in_specs=[spec] * (count + len(awaited)),
+        out_specs=(spec,) * count,
+        input_output_aliases={number: number for number in range(count)},
+    )(*arrays, *awaited)
+
+
+def pack_heads(query_ref, key_ref, value_ref, panel_ref, taps_ref, *rest):
+    outs, early_ref, late_ref, sem = rest[:N_CTX], *rest[N_CTX:]
     half = query_ref.shape[2] // 2
     place = lax.axis_index("ctx")
     pairs = []
@@ -335,11 +359,21 @@
         cols = columns((dest & 1) * half, half)
         for slot, ref in enumerate((query_ref, key_ref, value_ref)):
             pairs.append((ref.at[half_of(dest), :, cols], outs[apart].at[slot]))
-    run_copies(pairs, sem)
+    split = late_ref.shape[1]
+    pairs.append((panel_ref.at[0:split], late_ref.at[0]))
+    pairs.append((panel_ref.at[split : 2 * split], early_ref.at[0, 0:split]))
+    start_copies(pairs, sem)
+    taps = taps_ref[...].astype(jnp.float32)
+    high = jnp.concatenate(
+        [taps[TAP_PAD // 2 :], jnp.zeros((TAP_PAD - TAPS, taps.shape[1]), jnp.float32)], axis=0
+    )
+    joined = jnp.concatenate([taps[: TAP_PAD // 2], high], axis=1)
+    early_ref[0, split:, :] = joined.astype(jnp.bfloat16)
+    wait_copies(pairs, sem)
 
 
 def pack_channels(in_ref, *rest):
-    outs, sem = rest[:N_CTX], rest[N_CTX]
+    outs, sem = rest[-N_CTX - 1 : -1], rest[-1]
     width = in_ref.shape[2] // N_CTX
     place = lax.axis_index("ctx")
     pairs = []
@@ -413,7 +447,7 @@
         attended_ref[:, :, cols] = joined.reshape(N_CTX, frames, LANES)
 
 
-def forward(length_ref, weight_ref, *refs):
+def forward(length_ref, early_ref, late_ref, *refs):
     attended_refs, frame_refs = refs[:N_CTX], refs[N_CTX : 2 * N_CTX]
     out_refs = refs[2 * N_CTX : 3 * N_CTX]
     whole_ref, rows_ref, taps_ref, total_ref, masked_ref = refs[3 * N_CTX : 3 * N_CTX + 5]
@@ -431,13 +465,14 @@
         for block in range(N_CTX):
             whole_ref[half_of(source), block ^ source, :, cols] = attended_refs[apart][block]
         frame_ref[source] = frame_refs[apart][...]
+    split = late_ref.shape[1]
     for part in range(N_DP):
-        rows_ref[part * entries : (part + 1) * entries] = weight_ref[
-            slot_of(part, group), 0:entries
-        ]
+        first = part * entries
+        rows_ref[first : first + split] = late_ref[slot_of(part, group, Y_FIRST)]
+        rows_ref[first + split : first + entries] = early_ref[slot_of(part, group), 0:split]
     pieces = []
     for part in range(2):
-        block = weight_ref[slot_of(2 * place + part, group), entries:].astype(jnp.float32)
+        block = early_ref[slot_of(2 * place + part, group), split:].astype(jnp.float32)
         pieces.append(jnp.concatenate([block[:, :own], block[:, own:]], axis=0))
     taps = jnp.concatenate(pieces, axis=1)
     for chunk in range(chunks):
@@ -573,7 +608,7 @@
             ]
 
 
-def relay(keep_ref, came_ref, sums_ref, out_ref):
+def relay(keep_ref, came_ref, sums_ref, awaited_ref, out_ref):
     rows = keep_ref.shape[1]
     total = keep_ref[1].astype(jnp.float32) + came_ref[1, 0:rows, :].astype(jnp.float32)
     out_ref[0:rows, :] = total.astype(jnp.bfloat16)
@@ -658,24 +693,30 @@
     head_block = shape((3, frames, half), low)
     channel_block = shape((utts, frames, width), low)
 
-    packed = traded(
-        call_kernel(
-            pack_heads, (head_block,) * N_CTX, ["hbm"] * 3, scratch=[dma((3 * N_CTX,))]
-        )(queries, key_proj, value_proj)
-    )
-    tap_rows = jnp.pad(conv_weight, ((0, TAP_PAD - tap_count), (0, 0)))
-    tap_rows = jnp.concatenate([tap_rows[: TAP_PAD // 2], tap_rows[TAP_PAD // 2 :]], axis=1)
-    shard = jnp.concatenate([out_weight.T, tap_rows], axis=0)[None]
-    for bit in DP_BITS:
-        shard = jnp.concatenate([shard, swapped(shard, bit)], axis=0)
-
-    def spread(array):
+    split = entries // 2
+    *blocks, early, late = call_kernel(
+        pack_heads,
+        (head_block,) * N_CTX
+        + (shape((1, split + TAP_PAD // 2, width), low), shape((1, split, width), low)),
+        ["hbm"] * 4 + ["vmem"],
+        scratch=[dma((3 * N_CTX + 2,))],
+        room=63,
+    )(queries, key_proj, value_proj, out_weight.T, conv_weight)
+    packed = traded(blocks)
+    for early_bit, late_bit in zip(Z_FIRST, Y_FIRST):
+        early = jnp.concatenate([early, swapped(early, early_bit)], axis=0)
+        late = jnp.concatenate([late, swapped(late, late_bit)], axis=0)
+
+    def spread(array, *awaited):
         blocks = call_kernel(
-            pack_channels, (channel_block,) * N_CTX, ["hbm"], scratch=[dma((2 * N_CTX,))]
-        )(array)
+            pack_channels,
+            (channel_block,) * N_CTX,
+            ["hbm"] + ["any"] * len(awaited),
+            scratch=[dma((2 * N_CTX,))],
+        )(array, *awaited)
         return traded(blocks)
 
-    frame_blocks = spread(frame_input)
+    frame_blocks = spread(frame_input, blocks[0])
     attended, weights = call_kernel(
         attend,
         (
@@ -684,10 +725,11 @@
         ),
         ["smem"] + ["vmem"] * N_CTX,
     )(lengths, *packed)
+    (attended,) = gate([attended], frame_blocks[2])
     across = crossed(attended, 2)
     beside = crossed(attended, 1)
     diagonal = crossed(across, 1)
-    grad_blocks = spread(grad_output)
+    grad_blocks = spread(grad_output, attended)
     forward_out = call_kernel(
         forward,
         (channel_block,) * N_CTX
@@ -698,13 +740,13 @@
             shape((utts * chunks, rows, LANES), f32),
             shape((utts * chunks, rows + 32, LANES), f32),
         ),
-        ["smem"] + ["vmem"] * (1 + 2 * N_CTX),
+        ["smem"] + ["vmem"] * (2 + 2 * N_CTX),
         scratch=[
             pltpu.VMEM((utts * chunks, rows, LANES), f32),
             pltpu.VMEM((N_CTX, utts, frames, width), low),
             pltpu.VMEM((N_CTX, utts, frames, width), low),
         ],
-    )(lengths, shard, attended, beside, across, diagonal, *frame_blocks)
+    )(lengths, early, late, attended, beside, across, diagonal, *frame_blocks)
     output_blocks = traded(forward_out[:N_CTX])
     whole, weight_rows, taps, totals, masked = forward_out[N_CTX:]
     backward_out = call_kernel(
@@ -725,20 +767,16 @@
         ],
     )(lengths, totals, masked, taps, weight_rows, *grad_blocks)
     grad_hidden, keep, send, sums = backward_out[N_CTX:]
+    (send,) = gate([send], *output_blocks[2:])
     came = crossed(send, 1)
+    input_blocks = traded(backward_out[:N_CTX])
     (panels,) = call_kernel(
         make_panels, (shape((N_DP, entries, width), low),), ["vmem"] * 2
     )(whole, grad_hidden)
-
-    def added(kept, arrived):
-        return (kept.astype(f32) + arrived.astype(f32)).astype(low)
-
     (far,) = call_kernel(
-        relay, (shape((rows + 2 * TAP_PAD, half), low),), ["vmem"] * 3
-    )(keep, came, sums)
+        relay, (shape((rows + 2 * TAP_PAD, half), low),), ["vmem"] * 3 + ["any"]
+    )(keep, came, sums, input_blocks[2])
     far = crossed(far, 2)
-    input_blocks = traded(backward_out[:N_CTX])
-    panels = added(panels[:4], swapped(panels[4:], 1))
     back_out = call_kernel(
         attend_back,
         (head_block,) * N_CTX + (shape((N_DP, TAP_PAD // 2, width), low),),
@@ -746,6 +784,11 @@
     )(weights, keep, came, far, sums, *packed)
     grad_blocks = traded(back_out[:N_CTX])
     tap_slots = back_out[N_CTX]
+
+    def added(kept, arrived):
+        return (kept.astype(f32) + arrived.astype(f32)).astype(low)
+
+    panels = added(panels[:4], swapped(panels[4:], 1))
     tap_slots = added(tap_slots[:4], swapped(tap_slots[4:], 1))
     summed = jnp.concatenate([panels, tap_slots], axis=1)
     summed = added(summed[:2], swapped(summed[2:], 2))

time: 86.1 us -> 83.3 us (0.967)
  waiting for transfers between devices: 34.4 us -> 29.3 us
  local copies, waits for them, and re-layouts: 2.47 us -> 7.16 us
  starting transfers between devices: 29.5 us -> 25.4 us
  Pallas kernels: 16.7 us -> 19.1 us
  other arithmetic: 1.96 us -> 0.96 us
    ppermute x23, waiting for transfers between devices: 23.8 us -> 16 us  [crossed(): return lax.ppermute(array, 'ctx', [(i, i ^ apart) for i in range(N_CTX)])]
    unnamed x12 -> x42, local copies, waits for them, and re-layouts: 0.95 us -> 6.36 us
    ppermute x23, starting transfers between devices: 16.3 us -> 12.8 us  [crossed(): return lax.ppermute(array, 'ctx', [(i, i ^ apart) for i in range(N_CTX)])]
    ppermute x7 -> x10, waiting for transfers between devices: 10.6 us -> 13.3 us  [swapped(): return lax.ppermute(array, 'dp', [(i, i ^ bit) for i in range(N_DP)])]
    pallas_call x4 -> x6, Pallas kernels: 0.54 us -> 3.12 us  [the longest x1 2.79 us: per_device(): call_kernel(pack_heads, (head_block,) * N_CTX + (shape((1, split + TAP_PA...]
    broadcast_in_dim x1 -> x0, other arithmetic: 1 us -> none  [per_device(): shard = jnp.concatenate([out_weight.T, tap_rows], axis=0)[None]]
    ppermute x7 -> x10, starting transfers between devices: 13.1 us -> 12.6 us  [swapped(): return lax.ppermute(array, 'dp', [(i, i ^ bit) for i in range(N_DP)])]
  transfers between devices with their start and end apart: 30 -> 33, of which waited for: 15 -> 11; matrix products, arithmetic and copies ran while one was open for 0% -> 0% of each run, Pallas kernels for 13% -> 20%
where the time goes in v3:
time: 83.3 us; the launch traced here: 83 us
  waiting for transfers between devices  29.3 us (35%)
  starting transfers between devices  25.4 us (30%)
  Pallas kernels  19.1 us (23%)
  local copies, waits for them, and re-layouts  7.16 us (9%)
  between operations  0.99 us (1%)
  other arithmetic  0.96 us (1%)
    ppermute x23, waiting for transfers between devices, crossed(): return lax.ppermute(array, 'ctx', [(i, i ^ apart) for i in range(N_CTX)])  16 us
    ppermute x10, waiting for transfers between devices, swapped(): return lax.ppermute(array, 'dp', [(i, i ^ bit) for i in range(N_DP)])  13.3 us
    ppermute x23, starting transfers between devices, crossed(): return lax.ppermute(array, 'ctx', [(i, i ^ apart) for i in range(N_CTX)])  12.8 us
    ppermute x10, starting transfers between devices, swapped(): return lax.ppermute(array, 'dp', [(i, i ^ bit) for i in range(N_DP)])  12.6 us
    unnamed x42, local copies, waits for them, and re-layouts  6.36 us
    pallas_call x1, Pallas kernels, per_device(): call_kernel(backward, (channel_block,) * N_CTX + (shape((utts, rows, widt...  5.01 us
    pallas_call x1, Pallas kernels, per_device(): call_kernel(forward, (channel_block,) * N_CTX + (shape((utts, N_CTX, fram...  3.1 us
    pallas_call x1, Pallas kernels, per_device(): call_kernel(pack_heads, (head_block,) * N_CTX + (shape((1, split + TAP_PA...  2.79 us
  transfers between devices with their start and end apart: 33, of which 11 were waited for; matrix products, arithmetic and copies ran while one was open for 0% of the time, Pallas kernels for 20%

profile of v3, /device:TPU:0, one launch (start us, length us, event | category | flops | bytes accessed | tf_op | source)
XLA Modules:
  0.0 83.0 jit_solution(8490696283735417017)
XLA Ops:
  0.6 2.8 %shard_map.135 = (bf16[3,64,384]{2,1,0:T(8,128)(2,1)}, bf16[3,64,384]{2,1,0:T(8,128)(2,1)}, bf16[3,64,384]{2,1,0:T(8,128)(2,1)}, bf16[3,64,384]{2,1,0:T(8,128)(2...) custom-call(bf16[2,64,768]{2,1,0:T(8,128)(2,1)} %query_ref.1, bf16[2,64,768]{2,1,0:T(8,128)(2,1)} %key_ref.1, ...), custom_call_target="tpu_custom_call" | custom-call | tf_op jit(solution)/shard_map/pallas_call | solution.py:697
  3.4 3.0 %collective-permute-start.3 = (bf16[1,48,384]{2,1,0:T(8,128)(2,1)}, bf16[1,48,384]{2,1,0:T(8,128)(2,1)S(1)}, u32[]{:S(2)}, u32[]{:S(2)}) collective-permute-start(bf16[1,48,384]{2,1,0:T(8,128)(2,1)} %get-tuple-element.49), channel_id=1, source_target_pairs={{0,4},{4,0},{8,12},{12,8},{16,20},{20,16},{24,28},{28,24},{1,5},{5... | collective-permute-start | bytes 110600 | tf_op jit(solution)/shard_map/ppermute | solution.py:668
  6.5 2.6 %collective-permute-start = (bf16[1,64,384]{2,1,0:T(8,128)(2,1)}, bf16[1,64,384]{2,1,0:T(8,128)(2,1)S(1)}, u32[]{:S(2)}, u32[]{:S(2)}) collective-permute-start(bf16[1,64,384]{2,1,0:T(8,128)(2,1)} %get-tuple-element.48), channel_id=1, source_target_pairs={{0,16},{4,20},{8,24},{12,28},{16,0},{20,4},{24,8},{28,12},{1,17},{... | collective-permute-start | bytes 147464 | tf_op jit(solution)/shard_map/ppermute | solution.py:668
  9.1 1.5 %collective-permute-start.7 = (bf16[3,64,384]{2,1,0:T(8,128)(2,1)}, bf16[3,64,384]{2,1,0:T(8,128)(2,1)S(1)}, u32[]{:S(2)}, u32[]{:S(2)}) collective-permute-start(bf16[3,64,384]{2,1,0:T(8,128)(2,1)} %get-tuple-element.52), channel_id=1, source_target_pairs={{0,2},{1,3},{2,0},{3,1},{4,6},{5,7},{6,4},{7,5},{8,10},{9,11},{10,... | collective-permute-start | bytes 442376 | tf_op jit(solution)/shard_map/ppermute | solution.py:672
  10.9 0.9 %copy-done.2 = bf16[3,64,384]{2,1,0:T(8,128)(2,1)S(1)} copy-done((bf16[3,64,384]{2,1,0:T(8,128)(2,1)S(1)}, bf16[3,64,384]{2,1,0:T(8,128)(2,1)}, u32[]{:S(2)}) %copy-start.2) | copy-done | bytes 147480
  12.0 1.6 %collective-permute-start.9 = (bf16[2,64,384]{2,1,0:T(8,128)(2,1)S(1)}, bf16[2,64,384]{2,1,0:T(8,128)(2,1)S(1)}, u32[]{:S(2)}, u32[]{:S(2)}) collective-permute-start(bf16[2,64,384]{2,1,0:T(8,128)(2,1)S(1)} %get-tuple-element.55), channel_id=1, source_target_pairs={{0,2},{1,3},{2,0},{3,1},{4,6},{5,7},{6,4},{7,5},{8,10},{9,11},{10,... | collective-permute-start | bytes 294920 | tf_op jit(solution)/shard_map/ppermute | solution.py:672
  14.3 2.0 %collective-permute-start.1 = (bf16[2,64,384]{2,1,0:T(8,128)(2,1)S(1)}, bf16[2,64,384]{2,1,0:T(8,128)(2,1)S(1)}, u32[]{:S(2)}, u32[]{:S(2)}) collective-permute-start(bf16[2,64,384]{2,1,0:T(8,128)(2,1)S(1)} %pad_maximum_fusion.5), channel_id=1, source_target_pairs={{0,8},{4,12},{8,0},{12,4},{16,24},{20,28},{24,16},{28,20},{1,9},{5... | collective-permute-start | bytes 294920 | tf_op jit(solution)/shard_map/ppermute | solution.py:668
  16.4 2.0 %collective-permute-done.8.refs_3_ = bf16[3,64,384]{2,1,0:T(8,128)(2,1)S(1)} collective-permute-done((bf16[3,64,384]{2,1,0:T(8,128)(2,1)}, bf16[3,64,384]{2,1,0:T(8,128)(2,1)S(1)}, u32[]{:S(2)}, u32[]{:S(2)}) %collective-permute-start.8) | collective-permute-done | bytes 147488 | tf_op jit(solution)/shard_map/ppermute | solution.py:672
  18.3 2.8 %shard_map.136 = (bf16[4,64,384]{2,1,0:T(8,128)(2,1)S(1)}, bf16[6,256,256]{2,1,0:T(8,128)(2,1)S(1)}) custom-call(s32[2]{0:T(128)S(1)} %copy-done.13, bf16[3,64,384]{2,1,0:T(8,128)(2,1)S(1)} %copy-done.3, bf16[3,64,384]{2,1,0:T(8,128)(2,1)S(1)} %collective-permute-done.6.refs_1_, bf16[3,64,384]{2,1,0:T(8,128)(2,1)S(1)} %collective-permute-done.7.refs_2_, ...), custom_call_target="tpu_custom_call" | custom-call | tf_op jit(solution)/shard_map/pallas_call | solution.py:720
  22.4 1.5 %collective-permute-start.11 = (bf16[4,64,384]{2,1,0:T(8,128)(2,1)}, bf16[4,64,384]{2,1,0:T(8,128)(2,1)S(1)}, u32[]{:S(2)}, u32[]{:S(2)}) collective-permute-start(bf16[4,64,384]{2,1,0:T(8,128)(2,1)} %shard_map.138.refs_0_.rest_0_), channel_id=1, source_target_pairs={{0,2},{1,3},{2,0},{3,1},{4,6},{5,7},{6,4},{7,5},{8,10},{9,11},{10,... | collective-permute-start | bytes 589832 | tf_op jit(solution)/shard_map/ppermute | solution.py:672
  23.9 1.6 %collective-permute-start.5 = (bf16[4,48,384]{2,1,0:T(8,128)(2,1)S(1)}, bf16[4,48,384]{2,1,0:T(8,128)(2,1)S(1)}, u32[]{:S(2)}, u32[]{:S(2)}) collective-permute-start(bf16[4,48,384]{2,1,0:T(8,128)(2,1)S(1)} %pad_maximum_fusion.4), channel_id=1, source_target_pairs={{0,8},{4,12},{8,0},{12,4},{16,24},{20,28},{24,16},{28,20},{1,9},{5... | collective-permute-start | bytes 442376 | tf_op jit(solution)/shard_map/ppermute | solution.py:668
  27.0 3.4 %collective-permute-done.5 = bf16[4,48,384]{2,1,0:T(8,128)(2,1)S(1)} collective-permute-done((bf16[4,48,384]{2,1,0:T(8,128)(2,1)S(1)}, bf16[4,48,384]{2,1,0:T(8,128)(2,1)S(1)}, u32[]{:S(2)}, u32[]{:S(2)}) %collective-permute-start.5) | collective-permute-done | bytes 147488 | tf_op jit(solution)/shard_map/ppermute | solution.py:668
  30.9 1.9 %collective-permute-done.2 = bf16[4,64,384]{2,1,0:T(8,128)(2,1)S(1)} collective-permute-done((bf16[4,64,384]{2,1,0:T(8,128)(2,1)S(1)}, bf16[4,64,384]{2,1,0:T(8,128)(2,1)S(1)}, u32[]{:S(2)}, u32[]{:S(2)}) %collective-permute-start.2) | collective-permute-done | bytes 196640 | tf_op jit(solution)/shard_map/ppermute | solution.py:668
  33.5 1.3 %collective-permute-start.20 = (bf16[2,64,384]{2,1,0:T(8,128)(2,1)S(1)}, bf16[2,64,384]{2,1,0:T(8,128)(2,1)S(1)}, u32[]{:S(2)}, u32[]{:S(2)}) collective-permute-start(bf16[2,64,384]{2,1,0:T(8,128)(2,1)S(1)} %get-tuple-element.70), channel_id=1, source_target_pairs={{0,3},{1,2},{2,1},{3,0},{4,7},{5,6},{6,5},{7,4},{8,11},{9,10},{10,... | collective-permute-start | bytes 294920 | tf_op jit(solution)/shard_map/ppermute | solution.py:672
  34.8 3.1 %shard_map.139 = (bf16[2,64,384]{2,1,0:T(8,128)(2,1)S(1)}, bf16[2,64,384]{2,1,0:T(8,128)(2,1)S(1)}, bf16[2,64,384]{2,1,0:T(8,128)(2,1)S(1)}, bf16[2,64,384]{2,1,...) custom-call(s32[2]{0:T(128)S(1)} %copy-done.13, ...), custom_call_target="tpu_custom_call" | custom-call | tf_op jit(solution)/shard_map/pallas_call | solution.py:733
  38.5 1.1 %collective-permute-start.17 = (bf16[2,64,384]{2,1,0:T(8,128)(2,1)S(1)}, bf16[2,64,384]{2,1,0:T(8,128)(2,1)S(1)}, u32[]{:S(2)}, u32[]{:S(2)}) collective-permute-start(bf16[2,64,384]{2,1,0:T(8,128)(2,1)S(1)} %get-tuple-element.62), channel_id=1, source_target_pairs={{0,3},{1,2},{2,1},{3,0},{4,7},{5,6},{6,5},{7,4},{8,11},{9,10},{10,... | collective-permute-start | bytes 294920 | tf_op jit(solution)/shard_map/ppermute | solution.py:672
  39.9 5.0 %shard_map.142 = (bf16[2,64,384]{2,1,0:T(8,128)(2,1)S(1)}, bf16[2,64,384]{2,1,0:T(8,128)(2,1)S(1)}, bf16[2,64,384]{2,1,0:T(8,128)(2,1)S(1)}, bf16[2,64,384]{2,1,...) custom-call(s32[2]{0:T(128)S(1)} %copy-done.13, ...), custom_call_target="tpu_custom_call" | custom-call | tf_op jit(solution)/shard_map/pallas_call | solution.py:752
  50.3 3.4 %collective-permute-done.22.refs_2_.awaited_ref = bf16[2,64,384]{2,1,0:T(8,128)(2,1)S(1)} collective-permute-done((bf16[2,64,384]{2,1,0:T(8,128)(2,1)}, bf16[2,64,384]{2,1,0:T(8,128)(2,1)S(1)}, u32[]{:S(2)}, u32[]{:S(2)}) %collective-permute-start.22) | collective-permute-done | bytes 98336 | tf_op jit(solution)/shard_map/ppermute | solution.py:672
  54.3 6.7 %collective-permute-done.25.far_ref = bf16[320,384]{1,0:T(8,128)(2,1)S(1)} collective-permute-done((bf16[320,384]{1,0:T(8,128)(2,1)S(1)}, bf16[320,384]{1,0:T(8,128)(2,1)S(1)}, u32[]{:S(2)}, u32[]{:S(2)}) %collective-permute-start.25) | collective-permute-done | bytes 245792 | tf_op jit(solution)/shard_map/ppermute | solution.py:672
  61.1 2.0 %shard_map.146 = (bf16[3,64,384]{2,1,0:T(8,128)(2,1)S(1)}, bf16[3,64,384]{2,1,0:T(8,128)(2,1)S(1)}, bf16[3,64,384]{2,1,0:T(8,128)(2,1)S(1)}, bf16[3,64,384]{2,1,0:T(8,128)(2,1)S(1)}, bf16[8,16,384]{2,1,0:T(8,128)(2,1)S(1)}) custom-call(bf16[6,256,256]{2,1,0:T(8,128)(2,1)S(1)} %get-tuple-element.75.weight_ref, ...), custom_call_target="tpu_custom_call" | custom-call | tf_op jit(solution)/shard_map/pallas_call | solution.py:780
  63.7 3.5 %collective-permute-done.30 = bf16[4,16,384]{2,1,0:T(8,128)(2,1)S(1)} collective-permute-done((bf16[4,16,384]{2,1,0:T(8,128)(2,1)S(1)}, bf16[4,16,384]{2,1,0:T(8,128)(2,1)S(1)}, u32[]{:S(2)}, u32[]{:S(2)}) %collective-permute-start.30) | collective-permute-done | bytes 49184 | tf_op jit(solution)/shard_map/ppermute | solution.py:668
  69.3 3.5 %collective-permute-done.31 = bf16[2,112,384]{2,1,0:T(8,128)(2,1)S(1)} collective-permute-done((bf16[2,112,384]{2,1,0:T(8,128)(2,1)S(1)}, bf16[2,112,384]{2,1,0:T(8,128)(2,1)S(1)}, u32[]{:S(2)}, u32[]{:S(2)}) %collective-permute-start.31) | collective-permute-done | bytes 172064 | tf_op jit(solution)/shard_map/ppermute | solution.py:668
  75.9 3.5 %collective-permute-done.27.refs_2_ = bf16[3,64,384]{2,1,0:T(8,128)(2,1)S(1)} collective-permute-done((bf16[3,64,384]{2,1,0:T(8,128)(2,1)S(1)}, bf16[3,64,384]{2,1,0:T(8,128)(2,1)S(1)}, u32[]{:S(2)}, u32[]{:S(2)}) %collective-permute-start.27) | collective-permute-done | bytes 147488 | tf_op jit(solution)/shard_map/ppermute | solution.py:672
  80.5 1.1 %collective-permute-done.32 = bf16[112,384]{1,0:T(8,128)(2,1)S(1)} collective-permute-done((bf16[112,384]{1,0:T(8,128)(2,1)S(1)}, bf16[112,384]{1,0:T(8,128)(2,1)S(1)}, u32[]{:S(2)}, u32[]{:S(2)}) %collective-permute-start.32) | collective-permute-done | bytes 86048 | tf_op jit(solution)/shard_map/ppermute | solution.py:668
  (115 shorter events, 20.4 us)
Async XLA Ops:
  3.4 8.5 %collective-permute-start.3 = (bf16[1,48,384]{2,1,0:T(8,128)(2,1)}, bf16[1,48,384]{2,1,0:T(8,128)(2,1)S(1)}, u32[]{:S(2)}, u32[]{:S(2)}) collective-permute-start(bf16[1,48,384]{2,1,0:T(8,128)(2,1)} %get-tuple-element.49), channel_id=1, source_target_pairs={{0,4},{4,0},{8,12},{12,8},{16,20},{20,16},{24,28},{28,24},{1,5},{5... | collective-permute-start | bytes 110600 | tf_op jit(solution)/shard_map/ppermute | solution.py:668
  6.5 7.1 %collective-permute-start = (bf16[1,64,384]{2,1,0:T(8,128)(2,1)}, bf16[1,64,384]{2,1,0:T(8,128)(2,1)S(1)}, u32[]{:S(2)}, u32[]{:S(2)}) collective-permute-start(bf16[1,64,384]{2,1,0:T(8,128)(2,1)} %get-tuple-element.48), channel_id=1, source_target_pairs={{0,16},{4,20},{8,24},{12,28},{16,0},{20,4},{24,8},{28,12},{1,17},{... | collective-permute-start | bytes 147464 | tf_op jit(solution)/shard_map/ppermute | solution.py:668
  9.1 7.3 %collective-permute-start.7 = (bf16[3,64,384]{2,1,0:T(8,128)(2,1)}, bf16[3,64,384]{2,1,0:T(8,128)(2,1)S(1)}, u32[]{:S(2)}, u32[]{:S(2)}) collective-permute-start(bf16[3,64,384]{2,1,0:T(8,128)(2,1)} %get-tuple-element.52), channel_id=1, source_target_pairs={{0,2},{1,3},{2,0},{3,1},{4,6},{5,7},{6,4},{7,5},{8,10},{9,11},{10,... | collective-permute-start | bytes 442376 | tf_op jit(solution)/shard_map/ppermute | solution.py:672
  10.6 7.8 %collective-permute-start.8 = (bf16[3,64,384]{2,1,0:T(8,128)(2,1)}, bf16[3,64,384]{2,1,0:T(8,128)(2,1)S(1)}, u32[]{:S(2)}, u32[]{:S(2)}) collective-permute-start(bf16[3,64,384]{2,1,0:T(8,128)(2,1)} %get-tuple-element.53), channel_id=1, source_target_pairs={{0,3},{1,2},{2,1},{3,0},{4,7},{5,6},{6,5},{7,4},{8,11},{9,10},{10,... | collective-permute-start | bytes 442376 | tf_op jit(solution)/shard_map/ppermute | solution.py:672
  12.0 9.7 %collective-permute-start.9 = (bf16[2,64,384]{2,1,0:T(8,128)(2,1)S(1)}, bf16[2,64,384]{2,1,0:T(8,128)(2,1)S(1)}, u32[]{:S(2)}, u32[]{:S(2)}) collective-permute-start(bf16[2,64,384]{2,1,0:T(8,128)(2,1)S(1)} %get-tuple-element.55), channel_id=1, source_target_pairs={{0,2},{1,3},{2,0},{3,1},{4,6},{5,7},{6,4},{7,5},{8,10},{9,11},{10,... | collective-permute-start | bytes 294920 | tf_op jit(solution)/shard_map/ppermute | solution.py:672
  13.6 10.3 %collective-permute-start.4 = (bf16[2,48,384]{2,1,0:T(8,128)(2,1)S(1)}, bf16[2,48,384]{2,1,0:T(8,128)(2,1)S(1)}, u32[]{:S(2)}, u32[]{:S(2)}) collective-permute-start(bf16[2,48,384]{2,1,0:T(8,128)(2,1)S(1)} %pad_maximum_fusion.6), channel_id=1, source_target_pairs={{0,16},{4,20},{8,24},{12,28},{16,0},{20,4},{24,8},{28,12},{1,17},{... | collective-permute-start | bytes 221192 | tf_op jit(solution)/shard_map/ppermute | solution.py:668
  14.3 11.2 %collective-permute-start.1 = (bf16[2,64,384]{2,1,0:T(8,128)(2,1)S(1)}, bf16[2,64,384]{2,1,0:T(8,128)(2,1)S(1)}, u32[]{:S(2)}, u32[]{:S(2)}) collective-permute-start(bf16[2,64,384]{2,1,0:T(8,128)(2,1)S(1)} %pad_maximum_fusion.5), channel_id=1, source_target_pairs={{0,8},{4,12},{8,0},{12,4},{16,24},{20,28},{24,16},{28,20},{1,9},{5... | collective-permute-start | bytes 294920 | tf_op jit(solution)/shard_map/ppermute | solution.py:668
  22.4 8.0 %collective-permute-start.11 = (bf16[4,64,384]{2,1,0:T(8,128)(2,1)}, bf16[4,64,384]{2,1,0:T(8,128)(2,1)S(1)}, u32[]{:S(2)}, u32[]{:S(2)}) collective-permute-start(bf16[4,64,384]{2,1,0:T(8,128)(2,1)} %shard_map.138.refs_0_.rest_0_), channel_id=1, source_target_pairs={{0,2},{1,3},{2,0},{3,1},{4,6},{5,7},{6,4},{7,5},{8,10},{9,11},{10,... | collective-permute-start | bytes 589832 | tf_op jit(solution)/shard_map/ppermute | solution.py:672
  23.9 6.4 %collective-permute-start.5 = (bf16[4,48,384]{2,1,0:T(8,128)(2,1)S(1)}, bf16[4,48,384]{2,1,0:T(8,128)(2,1)S(1)}, u32[]{:S(2)}, u32[]{:S(2)}) collective-permute-start(bf16[4,48,384]{2,1,0:T(8,128)(2,1)S(1)} %pad_maximum_fusion.4), channel_id=1, source_target_pairs={{0,8},{4,12},{8,0},{12,4},{16,24},{20,28},{24,16},{28,20},{1,9},{5... | collective-permute-start | bytes 442376 | tf_op jit(solution)/shard_map/ppermute | solution.py:668
  25.6 7.2 %collective-permute-start.2 = (bf16[4,64,384]{2,1,0:T(8,128)(2,1)S(1)}, bf16[4,64,384]{2,1,0:T(8,128)(2,1)S(1)}, u32[]{:S(2)}, u32[]{:S(2)}) collective-permute-start(bf16[4,64,384]{2,1,0:T(8,128)(2,1)S(1)} %pad_maximum_fusion.2), channel_id=1, source_target_pairs={{0,4},{4,0},{8,12},{12,8},{16,20},{20,16},{24,28},{28,24},{1,5},{5... | collective-permute-start | bytes 589832 | tf_op jit(solution)/shard_map/ppermute | solution.py:668
  26.2 6.7 %collective-permute-start.13 = (bf16[2,64,384]{2,1,0:T(8,128)(2,1)S(1)}, bf16[2,64,384]{2,1,0:T(8,128)(2,1)S(1)}, u32[]{:S(2)}, u32[]{:S(2)}) collective-permute-start(bf16[2,64,384]{2,1,0:T(8,128)(2,1)S(1)} %get-tuple-element.57), channel_id=1, source_target_pairs={{0,1},{1,0},{2,3},{3,2},{4,5},{5,4},{6,7},{7,6},{8,9},{9,8},{10,11... | collective-permute-start | bytes 294920 | tf_op jit(solution)/shard_map/ppermute | solution.py:672
  26.2 7.3 %collective-permute-start.14 = (bf16[2,64,384]{2,1,0:T(8,128)(2,1)S(1)}, bf16[2,64,384]{2,1,0:T(8,128)(2,1)S(1)}, u32[]{:S(2)}, u32[]{:S(2)}) collective-permute-start(bf16[2,64,384]{2,1,0:T(8,128)(2,1)S(1)} %get-tuple-element.58), channel_id=1, source_target_pairs={{0,3},{1,2},{2,1},{3,0},{4,7},{5,6},{6,5},{7,4},{8,11},{9,10},{10,... | collective-permute-start | bytes 294920 | tf_op jit(solution)/shard_map/ppermute | solution.py:672
  32.8 6.8 %collective-permute-start.18 = (bf16[2,64,384]{2,1,0:T(8,128)(2,1)S(1)}, bf16[2,64,384]{2,1,0:T(8,128)(2,1)S(1)}, u32[]{:S(2)}, u32[]{:S(2)}) collective-permute-start(bf16[2,64,384]{2,1,0:T(8,128)(2,1)S(1)} %get-tuple-element.68), channel_id=1, source_target_pairs={{0,1},{1,0},{2,3},{3,2},{4,5},{5,4},{6,7},{7,6},{8,9},{9,8},{10,11... | collective-permute-start | bytes 294920 | tf_op jit(solution)/shard_map/ppermute | solution.py:672
  32.9 6.8 %collective-permute-start.19 = (bf16[2,64,384]{2,1,0:T(8,128)(2,1)S(1)}, bf16[2,64,384]{2,1,0:T(8,128)(2,1)S(1)}, u32[]{:S(2)}, u32[]{:S(2)}) collective-permute-start(bf16[2,64,384]{2,1,0:T(8,128)(2,1)S(1)} %get-tuple-element.69), channel_id=1, source_target_pairs={{0,2},{1,3},{2,0},{3,1},{4,6},{5,7},{6,4},{7,5},{8,10},{9,11},{10,... | collective-permute-start | bytes 294920 | tf_op jit(solution)/shard_map/ppermute | solution.py:672
  33.5 6.4 %collective-permute-start.20 = (bf16[2,64,384]{2,1,0:T(8,128)(2,1)S(1)}, bf16[2,64,384]{2,1,0:T(8,128)(2,1)S(1)}, u32[]{:S(2)}, u32[]{:S(2)}) collective-permute-start(bf16[2,64,384]{2,1,0:T(8,128)(2,1)S(1)} %get-tuple-element.70), channel_id=1, source_target_pairs={{0,3},{1,2},{2,1},{3,0},{4,7},{5,6},{6,5},{7,4},{8,11},{9,10},{10,... | collective-permute-start | bytes 294920 | tf_op jit(solution)/shard_map/ppermute | solution.py:672
  37.9 9.6 %collective-permute-start.16 = (bf16[2,64,384]{2,1,0:T(8,128)(2,1)S(1)}, bf16[2,64,384]{2,1,0:T(8,128)(2,1)S(1)}, u32[]{:S(2)}, u32[]{:S(2)}) collective-permute-start(bf16[2,64,384]{2,1,0:T(8,128)(2,1)S(1)} %get-tuple-element.61), channel_id=1, source_target_pairs={{0,2},{1,3},{2,0},{3,1},{4,6},{5,7},{6,4},{7,5},{8,10},{9,11},{10,... | collective-permute-start | bytes 294920 | tf_op jit(solution)/shard_map/ppermute | solution.py:672
  38.5 9.0 %collective-permute-start.17 = (bf16[2,64,384]{2,1,0:T(8,128)(2,1)S(1)}, bf16[2,64,384]{2,1,0:T(8,128)(2,1)S(1)}, u32[]{:S(2)}, u32[]{:S(2)}) collective-permute-start(bf16[2,64,384]{2,1,0:T(8,128)(2,1)S(1)} %get-tuple-element.62), channel_id=1, source_target_pairs={{0,3},{1,2},{2,1},{3,0},{4,7},{5,6},{6,5},{7,4},{8,11},{9,10},{10,... | collective-permute-start | bytes 294920 | tf_op jit(solution)/shard_map/ppermute | solution.py:672
  49.7 13.9 %collective-permute-start.29 = (bf16[4,96,384]{2,1,0:T(8,128)(2,1)S(1)}, bf16[4,96,384]{2,1,0:T(8,128)(2,1)S(1)}, u32[]{:S(2)}, u32[]{:S(2)}) collective-permute-start(bf16[4,96,384]{2,1,0:T(8,128)(2,1)S(1)} %slice.49), channel_id=1, source_target_pairs={{0,4},{4,0},{8,12},{12,8},{16,20},{20,16},{24,28},{28,24},{1,5},{5... | collective-permute-start | bytes 884744 | tf_op jit(solution)/shard_map/ppermute | solution.py:668
  53.7 7.3 %collective-permute-start.25 = (bf16[320,384]{1,0:T(8,128)(2,1)S(1)}, bf16[320,384]{1,0:T(8,128)(2,1)S(1)}, u32[]{:S(2)}, u32[]{:S(2)}) collective-permute-start(bf16[320,384]{1,0:T(8,128)(2,1)S(1)} %shard_map.145), channel_id=1, source_target_pairs={{0,2},{1,3},{2,0},{3,1},{4,6},{5,7},{6,4},{7,5},{8,10},{9,11},{10,... | collective-permute-start | bytes 737288 | tf_op jit(solution)/shard_map/ppermute | solution.py:672
  68.2 6.9 %collective-permute-start.23 = (bf16[2,64,384]{2,1,0:T(8,128)(2,1)S(1)}, bf16[2,64,384]{2,1,0:T(8,128)(2,1)S(1)}, u32[]{:S(2)}, u32[]{:S(2)}) collective-permute-start(bf16[2,64,384]{2,1,0:T(8,128)(2,1)S(1)} %copy-done.15), channel_id=1, source_target_pairs={{0,3},{1,2},{2,1},{3,0},{4,7},{5,6},{6,5},{7,4},{8,11},{9,10},{10,... | collective-permute-start | bytes 294920 | tf_op jit(solution)/shard_map/ppermute | solution.py:672
  68.8 7.1 %collective-permute-start.26 = (bf16[3,64,384]{2,1,0:T(8,128)(2,1)S(1)}, bf16[3,64,384]{2,1,0:T(8,128)(2,1)S(1)}, u32[]{:S(2)}, u32[]{:S(2)}) collective-permute-start(bf16[3,64,384]{2,1,0:T(8,128)(2,1)S(1)} %get-tuple-element.80), channel_id=1, source_target_pairs={{0,1},{1,0},{2,3},{3,2},{4,5},{5,4},{6,7},{7,6},{8,9},{9,8},{10,11... | collective-permute-start | bytes 442376 | tf_op jit(solution)/shard_map/ppermute | solution.py:672
  72.8 6.6 %collective-permute-start.27 = (bf16[3,64,384]{2,1,0:T(8,128)(2,1)S(1)}, bf16[3,64,384]{2,1,0:T(8,128)(2,1)S(1)}, u32[]{:S(2)}, u32[]{:S(2)}) collective-permute-start(bf16[3,64,384]{2,1,0:T(8,128)(2,1)S(1)} %get-tuple-element.81), channel_id=1, source_target_pairs={{0,2},{1,3},{2,0},{3,1},{4,6},{5,7},{6,4},{7,5},{8,10},{9,11},{10,... | collective-permute-start | bytes 442376 | tf_op jit(solution)/shard_map/ppermute | solution.py:672
  73.4 6.2 %collective-permute-start.28 = (bf16[3,64,384]{2,1,0:T(8,128)(2,1)S(1)}, bf16[3,64,384]{2,1,0:T(8,128)(2,1)S(1)}, u32[]{:S(2)}, u32[]{:S(2)}) collective-permute-start(bf16[3,64,384]{2,1,0:T(8,128)(2,1)S(1)} %get-tuple-element.82), channel_id=1, source_target_pairs={{0,3},{1,2},{2,1},{3,0},{4,7},{5,6},{6,5},{7,4},{8,11},{9,10},{10,... | collective-permute-start | bytes 442376 | tf_op jit(solution)/shard_map/ppermute | solution.py:672
  73.5 8.1 %collective-permute-start.32 = (bf16[112,384]{1,0:T(8,128)(2,1)S(1)}, bf16[112,384]{1,0:T(8,128)(2,1)S(1)}, u32[]{:S(2)}, u32[]{:S(2)}) collective-permute-start(bf16[112,384]{1,0:T(8,128)(2,1)S(1)} %slice_bitcast_fusion.1), channel_id=1, source_target_pairs={{0,16},{4,20},{8,24},{12,28},{16,0},{20,4},{24,8},{28,12},{1,17},{... | collective-permute-start | bytes 258056 | tf_op jit(solution)/shard_map/ppermute | solution.py:668
  (30 other events, 88.8 us)

commit v4 on v3

--- a/solution.py
+++ b/solution.py
@@ -274,7 +274,9 @@
 N_DP = 8
 Z_FIRST = (4, 2, 1)
 Y_FIRST = (1, 4, 2)
+Y_LAST = (1, 4, 2)
 TAP_PAD = 32
+FLOPS_A_MICRO = 1.15e9
 TAPS = 31
 REACH = 15
 
@@ -293,7 +295,7 @@
     )
 
 
-def call_kernel(body, out_shape, ins, outs=None, scratch=(), room=40):
+def call_kernel(body, out_shape, ins, outs=None, scratch=(), room=40, micros=1.0):
     spaces = {
         "smem": pl.BlockSpec(memory_space=pltpu.SMEM),
         "vmem": pl.BlockSpec(memory_space=pltpu.VMEM),
@@ -307,6 +309,9 @@
         out_specs=[spaces[space] for space in (outs or ["vmem"] * len(out_shape))],
         scratch_shapes=list(scratch),
         compiler_params=pltpu.CompilerParams(vmem_limit_bytes=room * 1024 * 1024),
+        cost_estimate=pl.CostEstimate(
+            flops=int(micros * FLOPS_A_MICRO), bytes_accessed=0, transcendentals=0
+        ),
     )
 
 
@@ -346,11 +351,12 @@
         in_specs=[spec] * (count + len(awaited)),
         out_specs=(spec,) * count,
         input_output_aliases={number: number for number in range(count)},
+        compiler_params=pltpu.CompilerParams(vmem_limit_bytes=1024 * 1024),
     )(*arrays, *awaited)
 
 
-def pack_heads(query_ref, key_ref, value_ref, panel_ref, taps_ref, *rest):
-    outs, early_ref, late_ref, sem = rest[:N_CTX], *rest[N_CTX:]
+def pack_heads(query_ref, key_ref, value_ref, *rest):
+    outs, sem = rest[:N_CTX], rest[N_CTX]
     half = query_ref.shape[2] // 2
     place = lax.axis_index("ctx")
     pairs = []
@@ -359,53 +365,58 @@
         cols = columns((dest & 1) * half, half)
         for slot, ref in enumerate((query_ref, key_ref, value_ref)):
             pairs.append((ref.at[half_of(dest), :, cols], outs[apart].at[slot]))
+    run_copies(pairs, sem)
+
+
+def pack_weights(panel_ref, taps_ref, awaited_ref, early_ref, late_ref):
     split = late_ref.shape[1]
-    pairs.append((panel_ref.at[0:split], late_ref.at[0]))
-    pairs.append((panel_ref.at[split : 2 * split], early_ref.at[0, 0:split]))
-    start_copies(pairs, sem)
+    late_ref[0] = panel_ref[0:split]
+    early_ref[0, 0:split] = panel_ref[split : 2 * split]
     taps = taps_ref[...].astype(jnp.float32)
     high = jnp.concatenate(
         [taps[TAP_PAD // 2 :], jnp.zeros((TAP_PAD - TAPS, taps.shape[1]), jnp.float32)], axis=0
     )
     joined = jnp.concatenate([taps[: TAP_PAD // 2], high], axis=1)
     early_ref[0, split:, :] = joined.astype(jnp.bfloat16)
-    wait_copies(pairs, sem)
-
-
-def pack_channels(in_ref, *rest):
-    outs, sem = rest[-N_CTX - 1 : -1], rest[-1]
-    width = in_ref.shape[2] // N_CTX
+
+
+def pack_channels(frame_ref, grad_ref, awaited_ref, *rest):
+    frame_outs, grad_outs, beside_ref, own_ref, sem = rest[:2], rest[2:4], *rest[4:]
+    width = frame_ref.shape[2] // N_CTX
     place = lax.axis_index("ctx")
     pairs = []
-    for apart in (2, 3, 1, 0):
-        cols = columns((place ^ apart) * width, width)
-        for utt in range(2):
-            pairs.append((in_ref.at[utt, :, cols], outs[apart].at[utt]))
+    for slot, (ref, outs) in enumerate(((frame_ref, frame_outs), (grad_ref, grad_outs))):
+        targets = [own_ref.at[slot], beside_ref.at[slot], outs[0], outs[1]]
+        for apart in (2, 3, 1, 0):
+            cols = columns((place ^ apart) * width, width)
+            for utt in range(2):
+                pairs.append((ref.at[utt, :, cols], targets[apart].at[utt]))
     run_copies(pairs, sem)
 
 
-def unpack_channels(*refs):
-    ins, out_ref, sem = refs[:N_CTX], refs[N_CTX], refs[N_CTX + 1]
-    width = ins[0].shape[2]
-    place = lax.axis_index("ctx")
-    pairs = []
-    for apart in range(N_CTX):
-        cols = columns((place ^ apart) * width, width)
-        for utt in range(2):
-            pairs.append((ins[apart].at[utt], out_ref.at[utt, :, cols]))
-    run_copies(pairs, sem)
-
-
-def unpack_heads(*refs):
-    ins, outs, sem = refs[:N_CTX], refs[N_CTX : N_CTX + 3], refs[N_CTX + 3]
-    half = ins[0].shape[2]
+def unpack(*refs):
+    ins, own_ref, beside_ref = refs[:N_CTX], refs[N_CTX], refs[N_CTX + 1]
+    across_refs, diagonal_refs = refs[N_CTX + 2 : N_CTX + 4], refs[N_CTX + 4 : N_CTX + 6]
+    heads, channels, sem = refs[N_CTX + 7 : N_CTX + 10], refs[N_CTX + 10 : N_CTX + 12], refs[-1]
+    half, width = ins[0].shape[2], own_ref.shape[3]
+    frames = own_ref.shape[2]
     place = lax.axis_index("ctx")
     pairs = []
     for apart in range(N_CTX):
         source = place ^ apart
         cols = columns((source & 1) * half, half)
-        for slot in range(3):
-            pairs.append((ins[apart].at[slot], outs[slot].at[half_of(source), :, cols]))
+        for slot, ref in enumerate(heads):
+            pairs.append((ins[apart].at[slot], ref.at[half_of(source), :, cols]))
+    for slot, ref in enumerate(channels):
+        for apart in range(N_CTX):
+            cols = columns((place ^ apart) * width, width)
+            for utt in range(2):
+                if apart < 2:
+                    block = (own_ref, beside_ref)[apart].at[slot, utt]
+                else:
+                    block = (across_refs, diagonal_refs)[apart - 2][slot]
+                    block = block.at[utt * frames : (utt + 1) * frames]
+                pairs.append((block, ref.at[utt, :, cols]))
     run_copies(pairs, sem)
 
 
@@ -447,8 +458,12 @@
         attended_ref[:, :, cols] = joined.reshape(N_CTX, frames, LANES)
 
 
+def side_blocks(slot, refs):
+    return refs[0].at[slot], refs[1].at[slot], refs[2], refs[3]
+
+
 def forward(length_ref, early_ref, late_ref, *refs):
-    attended_refs, frame_refs = refs[:N_CTX], refs[N_CTX : 2 * N_CTX]
+    attended_refs, frame_refs = refs[:N_CTX], side_blocks(0, refs[N_CTX : 2 * N_CTX])
     out_refs = refs[2 * N_CTX : 3 * N_CTX]
     whole_ref, rows_ref, taps_ref, total_ref, masked_ref = refs[3 * N_CTX : 3 * N_CTX + 5]
     hidden_ref, frame_ref, result_ref = refs[3 * N_CTX + 5 :]
@@ -513,14 +528,18 @@
 
     lax.fori_loop(0, 2 * chunks, convolve, 0)
     for apart in range(N_CTX):
-        out_refs[apart][...] = result_ref[place ^ apart]
+        mine = result_ref[place ^ apart]
+        out_refs[apart][...] = mine.reshape(out_refs[apart].shape)
 
 
 def backward(length_ref, total_ref, masked_ref, taps_ref, rows_ref, *refs):
-    side_refs, out_refs = refs[:N_CTX], refs[N_CTX : 2 * N_CTX]
-    grad_ref, keep_ref, send_ref, sums_ref = refs[2 * N_CTX : 2 * N_CTX + 4]
-    side_ref, result_ref, cotangent_ref, tap_sum_ref = refs[2 * N_CTX + 4 :]
-    frames, width = side_refs[0].shape[1], side_refs[0].shape[2]
+    own_ref, beside_ref = refs[:2]
+    side_refs, refs = side_blocks(1, refs[2 : 2 + N_CTX]), refs[2 + N_CTX :]
+    own_pair_ref, beside_pair_ref, across_ref, diagonal_ref = refs[:N_CTX]
+    grad_ref, keep_ref, send_ref, sums_ref = refs[N_CTX : N_CTX + 4]
+    side_ref, result_ref, cotangent_ref, tap_sum_ref = refs[N_CTX + 4 :]
+    own_pair_ref[0], beside_pair_ref[0] = own_ref[...], beside_ref[...]
+    utts, frames, width = own_ref.shape
     rows = N_CTX * frames
     chunks = width // LANES
     half = rows_ref.shape[0] // 2
@@ -575,8 +594,17 @@
     ]
     sums = jnp.concatenate(sums, axis=1).astype(jnp.bfloat16)
     sums_ref[...] = sums
+    for ref in (across_ref, diagonal_ref):
+        ref[utts * frames :, :] = sums
+    for part in range(2):
+        send_ref[part, rows:, :] = sums[part * TAP_PAD // 2 : (part + 1) * TAP_PAD // 2]
     for apart in range(N_CTX):
-        out_refs[apart][...] = result_ref[place ^ apart]
+        mine = result_ref[place ^ apart]
+        if apart < 2:
+            (own_pair_ref, beside_pair_ref)[apart][1] = mine
+        else:
+            ref = (across_ref, diagonal_ref)[apart - 2]
+            ref[: utts * frames, :] = mine.reshape(utts * frames, width)
         dest = place ^ apart
         mixed = dot_tt(
             grad_ref[half_of(dest)],
@@ -588,13 +616,12 @@
         for block in range(N_CTX):
             first = pl.multiple_of((block ^ dest) * frames, frames)
             ref[apart // 2, pl.ds(first, frames), :] = mixed[block * frames : (block + 1) * frames]
-    for part in range(2):
-        send_ref[part, rows:, :] = sums[part * TAP_PAD // 2 : (part + 1) * TAP_PAD // 2]
-
-
-def make_panels(whole_ref, grad_ref, panel_ref):
+
+
+def make_panels(whole_ref, grad_ref, awaited_ref, early_ref, late_ref):
     rows, half = grad_ref.shape[1], whole_ref.shape[3] // 2
     entries = 2 * half // N_DP
+    split = entries // 2
     group = lax.axis_index("dp")
     for side in range(2):
         panel = 0.0
@@ -603,32 +630,44 @@
             panel += dot_tt(mixed, grad_ref[utt], 0, 0)
         panel = panel.astype(jnp.bfloat16)
         for part in range(N_DP // 2):
-            panel_ref[slot_of(side * N_DP // 2 + part, group)] = panel[
-                part * entries : (part + 1) * entries
-            ]
-
-
-def relay(keep_ref, came_ref, sums_ref, awaited_ref, out_ref):
+            index, first = side * N_DP // 2 + part, part * entries
+            late_ref[slot_of(index, group, Y_LAST)] = panel[first : first + split]
+            early_ref[slot_of(index, group)] = panel[first + split : first + entries]
+
+
+def make_tap_slots(sums_ref, came_ref, across_ref, diagonal_ref, awaited_ref, out_ref):
+    own = sums_ref.shape[1] // 2
+    rows, start = came_ref.shape[1] - TAP_PAD // 2, across_ref.shape[0] - TAP_PAD
+    group, place = lax.axis_index("dp"), lax.axis_index("ctx")
+    pieces = [
+        sums_ref[...],
+        jnp.concatenate([came_ref[0, rows:, :], came_ref[1, rows:, :]], axis=0),
+        across_ref[start:, :],
+        diagonal_ref[start:, :],
+    ]
+    for apart, piece in enumerate(pieces):
+        block = piece.astype(jnp.float32)
+        for part in range(2):
+            mine = block[:, part * own : (part + 1) * own]
+            mine = jnp.concatenate([mine[: TAP_PAD // 2], mine[TAP_PAD // 2 :]], axis=1)
+            out_ref[slot_of(2 * (place ^ apart) + part, group)] = mine.astype(jnp.bfloat16)
+
+
+def relay(keep_ref, came_ref, out_ref):
     rows = keep_ref.shape[1]
     total = keep_ref[1].astype(jnp.float32) + came_ref[1, 0:rows, :].astype(jnp.float32)
-    out_ref[0:rows, :] = total.astype(jnp.bfloat16)
-    out_ref[rows : rows + TAP_PAD, :] = sums_ref[...]
-    for part in range(2):
-        first = rows + TAP_PAD + part * TAP_PAD // 2
-        out_ref[first : first + TAP_PAD // 2, :] = came_ref[part, rows:, :]
-
-
-def attend_back(weight_ref, keep_ref, came_ref, far_ref, sums_ref, *refs):
-    ins, out_refs, taps_ref = refs[:N_CTX], refs[N_CTX : 2 * N_CTX], refs[2 * N_CTX]
+    out_ref[...] = total.astype(jnp.bfloat16)
+
+
+def attend_back(weight_ref, keep_ref, came_ref, far_ref, *refs):
+    ins, out_refs = refs[:N_CTX], refs[N_CTX:]
     frames, half = ins[0].shape[1], ins[0].shape[2]
     rows = N_CTX * frames
-    own = half // 2
-    group, place = lax.axis_index("dp"), lax.axis_index("ctx")
     query, key, value = (head_parts(ins, slot) for slot in range(3))
     masks = half_masks(rows)
     scale = HEAD_DIM ** (-0.5)
     arriving = keep_ref[0].astype(jnp.float32) + came_ref[0, 0:rows, :].astype(jnp.float32)
-    arriving = (arriving + far_ref[0:rows, :].astype(jnp.float32)).astype(jnp.bfloat16)
+    arriving = (arriving + far_ref[...].astype(jnp.float32)).astype(jnp.bfloat16)
     low_lanes = lax.broadcasted_iota(jnp.int32, (rows, LANES), 1) < HEAD_DIM
     for pair in range(half // LANES):
         cols = slice(pair * LANES, (pair + 1) * LANES)
@@ -651,17 +690,6 @@
         for slot, total in enumerate((query_sum, key_sum, value_sum)):
             for apart in range(N_CTX):
                 out_refs[apart][slot, :, cols] = total[apart * frames : (apart + 1) * frames]
-    pieces = [sums_ref[...]]
-    pieces.append(jnp.concatenate([came_ref[0, rows:, :], came_ref[1, rows:, :]], axis=0))
-    for part in range(2):
-        first = rows + part * TAP_PAD
-        pieces.append(far_ref[first : first + TAP_PAD, :])
-    for apart, piece in enumerate(pieces):
-        block = piece.astype(jnp.float32)
-        for part in range(2):
-            mine = block[:, part * own : (part + 1) * own]
-            mine = jnp.concatenate([mine[: TAP_PAD // 2], mine[TAP_PAD // 2 :]], axis=1)
-            taps_ref[slot_of(2 * (place ^ apart) + part, group)] = mine.astype(jnp.bfloat16)
 
 
 def swapped(array, bit):
@@ -694,29 +722,32 @@
     channel_block = shape((utts, frames, width), low)
 
     split = entries // 2
-    *blocks, early, late = call_kernel(
+    blocks = call_kernel(
         pack_heads,
-        (head_block,) * N_CTX
-        + (shape((1, split + TAP_PAD // 2, width), low), shape((1, split, width), low)),
-        ["hbm"] * 4 + ["vmem"],
-        scratch=[dma((3 * N_CTX + 2,))],
+        (head_block,) * N_CTX,
+        ["hbm"] * 3,
+        ["hbm"] * N_CTX,
+        [dma((3 * N_CTX,))],
         room=63,
-    )(queries, key_proj, value_proj, out_weight.T, conv_weight)
+    )(queries, key_proj, value_proj)
     packed = traded(blocks)
+    early, late = call_kernel(
+        pack_weights,
+        (shape((1, split + TAP_PAD // 2, width), low), shape((1, split, width), low)),
+        ["vmem"] * 2 + ["any"],
+    )(out_weight.T, conv_weight, packed[1])
     for early_bit, late_bit in zip(Z_FIRST, Y_FIRST):
         early = jnp.concatenate([early, swapped(early, early_bit)], axis=0)
         late = jnp.concatenate([late, swapped(late, late_bit)], axis=0)
-
-    def spread(array, *awaited):
-        blocks = call_kernel(
-            pack_channels,
-            (channel_block,) * N_CTX,
-            ["hbm"] + ["any"] * len(awaited),
-            scratch=[dma((2 * N_CTX,))],
-        )(array, *awaited)
-        return traded(blocks)
-
-    frame_blocks = spread(frame_input, blocks[0])
+    pair_block = shape((2, utts, frames, width), low)
+    *sides, beside_sides, own_sides = call_kernel(
+        pack_channels,
+        (channel_block,) * 4 + (pair_block,) * 2,
+        ["hbm"] * 2 + ["any"],
+        scratch=[dma((4 * N_CTX,))],
+    )(frame_input, grad_output, blocks[0])
+    frame_across, frame_diagonal = crossed(sides[0], 2), crossed(sides[1], 3)
+    beside_sides = crossed(beside_sides, 1)
     attended, weights = call_kernel(
         attend,
         (
@@ -724,15 +755,19 @@
             shape((half // HEAD_DIM, rows, rows), low),
         ),
         ["smem"] + ["vmem"] * N_CTX,
+        micros=3.0,
     )(lengths, *packed)
-    (attended,) = gate([attended], frame_blocks[2])
+    (attended,) = gate([attended], frame_across, frame_diagonal)
     across = crossed(attended, 2)
     beside = crossed(attended, 1)
     diagonal = crossed(across, 1)
-    grad_blocks = spread(grad_output, attended)
+    grad_across, grad_diagonal = crossed(sides[2], 2), crossed(sides[3], 3)
+    frame_blocks = (own_sides, beside_sides, frame_across, frame_diagonal)
+    grad_blocks = (own_sides, beside_sides, grad_across, grad_diagonal)
     forward_out = call_kernel(
         forward,
-        (channel_block,) * N_CTX
+        (channel_block,) * 2
+        + (shape((utts * frames, width), low),) * 2
         + (
             shape((utts, N_CTX, frames, inner), low),
             shape((inner, width), low),
@@ -746,75 +781,99 @@
             pltpu.VMEM((N_CTX, utts, frames, width), low),
             pltpu.VMEM((N_CTX, utts, frames, width), low),
         ],
+        micros=3.2,
     )(lengths, early, late, attended, beside, across, diagonal, *frame_blocks)
-    output_blocks = traded(forward_out[:N_CTX])
+    output_across, output_diagonal = crossed(forward_out[2], 2), crossed(forward_out[3], 3)
     whole, weight_rows, taps, totals, masked = forward_out[N_CTX:]
     backward_out = call_kernel(
         backward,
-        (channel_block,) * N_CTX
+        (pair_block,) * 2
+        + (shape((utts * frames + TAP_PAD, width), low),) * 2
         + (
             shape((utts, rows, width), low),
             shape((2, rows, half), low),
             shape((2, rows + TAP_PAD // 2, half), low),
             shape((TAP_PAD, width), low),
         ),
-        ["smem"] + ["vmem"] * (4 + N_CTX),
+        ["smem"] + ["vmem"] * (6 + N_CTX),
         scratch=[
             pltpu.VMEM((N_CTX, utts, frames, width), low),
             pltpu.VMEM((N_CTX, utts, frames, width), low),
             pltpu.VMEM((utts * chunks, rows + 32, LANES), f32),
             pltpu.VMEM((chunks, TAP_PAD, 8, LANES), f32),
         ],
-    )(lengths, totals, masked, taps, weight_rows, *grad_blocks)
+        micros=5.2,
+    )(lengths, totals, masked, taps, weight_rows, *forward_out[:2], *grad_blocks)
     grad_hidden, keep, send, sums = backward_out[N_CTX:]
-    (send,) = gate([send], *output_blocks[2:])
+    (send,) = gate([send], output_across, output_diagonal)
     came = crossed(send, 1)
-    input_blocks = traded(backward_out[:N_CTX])
-    (panels,) = call_kernel(
-        make_panels, (shape((N_DP, entries, width), low),), ["vmem"] * 2
-    )(whole, grad_hidden)
     (far,) = call_kernel(
-        relay, (shape((rows + 2 * TAP_PAD, half), low),), ["vmem"] * 3 + ["any"]
-    )(keep, came, sums, input_blocks[2])
+        relay, (shape((rows, half), low),), ["vmem"] * 2, micros=0.2
+    )(keep, came)
+    early_panels, late_panels = call_kernel(
+        make_panels,
+        (shape((N_DP, entries - split, width), low), shape((N_DP, split, width), low)),
+        ["vmem"] * 2 + ["any"],
+        micros=0.7,
+    )(whole, grad_hidden, far)
     far = crossed(far, 2)
-    back_out = call_kernel(
+
+    def halved(slots, bit):
+        count = slots.shape[0] // 2
+        return (slots[:count].astype(f32) + swapped(slots[count:], bit).astype(f32)).astype(low)
+
+    late_panels = halved(late_panels, Y_LAST[2])
+    input_blocks = gate(backward_out[2:4], late_panels)
+    input_across, input_diagonal = crossed(input_blocks[0], 2), crossed(input_blocks[1], 3)
+    back_blocks = call_kernel(
         attend_back,
-        (head_block,) * N_CTX + (shape((N_DP, TAP_PAD // 2, width), low),),
-        ["vmem"] * (5 + N_CTX),
-    )(weights, keep, came, far, sums, *packed)
-    grad_blocks = traded(back_out[:N_CTX])
-    tap_slots = back_out[N_CTX]
-
-    def added(kept, arrived):
-        return (kept.astype(f32) + arrived.astype(f32)).astype(low)
-
-    panels = added(panels[:4], swapped(panels[4:], 1))
-    tap_slots = added(tap_slots[:4], swapped(tap_slots[4:], 1))
-    summed = jnp.concatenate([panels, tap_slots], axis=1)
-    summed = added(summed[:2], swapped(summed[2:], 2))
-    last = summed[0].astype(f32) + swapped(summed[1], 4).astype(f32)
-
-    def gathered(blocks):
-        return call_kernel(
-            unpack_channels,
-            (shape((utts, frames, wide), low),),
-            ["any"] * N_CTX,
-            ["hbm"],
-            [dma((2 * N_CTX,))],
-        )(*blocks)[0]
-
-    block_output = gathered(output_blocks)
-    grad_input = gathered(input_blocks)
-    grad_queries, grad_keys, grad_values = call_kernel(
-        unpack_heads,
-        (shape((utts, frames, inner), low),) * 3,
-        ["any"] * N_CTX,
-        ["hbm"] * 3,
-        [dma((3 * N_CTX,))],
-    )(*grad_blocks)
-    grad_out_weight = last[:entries].T
+        (head_block,) * N_CTX,
+        ["vmem"] * (4 + N_CTX),
+        micros=2.2,
+    )(weights, keep, came, far, *packed)
+    grad_blocks = traded(gate(back_blocks, input_across))
+    own_pair, beside_pair = backward_out[:2]
+    (beside_pair,) = gate([beside_pair], grad_blocks[1])
+    beside_pair = crossed(beside_pair, 1)
+
+    def finished(slots, bit):
+        return slots[0].astype(f32) + swapped(slots[1], bit).astype(f32)
+
+    tap_slots = call_kernel(
+        make_tap_slots,
+        (shape((N_DP, TAP_PAD // 2, width), low),),
+        ["vmem"] * 4 + ["any"],
+        micros=0.2,
+    )(sums, came, input_across, input_diagonal, grad_blocks[1])[0]
+    tap_slots = halved(halved(tap_slots, 1), 2)
+    late_panels = halved(late_panels, Y_LAST[1])
+    early_panels = halved(halved(early_panels, 1), 2)
+    late_panels, early_panels = gate([late_panels, early_panels], grad_blocks[1])
+    grad_out_weight = jnp.concatenate(
+        [finished(late_panels, Y_LAST[0]), finished(early_panels, 4)], axis=0
+    ).T
+
+    grad_queries, grad_keys, grad_values, block_output, grad_input = call_kernel(
+        unpack,
+        (shape((utts, frames, inner), low),) * 3 + (shape((utts, frames, wide), low),) * 2,
+        ["any"] * (N_CTX + 7),
+        ["hbm"] * 5,
+        [dma((7 * N_CTX + 4 * N_CTX,))],
+        micros=10.0,
+    )(
+        *grad_blocks,
+        own_pair,
+        beside_pair,
+        output_across,
+        input_across,
+        output_diagonal,
+        input_diagonal,
+        tap_slots,
+    )
+    (tap_slots,) = gate([tap_slots], grad_queries)
+    tap_sums = finished(tap_slots, 4)
     own = width // 2
-    grad_taps = jnp.concatenate([last[entries:, :own], last[entries:, own:]], axis=0)[:tap_count]
+    grad_taps = jnp.concatenate([tap_sums[:, :own], tap_sums[:, own:]], axis=0)[:tap_count]
     return (
         block_output,
         grad_input,

time: 83.3 us -> 101 us (1.21)
  Pallas kernels: 19.1 us -> 34.8 us
  starting transfers between devices: 25.4 us -> 37.9 us
  waiting for transfers between devices: 29.3 us -> 22.3 us
  local copies, waits for them, and re-layouts: 7.16 us -> 2.78 us
    pallas_call x11 -> x10, Pallas kernels: 16.3 us -> 32 us  [the longest x1 19.1 us: per_device(): call_kernel(pack_heads, (head_block,) * N_CTX, ['hbm'] * 3, ['hbm'] * N_C...]
    ppermute x10 -> x15, starting transfers between devices: 12.6 us -> 24.5 us  [swapped(): return lax.ppermute(array, 'dp', [(i, i ^ bit) for i in range(N_DP)])]
    ppermute x23 -> x21, waiting for transfers between devices: 16 us -> 5.43 us  [crossed(): return lax.ppermute(array, 'ctx', [(i, i ^ apart) for i in range(N_CTX)])]
    unnamed x42 -> x16, local copies, waits for them, and re-layouts: 6.36 us -> 2.63 us
    ppermute x10 -> x15, waiting for transfers between devices: 13.3 us -> 16.9 us  [swapped(): return lax.ppermute(array, 'dp', [(i, i ^ bit) for i in range(N_DP)])]
    ppermute x23 -> x21, starting transfers between devices: 12.8 us -> 13.4 us  [crossed(): return lax.ppermute(array, 'ctx', [(i, i ^ apart) for i in range(N_CTX)])]
  transfers between devices with their start and end apart: 33 -> 36, of which waited for: 11 -> 11; matrix products, arithmetic and copies ran while one was open for 0% -> 1% of each run, Pallas kernels for 20% -> 14%
where the time goes in v4:
time: 101 us; the launch traced here: 100 us
  starting transfers between devices  37.9 us (38%)
  Pallas kernels  34.8 us (34%)
  waiting for transfers between devices  22.3 us (22%)
  local copies, waits for them, and re-layouts  2.78 us (3%)
  other arithmetic  1.64 us (2%)
    ppermute x15, starting transfers between devices, swapped(): return lax.ppermute(array, 'dp', [(i, i ^ bit) for i in range(N_DP)])  24.5 us
    pallas_call x1, Pallas kernels, per_device(): call_kernel(pack_heads, (head_block,) * N_CTX, ['hbm'] * 3, ['hbm'] * N_C...  19.1 us
    ppermute x15, waiting for transfers between devices, swapped(): return lax.ppermute(array, 'dp', [(i, i ^ bit) for i in range(N_DP)])  16.9 us
    ppermute x21, starting transfers between devices, crossed(): return lax.ppermute(array, 'ctx', [(i, i ^ apart) for i in range(N_CTX)])  13.4 us
    ppermute x21, waiting for transfers between devices, crossed(): return lax.ppermute(array, 'ctx', [(i, i ^ apart) for i in range(N_CTX)])  5.43 us
    pallas_call x1, Pallas kernels, per_device(): call_kernel(backward, (pair_block,) * 2 + (shape((utts * frames + TAP_PAD...  5.24 us
    pallas_call x1, Pallas kernels, per_device(): call_kernel(forward, (channel_block,) * 2 + (shape((utts * frames, width)...  3.15 us
    pallas_call x1, Pallas kernels, per_device(): call_kernel(attend, (shape((N_CTX, frames, half), low), shape((half // HE...  2.77 us
  transfers between devices with their start and end apart: 36, of which 11 were waited for; matrix products, arithmetic and copies ran while one was open for 1% of the time, Pallas kernels for 14%

profile of v4, /device:TPU:0, one launch (start us, length us, event | category | flops | bytes accessed | tf_op | source)
XLA Modules:
  0.0 100.4 jit_solution(14758873550508963570)
XLA Ops:
  0.7 19.1 %shard_map.135 = (bf16[3,64,384]{2,1,0:T(8,128)(2,1)}, bf16[3,64,384]{2,1,0:T(8,128)(2,1)}, bf16[3,64,384]{2,1,0:T(8,128)(2,1)}, bf16[3,64,384]{2,1,0:T(8,128)(2,1)}) custom-call(bf16[2,64,768]{2,1,0:T(8,128)(2,1)} %query_ref.1, bf16[2,64,768]{2,1,0:T(8,128)(2,1)} %key_ref.1, bf16[2,64,768]{2,1,0:T(8,128)(2,1)} %value_ref.1), custom_call_target="tpu_custom_call" | custom-call | flops 1150000000 | tf_op jit(solution)/shard_map/pallas_call | solution.py:725
  20.3 2.6 %collective-permute-start.1 = (bf16[3,64,384]{2,1,0:T(8,128)(2,1)}, bf16[3,64,384]{2,1,0:T(8,128)(2,1)S(1)}, u32[]{:S(2)}, u32[]{:S(2)}) collective-permute-start(bf16[3,64,384]{2,1,0:T(8,128)(2,1)} %get-tuple-element.59), channel_id=1, source_target_pairs={{0,2},{1,3},{2,0},{3,1},{4,6},{5,7},{6,4},{7,5},{8,10},{9,11},{10,... | collective-permute-start | bytes 442376 | tf_op jit(solution)/shard_map/ppermute | solution.py:700
  24.1 1.8 %collective-permute-start.9 = (bf16[2,64,384]{2,1,0:T(8,128)(2,1)S(1)}, bf16[2,64,384]{2,1,0:T(8,128)(2,1)S(1)}, u32[]{:S(2)}, u32[]{:S(2)}) collective-permute-start(bf16[2,64,384]{2,1,0:T(8,128)(2,1)S(1)} %get-tuple-element.65), channel_id=1, source_target_pairs={{0,2},{1,3},{2,0},{3,1},{4,6},{5,7},{6,4},{7,5},{8,10},{9,11},{10,... | collective-permute-start | bytes 294920 | tf_op jit(solution)/shard_map/ppermute | solution.py:700
  26.0 1.7 %collective-permute-start.6 = (bf16[1,48,384]{2,1,0:T(8,128)(2,1)S(1)}, bf16[1,48,384]{2,1,0:T(8,128)(2,1)S(1)}, u32[]{:S(2)}, u32[]{:S(2)}) collective-permute-start(bf16[1,48,384]{2,1,0:T(8,128)(2,1)S(1)} %get-tuple-element.63), channel_id=1, source_target_pairs={{0,4},{4,0},{8,12},{12,8},{16,20},{20,16},{24,28},{28,24},{1,5},{5... | collective-permute-start | bytes 110600 | tf_op jit(solution)/shard_map/ppermute | solution.py:696
  27.7 3.0 %collective-permute-start.3 = (bf16[1,64,384]{2,1,0:T(8,128)(2,1)S(1)}, bf16[1,64,384]{2,1,0:T(8,128)(2,1)S(1)}, u32[]{:S(2)}, u32[]{:S(2)}) collective-permute-start(bf16[1,64,384]{2,1,0:T(8,128)(2,1)S(1)} %get-tuple-element.62), channel_id=1, source_target_pairs={{0,16},{4,20},{8,24},{12,28},{16,0},{20,4},{24,8},{28,12},{1,17},{... | collective-permute-start | bytes 147464 | tf_op jit(solution)/shard_map/ppermute | solution.py:696
  30.8 2.8 %shard_map.136 = (bf16[4,64,384]{2,1,0:T(8,128)(2,1)S(1)}, bf16[6,256,256]{2,1,0:T(8,128)(2,1)S(1)}) custom-call(s32[2]{0:T(128)S(1)} %copy-done.5, bf16[3,64,384]{2,1,0:T(8,128)(2,1)S(1)} %copy-done.6, bf16[3,64,384]{2,1,0:T(8,128)(2,1)S(1)} %collective-permute-done.refs_1_.awaited_ref, bf16[3,64,384]{2,1,0:T(8,128)(2,1)S(1)} %collective-permute-done.1.refs_2_, ...), custom_call_target="tpu_custom_call" | custom-call | flops 3449999872 | tf_op jit(solution)/shard_map/pallas_call | solution.py:751
  34.6 1.6 %collective-permute-start.12 = (bf16[4,64,384]{2,1,0:T(8,128)(2,1)S(1)}, bf16[4,64,384]{2,1,0:T(8,128)(2,1)S(1)}, u32[]{:S(2)}, u32[]{:S(2)}) collective-permute-start(bf16[4,64,384]{2,1,0:T(8,128)(2,1)S(1)} %shard_map.139.refs_0_), channel_id=1, source_target_pairs={{0,2},{1,3},{2,0},{3,1},{4,6},{5,7},{6,4},{7,5},{8,10},{9,11},{10,... | collective-permute-start | bytes 589832 | tf_op jit(solution)/shard_map/ppermute | solution.py:700
  36.2 2.7 %collective-permute-start.7 = (bf16[2,48,384]{2,1,0:T(8,128)(2,1)S(1)}, bf16[2,48,384]{2,1,0:T(8,128)(2,1)S(1)}, u32[]{:S(2)}, u32[]{:S(2)}) collective-permute-start(bf16[2,48,384]{2,1,0:T(8,128)(2,1)S(1)} %pad_maximum_fusion.5), channel_id=1, source_target_pairs={{0,16},{4,20},{8,24},{12,28},{16,0},{20,4},{24,8},{28,12},{1,17},{... | collective-permute-start | bytes 221192 | tf_op jit(solution)/shard_map/ppermute | solution.py:696
  38.9 1.6 %collective-permute-start.4 = (bf16[2,64,384]{2,1,0:T(8,128)(2,1)S(1)}, bf16[2,64,384]{2,1,0:T(8,128)(2,1)S(1)}, u32[]{:S(2)}, u32[]{:S(2)}) collective-permute-start(bf16[2,64,384]{2,1,0:T(8,128)(2,1)S(1)} %pad_maximum_fusion.4), channel_id=1, source_target_pairs={{0,8},{4,12},{8,0},{12,4},{16,24},{20,28},{24,16},{28,20},{1,9},{5... | collective-permute-start | bytes 294920 | tf_op jit(solution)/shard_map/ppermute | solution.py:696
  40.5 2.4 %collective-permute-done.7 = bf16[2,48,384]{2,1,0:T(8,128)(2,1)S(1)} collective-permute-done((bf16[2,48,384]{2,1,0:T(8,128)(2,1)S(1)}, bf16[2,48,384]{2,1,0:T(8,128)(2,1)S(1)}, u32[]{:S(2)}, u32[]{:S(2)}) %collective-permute-start.7) | collective-permute-done | bytes 73760 | tf_op jit(solution)/shard_map/ppermute | solution.py:696
  44.0 1.6 %collective-permute-start.5 = (bf16[4,64,384]{2,1,0:T(8,128)(2,1)S(1)}, bf16[4,64,384]{2,1,0:T(8,128)(2,1)S(1)}, u32[]{:S(2)}, u32[]{:S(2)}) collective-permute-start(bf16[4,64,384]{2,1,0:T(8,128)(2,1)S(1)} %pad_maximum_fusion.2), channel_id=1, source_target_pairs={{0,4},{4,0},{8,12},{12,8},{16,20},{20,16},{24,28},{28,24},{1,5},{5... | collective-permute-start | bytes 589832 | tf_op jit(solution)/shard_map/ppermute | solution.py:696
  48.1 2.0 %collective-permute-done.5 = bf16[4,64,384]{2,1,0:T(8,128)(2,1)S(1)} collective-permute-done((bf16[4,64,384]{2,1,0:T(8,128)(2,1)S(1)}, bf16[4,64,384]{2,1,0:T(8,128)(2,1)S(1)}, u32[]{:S(2)}, u32[]{:S(2)}) %collective-permute-start.5) | collective-permute-done | bytes 196640 | tf_op jit(solution)/shard_map/ppermute | solution.py:696
  50.3 3.1 %shard_map.140 = (bf16[2,64,384]{2,1,0:T(8,128)(2,1)S(1)}, bf16[2,64,384]{2,1,0:T(8,128)(2,1)S(1)}, bf16[128,384]{1,0:T(8,128)(2,1)S(1)}, bf16[128,384]{1,0:T(8,...) custom-call(s32[2]{0:T(128)S(1)} %copy-done.5, ...), custom_call_target="tpu_custom_call" | custom-call | flops 3680000000 | tf_op jit(solution)/shard_map/pallas_call | solution.py:767
  55.4 5.2 %shard_map.141 = (bf16[2,2,64,384]{3,2,1,0:T(8,128)(2,1)S(1)}, bf16[2,2,64,384]{3,2,1,0:T(8,128)(2,1)S(1)}, bf16[160,384]{1,0:T(8,128)(2,1)S(1)}, bf16[160,384]{...) custom-call(s32[2]{0:T(128)S(1)} %copy-done.5, ...), custom_call_target="tpu_custom_call" | custom-call | flops 5980000256 | tf_op jit(solution)/shard_map/pallas_call | solution.py:788
  63.2 1.7 %collective-permute-start.31 = (bf16[4,48,384]{2,1,0:T(8,128)(2,1)S(1)}, bf16[4,48,384]{2,1,0:T(8,128)(2,1)S(1)}, u32[]{:S(2)}, u32[]{:S(2)}) collective-permute-start(bf16[4,48,384]{2,1,0:T(8,128)(2,1)S(1)} %slice.72), channel_id=1, source_target_pairs={{0,4},{4,0},{8,12},{12,8},{16,20},{20,16},{24,28},{28,24},{1,5},{5... | collective-permute-start | bytes 442376 | tf_op jit(solution)/shard_map/ppermute | solution.py:696
  67.7 1.6 %collective-permute-done.31 = bf16[4,48,384]{2,1,0:T(8,128)(2,1)S(1)} collective-permute-done((bf16[4,48,384]{2,1,0:T(8,128)(2,1)S(1)}, bf16[4,48,384]{2,1,0:T(8,128)(2,1)S(1)}, u32[]{:S(2)}, u32[]{:S(2)}) %collective-permute-start.31) | collective-permute-done | bytes 147488 | tf_op jit(solution)/shard_map/ppermute | solution.py:696
  72.2 3.6 %collective-permute-start.30 = (bf16[2,48,384]{2,1,0:T(8,128)(2,1)S(1)}, bf16[2,48,384]{2,1,0:T(8,128)(2,1)S(1)}, u32[]{:S(2)}, u32[]{:S(2)}) collective-permute-start(bf16[2,48,384]{2,1,0:T(8,128)(2,1)S(1)} %slice.89), channel_id=1, source_target_pairs={{0,16},{4,20},{8,24},{12,28},{16,0},{20,4},{24,8},{28,12},{1,17},{... | collective-permute-start | bytes 221192 | tf_op jit(solution)/shard_map/ppermute | solution.py:696
  76.7 2.0 %shard_map.144 = (bf16[3,64,384]{2,1,0:T(8,128)(2,1)S(1)}, bf16[3,64,384]{2,1,0:T(8,128)(2,1)S(1)}, bf16[3,64,384]{2,1,0:T(8,128)(2,1)S(1)}, bf16[3,64,384]{2,1,0:T(8,128)(2,1)S(1)}) custom-call(bf16[6,256,256]{2,1,0:T(8,128)(2,1)S(1)} %get-tuple-element.61.weight_ref, bf16[2,256,384]{2,1,0:T(8,128)(2,1)S(1)} %get-tuple-element.77.keep_ref, ...), custom_call_target="tpu_custom_call" | custom-call | flops 2529999872 | tf_op jit(solution)/shard_map/pallas_call | solution.py:828
  78.7 2.8 %collective-permute-done.22.refs_4_.across_ref.refs_7_ = bf16[160,384]{1,0:T(8,128)(2,1)S(1)} collective-permute-done((bf16[160,384]{1,0:T(8,128)(2,1)S(1)}, bf16[160,384]{1,0:T(8,128)(2,1)S(1)}, u32[]{:S(2)}, u32[]{:S(2)}) %collective-permute-start.22) | collective-permute-done | bytes 122912 | tf_op jit(solution)/shard_map/ppermute | solution.py:700
  81.6 1.9 %collective-permute-start.25 = (bf16[3,64,384]{2,1,0:T(8,128)(2,1)S(1)}, bf16[3,64,384]{2,1,0:T(8,128)(2,1)S(1)}, u32[]{:S(2)}, u32[]{:S(2)}) collective-permute-start(bf16[3,64,384]{2,1,0:T(8,128)(2,1)S(1)} %get-tuple-element.94), channel_id=1, source_target_pairs={{0,3},{1,2},{2,1},{3,0},{4,7},{5,6},{6,5},{7,4},{8,11},{9,10},{10,... | collective-permute-start | bytes 442376 | tf_op jit(solution)/shard_map/ppermute | solution.py:700
  84.3 1.6 %collective-permute-start.28 = (bf16[4,16,384]{2,1,0:T(8,128)(2,1)S(1)}, bf16[4,16,384]{2,1,0:T(8,128)(2,1)S(1)}, u32[]{:S(2)}, u32[]{:S(2)}) collective-permute-start(bf16[4,16,384]{2,1,0:T(8,128)(2,1)S(1)} %slice.85), channel_id=1, source_target_pairs={{0,4},{4,0},{8,12},{12,8},{16,20},{20,16},{24,28},{28,24},{1,5},{5... | collective-permute-start | bytes 147464 | tf_op jit(solution)/shard_map/ppermute | solution.py:696
  85.9 2.8 %collective-permute-done.34 = bf16[48,384]{1,0:T(8,128)(2,1)S(1)} collective-permute-done((bf16[48,384]{1,0:T(8,128)(2,1)S(1)}, bf16[48,384]{1,0:T(8,128)(2,1)S(1)}, u32[]{:S(2)}, u32[]{:S(2)}) %collective-permute-start.34) | collective-permute-done | bytes 36896 | tf_op jit(solution)/shard_map/ppermute | solution.py:696
  89.0 3.7 %collective-permute-done.29 = bf16[2,16,384]{2,1,0:T(8,128)(2,1)S(1)} collective-permute-done((bf16[2,16,384]{2,1,0:T(8,128)(2,1)S(1)}, bf16[2,16,384]{2,1,0:T(8,128)(2,1)S(1)}, u32[]{:S(2)}, u32[]{:S(2)}) %collective-permute-start.29) | collective-permute-done | bytes 24608 | tf_op jit(solution)/shard_map/ppermute | solution.py:696
  95.1 2.5 %collective-permute-start.35 = (bf16[16,384]{1,0:T(8,128)(2,1)S(1)}, bf16[16,384]{1,0:T(8,128)(2,1)S(1)}, u32[]{:S(2)}, u32[]{:S(2)}) collective-permute-start(bf16[16,384]{1,0:T(8,128)(2,1)S(1)} %slice_bitcast_fusion.2), channel_id=1, source_target_pairs={{0,16},{4,20},{8,24},{12,28},{16,0},{20,4},{24,8},{28,12},{1,17},{... | collective-permute-start | bytes 36872 | tf_op jit(solution)/shard_map/ppermute | solution.py:696
  (109 shorter events, 24.2 us)
Async XLA Ops:
  19.7 6.2 %collective-permute-start = (bf16[3,64,384]{2,1,0:T(8,128)(2,1)}, bf16[3,64,384]{2,1,0:T(8,128)(2,1)S(1)}, u32[]{:S(2)}, u32[]{:S(2)}) collective-permute-start(bf16[3,64,384]{2,1,0:T(8,128)(2,1)} %get-tuple-element.58), channel_id=1, source_target_pairs={{0,1},{1,0},{2,3},{3,2},{4,5},{5,4},{6,7},{7,6},{8,9},{9,8},{10,11... | collective-permute-start | bytes 442376 | tf_op jit(solution)/shard_map/ppermute | solution.py:700
  20.3 7.5 %collective-permute-start.1 = (bf16[3,64,384]{2,1,0:T(8,128)(2,1)}, bf16[3,64,384]{2,1,0:T(8,128)(2,1)S(1)}, u32[]{:S(2)}, u32[]{:S(2)}) collective-permute-start(bf16[3,64,384]{2,1,0:T(8,128)(2,1)} %get-tuple-element.59), channel_id=1, source_target_pairs={{0,2},{1,3},{2,0},{3,1},{4,6},{5,7},{6,4},{7,5},{8,10},{9,11},{10,... | collective-permute-start | bytes 442376 | tf_op jit(solution)/shard_map/ppermute | solution.py:700
  22.8 8.0 %collective-permute-start.2 = (bf16[3,64,384]{2,1,0:T(8,128)(2,1)}, bf16[3,64,384]{2,1,0:T(8,128)(2,1)S(1)}, u32[]{:S(2)}, u32[]{:S(2)}) collective-permute-start(bf16[3,64,384]{2,1,0:T(8,128)(2,1)} %get-tuple-element.60), channel_id=1, source_target_pairs={{0,3},{1,2},{2,1},{3,0},{4,7},{5,6},{6,5},{7,4},{8,11},{9,10},{10,... | collective-permute-start | bytes 442376 | tf_op jit(solution)/shard_map/ppermute | solution.py:700
  24.1 9.5 %collective-permute-start.9 = (bf16[2,64,384]{2,1,0:T(8,128)(2,1)S(1)}, bf16[2,64,384]{2,1,0:T(8,128)(2,1)S(1)}, u32[]{:S(2)}, u32[]{:S(2)}) collective-permute-start(bf16[2,64,384]{2,1,0:T(8,128)(2,1)S(1)} %get-tuple-element.65), channel_id=1, source_target_pairs={{0,2},{1,3},{2,0},{3,1},{4,6},{5,7},{6,4},{7,5},{8,10},{9,11},{10,... | collective-permute-start | bytes 294920 | tf_op jit(solution)/shard_map/ppermute | solution.py:700
  25.9 8.7 %collective-permute-start.10 = (bf16[2,64,384]{2,1,0:T(8,128)(2,1)S(1)}, bf16[2,64,384]{2,1,0:T(8,128)(2,1)S(1)}, u32[]{:S(2)}, u32[]{:S(2)}) collective-permute-start(bf16[2,64,384]{2,1,0:T(8,128)(2,1)S(1)} %get-tuple-element.66), channel_id=1, source_target_pairs={{0,3},{1,2},{2,1},{3,0},{4,7},{5,6},{6,5},{7,4},{8,11},{9,10},{10,... | collective-permute-start | bytes 294920 | tf_op jit(solution)/shard_map/ppermute | solution.py:700
  26.0 10.1 %collective-permute-start.6 = (bf16[1,48,384]{2,1,0:T(8,128)(2,1)S(1)}, bf16[1,48,384]{2,1,0:T(8,128)(2,1)S(1)}, u32[]{:S(2)}, u32[]{:S(2)}) collective-permute-start(bf16[1,48,384]{2,1,0:T(8,128)(2,1)S(1)} %get-tuple-element.63), channel_id=1, source_target_pairs={{0,4},{4,0},{8,12},{12,8},{16,20},{20,16},{24,28},{28,24},{1,5},{5... | collective-permute-start | bytes 110600 | tf_op jit(solution)/shard_map/ppermute | solution.py:696
  27.7 11.1 %collective-permute-start.3 = (bf16[1,64,384]{2,1,0:T(8,128)(2,1)S(1)}, bf16[1,64,384]{2,1,0:T(8,128)(2,1)S(1)}, u32[]{:S(2)}, u32[]{:S(2)}) collective-permute-start(bf16[1,64,384]{2,1,0:T(8,128)(2,1)S(1)} %get-tuple-element.62), channel_id=1, source_target_pairs={{0,16},{4,20},{8,24},{12,28},{16,0},{20,4},{24,8},{28,12},{1,17},{... | collective-permute-start | bytes 147464 | tf_op jit(solution)/shard_map/ppermute | solution.py:696
  34.6 11.5 %collective-permute-start.12 = (bf16[4,64,384]{2,1,0:T(8,128)(2,1)S(1)}, bf16[4,64,384]{2,1,0:T(8,128)(2,1)S(1)}, u32[]{:S(2)}, u32[]{:S(2)}) collective-permute-start(bf16[4,64,384]{2,1,0:T(8,128)(2,1)S(1)} %shard_map.139.refs_0_), channel_id=1, source_target_pairs={{0,2},{1,3},{2,0},{3,1},{4,6},{5,7},{6,4},{7,5},{8,10},{9,11},{10,... | collective-permute-start | bytes 589832 | tf_op jit(solution)/shard_map/ppermute | solution.py:700
  36.2 6.7 %collective-permute-start.7 = (bf16[2,48,384]{2,1,0:T(8,128)(2,1)S(1)}, bf16[2,48,384]{2,1,0:T(8,128)(2,1)S(1)}, u32[]{:S(2)}, u32[]{:S(2)}) collective-permute-start(bf16[2,48,384]{2,1,0:T(8,128)(2,1)S(1)} %pad_maximum_fusion.5), channel_id=1, source_target_pairs={{0,16},{4,20},{8,24},{12,28},{16,0},{20,4},{24,8},{28,12},{1,17},{... | collective-permute-start | bytes 221192 | tf_op jit(solution)/shard_map/ppermute | solution.py:696
  44.0 6.2 %collective-permute-start.5 = (bf16[4,64,384]{2,1,0:T(8,128)(2,1)S(1)}, bf16[4,64,384]{2,1,0:T(8,128)(2,1)S(1)}, u32[]{:S(2)}, u32[]{:S(2)}) collective-permute-start(bf16[4,64,384]{2,1,0:T(8,128)(2,1)S(1)} %pad_maximum_fusion.2), channel_id=1, source_target_pairs={{0,4},{4,0},{8,12},{12,8},{16,20},{20,16},{24,28},{28,24},{1,5},{5... | collective-permute-start | bytes 589832 | tf_op jit(solution)/shard_map/ppermute | solution.py:696
  45.6 9.8 %collective-permute-start.15 = (bf16[2,64,384]{2,1,0:T(8,128)(2,1)S(1)}, bf16[2,64,384]{2,1,0:T(8,128)(2,1)S(1)}, u32[]{:S(2)}, u32[]{:S(2)}) collective-permute-start(bf16[2,64,384]{2,1,0:T(8,128)(2,1)S(1)} %get-tuple-element.75), channel_id=1, source_target_pairs={{0,2},{1,3},{2,0},{3,1},{4,6},{5,7},{6,4},{7,5},{8,10},{9,11},{10,... | collective-permute-start | bytes 294920 | tf_op jit(solution)/shard_map/ppermute | solution.py:700
  50.2 5.2 %collective-permute-start.16 = (bf16[2,64,384]{2,1,0:T(8,128)(2,1)S(1)}, bf16[2,64,384]{2,1,0:T(8,128)(2,1)S(1)}, u32[]{:S(2)}, u32[]{:S(2)}) collective-permute-start(bf16[2,64,384]{2,1,0:T(8,128)(2,1)S(1)} %get-tuple-element.76), channel_id=1, source_target_pairs={{0,3},{1,2},{2,1},{3,0},{4,7},{5,6},{6,5},{7,4},{8,11},{9,10},{10,... | collective-permute-start | bytes 294920 | tf_op jit(solution)/shard_map/ppermute | solution.py:700
  53.4 7.2 %collective-permute-start.17 = (bf16[128,384]{1,0:T(8,128)(2,1)S(1)}, bf16[128,384]{1,0:T(8,128)(2,1)S(1)}, u32[]{:S(2)}, u32[]{:S(2)}) collective-permute-start(bf16[128,384]{1,0:T(8,128)(2,1)S(1)} %get-tuple-element.79), channel_id=1, source_target_pairs={{0,2},{1,3},{2,0},{3,1},{4,6},{5,7},{6,4},{7,5},{8,10},{9,11},{10,... | collective-permute-start | bytes 294920 | tf_op jit(solution)/shard_map/ppermute | solution.py:700
  54.0 6.7 %collective-permute-start.18 = (bf16[128,384]{1,0:T(8,128)(2,1)S(1)}, bf16[128,384]{1,0:T(8,128)(2,1)S(1)}, u32[]{:S(2)}, u32[]{:S(2)}) collective-permute-start(bf16[128,384]{1,0:T(8,128)(2,1)S(1)} %get-tuple-element.80), channel_id=1, source_target_pairs={{0,3},{1,2},{2,1},{3,0},{4,7},{5,6},{6,5},{7,4},{8,11},{9,10},{10,... | collective-permute-start | bytes 294920 | tf_op jit(solution)/shard_map/ppermute | solution.py:700
  63.2 6.0 %collective-permute-start.31 = (bf16[4,48,384]{2,1,0:T(8,128)(2,1)S(1)}, bf16[4,48,384]{2,1,0:T(8,128)(2,1)S(1)}, u32[]{:S(2)}, u32[]{:S(2)}) collective-permute-start(bf16[4,48,384]{2,1,0:T(8,128)(2,1)S(1)} %slice.72), channel_id=1, source_target_pairs={{0,4},{4,0},{8,12},{12,8},{16,20},{20,16},{24,28},{28,24},{1,5},{5... | collective-permute-start | bytes 442376 | tf_op jit(solution)/shard_map/ppermute | solution.py:696
  64.9 11.0 %collective-permute-start.20 = (bf16[256,384]{1,0:T(8,128)(2,1)S(1)}, bf16[256,384]{1,0:T(8,128)(2,1)S(1)}, u32[]{:S(2)}, u32[]{:S(2)}) collective-permute-start(bf16[256,384]{1,0:T(8,128)(2,1)S(1)} %shard_map.143.awaited_ref), channel_id=1, source_target_pairs={{0,2},{1,3},{2,0},{3,1},{4,6},{5,7},{6,4},{7,5},{8,10},{9,11},{10,... | collective-permute-start | bytes 589832 | tf_op jit(solution)/shard_map/ppermute | solution.py:700
  66.4 5.8 %collective-permute-start.21 = (bf16[4,48,384]{2,1,0:T(8,128)(2,1)S(1)}, bf16[4,48,384]{2,1,0:T(8,128)(2,1)S(1)}, u32[]{:S(2)}, u32[]{:S(2)}) collective-permute-start(bf16[4,48,384]{2,1,0:T(8,128)(2,1)S(1)} %slice.64), channel_id=1, source_target_pairs={{0,8},{4,12},{8,0},{12,4},{16,24},{20,28},{24,16},{28,20},{1,9},{5... | collective-permute-start | bytes 442376 | tf_op jit(solution)/shard_map/ppermute | solution.py:696
  69.3 9.3 %collective-permute-start.32 = (bf16[2,48,384]{2,1,0:T(8,128)(2,1)S(1)}, bf16[2,48,384]{2,1,0:T(8,128)(2,1)S(1)}, u32[]{:S(2)}, u32[]{:S(2)}) collective-permute-start(bf16[2,48,384]{2,1,0:T(8,128)(2,1)S(1)} %slice.91), channel_id=1, source_target_pairs={{0,8},{4,12},{8,0},{12,4},{16,24},{20,28},{24,16},{28,20},{1,9},{5... | collective-permute-start | bytes 221192 | tf_op jit(solution)/shard_map/ppermute | solution.py:696
  72.2 9.3 %collective-permute-start.30 = (bf16[2,48,384]{2,1,0:T(8,128)(2,1)S(1)}, bf16[2,48,384]{2,1,0:T(8,128)(2,1)S(1)}, u32[]{:S(2)}, u32[]{:S(2)}) collective-permute-start(bf16[2,48,384]{2,1,0:T(8,128)(2,1)S(1)} %slice.89), channel_id=1, source_target_pairs={{0,16},{4,20},{8,24},{12,28},{16,0},{20,4},{24,8},{28,12},{1,17},{... | collective-permute-start | bytes 221192 | tf_op jit(solution)/shard_map/ppermute | solution.py:696
  75.8 5.7 %collective-permute-start.22 = (bf16[160,384]{1,0:T(8,128)(2,1)S(1)}, bf16[160,384]{1,0:T(8,128)(2,1)S(1)}, u32[]{:S(2)}, u32[]{:S(2)}) collective-permute-start(bf16[160,384]{1,0:T(8,128)(2,1)S(1)} %get-tuple-element.90), channel_id=1, source_target_pairs={{0,2},{1,3},{2,0},{3,1},{4,6},{5,7},{6,4},{7,5},{8,10},{9,11},{10,... | collective-permute-start | bytes 368648 | tf_op jit(solution)/shard_map/ppermute | solution.py:700
  75.9 8.3 %collective-permute-start.27 = (bf16[160,384]{1,0:T(8,128)(2,1)S(1)}, bf16[160,384]{1,0:T(8,128)(2,1)S(1)}, u32[]{:S(2)}, u32[]{:S(2)}) collective-permute-start(bf16[160,384]{1,0:T(8,128)(2,1)S(1)} %get-tuple-element.97), channel_id=1, source_target_pairs={{0,3},{1,2},{2,1},{3,0},{4,7},{5,6},{6,5},{7,4},{8,11},{9,10},{10,... | collective-permute-start | bytes 368648 | tf_op jit(solution)/shard_map/ppermute | solution.py:700
  81.6 11.1 %collective-permute-start.24 = (bf16[3,64,384]{2,1,0:T(8,128)(2,1)S(1)}, bf16[3,64,384]{2,1,0:T(8,128)(2,1)S(1)}, u32[]{:S(2)}, u32[]{:S(2)}) collective-permute-start(bf16[3,64,384]{2,1,0:T(8,128)(2,1)S(1)} %get-tuple-element.93), channel_id=1, source_target_pairs={{0,2},{1,3},{2,0},{3,1},{4,6},{5,7},{6,4},{7,5},{8,10},{9,11},{10,... | collective-permute-start | bytes 442376 | tf_op jit(solution)/shard_map/ppermute | solution.py:700
  81.6 11.1 %collective-permute-start.25 = (bf16[3,64,384]{2,1,0:T(8,128)(2,1)S(1)}, bf16[3,64,384]{2,1,0:T(8,128)(2,1)S(1)}, u32[]{:S(2)}, u32[]{:S(2)}) collective-permute-start(bf16[3,64,384]{2,1,0:T(8,128)(2,1)S(1)} %get-tuple-element.94), channel_id=1, source_target_pairs={{0,3},{1,2},{2,1},{3,0},{4,7},{5,6},{6,5},{7,4},{8,11},{9,10},{10,... | collective-permute-start | bytes 442376 | tf_op jit(solution)/shard_map/ppermute | solution.py:700
  83.7 5.3 %collective-permute-start.33 = (bf16[48,384]{1,0:T(8,128)(2,1)S(1)}, bf16[48,384]{1,0:T(8,128)(2,1)S(1)}, u32[]{:S(2)}, u32[]{:S(2)}) collective-permute-start(bf16[48,384]{1,0:T(8,128)(2,1)S(1)} %slice_bitcast_fusion.1), channel_id=1, source_target_pairs={{0,4},{4,0},{8,12},{12,8},{16,20},{20,16},{24,28},{28,24},{1,5},{5... | collective-permute-start | bytes 110600 | tf_op jit(solution)/shard_map/ppermute | solution.py:696
  (20 other events, 103.0 us)

commit v5 on v4

--- a/solution.py
+++ b/solution.py
@@ -272,21 +272,15 @@
 LANES = 128
 N_CTX = 4
 N_DP = 8
-Z_FIRST = (4, 2, 1)
-Y_FIRST = (1, 4, 2)
-Y_LAST = (1, 4, 2)
 TAP_PAD = 32
 FLOPS_A_MICRO = 1.15e9
 TAPS = 31
 REACH = 15
 
 
-def slot_of(index, me, bits=Z_FIRST):
-    apart = jnp.bitwise_xor(index, me)
-    place = 0
-    for order, bit in enumerate(bits):
-        place += jnp.where((apart & bit) != 0, 1 << order, 0)
-    return place
+def slot_of(index, me):
+    apart = index ^ me
+    return ((apart & 1) << 2) | (apart & 2) | ((apart >> 2) & 1)
 
 
 def dot_tt(lhs, rhs, lhs_dim, rhs_dim):
@@ -342,7 +336,7 @@
     pass
 
 
-def gate(arrays, *awaited):
+def gate(arrays, *awaited, micros=0.0):
     count = len(arrays)
     spec = pl.BlockSpec(memory_space=pl.ANY)
     return pl.pallas_call(
@@ -352,6 +346,9 @@
         out_specs=(spec,) * count,
         input_output_aliases={number: number for number in range(count)},
         compiler_params=pltpu.CompilerParams(vmem_limit_bytes=1024 * 1024),
+        cost_estimate=pl.CostEstimate(
+            flops=int(micros * FLOPS_A_MICRO), bytes_accessed=0, transcendentals=0
+        ),
     )(*arrays, *awaited)
 
 
@@ -368,16 +365,16 @@
     run_copies(pairs, sem)
 
 
-def pack_weights(panel_ref, taps_ref, awaited_ref, early_ref, late_ref):
-    split = late_ref.shape[1]
-    late_ref[0] = panel_ref[0:split]
-    early_ref[0, 0:split] = panel_ref[split : 2 * split]
+def pack_weights(panel_ref, taps_ref, awaited_ref, out_ref):
+    entries = panel_ref.shape[0]
     taps = taps_ref[...].astype(jnp.float32)
     high = jnp.concatenate(
         [taps[TAP_PAD // 2 :], jnp.zeros((TAP_PAD - TAPS, taps.shape[1]), jnp.float32)], axis=0
     )
-    joined = jnp.concatenate([taps[: TAP_PAD // 2], high], axis=1)
-    early_ref[0, split:, :] = joined.astype(jnp.bfloat16)
+    joined = jnp.concatenate([taps[: TAP_PAD // 2], high], axis=1).astype(jnp.bfloat16)
+    for target in range(N_DP):
+        out_ref[target, 0:entries] = panel_ref[...]
+        out_ref[target, entries:] = joined
 
 
 def pack_channels(frame_ref, grad_ref, awaited_ref, *rest):
@@ -397,7 +394,7 @@
 def unpack(*refs):
     ins, own_ref, beside_ref = refs[:N_CTX], refs[N_CTX], refs[N_CTX + 1]
     across_refs, diagonal_refs = refs[N_CTX + 2 : N_CTX + 4], refs[N_CTX + 4 : N_CTX + 6]
-    heads, channels, sem = refs[N_CTX + 7 : N_CTX + 10], refs[N_CTX + 10 : N_CTX + 12], refs[-1]
+    heads, channels, sem = refs[N_CTX + 6 : N_CTX + 9], refs[N_CTX + 9 : N_CTX + 11], refs[-1]
     half, width = ins[0].shape[2], own_ref.shape[3]
     frames = own_ref.shape[2]
     place = lax.axis_index("ctx")
@@ -462,7 +459,7 @@
     return refs[0].at[slot], refs[1].at[slot], refs[2], refs[3]
 
 
-def forward(length_ref, early_ref, late_ref, *refs):
+def forward(length_ref, weight_ref, *refs):
     attended_refs, frame_refs = refs[:N_CTX], side_blocks(0, refs[N_CTX : 2 * N_CTX])
     out_refs = refs[2 * N_CTX : 3 * N_CTX]
     whole_ref, rows_ref, taps_ref, total_ref, masked_ref = refs[3 * N_CTX : 3 * N_CTX + 5]
@@ -473,21 +470,18 @@
     chunks = width // LANES
     entries = 2 * half // N_DP
     own = width // 2
-    group, place = lax.axis_index("dp"), lax.axis_index("ctx")
+    place = lax.axis_index("ctx")
     for apart in range(N_CTX):
         source = place ^ apart
         cols = columns((source & 1) * half, half)
         for block in range(N_CTX):
             whole_ref[half_of(source), block ^ source, :, cols] = attended_refs[apart][block]
         frame_ref[source] = frame_refs[apart][...]
-    split = late_ref.shape[1]
     for part in range(N_DP):
-        first = part * entries
-        rows_ref[first : first + split] = late_ref[slot_of(part, group, Y_FIRST)]
-        rows_ref[first + split : first + entries] = early_ref[slot_of(part, group), 0:split]
+        rows_ref[part * entries : (part + 1) * entries] = weight_ref[part, 0:entries]
     pieces = []
     for part in range(2):
-        block = early_ref[slot_of(2 * place + part, group), split:].astype(jnp.float32)
+        block = weight_ref[2 * place + part, entries:].astype(jnp.float32)
         pieces.append(jnp.concatenate([block[:, :own], block[:, own:]], axis=0))
     taps = jnp.concatenate(pieces, axis=1)
     for chunk in range(chunks):
@@ -618,10 +612,9 @@
             ref[apart // 2, pl.ds(first, frames), :] = mixed[block * frames : (block + 1) * frames]
 
 
-def make_panels(whole_ref, grad_ref, awaited_ref, early_ref, late_ref):
+def make_panels(whole_ref, grad_ref, awaited_ref, panel_ref):
     rows, half = grad_ref.shape[1], whole_ref.shape[3] // 2
     entries = 2 * half // N_DP
-    split = entries // 2
     group = lax.axis_index("dp")
     for side in range(2):
         panel = 0.0
@@ -630,15 +623,22 @@
             panel += dot_tt(mixed, grad_ref[utt], 0, 0)
         panel = panel.astype(jnp.bfloat16)
         for part in range(N_DP // 2):
-            index, first = side * N_DP // 2 + part, part * entries
-            late_ref[slot_of(index, group, Y_LAST)] = panel[first : first + split]
-            early_ref[slot_of(index, group)] = panel[first + split : first + entries]
+            panel_ref[slot_of(side * N_DP // 2 + part, group)] = panel[
+                part * entries : (part + 1) * entries
+            ]
+
+
+def total_of(in_ref, out_ref):
+    total = in_ref[0].astype(jnp.float32)
+    for source in range(1, N_DP):
+        total += in_ref[source].astype(jnp.float32)
+    out_ref[...] = total
 
 
 def make_tap_slots(sums_ref, came_ref, across_ref, diagonal_ref, awaited_ref, out_ref):
     own = sums_ref.shape[1] // 2
     rows, start = came_ref.shape[1] - TAP_PAD // 2, across_ref.shape[0] - TAP_PAD
-    group, place = lax.axis_index("dp"), lax.axis_index("ctx")
+    place = lax.axis_index("ctx")
     pieces = [
         sums_ref[...],
         jnp.concatenate([came_ref[0, rows:, :], came_ref[1, rows:, :]], axis=0),
@@ -650,7 +650,7 @@
         for part in range(2):
             mine = block[:, part * own : (part + 1) * own]
             mine = jnp.concatenate([mine[: TAP_PAD // 2], mine[TAP_PAD // 2 :]], axis=1)
-            out_ref[slot_of(2 * (place ^ apart) + part, group)] = mine.astype(jnp.bfloat16)
+            out_ref[2 * (place ^ apart) + part] = mine.astype(jnp.bfloat16)
 
 
 def relay(keep_ref, came_ref, out_ref):
@@ -696,6 +696,10 @@
     return lax.ppermute(array, "dp", [(i, i ^ bit) for i in range(N_DP)])
 
 
+def dealt(slots):
+    return lax.all_to_all(slots, "dp", 0, 0, tiled=True)
+
+
 def crossed(array, apart):
     return lax.ppermute(array, "ctx", [(i, i ^ apart) for i in range(N_CTX)])
 
@@ -721,24 +725,20 @@
     head_block = shape((3, frames, half), low)
     channel_block = shape((utts, frames, width), low)
 
-    split = entries // 2
     blocks = call_kernel(
         pack_heads,
         (head_block,) * N_CTX,
         ["hbm"] * 3,
-        ["hbm"] * N_CTX,
-        [dma((3 * N_CTX,))],
+        scratch=[dma((3 * N_CTX,))],
         room=63,
     )(queries, key_proj, value_proj)
     packed = traded(blocks)
-    early, late = call_kernel(
+    (shards,) = call_kernel(
         pack_weights,
-        (shape((1, split + TAP_PAD // 2, width), low), shape((1, split, width), low)),
+        (shape((N_DP, entries + TAP_PAD // 2, width), low),),
         ["vmem"] * 2 + ["any"],
     )(out_weight.T, conv_weight, packed[1])
-    for early_bit, late_bit in zip(Z_FIRST, Y_FIRST):
-        early = jnp.concatenate([early, swapped(early, early_bit)], axis=0)
-        late = jnp.concatenate([late, swapped(late, late_bit)], axis=0)
+    shards = dealt(shards)
     pair_block = shape((2, utts, frames, width), low)
     *sides, beside_sides, own_sides = call_kernel(
         pack_channels,
@@ -757,13 +757,12 @@
         ["smem"] + ["vmem"] * N_CTX,
         micros=3.0,
     )(lengths, *packed)
-    (attended,) = gate([attended], frame_across, frame_diagonal)
+    (attended,) = gate([attended], frame_across, frame_diagonal, micros=20.0)
     across = crossed(attended, 2)
     beside = crossed(attended, 1)
     diagonal = crossed(across, 1)
     grad_across, grad_diagonal = crossed(sides[2], 2), crossed(sides[3], 3)
     frame_blocks = (own_sides, beside_sides, frame_across, frame_diagonal)
-    grad_blocks = (own_sides, beside_sides, grad_across, grad_diagonal)
     forward_out = call_kernel(
         forward,
         (channel_block,) * 2
@@ -775,16 +774,18 @@
             shape((utts * chunks, rows, LANES), f32),
             shape((utts * chunks, rows + 32, LANES), f32),
         ),
-        ["smem"] + ["vmem"] * (2 + 2 * N_CTX),
+        ["smem"] + ["vmem"] * (1 + 2 * N_CTX),
         scratch=[
             pltpu.VMEM((utts * chunks, rows, LANES), f32),
             pltpu.VMEM((N_CTX, utts, frames, width), low),
             pltpu.VMEM((N_CTX, utts, frames, width), low),
         ],
         micros=3.2,
-    )(lengths, early, late, attended, beside, across, diagonal, *frame_blocks)
+    )(lengths, shards, attended, beside, across, diagonal, *frame_blocks)
     output_across, output_diagonal = crossed(forward_out[2], 2), crossed(forward_out[3], 3)
     whole, weight_rows, taps, totals, masked = forward_out[N_CTX:]
+    grad_blocks = gate([grad_across, grad_diagonal], totals, micros=10.0)
+    grad_blocks = (own_sides, beside_sides, *grad_blocks)
     backward_out = call_kernel(
         backward,
         (pair_block,) * 2
@@ -810,20 +811,20 @@
     (far,) = call_kernel(
         relay, (shape((rows, half), low),), ["vmem"] * 2, micros=0.2
     )(keep, came)
-    early_panels, late_panels = call_kernel(
+    (panels,) = call_kernel(
         make_panels,
-        (shape((N_DP, entries - split, width), low), shape((N_DP, split, width), low)),
+        (shape((N_DP, entries, width), low),),
         ["vmem"] * 2 + ["any"],
         micros=0.7,
     )(whole, grad_hidden, far)
-    far = crossed(far, 2)
 
     def halved(slots, bit):
         count = slots.shape[0] // 2
         return (slots[:count].astype(f32) + swapped(slots[count:], bit).astype(f32)).astype(low)
 
-    late_panels = halved(late_panels, Y_LAST[2])
-    input_blocks = gate(backward_out[2:4], late_panels)
+    panels = halved(halved(panels, 1), 2)
+    input_blocks = gate(backward_out[2:4], far)
+    far = crossed(far, 2)
     input_across, input_diagonal = crossed(input_blocks[0], 2), crossed(input_blocks[1], 3)
     back_blocks = call_kernel(
         attend_back,
@@ -836,30 +837,29 @@
     (beside_pair,) = gate([beside_pair], grad_blocks[1])
     beside_pair = crossed(beside_pair, 1)
 
-    def finished(slots, bit):
-        return slots[0].astype(f32) + swapped(slots[1], bit).astype(f32)
-
-    tap_slots = call_kernel(
+    def summed(slots, micros):
+        return call_kernel(
+            total_of, (shape(slots.shape[1:], f32),), ["vmem"], micros=micros
+        )(slots)[0]
+
+    (tap_slots,) = call_kernel(
         make_tap_slots,
         (shape((N_DP, TAP_PAD // 2, width), low),),
         ["vmem"] * 4 + ["any"],
         micros=0.2,
-    )(sums, came, input_across, input_diagonal, grad_blocks[1])[0]
-    tap_slots = halved(halved(tap_slots, 1), 2)
-    late_panels = halved(late_panels, Y_LAST[1])
-    early_panels = halved(halved(early_panels, 1), 2)
-    late_panels, early_panels = gate([late_panels, early_panels], grad_blocks[1])
-    grad_out_weight = jnp.concatenate(
-        [finished(late_panels, Y_LAST[0]), finished(early_panels, 4)], axis=0
-    ).T
-
-    grad_queries, grad_keys, grad_values, block_output, grad_input = call_kernel(
+    )(sums, came, input_across, input_diagonal, grad_blocks[1])
+
+    tap_sums = summed(dealt(tap_slots), 1.0)
+    (panels,) = gate([panels], grad_blocks[1])
+    grad_out_weight = (panels[0].astype(f32) + swapped(panels[1], 4).astype(f32)).T
+
+    unpacked = call_kernel(
         unpack,
         (shape((utts, frames, inner), low),) * 3 + (shape((utts, frames, wide), low),) * 2,
-        ["any"] * (N_CTX + 7),
+        ["any"] * (N_CTX + 6),
         ["hbm"] * 5,
         [dma((7 * N_CTX + 4 * N_CTX,))],
-        micros=10.0,
+        micros=1.0,
     )(
         *grad_blocks,
         own_pair,
@@ -868,10 +868,8 @@
         input_across,
         output_diagonal,
         input_diagonal,
-        tap_slots,
-    )
-    (tap_slots,) = gate([tap_slots], grad_queries)
-    tap_sums = finished(tap_slots, 4)
+    )
+    grad_queries, grad_keys, grad_values, block_output, grad_input = unpacked
     own = width // 2
     grad_taps = jnp.concatenate([tap_sums[:, :own], tap_sums[:, own:]], axis=0)[:tap_count]
     return (

time: 101 us -> 79.5 us (0.79)
  Pallas kernels: 34.8 us -> 19.3 us
  starting transfers between devices: 37.9 us -> 28.9 us
  waiting for transfers between devices: 22.3 us -> 26.8 us
    ppermute x15 -> x3, starting transfers between devices: 24.5 us -> 2.33 us  [swapped(): return lax.ppermute(array, 'dp', [(i, i ^ bit) for i in range(N_DP)])]
    pallas_call x3 -> x4, Pallas kernels: 19.8 us -> 3.61 us  [the longest x1 2.05 us: per_device(): call_kernel(pack_heads, (head_block,) * N_CTX, ['hbm'] * 3, scratch=[dma(...]
    all_to_all x0 -> x2, waiting for transfers between devices: none -> 12.3 us  [dealt(): return lax.all_to_all(slots, 'dp', 0, 0, tiled=True)]
    all_to_all x0 -> x2, starting transfers between devices: none -> 10.9 us  [dealt(): return lax.all_to_all(slots, 'dp', 0, 0, tiled=True)]
    ppermute x15 -> x3, waiting for transfers between devices: 16.9 us -> 8.08 us  [swapped(): return lax.ppermute(array, 'dp', [(i, i ^ bit) for i in range(N_DP)])]
    ppermute x21, starting transfers between devices: 13.4 us -> 15.7 us  [crossed(): return lax.ppermute(array, 'ctx', [(i, i ^ apart) for i in range(N_CTX)])]
    ppermute x21, waiting for transfers between devices: 5.43 us -> 6.45 us  [crossed(): return lax.ppermute(array, 'ctx', [(i, i ^ apart) for i in range(N_CTX)])]
    unnamed x16 -> x18, local copies, waits for them, and re-layouts: 2.63 us -> 1.8 us
  transfers between devices with their start and end apart: 36 -> 26, of which waited for: 11 -> 6; matrix products, arithmetic and copies ran while one was open for 1% -> 2% of each run, Pallas kernels for 14% -> 19%
where the time goes in v5:
time: 79.5 us; the launch traced here: 79.2 us
  starting transfers between devices  28.9 us (36%)
  waiting for transfers between devices  26.8 us (34%)
  Pallas kernels  19.3 us (24%)
  local copies, waits for them, and re-layouts  1.94 us (2%)
  other arithmetic  1.41 us (2%)
  between operations  0.89 us (1%)
    ppermute x21, starting transfers between devices, crossed(): return lax.ppermute(array, 'ctx', [(i, i ^ apart) for i in range(N_CTX)])  15.7 us
    all_to_all x2, waiting for transfers between devices, dealt(): return lax.all_to_all(slots, 'dp', 0, 0, tiled=True)  12.3 us
    all_to_all x2, starting transfers between devices, dealt(): return lax.all_to_all(slots, 'dp', 0, 0, tiled=True)  10.9 us
    ppermute x3, waiting for transfers between devices, swapped(): return lax.ppermute(array, 'dp', [(i, i ^ bit) for i in range(N_DP)])  8.08 us
    ppermute x21, waiting for transfers between devices, crossed(): return lax.ppermute(array, 'ctx', [(i, i ^ apart) for i in range(N_CTX)])  6.45 us
    pallas_call x1, Pallas kernels, per_device(): call_kernel(backward, (pair_block,) * 2 + (shape((utts * frames + TAP_PAD...  5.25 us
    pallas_call x1, Pallas kernels, per_device(): call_kernel(forward, (channel_block,) * 2 + (shape((utts * frames, width)...  3.12 us
    pallas_call x1, Pallas kernels, per_device(): call_kernel(attend, (shape((N_CTX, frames, half), low), shape((half // HE...  2.77 us
  transfers between devices with their start and end apart: 26, of which 6 were waited for; matrix products, arithmetic and copies ran while one was open for 2% of the time, Pallas kernels for 19%

profile of v5, /device:TPU:0, one launch (start us, length us, event | category | flops | bytes accessed | tf_op | source)
XLA Modules:
  0.0 79.2 jit_solution(15792856634531074157)
XLA Ops:
  0.7 2.0 %shard_map.135 = (bf16[3,64,384]{2,1,0:T(8,128)(2,1)}, bf16[3,64,384]{2,1,0:T(8,128)(2,1)}, bf16[3,64,384]{2,1,0:T(8,128)(2,1)}, bf16[3,64,384]{2,1,0:T(8,128)(2,1)}) custom-call(bf16[2,64,768]{2,1,0:T(8,128)(2,1)} %query_ref.1, bf16[2,64,768]{2,1,0:T(8,128)(2,1)} %key_ref.1, bf16[2,64,768]{2,1,0:T(8,128)(2,1)} %value_ref.1), custom_call_target="tpu_custom_call" | custom-call | flops 1150000000 | tf_op jit(solution)/shard_map/pallas_call | solution.py:728
  3.2 2.6 %collective-permute-start.1 = (bf16[3,64,384]{2,1,0:T(8,128)(2,1)}, bf16[3,64,384]{2,1,0:T(8,128)(2,1)S(1)}, u32[]{:S(2)}, u32[]{:S(2)}) collective-permute-start(bf16[3,64,384]{2,1,0:T(8,128)(2,1)} %get-tuple-element.55), channel_id=1, source_target_pairs={{0,2},{1,3},{2,0},{3,1},{4,6},{5,7},{6,4},{7,5},{8,10},{9,11},{10,... | collective-permute-start | bytes 442376 | tf_op jit(solution)/shard_map/ppermute | solution.py:704
  5.9 0.9 %copy-done.7 = bf16[3,64,384]{2,1,0:T(8,128)(2,1)S(1)} copy-done((bf16[3,64,384]{2,1,0:T(8,128)(2,1)S(1)}, bf16[3,64,384]{2,1,0:T(8,128)(2,1)}, u32[]{:S(2)}) %copy-start.7) | copy-done | bytes 147480
  7.1 1.8 %collective-permute-start.3 = (bf16[2,64,384]{2,1,0:T(8,128)(2,1)S(1)}, bf16[2,64,384]{2,1,0:T(8,128)(2,1)S(1)}, u32[]{:S(2)}, u32[]{:S(2)}) collective-permute-start(bf16[2,64,384]{2,1,0:T(8,128)(2,1)S(1)} %get-tuple-element.59), channel_id=1, source_target_pairs={{0,2},{1,3},{2,0},{3,1},{4,6},{5,7},{6,4},{7,5},{8,10},{9,11},{10,... | collective-permute-start | bytes 294920 | tf_op jit(solution)/shard_map/ppermute | solution.py:704
  8.9 0.9 %shard_map.137 = bf16[8,112,384]{2,1,0:T(8,128)(2,1)} custom-call(bf16[96,384]{1,0:T(8,128)(2,1)S(1)} %bitcast.10, bf16[31,192]{1,0:T(8,128)(2,1)S(1)} %copy-done.3, bf16[3,64,384]{2,1,0:T(8,128)(2,1)S(1)} %collective-permute-done.refs_1_.awaited_ref), custom_call_target="tpu_custom_call" | custom-call | flops 1150000000 | tf_op jit(solution)/shard_map/pallas_call | solution.py:736
  9.9 6.1 %all-to-all-start = ((bf16[8,112,384]{2,1,0:T(8,128)(2,1)}), bf16[8,112,384]{2,1,0:T(8,128)(2,1)S(1)}, u32[]{:S(2)}, u32[]{:S(2)}) async-start(bf16[8,112,384]{2,1,0:T(8,128)(2,1)} %shard_map.137), calls=%async_computation | async-start | bytes 1376256 | tf_op jit(solution)/shard_map/all_to_all | solution.py:700
  16.0 2.8 %shard_map.136 = (bf16[4,64,384]{2,1,0:T(8,128)(2,1)S(1)}, bf16[6,256,256]{2,1,0:T(8,128)(2,1)S(1)}) custom-call(s32[2]{0:T(128)S(1)} %copy-done.4, bf16[3,64,384]{2,1,0:T(8,128)(2,1)S(1)} %copy-done.8, bf16[3,64,384]{2,1,0:T(8,128)(2,1)S(1)} %collective-permute-done.refs_1_.awaited_ref, bf16[3,64,384]{2,1,0:T(8,128)(2,1)S(1)} %collective-permute-done.1.refs_2_, ...), custom_call_target="tpu_custom_call" | custom-call | flops 3449999872 | tf_op jit(solution)/shard_map/pallas_call | solution.py:751
  19.7 1.5 %collective-permute-start.6 = (bf16[4,64,384]{2,1,0:T(8,128)(2,1)S(1)}, bf16[4,64,384]{2,1,0:T(8,128)(2,1)S(1)}, u32[]{:S(2)}, u32[]{:S(2)}) collective-permute-start(bf16[4,64,384]{2,1,0:T(8,128)(2,1)S(1)} %shard_map.139.refs_0_), channel_id=1, source_target_pairs={{0,2},{1,3},{2,0},{3,1},{4,6},{5,7},{6,4},{7,5},{8,10},{9,11},{10,... | collective-permute-start | bytes 589832 | tf_op jit(solution)/shard_map/ppermute | solution.py:704
  21.7 5.0 %collective-permute-done.6.refs_2_ = bf16[4,64,384]{2,1,0:T(8,128)(2,1)S(1)} collective-permute-done((bf16[4,64,384]{2,1,0:T(8,128)(2,1)S(1)}, bf16[4,64,384]{2,1,0:T(8,128)(2,1)S(1)}, u32[]{:S(2)}, u32[]{:S(2)}) %collective-permute-start.6) | collective-permute-done | bytes 196640 | tf_op jit(solution)/shard_map/ppermute | solution.py:704
  26.7 1.5 %collective-permute-start.9 = (bf16[2,64,384]{2,1,0:T(8,128)(2,1)S(1)}, bf16[2,64,384]{2,1,0:T(8,128)(2,1)S(1)}, u32[]{:S(2)}, u32[]{:S(2)}) collective-permute-start(bf16[2,64,384]{2,1,0:T(8,128)(2,1)S(1)} %get-tuple-element.69), channel_id=1, source_target_pairs={{0,2},{1,3},{2,0},{3,1},{4,6},{5,7},{6,4},{7,5},{8,10},{9,11},{10,... | collective-permute-start | bytes 294920 | tf_op jit(solution)/shard_map/ppermute | solution.py:704
  28.6 6.1 %all-to-all-done.weight_ref = bf16[8,112,384]{2,1,0:T(8,128)(2,1)S(1)} async-done(((bf16[8,112,384]{2,1,0:T(8,128)(2,1)}), bf16[8,112,384]{2,1,0:T(8,128)(2,1)S(1)}, u32[]{:S(2)}, u32[]{:S(2)}) %all-to-all-start) | async-done | bytes 688160 | tf_op jit(solution)/shard_map/all_to_all | solution.py:700
  34.6 3.1 %shard_map.140 = (bf16[2,64,384]{2,1,0:T(8,128)(2,1)S(1)}, bf16[2,64,384]{2,1,0:T(8,128)(2,1)S(1)}, bf16[128,384]{1,0:T(8,128)(2,1)S(1)}, bf16[128,384]{1,0:T(8,...) custom-call(s32[2]{0:T(128)S(1)} %copy-done.4, ...), custom_call_target="tpu_custom_call" | custom-call | flops 3680000000 | tf_op jit(solution)/shard_map/pallas_call | solution.py:766
  37.8 1.6 %collective-permute-start.11 = (bf16[128,384]{1,0:T(8,128)(2,1)S(1)}, bf16[128,384]{1,0:T(8,128)(2,1)S(1)}, u32[]{:S(2)}, u32[]{:S(2)}) collective-permute-start(bf16[128,384]{1,0:T(8,128)(2,1)S(1)} %get-tuple-element.75), channel_id=1, source_target_pairs={{0,2},{1,3},{2,0},{3,1},{4,6},{5,7},{6,4},{7,5},{8,10},{9,11},{10,... | collective-permute-start | bytes 294920 | tf_op jit(solution)/shard_map/ppermute | solution.py:704
  39.3 5.2 %shard_map.142 = (bf16[2,2,64,384]{3,2,1,0:T(8,128)(2,1)S(1)}, bf16[2,2,64,384]{3,2,1,0:T(8,128)(2,1)S(1)}, bf16[160,384]{1,0:T(8,128)(2,1)S(1)}, bf16[160,384]{...) custom-call(s32[2]{0:T(128)S(1)} %copy-done.4, ...), custom_call_target="tpu_custom_call" | custom-call | flops 5980000256 | tf_op jit(solution)/shard_map/pallas_call | solution.py:789
  45.3 1.4 %collective-permute-done.13.came_ref = bf16[2,272,384]{2,1,0:T(8,128)(2,1)S(1)} collective-permute-done((bf16[2,272,384]{2,1,0:T(8,128)(2,1)S(1)}, bf16[2,272,384]{2,1,0:T(8,128)(2,1)S(1)}, u32[]{:S(2)}, u32[]{:S(2)}) %collective-permute-start.13) | collective-permute-done | bytes 417824 | tf_op jit(solution)/shard_map/ppermute | solution.py:704
  47.4 1.5 %collective-permute-start.21 = (bf16[4,96,384]{2,1,0:T(8,128)(2,1)S(1)}, bf16[4,96,384]{2,1,0:T(8,128)(2,1)S(1)}, u32[]{:S(2)}, u32[]{:S(2)}) collective-permute-start(bf16[4,96,384]{2,1,0:T(8,128)(2,1)S(1)} %slice.37), channel_id=1, source_target_pairs={{0,4},{4,0},{8,12},{12,8},{16,20},{20,16},{24,28},{28,24},{1,5},{5... | collective-permute-start | bytes 884744 | tf_op jit(solution)/shard_map/ppermute | solution.py:696
  48.9 1.5 %collective-permute-start.14 = (bf16[256,384]{1,0:T(8,128)(2,1)S(1)}, bf16[256,384]{1,0:T(8,128)(2,1)S(1)}, u32[]{:S(2)}, u32[]{:S(2)}) collective-permute-start(bf16[256,384]{1,0:T(8,128)(2,1)S(1)} %shard_map.144.refs_2_.awaited_ref), channel_id=1, source_target_pairs={{0,2},{1,3},{2,0},{3,1},{4,6},{5,7},{6,4},{7,5},{8,10},{9,11},{10,... | collective-permute-start | bytes 589832 | tf_op jit(solution)/shard_map/ppermute | solution.py:704
  51.6 5.2 %collective-permute-done.21 = bf16[4,96,384]{2,1,0:T(8,128)(2,1)S(1)} collective-permute-done((bf16[4,96,384]{2,1,0:T(8,128)(2,1)S(1)}, bf16[4,96,384]{2,1,0:T(8,128)(2,1)S(1)}, u32[]{:S(2)}, u32[]{:S(2)}) %collective-permute-start.21) | collective-permute-done | bytes 294944 | tf_op jit(solution)/shard_map/ppermute | solution.py:696
  57.3 2.0 %shard_map.145 = (bf16[3,64,384]{2,1,0:T(8,128)(2,1)S(1)}, bf16[3,64,384]{2,1,0:T(8,128)(2,1)S(1)}, bf16[3,64,384]{2,1,0:T(8,128)(2,1)S(1)}, bf16[3,64,384]{2,1,0:T(8,128)(2,1)S(1)}) custom-call(bf16[6,256,256]{2,1,0:T(8,128)(2,1)S(1)} %copy-done.6, bf16[2,256,384]{2,1,0:T(8,128)(2,1)S(1)} %get-tuple-element.73.keep_ref, ...), custom_call_target="tpu_custom_call" | custom-call | flops 2529999872 | tf_op jit(solution)/shard_map/pallas_call | solution.py:829
  59.4 2.9 %collective-permute-done.22 = bf16[2,96,384]{2,1,0:T(8,128)(2,1)S(1)} collective-permute-done((bf16[2,96,384]{2,1,0:T(8,128)(2,1)S(1)}, bf16[2,96,384]{2,1,0:T(8,128)(2,1)S(1)}, u32[]{:S(2)}, u32[]{:S(2)}) %collective-permute-start.22) | collective-permute-done | bytes 147488 | tf_op jit(solution)/shard_map/ppermute | solution.py:696
  62.7 1.5 %collective-permute-start.17 = (bf16[3,64,384]{2,1,0:T(8,128)(2,1)S(1)}, bf16[3,64,384]{2,1,0:T(8,128)(2,1)S(1)}, u32[]{:S(2)}, u32[]{:S(2)}) collective-permute-start(bf16[3,64,384]{2,1,0:T(8,128)(2,1)S(1)} %get-tuple-element.86), channel_id=1, source_target_pairs={{0,2},{1,3},{2,0},{3,1},{4,6},{5,7},{6,4},{7,5},{8,10},{9,11},{10,... | collective-permute-start | bytes 442376 | tf_op jit(solution)/shard_map/ppermute | solution.py:704
  65.0 4.7 %all-to-all-start.1 = ((bf16[8,16,384]{2,1,0:T(8,128)(2,1)}), bf16[8,16,384]{2,1,0:T(8,128)(2,1)S(1)}, u32[]{:S(2)}, u32[]{:S(2)}) async-start(bf16[8,16,384]{2,1,0:T(8,128)(2,1)} %shard_map.152), calls=%async_computation.1 | async-start | bytes 196608 | tf_op jit(solution)/shard_map/all_to_all | solution.py:700
  70.8 6.2 %all-to-all-done.1.in_ref = bf16[8,16,384]{2,1,0:T(8,128)(2,1)S(1)} async-done(((bf16[8,16,384]{2,1,0:T(8,128)(2,1)}), bf16[8,16,384]{2,1,0:T(8,128)(2,1)S(1)}, u32[]{:S(2)}, u32[]{:S(2)}) %all-to-all-start.1) | async-done | bytes 98336 | tf_op jit(solution)/shard_map/all_to_all | solution.py:700
  77.7 1.5 %shard_map.149 = (bf16[2,64,768]{2,1,0:T(8,128)(2,1)}, bf16[2,64,768]{2,1,0:T(8,128)(2,1)}, bf16[2,64,768]{2,1,0:T(8,128)(2,1)}, bf16[2,64,1536]{2,1,0:T(8,128)(2,1)}, bf16[2,64,1536]{2,1,0:T(8,128)(2,1)}) custom-call(bf16[3,64,384]{2,1,0:T(8,128)(2,1)S(1)} %get-tuple-element.84.refs_0_, bf16[3,64,384]{2,1,0:T(8,128)(2,1)S(1)} %collective-permute-done.16.refs_1_.awaited_ref, ...), custom_call_target="tpu_custom_call" | custom-call | flops 1150000000 | tf_op jit(solution)/shard_map/pallas_call | solution.py:856
  (73 shorter events, 8.9 us)
Async XLA Ops:
  2.7 6.2 %collective-permute-start = (bf16[3,64,384]{2,1,0:T(8,128)(2,1)}, bf16[3,64,384]{2,1,0:T(8,128)(2,1)S(1)}, u32[]{:S(2)}, u32[]{:S(2)}) collective-permute-start(bf16[3,64,384]{2,1,0:T(8,128)(2,1)} %get-tuple-element.54), channel_id=1, source_target_pairs={{0,1},{1,0},{2,3},{3,2},{4,5},{5,4},{6,7},{7,6},{8,9},{9,8},{10,11... | collective-permute-start | bytes 442376 | tf_op jit(solution)/shard_map/ppermute | solution.py:704
  3.2 12.8 %collective-permute-start.1 = (bf16[3,64,384]{2,1,0:T(8,128)(2,1)}, bf16[3,64,384]{2,1,0:T(8,128)(2,1)S(1)}, u32[]{:S(2)}, u32[]{:S(2)}) collective-permute-start(bf16[3,64,384]{2,1,0:T(8,128)(2,1)} %get-tuple-element.55), channel_id=1, source_target_pairs={{0,2},{1,3},{2,0},{3,1},{4,6},{5,7},{6,4},{7,5},{8,10},{9,11},{10,... | collective-permute-start | bytes 442376 | tf_op jit(solution)/shard_map/ppermute | solution.py:704
  5.8 10.2 %collective-permute-start.2 = (bf16[3,64,384]{2,1,0:T(8,128)(2,1)}, bf16[3,64,384]{2,1,0:T(8,128)(2,1)S(1)}, u32[]{:S(2)}, u32[]{:S(2)}) collective-permute-start(bf16[3,64,384]{2,1,0:T(8,128)(2,1)} %get-tuple-element.56), channel_id=1, source_target_pairs={{0,3},{1,2},{2,1},{3,0},{4,7},{5,6},{6,5},{7,4},{8,11},{9,10},{10,... | collective-permute-start | bytes 442376 | tf_op jit(solution)/shard_map/ppermute | solution.py:704
  7.1 11.7 %collective-permute-start.3 = (bf16[2,64,384]{2,1,0:T(8,128)(2,1)S(1)}, bf16[2,64,384]{2,1,0:T(8,128)(2,1)S(1)}, u32[]{:S(2)}, u32[]{:S(2)}) collective-permute-start(bf16[2,64,384]{2,1,0:T(8,128)(2,1)S(1)} %get-tuple-element.59), channel_id=1, source_target_pairs={{0,2},{1,3},{2,0},{3,1},{4,6},{5,7},{6,4},{7,5},{8,10},{9,11},{10,... | collective-permute-start | bytes 294920 | tf_op jit(solution)/shard_map/ppermute | solution.py:704
  8.9 10.0 %collective-permute-start.4 = (bf16[2,64,384]{2,1,0:T(8,128)(2,1)S(1)}, bf16[2,64,384]{2,1,0:T(8,128)(2,1)S(1)}, u32[]{:S(2)}, u32[]{:S(2)}) collective-permute-start(bf16[2,64,384]{2,1,0:T(8,128)(2,1)S(1)} %get-tuple-element.60), channel_id=1, source_target_pairs={{0,3},{1,2},{2,1},{3,0},{4,7},{5,6},{6,5},{7,4},{8,11},{9,10},{10,... | collective-permute-start | bytes 294920 | tf_op jit(solution)/shard_map/ppermute | solution.py:704
  9.9 24.8 %all-to-all-start = ((bf16[8,112,384]{2,1,0:T(8,128)(2,1)}), bf16[8,112,384]{2,1,0:T(8,128)(2,1)S(1)}, u32[]{:S(2)}, u32[]{:S(2)}) async-start(bf16[8,112,384]{2,1,0:T(8,128)(2,1)} %shard_map.137), calls=%async_computation | async-start | bytes 1376256 | tf_op jit(solution)/shard_map/all_to_all | solution.py:700
  19.7 7.0 %collective-permute-start.6 = (bf16[4,64,384]{2,1,0:T(8,128)(2,1)S(1)}, bf16[4,64,384]{2,1,0:T(8,128)(2,1)S(1)}, u32[]{:S(2)}, u32[]{:S(2)}) collective-permute-start(bf16[4,64,384]{2,1,0:T(8,128)(2,1)S(1)} %shard_map.139.refs_0_), channel_id=1, source_target_pairs={{0,2},{1,3},{2,0},{3,1},{4,6},{5,7},{6,4},{7,5},{8,10},{9,11},{10,... | collective-permute-start | bytes 589832 | tf_op jit(solution)/shard_map/ppermute | solution.py:704
  21.2 7.3 %collective-permute-start.8 = (bf16[2,2,64,384]{3,2,1,0:T(8,128)(2,1)S(1)}, bf16[2,2,64,384]{3,2,1,0:T(8,128)(2,1)S(1)}, u32[]{:S(2)}, u32[]{:S(2)}) collective-permute-start(bf16[2,2,64,384]{3,2,1,0:T(8,128)(2,1)S(1)} %get-tuple-element.62), channel_id=1, source_target_pairs={{0,1},{1,0},{2,3},{3,2},{4,5},{5,4},{6,7},{7,6},{8,9},{9,8},{10,11... | collective-permute-start | bytes 589832 | tf_op jit(solution)/shard_map/ppermute | solution.py:704
  21.2 7.3 %collective-permute-start.5 = (bf16[4,64,384]{2,1,0:T(8,128)(2,1)S(1)}, bf16[4,64,384]{2,1,0:T(8,128)(2,1)S(1)}, u32[]{:S(2)}, u32[]{:S(2)}) collective-permute-start(bf16[4,64,384]{2,1,0:T(8,128)(2,1)S(1)} %shard_map.139.refs_0_), channel_id=1, source_target_pairs={{0,1},{1,0},{2,3},{3,2},{4,5},{5,4},{6,7},{7,6},{8,9},{9,8},{10,11... | collective-permute-start | bytes 589832 | tf_op jit(solution)/shard_map/ppermute | solution.py:704
  26.7 12.6 %collective-permute-start.9 = (bf16[2,64,384]{2,1,0:T(8,128)(2,1)S(1)}, bf16[2,64,384]{2,1,0:T(8,128)(2,1)S(1)}, u32[]{:S(2)}, u32[]{:S(2)}) collective-permute-start(bf16[2,64,384]{2,1,0:T(8,128)(2,1)S(1)} %get-tuple-element.69), channel_id=1, source_target_pairs={{0,2},{1,3},{2,0},{3,1},{4,6},{5,7},{6,4},{7,5},{8,10},{9,11},{10,... | collective-permute-start | bytes 294920 | tf_op jit(solution)/shard_map/ppermute | solution.py:704
  28.2 11.2 %collective-permute-start.10 = (bf16[2,64,384]{2,1,0:T(8,128)(2,1)S(1)}, bf16[2,64,384]{2,1,0:T(8,128)(2,1)S(1)}, u32[]{:S(2)}, u32[]{:S(2)}) collective-permute-start(bf16[2,64,384]{2,1,0:T(8,128)(2,1)S(1)} %get-tuple-element.70), channel_id=1, source_target_pairs={{0,3},{1,2},{2,1},{3,0},{4,7},{5,6},{6,5},{7,4},{8,11},{9,10},{10,... | collective-permute-start | bytes 294920 | tf_op jit(solution)/shard_map/ppermute | solution.py:704
  37.8 6.8 %collective-permute-start.11 = (bf16[128,384]{1,0:T(8,128)(2,1)S(1)}, bf16[128,384]{1,0:T(8,128)(2,1)S(1)}, u32[]{:S(2)}, u32[]{:S(2)}) collective-permute-start(bf16[128,384]{1,0:T(8,128)(2,1)S(1)} %get-tuple-element.75), channel_id=1, source_target_pairs={{0,2},{1,3},{2,0},{3,1},{4,6},{5,7},{6,4},{7,5},{8,10},{9,11},{10,... | collective-permute-start | bytes 294920 | tf_op jit(solution)/shard_map/ppermute | solution.py:704
  39.3 5.3 %collective-permute-start.12 = (bf16[128,384]{1,0:T(8,128)(2,1)S(1)}, bf16[128,384]{1,0:T(8,128)(2,1)S(1)}, u32[]{:S(2)}, u32[]{:S(2)}) collective-permute-start(bf16[128,384]{1,0:T(8,128)(2,1)S(1)} %get-tuple-element.76), channel_id=1, source_target_pairs={{0,3},{1,2},{2,1},{3,0},{4,7},{5,6},{6,5},{7,4},{8,11},{9,10},{10,... | collective-permute-start | bytes 294920 | tf_op jit(solution)/shard_map/ppermute | solution.py:704
  47.4 9.3 %collective-permute-start.21 = (bf16[4,96,384]{2,1,0:T(8,128)(2,1)S(1)}, bf16[4,96,384]{2,1,0:T(8,128)(2,1)S(1)}, u32[]{:S(2)}, u32[]{:S(2)}) collective-permute-start(bf16[4,96,384]{2,1,0:T(8,128)(2,1)S(1)} %slice.37), channel_id=1, source_target_pairs={{0,4},{4,0},{8,12},{12,8},{16,20},{20,16},{24,28},{28,24},{1,5},{5... | collective-permute-start | bytes 884744 | tf_op jit(solution)/shard_map/ppermute | solution.py:696
  48.9 8.4 %collective-permute-start.14 = (bf16[256,384]{1,0:T(8,128)(2,1)S(1)}, bf16[256,384]{1,0:T(8,128)(2,1)S(1)}, u32[]{:S(2)}, u32[]{:S(2)}) collective-permute-start(bf16[256,384]{1,0:T(8,128)(2,1)S(1)} %shard_map.144.refs_2_.awaited_ref), channel_id=1, source_target_pairs={{0,2},{1,3},{2,0},{3,1},{4,6},{5,7},{6,4},{7,5},{8,10},{9,11},{10,... | collective-permute-start | bytes 589832 | tf_op jit(solution)/shard_map/ppermute | solution.py:704
  50.4 8.9 %collective-permute-start.15 = (bf16[160,384]{1,0:T(8,128)(2,1)S(1)}, bf16[160,384]{1,0:T(8,128)(2,1)S(1)}, u32[]{:S(2)}, u32[]{:S(2)}) collective-permute-start(bf16[160,384]{1,0:T(8,128)(2,1)S(1)} %get-tuple-element.83), channel_id=1, source_target_pairs={{0,2},{1,3},{2,0},{3,1},{4,6},{5,7},{6,4},{7,5},{8,10},{9,11},{10,... | collective-permute-start | bytes 368648 | tf_op jit(solution)/shard_map/ppermute | solution.py:704
  50.9 13.3 %collective-permute-start.20 = (bf16[160,384]{1,0:T(8,128)(2,1)S(1)}, bf16[160,384]{1,0:T(8,128)(2,1)S(1)}, u32[]{:S(2)}, u32[]{:S(2)}) collective-permute-start(bf16[160,384]{1,0:T(8,128)(2,1)S(1)} %get-tuple-element.90), channel_id=1, source_target_pairs={{0,3},{1,2},{2,1},{3,0},{4,7},{5,6},{6,5},{7,4},{8,11},{9,10},{10,... | collective-permute-start | bytes 368648 | tf_op jit(solution)/shard_map/ppermute | solution.py:704
  56.9 5.4 %collective-permute-start.22 = (bf16[2,96,384]{2,1,0:T(8,128)(2,1)S(1)}, bf16[2,96,384]{2,1,0:T(8,128)(2,1)S(1)}, u32[]{:S(2)}, u32[]{:S(2)}) collective-permute-start(bf16[2,96,384]{2,1,0:T(8,128)(2,1)S(1)} %slice.39), channel_id=1, source_target_pairs={{0,8},{4,12},{8,0},{12,4},{16,24},{20,28},{24,16},{28,20},{1,9},{5... | collective-permute-start | bytes 442376 | tf_op jit(solution)/shard_map/ppermute | solution.py:696
  59.3 3.0 %collective-permute-start.16 = (bf16[3,64,384]{2,1,0:T(8,128)(2,1)S(1)}, bf16[3,64,384]{2,1,0:T(8,128)(2,1)S(1)}, u32[]{:S(2)}, u32[]{:S(2)}) collective-permute-start(bf16[3,64,384]{2,1,0:T(8,128)(2,1)S(1)} %get-tuple-element.85), channel_id=1, source_target_pairs={{0,1},{1,0},{2,3},{3,2},{4,5},{5,4},{6,7},{7,6},{8,9},{9,8},{10,11... | collective-permute-start | bytes 442376 | tf_op jit(solution)/shard_map/ppermute | solution.py:704
  62.3 7.8 %collective-permute-start.23 = (bf16[96,384]{1,0:T(8,128)(2,1)S(1)}, bf16[96,384]{1,0:T(8,128)(2,1)S(1)}, u32[]{:S(2)}, u32[]{:S(2)}) collective-permute-start(bf16[96,384]{1,0:T(8,128)(2,1)S(1)} %slice_bitcast_fusion), channel_id=1, source_target_pairs={{0,16},{4,20},{8,24},{12,28},{16,0},{20,4},{24,8},{28,12},{1,17},{... | collective-permute-start | bytes 221192 | tf_op jit(solution)/shard_map/ppermute | solution.py:696
  62.7 15.0 %collective-permute-start.17 = (bf16[3,64,384]{2,1,0:T(8,128)(2,1)S(1)}, bf16[3,64,384]{2,1,0:T(8,128)(2,1)S(1)}, u32[]{:S(2)}, u32[]{:S(2)}) collective-permute-start(bf16[3,64,384]{2,1,0:T(8,128)(2,1)S(1)} %get-tuple-element.86), channel_id=1, source_target_pairs={{0,2},{1,3},{2,0},{3,1},{4,6},{5,7},{6,4},{7,5},{8,10},{9,11},{10,... | collective-permute-start | bytes 442376 | tf_op jit(solution)/shard_map/ppermute | solution.py:704
  64.2 13.5 %collective-permute-start.18 = (bf16[3,64,384]{2,1,0:T(8,128)(2,1)S(1)}, bf16[3,64,384]{2,1,0:T(8,128)(2,1)S(1)}, u32[]{:S(2)}, u32[]{:S(2)}) collective-permute-start(bf16[3,64,384]{2,1,0:T(8,128)(2,1)S(1)} %get-tuple-element.87), channel_id=1, source_target_pairs={{0,3},{1,2},{2,1},{3,0},{4,7},{5,6},{6,5},{7,4},{8,11},{9,10},{10,... | collective-permute-start | bytes 442376 | tf_op jit(solution)/shard_map/ppermute | solution.py:704
  65.0 12.0 %all-to-all-start.1 = ((bf16[8,16,384]{2,1,0:T(8,128)(2,1)}), bf16[8,16,384]{2,1,0:T(8,128)(2,1)S(1)}, u32[]{:S(2)}, u32[]{:S(2)}) async-start(bf16[8,16,384]{2,1,0:T(8,128)(2,1)} %shard_map.152), calls=%async_computation.1 | async-start | bytes 196608 | tf_op jit(solution)/shard_map/all_to_all | solution.py:700
  69.7 8.0 %collective-permute-start.19 = (bf16[2,2,64,384]{3,2,1,0:T(8,128)(2,1)S(1)}, bf16[2,2,64,384]{3,2,1,0:T(8,128)(2,1)S(1)}, u32[]{:S(2)}, u32[]{:S(2)}) collective-permute-start(bf16[2,2,64,384]{3,2,1,0:T(8,128)(2,1)S(1)} %shard_map.148), channel_id=1, source_target_pairs={{0,1},{1,0},{2,3},{3,2},{4,5},{5,4},{6,7},{7,6},{8,9},{9,8},{10,11... | collective-permute-start | bytes 589832 | tf_op jit(solution)/shard_map/ppermute | solution.py:704
  (11 other events, 39.7 us)

commit v6 on v5

--- a/solution.py
+++ b/solution.py
@@ -392,9 +392,9 @@
 
 
 def unpack(*refs):
-    ins, own_ref, beside_ref = refs[:N_CTX], refs[N_CTX], refs[N_CTX + 1]
-    across_refs, diagonal_refs = refs[N_CTX + 2 : N_CTX + 4], refs[N_CTX + 4 : N_CTX + 6]
-    heads, channels, sem = refs[N_CTX + 6 : N_CTX + 9], refs[N_CTX + 9 : N_CTX + 11], refs[-1]
+    ins, refs = refs[:N_CTX], refs[N_CTX:]
+    own_ref, beside_ref, output_ref, input_ref = refs[:4]
+    heads, channels, sem = refs[4:7], refs[7:9], refs[9]
     half, width = ins[0].shape[2], own_ref.shape[3]
     frames = own_ref.shape[2]
     place = lax.axis_index("ctx")
@@ -405,14 +405,16 @@
         for slot, ref in enumerate(heads):
             pairs.append((ins[apart].at[slot], ref.at[half_of(source), :, cols]))
     for slot, ref in enumerate(channels):
-        for apart in range(N_CTX):
-            cols = columns((place ^ apart) * width, width)
-            for utt in range(2):
-                if apart < 2:
-                    block = (own_ref, beside_ref)[apart].at[slot, utt]
-                else:
-                    block = (across_refs, diagonal_refs)[apart - 2][slot]
-                    block = block.at[utt * frames : (utt + 1) * frames]
+        for utt in range(2):
+            part = pl.ds(utt * frames, frames)
+            blocks = (
+                own_ref.at[slot, utt],
+                beside_ref.at[slot, part],
+                (output_ref, input_ref)[slot].at[0, part],
+                beside_ref.at[2 + slot, part],
+            )
+            for apart, block in enumerate(blocks):
+                cols = columns((place ^ apart) * width, width)
                 pairs.append((block, ref.at[utt, :, cols]))
     run_copies(pairs, sem)
 
@@ -461,9 +463,9 @@
 
 def forward(length_ref, weight_ref, *refs):
     attended_refs, frame_refs = refs[:N_CTX], side_blocks(0, refs[N_CTX : 2 * N_CTX])
-    out_refs = refs[2 * N_CTX : 3 * N_CTX]
-    whole_ref, rows_ref, taps_ref, total_ref, masked_ref = refs[3 * N_CTX : 3 * N_CTX + 5]
-    hidden_ref, frame_ref, result_ref = refs[3 * N_CTX + 5 :]
+    out_refs, refs = refs[2 * N_CTX : 2 * N_CTX + 3], refs[2 * N_CTX + 3 :]
+    whole_ref, rows_ref, taps_ref, total_ref, masked_ref = refs[:5]
+    hidden_ref, frame_ref, result_ref = refs[5:]
     frames, half = attended_refs[0].shape[1], attended_refs[0].shape[2]
     width = frame_ref.shape[3]
     rows = N_CTX * frames
@@ -521,17 +523,17 @@
         return carry
 
     lax.fori_loop(0, 2 * chunks, convolve, 0)
-    for apart in range(N_CTX):
-        mine = result_ref[place ^ apart]
-        out_refs[apart][...] = mine.reshape(out_refs[apart].shape)
+    for apart in range(2):
+        out_refs[apart][...] = result_ref[place ^ apart]
+        out_refs[2][apart] = result_ref[place ^ (2 + apart)].reshape(2 * frames, width)
 
 
 def backward(length_ref, total_ref, masked_ref, taps_ref, rows_ref, *refs):
     own_ref, beside_ref = refs[:2]
     side_refs, refs = side_blocks(1, refs[2 : 2 + N_CTX]), refs[2 + N_CTX :]
-    own_pair_ref, beside_pair_ref, across_ref, diagonal_ref = refs[:N_CTX]
-    grad_ref, keep_ref, send_ref, sums_ref = refs[N_CTX : N_CTX + 4]
-    side_ref, result_ref, cotangent_ref, tap_sum_ref = refs[N_CTX + 4 :]
+    own_pair_ref, beside_pair_ref, across_ref = refs[:3]
+    grad_ref, keep_ref, send_ref, sums_ref = refs[3:7]
+    side_ref, result_ref, cotangent_ref, tap_sum_ref = refs[7:]
     own_pair_ref[0], beside_pair_ref[0] = own_ref[...], beside_ref[...]
     utts, frames, width = own_ref.shape
     rows = N_CTX * frames
@@ -586,19 +588,13 @@
         )
         for chunk in range(chunks)
     ]
-    sums = jnp.concatenate(sums, axis=1).astype(jnp.bfloat16)
-    sums_ref[...] = sums
-    for ref in (across_ref, diagonal_ref):
-        ref[utts * frames :, :] = sums
-    for part in range(2):
-        send_ref[part, rows:, :] = sums[part * TAP_PAD // 2 : (part + 1) * TAP_PAD // 2]
+    sums_ref[...] = jnp.concatenate(sums, axis=1)
     for apart in range(N_CTX):
         mine = result_ref[place ^ apart]
         if apart < 2:
             (own_pair_ref, beside_pair_ref)[apart][1] = mine
         else:
-            ref = (across_ref, diagonal_ref)[apart - 2]
-            ref[: utts * frames, :] = mine.reshape(utts * frames, width)
+            across_ref[apart - 2] = mine.reshape(utts * frames, width)
         dest = place ^ apart
         mixed = dot_tt(
             grad_ref[half_of(dest)],
@@ -612,10 +608,10 @@
             ref[apart // 2, pl.ds(first, frames), :] = mixed[block * frames : (block + 1) * frames]
 
 
-def make_panels(whole_ref, grad_ref, awaited_ref, panel_ref):
+def make_panels(whole_ref, grad_ref, sums_ref, panel_ref):
     rows, half = grad_ref.shape[1], whole_ref.shape[3] // 2
     entries = 2 * half // N_DP
-    group = lax.axis_index("dp")
+    group, place = lax.axis_index("dp"), lax.axis_index("ctx")
     for side in range(2):
         panel = 0.0
         for utt in range(2):
@@ -623,40 +619,36 @@
             panel += dot_tt(mixed, grad_ref[utt], 0, 0)
         panel = panel.astype(jnp.bfloat16)
         for part in range(N_DP // 2):
-            panel_ref[slot_of(side * N_DP // 2 + part, group)] = panel[
+            panel_ref[slot_of(side * N_DP // 2 + part, group), 0:entries] = panel[
                 part * entries : (part + 1) * entries
             ]
-
-
-def total_of(in_ref, out_ref):
-    total = in_ref[0].astype(jnp.float32)
-    for source in range(1, N_DP):
-        total += in_ref[source].astype(jnp.float32)
-    out_ref[...] = total
-
-
-def make_tap_slots(sums_ref, came_ref, across_ref, diagonal_ref, awaited_ref, out_ref):
-    own = sums_ref.shape[1] // 2
-    rows, start = came_ref.shape[1] - TAP_PAD // 2, across_ref.shape[0] - TAP_PAD
-    place = lax.axis_index("ctx")
-    pieces = [
-        sums_ref[...],
-        jnp.concatenate([came_ref[0, rows:, :], came_ref[1, rows:, :]], axis=0),
-        across_ref[start:, :],
-        diagonal_ref[start:, :],
-    ]
-    for apart, piece in enumerate(pieces):
-        block = piece.astype(jnp.float32)
-        for part in range(2):
-            mine = block[:, part * own : (part + 1) * own]
-            mine = jnp.concatenate([mine[: TAP_PAD // 2], mine[TAP_PAD // 2 :]], axis=1)
-            out_ref[2 * (place ^ apart) + part] = mine.astype(jnp.bfloat16)
+    panel_ref[:, entries:, :] = jnp.zeros((N_DP, TAP_PAD // 2, half), jnp.bfloat16)
+    own = half // 2
+    for part in range(2):
+        mine = sums_ref[:, part * own : (part + 1) * own]
+        mine = jnp.concatenate([mine[: TAP_PAD // 2], mine[TAP_PAD // 2 :]], axis=1)
+        panel_ref[slot_of(2 * place + part, group), entries:, :] = mine.astype(jnp.bfloat16)
+
+
+def pick_taps(*refs):
+    ins, held_ref, out_ref = refs[:N_CTX], refs[N_CTX + 1], refs[N_CTX]
+    own = ins[0].shape[1] // 2
+    for apart in range(N_CTX):
+        held_ref[apart] = ins[apart][...]
+    mine = held_ref[lax.axis_index("ctx") ^ half_of(lax.axis_index("dp"))]
+    out_ref[...] = jnp.concatenate([mine[:, :own], mine[:, own:]], axis=0)[:TAPS]
 
 
 def relay(keep_ref, came_ref, out_ref):
-    rows = keep_ref.shape[1]
-    total = keep_ref[1].astype(jnp.float32) + came_ref[1, 0:rows, :].astype(jnp.float32)
+    total = keep_ref[1].astype(jnp.float32) + came_ref[1].astype(jnp.float32)
     out_ref[...] = total.astype(jnp.bfloat16)
+
+
+def make_pair(pair_ref, output_ref, input_ref, awaited_ref, out_ref):
+    for slot in range(2):
+        out_ref[slot] = pair_ref[slot].reshape(out_ref.shape[1:])
+    out_ref[2] = output_ref[1]
+    out_ref[3] = input_ref[1]
 
 
 def attend_back(weight_ref, keep_ref, came_ref, far_ref, *refs):
@@ -666,7 +658,7 @@
     query, key, value = (head_parts(ins, slot) for slot in range(3))
     masks = half_masks(rows)
     scale = HEAD_DIM ** (-0.5)
-    arriving = keep_ref[0].astype(jnp.float32) + came_ref[0, 0:rows, :].astype(jnp.float32)
+    arriving = keep_ref[0].astype(jnp.float32) + came_ref[0].astype(jnp.float32)
     arriving = (arriving + far_ref[...].astype(jnp.float32)).astype(jnp.bfloat16)
     low_lanes = lax.broadcasted_iota(jnp.int32, (rows, LANES), 1) < HEAD_DIM
     for pair in range(half // LANES):
@@ -745,7 +737,7 @@
         (channel_block,) * 4 + (pair_block,) * 2,
         ["hbm"] * 2 + ["any"],
         scratch=[dma((4 * N_CTX,))],
-    )(frame_input, grad_output, blocks[0])
+    )(frame_input, grad_output, packed[2])
     frame_across, frame_diagonal = crossed(sides[0], 2), crossed(sides[1], 3)
     beside_sides = crossed(beside_sides, 1)
     attended, weights = call_kernel(
@@ -766,8 +758,8 @@
     forward_out = call_kernel(
         forward,
         (channel_block,) * 2
-        + (shape((utts * frames, width), low),) * 2
         + (
+            shape((2, utts * frames, width), low),
             shape((utts, N_CTX, frames, inner), low),
             shape((inner, width), low),
             shape((chunks, TAP_PAD, 8, LANES), f32),
@@ -782,19 +774,19 @@
         ],
         micros=3.2,
     )(lengths, shards, attended, beside, across, diagonal, *frame_blocks)
-    output_across, output_diagonal = crossed(forward_out[2], 2), crossed(forward_out[3], 3)
-    whole, weight_rows, taps, totals, masked = forward_out[N_CTX:]
+    output_across = crossed(forward_out[2], 2)
+    whole, weight_rows, taps, totals, masked = forward_out[3:]
     grad_blocks = gate([grad_across, grad_diagonal], totals, micros=10.0)
     grad_blocks = (own_sides, beside_sides, *grad_blocks)
     backward_out = call_kernel(
         backward,
         (pair_block,) * 2
-        + (shape((utts * frames + TAP_PAD, width), low),) * 2
         + (
+            shape((2, utts * frames, width), low),
             shape((utts, rows, width), low),
             shape((2, rows, half), low),
-            shape((2, rows + TAP_PAD // 2, half), low),
-            shape((TAP_PAD, width), low),
+            shape((2, rows, half), low),
+            shape((TAP_PAD, width), f32),
         ),
         ["smem"] + ["vmem"] * (6 + N_CTX),
         scratch=[
@@ -805,58 +797,60 @@
         ],
         micros=5.2,
     )(lengths, totals, masked, taps, weight_rows, *forward_out[:2], *grad_blocks)
-    grad_hidden, keep, send, sums = backward_out[N_CTX:]
-    (send,) = gate([send], output_across, output_diagonal)
+    grad_hidden, keep, send, sums = backward_out[3:]
+    (send,) = gate([send], output_across)
     came = crossed(send, 1)
     (far,) = call_kernel(
         relay, (shape((rows, half), low),), ["vmem"] * 2, micros=0.2
     )(keep, came)
+    (input_across,) = gate([backward_out[2]], far)
     (panels,) = call_kernel(
         make_panels,
-        (shape((N_DP, entries, width), low),),
-        ["vmem"] * 2 + ["any"],
+        (shape((N_DP, entries + TAP_PAD // 2, width), low),),
+        ["vmem"] * 3,
         micros=0.7,
-    )(whole, grad_hidden, far)
-
-    def halved(slots, bit):
+    )(whole, grad_hidden, sums)
+
+    def halved(slots, bit, *awaited):
         count = slots.shape[0] // 2
-        return (slots[:count].astype(f32) + swapped(slots[count:], bit).astype(f32)).astype(low)
-
-    panels = halved(halved(panels, 1), 2)
-    input_blocks = gate(backward_out[2:4], far)
-    far = crossed(far, 2)
-    input_across, input_diagonal = crossed(input_blocks[0], 2), crossed(input_blocks[1], 3)
+        came = swapped(slots[count:], bit)
+        if awaited:
+            (came,) = gate([came], *awaited)
+        return (slots[:count].astype(f32) + came.astype(f32)).astype(low)
+
+    far, input_across = crossed(far, 2), crossed(input_across, 2)
+    panels = halved(panels, 1, far)
     back_blocks = call_kernel(
         attend_back,
         (head_block,) * N_CTX,
         ["vmem"] * (4 + N_CTX),
         micros=2.2,
     )(weights, keep, came, far, *packed)
-    grad_blocks = traded(gate(back_blocks, input_across))
-    own_pair, beside_pair = backward_out[:2]
-    (beside_pair,) = gate([beside_pair], grad_blocks[1])
+    (across_block,) = gate([back_blocks[2]], input_across)
+    grad_blocks = traded([*back_blocks[:2], across_block, back_blocks[3]])
+    own_pair = backward_out[0]
+    (beside_pair,) = call_kernel(
+        make_pair,
+        (shape((4, utts * frames, width), low),),
+        ["vmem"] * 3 + ["any"],
+        micros=0.2,
+    )(backward_out[1], output_across, input_across, grad_blocks[2])
     beside_pair = crossed(beside_pair, 1)
 
-    def summed(slots, micros):
-        return call_kernel(
-            total_of, (shape(slots.shape[1:], f32),), ["vmem"], micros=micros
-        )(slots)[0]
-
-    (tap_slots,) = call_kernel(
-        make_tap_slots,
-        (shape((N_DP, TAP_PAD // 2, width), low),),
-        ["vmem"] * 4 + ["any"],
-        micros=0.2,
-    )(sums, came, input_across, input_diagonal, grad_blocks[1])
-
-    tap_sums = summed(dealt(tap_slots), 1.0)
-    (panels,) = gate([panels], grad_blocks[1])
-    grad_out_weight = (panels[0].astype(f32) + swapped(panels[1], 4).astype(f32)).T
-
+    panels = halved(panels, 2, grad_blocks[1])
+    total = panels[0].astype(f32) + swapped(panels[1], 4).astype(f32)
+    grad_out_weight = total[:entries].T
+    (tap_sums,) = gate([total[entries:]], grad_blocks[3], beside_pair)
+    (grad_taps,) = call_kernel(
+        pick_taps,
+        (shape(conv_weight.shape, f32),),
+        ["vmem"] * N_CTX,
+        scratch=[pltpu.VMEM((N_CTX, TAP_PAD // 2, width), f32)],
+    )(*traded([tap_sums] * N_CTX))
     unpacked = call_kernel(
         unpack,
         (shape((utts, frames, inner), low),) * 3 + (shape((utts, frames, wide), low),) * 2,
-        ["any"] * (N_CTX + 6),
+        ["any"] * (N_CTX + 4),
         ["hbm"] * 5,
         [dma((7 * N_CTX + 4 * N_CTX,))],
         micros=1.0,
@@ -866,12 +860,8 @@
         beside_pair,
         output_across,
         input_across,
-        output_diagonal,
-        input_diagonal,
     )
     grad_queries, grad_keys, grad_values, block_output, grad_input = unpacked
-    own = width // 2
-    grad_taps = jnp.concatenate([tap_sums[:, :own], tap_sums[:, own:]], axis=0)[:tap_count]
     return (
         block_output,
         grad_input,

time: 79.5 us -> 70.9 us (0.89)
  starting transfers between devices: 28.9 us -> 23.4 us
  waiting for transfers between devices: 26.8 us -> 24.2 us
  other arithmetic: 1.41 us -> 0.15 us
  local copies, waits for them, and re-layouts: 1.94 us -> 2.77 us
    all_to_all x2 -> x1, waiting for transfers between devices: 12.3 us -> 2.44 us  [dealt(): return lax.all_to_all(slots, 'dp', 0, 0, tiled=True)]
    all_to_all x2 -> x1, starting transfers between devices: 10.9 us -> 6.2 us  [dealt(): return lax.all_to_all(slots, 'dp', 0, 0, tiled=True)]
    ppermute x21 -> x22, waiting for transfers between devices: 6.45 us -> 10.3 us  [crossed(): return lax.ppermute(array, 'ctx', [(i, i ^ apart) for i in range(N_CTX)])]
    ppermute x3, waiting for transfers between devices: 8.08 us -> 11.5 us  [swapped(): return lax.ppermute(array, 'dp', [(i, i ^ bit) for i in range(N_DP)])]
    ppermute x21 -> x22, starting transfers between devices: 15.7 us -> 14.7 us  [crossed(): return lax.ppermute(array, 'ctx', [(i, i ^ apart) for i in range(N_CTX)])]
    unnamed x18 -> x16, local copies, waits for them, and re-layouts: 1.8 us -> 2.03 us
  transfers between devices with their start and end apart: 26 -> 26, of which waited for: 6 -> 10; matrix products, arithmetic and copies ran while one was open for 2% -> 1% of each run, Pallas kernels for 19% -> 23%
where the time goes in v6:
time: 70.9 us; the launch traced here: 70.6 us
  waiting for transfers between devices  24.2 us (34%)
  starting transfers between devices  23.4 us (33%)
  Pallas kernels  19.2 us (27%)
  local copies, waits for them, and re-layouts  2.77 us (4%)
  between operations  0.9 us (1%)
    ppermute x22, starting transfers between devices, crossed(): return lax.ppermute(array, 'ctx', [(i, i ^ apart) for i in range(N_CTX)])  14.7 us
    ppermute x3, waiting for transfers between devices, swapped(): return lax.ppermute(array, 'dp', [(i, i ^ bit) for i in range(N_DP)])  11.5 us
    ppermute x22, waiting for transfers between devices, crossed(): return lax.ppermute(array, 'ctx', [(i, i ^ apart) for i in range(N_CTX)])  10.3 us
    all_to_all x1, starting transfers between devices, dealt(): return lax.all_to_all(slots, 'dp', 0, 0, tiled=True)  6.2 us
    pallas_call x1, Pallas kernels, per_device(): call_kernel(backward, (pair_block,) * 2 + (shape((2, utts * frames, width...  5.24 us
    pallas_call x1, Pallas kernels, per_device(): call_kernel(forward, (channel_block,) * 2 + (shape((2, utts * frames, wid...  3.12 us
    pallas_call x1, Pallas kernels, per_device(): call_kernel(attend, (shape((N_CTX, frames, half), low), shape((half // HE...  2.77 us
    ppermute x3, starting transfers between devices, swapped(): return lax.ppermute(array, 'dp', [(i, i ^ bit) for i in range(N_DP)])  2.55 us
  transfers between devices with their start and end apart: 26, of which 10 were waited for; matrix products, arithmetic and copies ran while one was open for 1% of the time, Pallas kernels for 23%

profile of v6, /device:TPU:0, one launch (start us, length us, event | category | flops | bytes accessed | tf_op | source)
XLA Modules:
  0.0 70.6 jit_solution(7744358343051906594)
XLA Ops:
  0.7 2.0 %shard_map.135 = (bf16[3,64,384]{2,1,0:T(8,128)(2,1)}, bf16[3,64,384]{2,1,0:T(8,128)(2,1)}, bf16[3,64,384]{2,1,0:T(8,128)(2,1)}, bf16[3,64,384]{2,1,0:T(8,128)(2,1)}) custom-call(bf16[2,64,768]{2,1,0:T(8,128)(2,1)} %query_ref.1, bf16[2,64,768]{2,1,0:T(8,128)(2,1)} %key_ref.1, bf16[2,64,768]{2,1,0:T(8,128)(2,1)} %value_ref.1), custom_call_target="tpu_custom_call" | custom-call | flops 1150000000 | tf_op jit(solution)/shard_map/pallas_call | solution.py:720
  3.2 2.6 %collective-permute-start.1 = (bf16[3,64,384]{2,1,0:T(8,128)(2,1)}, bf16[3,64,384]{2,1,0:T(8,128)(2,1)S(1)}, u32[]{:S(2)}, u32[]{:S(2)}) collective-permute-start(bf16[3,64,384]{2,1,0:T(8,128)(2,1)} %get-tuple-element.47), channel_id=1, source_target_pairs={{0,2},{1,3},{2,0},{3,1},{4,6},{5,7},{6,4},{7,5},{8,10},{9,11},{10,... | collective-permute-start | bytes 442376 | tf_op jit(solution)/shard_map/ppermute | solution.py:696
  5.8 0.9 %shard_map.137 = bf16[8,112,384]{2,1,0:T(8,128)(2,1)} custom-call(bf16[96,384]{1,0:T(8,128)(2,1)S(1)} %bitcast.10, bf16[31,192]{1,0:T(8,128)(2,1)S(1)} %copy-done.3, bf16[3,64,384]{2,1,0:T(8,128)(2,1)S(1)} %collective-permute-done.refs_1_.awaited_ref), custom_call_target="tpu_custom_call" | custom-call | flops 1150000000 | tf_op jit(solution)/shard_map/pallas_call | solution.py:728
  6.8 6.2 %all-to-all-start = ((bf16[8,112,384]{2,1,0:T(8,128)(2,1)}), bf16[8,112,384]{2,1,0:T(8,128)(2,1)S(1)}, u32[]{:S(2)}, u32[]{:S(2)}) async-start(bf16[8,112,384]{2,1,0:T(8,128)(2,1)} %shard_map.137), calls=%async_computation | async-start | bytes 1376256 | tf_op jit(solution)/shard_map/all_to_all | solution.py:692
  13.3 1.6 %collective-permute-start.3 = (bf16[2,64,384]{2,1,0:T(8,128)(2,1)S(1)}, bf16[2,64,384]{2,1,0:T(8,128)(2,1)S(1)}, u32[]{:S(2)}, u32[]{:S(2)}) collective-permute-start(bf16[2,64,384]{2,1,0:T(8,128)(2,1)S(1)} %get-tuple-element.51), channel_id=1, source_target_pairs={{0,2},{1,3},{2,0},{3,1},{4,6},{5,7},{6,4},{7,5},{8,10},{9,11},{10,... | collective-permute-start | bytes 294920 | tf_op jit(solution)/shard_map/ppermute | solution.py:696
  15.5 2.8 %shard_map.136 = (bf16[4,64,384]{2,1,0:T(8,128)(2,1)S(1)}, bf16[6,256,256]{2,1,0:T(8,128)(2,1)S(1)}) custom-call(s32[2]{0:T(128)S(1)} %copy-done.4, bf16[3,64,384]{2,1,0:T(8,128)(2,1)S(1)} %copy-done.7, bf16[3,64,384]{2,1,0:T(8,128)(2,1)S(1)} %collective-permute-done.refs_1_.awaited_ref, bf16[3,64,384]{2,1,0:T(8,128)(2,1)S(1)} %collective-permute-done.1.refs_2_.awaited_ref, ...), custom_call_target="tpu_custom_call" | custom-call | flops 3449999872 | tf_op jit(solution)/shard_map/pallas_call | solution.py:743
  18.3 0.9 %copy-done.5 = bf16[6,256,256]{2,1,0:T(8,128)(2,1)} copy-done((bf16[6,256,256]{2,1,0:T(8,128)(2,1)}, bf16[6,256,256]{2,1,0:T(8,128)(2,1)S(1)}, u32[]{:S(2)}) %copy-start.5) | copy-done | bytes 786456
  20.0 0.9 %collective-permute-start.6 = (bf16[4,64,384]{2,1,0:T(8,128)(2,1)S(1)}, bf16[4,64,384]{2,1,0:T(8,128)(2,1)S(1)}, u32[]{:S(2)}, u32[]{:S(2)}) collective-permute-start(bf16[4,64,384]{2,1,0:T(8,128)(2,1)S(1)} %shard_map.139.refs_0_), channel_id=1, source_target_pairs={{0,2},{1,3},{2,0},{3,1},{4,6},{5,7},{6,4},{7,5},{8,10},{9,11},{10,... | collective-permute-start | bytes 589832 | tf_op jit(solution)/shard_map/ppermute | solution.py:696
  21.6 5.6 %collective-permute-done.6.refs_2_ = bf16[4,64,384]{2,1,0:T(8,128)(2,1)S(1)} collective-permute-done((bf16[4,64,384]{2,1,0:T(8,128)(2,1)S(1)}, bf16[4,64,384]{2,1,0:T(8,128)(2,1)S(1)}, u32[]{:S(2)}, u32[]{:S(2)}) %collective-permute-start.6) | collective-permute-done | bytes 196640 | tf_op jit(solution)/shard_map/ppermute | solution.py:696
  27.2 1.5 %collective-permute-start.9 = (bf16[2,64,384]{2,1,0:T(8,128)(2,1)S(1)}, bf16[2,64,384]{2,1,0:T(8,128)(2,1)S(1)}, u32[]{:S(2)}, u32[]{:S(2)}) collective-permute-start(bf16[2,64,384]{2,1,0:T(8,128)(2,1)S(1)} %get-tuple-element.61), channel_id=1, source_target_pairs={{0,2},{1,3},{2,0},{3,1},{4,6},{5,7},{6,4},{7,5},{8,10},{9,11},{10,... | collective-permute-start | bytes 294920 | tf_op jit(solution)/shard_map/ppermute | solution.py:696
  29.1 2.4 %all-to-all-done.weight_ref = bf16[8,112,384]{2,1,0:T(8,128)(2,1)S(1)} async-done(((bf16[8,112,384]{2,1,0:T(8,128)(2,1)}), bf16[8,112,384]{2,1,0:T(8,128)(2,1)S(1)}, u32[]{:S(2)}, u32[]{:S(2)}) %all-to-all-start) | async-done | bytes 688160 | tf_op jit(solution)/shard_map/all_to_all | solution.py:692
  31.5 3.1 %shard_map.140 = (bf16[2,64,384]{2,1,0:T(8,128)(2,1)S(1)}, bf16[2,64,384]{2,1,0:T(8,128)(2,1)S(1)}, bf16[2,128,384]{2,1,0:T(8,128)(2,1)S(1)}, bf16[2,4,64,768]{3...) custom-call(s32[2]{0:T(128)S(1)} %copy-done.4, ...), custom_call_target="tpu_custom_call" | custom-call | flops 3680000000 | tf_op jit(solution)/shard_map/pallas_call | solution.py:758
  34.6 1.6 %collective-permute-start.11 = (bf16[2,128,384]{2,1,0:T(8,128)(2,1)S(1)}, bf16[2,128,384]{2,1,0:T(8,128)(2,1)S(1)}, u32[]{:S(2)}, u32[]{:S(2)}) collective-permute-start(bf16[2,128,384]{2,1,0:T(8,128)(2,1)S(1)} %get-tuple-element.67), channel_id=1, source_target_pairs={{0,2},{1,3},{2,0},{3,1},{4,6},{5,7},{6,4},{7,5},{8,10},{9,11},{10,... | collective-permute-start | bytes 589832 | tf_op jit(solution)/shard_map/ppermute | solution.py:696
  36.2 5.2 %shard_map.142 = (bf16[2,2,64,384]{3,2,1,0:T(8,128)(2,1)S(1)}, bf16[2,2,64,384]{3,2,1,0:T(8,128)(2,1)S(1)}, bf16[2,128,384]{2,1,0:T(8,128)(2,1)S(1)}, bf16[2,256...) custom-call(s32[2]{0:T(128)S(1)} %copy-done.4, ...), custom_call_target="tpu_custom_call" | custom-call | flops 5980000256 | tf_op jit(solution)/shard_map/pallas_call | solution.py:781
  42.2 1.5 %collective-permute-start.19 = (bf16[4,112,384]{2,1,0:T(8,128)(2,1)S(1)}, bf16[4,112,384]{2,1,0:T(8,128)(2,1)S(1)}, u32[]{:S(2)}, u32[]{:S(2)}) collective-permute-start(bf16[4,112,384]{2,1,0:T(8,128)(2,1)S(1)} %slice.33), channel_id=1, source_target_pairs={{0,4},{4,0},{8,12},{12,8},{16,20},{20,16},{24,28},{28,24},{1,5},{5... | collective-permute-start | bytes 1032200 | tf_op jit(solution)/shard_map/ppermute | solution.py:688
  44.5 1.3 %collective-permute-start.15 = (bf16[2,128,384]{2,1,0:T(8,128)(2,1)S(1)}, bf16[2,128,384]{2,1,0:T(8,128)(2,1)S(1)}, u32[]{:S(2)}, u32[]{:S(2)}) collective-permute-start(bf16[2,128,384]{2,1,0:T(8,128)(2,1)S(1)} %shard_map.146), channel_id=1, source_target_pairs={{0,2},{1,3},{2,0},{3,1},{4,6},{5,7},{6,4},{7,5},{8,10},{9,11},{10,... | collective-permute-start | bytes 589832 | tf_op jit(solution)/shard_map/ppermute | solution.py:696
  45.9 6.9 %collective-permute-done.19.refs_0_ = bf16[4,112,384]{2,1,0:T(8,128)(2,1)S(1)} collective-permute-done((bf16[4,112,384]{2,1,0:T(8,128)(2,1)S(1)}, bf16[4,112,384]{2,1,0:T(8,128)(2,1)S(1)}, u32[]{:S(2)}, u32[]{:S(2)}) %collective-permute-start.19) | collective-permute-done | bytes 344096 | tf_op jit(solution)/shard_map/ppermute | solution.py:688
  53.9 2.0 %shard_map.145 = (bf16[3,64,384]{2,1,0:T(8,128)(2,1)S(1)}, bf16[3,64,384]{2,1,0:T(8,128)(2,1)S(1)}, bf16[3,64,384]{2,1,0:T(8,128)(2,1)S(1)}, bf16[3,64,384]{2,1,0:T(8,128)(2,1)S(1)}) custom-call(bf16[6,256,256]{2,1,0:T(8,128)(2,1)S(1)} %copy-done.6, bf16[2,256,384]{2,1,0:T(8,128)(2,1)S(1)} %get-tuple-element.65.keep_ref, ...), custom_call_target="tpu_custom_call" | custom-call | flops 2529999872 | tf_op jit(solution)/shard_map/pallas_call | solution.py:823
  56.0 0.7 %collective-permute-start.16 = (bf16[3,64,384]{2,1,0:T(8,128)(2,1)S(1)}, bf16[3,64,384]{2,1,0:T(8,128)(2,1)S(1)}, u32[]{:S(2)}, u32[]{:S(2)}) collective-permute-start(bf16[3,64,384]{2,1,0:T(8,128)(2,1)S(1)} %shard_map.147), channel_id=1, source_target_pairs={{0,2},{1,3},{2,0},{3,1},{4,6},{5,7},{6,4},{7,5},{8,10},{9,11},{10,... | collective-permute-start | bytes 442376 | tf_op jit(solution)/shard_map/ppermute | solution.py:696
  57.3 1.6 %collective-permute-done.20.refs_0_ = bf16[2,112,384]{2,1,0:T(8,128)(2,1)S(1)} collective-permute-done((bf16[2,112,384]{2,1,0:T(8,128)(2,1)S(1)}, bf16[2,112,384]{2,1,0:T(8,128)(2,1)S(1)}, u32[]{:S(2)}, u32[]{:S(2)}) %collective-permute-start.20) | collective-permute-done | bytes 172064 | tf_op jit(solution)/shard_map/ppermute | solution.py:688
  59.5 2.7 %collective-permute-done.16.awaited_ref.refs_2_ = bf16[3,64,384]{2,1,0:T(8,128)(2,1)S(1)} collective-permute-done((bf16[3,64,384]{2,1,0:T(8,128)(2,1)S(1)}, bf16[3,64,384]{2,1,0:T(8,128)(2,1)S(1)}, u32[]{:S(2)}, u32[]{:S(2)}) %collective-permute-start.16) | collective-permute-done | bytes 147488 | tf_op jit(solution)/shard_map/ppermute | solution.py:696
  62.3 3.0 %collective-permute-done.21 = bf16[112,384]{1,0:T(8,128)(2,1)S(1)} collective-permute-done((bf16[112,384]{1,0:T(8,128)(2,1)S(1)}, bf16[112,384]{1,0:T(8,128)(2,1)S(1)}, u32[]{:S(2)}, u32[]{:S(2)}) %collective-permute-start.21) | collective-permute-done | bytes 86048 | tf_op jit(solution)/shard_map/ppermute | solution.py:688
  66.0 1.3 %collective-permute-start.23 = (f32[16,384]{1,0:T(8,128)S(1)}, f32[16,384]{1,0:T(8,128)S(1)}, u32[]{:S(2)}, u32[]{:S(2)}) collective-permute-start(f32[16,384]{1,0:T(8,128)S(1)} %shard_map.153.refs_0_), channel_id=1, source_target_pairs={{0,2},{1,3},{2,0},{3,1},{4,6},{5,7},{6,4},{7,5},{8,10},{9,11},{10,... | collective-permute-start | bytes 73736 | tf_op jit(solution)/shard_map/ppermute | solution.py:696
  67.9 1.4 %shard_map.149 = (bf16[2,64,768]{2,1,0:T(8,128)(2,1)}, bf16[2,64,768]{2,1,0:T(8,128)(2,1)}, bf16[2,64,768]{2,1,0:T(8,128)(2,1)}, bf16[2,64,1536]{2,1,0:T(8,128)(2,1)}, bf16[2,64,1536]{2,1,0:T(8,128)(2,1)}) custom-call(bf16[3,64,384]{2,1,0:T(8,128)(2,1)S(1)} %get-tuple-element.68.refs_0_, bf16[3,64,384]{2,1,0:T(8,128)(2,1)S(1)} %collective-permute-done.14.refs_1_, ...), custom_call_target="tpu_custom_call" | custom-call | flops 1150000000 | tf_op jit(solution)/shard_map/pallas_call | solution.py:850
  (72 shorter events, 9.9 us)
Async XLA Ops:
  2.7 3.2 %collective-permute-start = (bf16[3,64,384]{2,1,0:T(8,128)(2,1)}, bf16[3,64,384]{2,1,0:T(8,128)(2,1)S(1)}, u32[]{:S(2)}, u32[]{:S(2)}) collective-permute-start(bf16[3,64,384]{2,1,0:T(8,128)(2,1)} %get-tuple-element.46), channel_id=1, source_target_pairs={{0,1},{1,0},{2,3},{3,2},{4,5},{5,4},{6,7},{7,6},{8,9},{9,8},{10,11... | collective-permute-start | bytes 442376 | tf_op jit(solution)/shard_map/ppermute | solution.py:696
  3.2 9.8 %collective-permute-start.1 = (bf16[3,64,384]{2,1,0:T(8,128)(2,1)}, bf16[3,64,384]{2,1,0:T(8,128)(2,1)S(1)}, u32[]{:S(2)}, u32[]{:S(2)}) collective-permute-start(bf16[3,64,384]{2,1,0:T(8,128)(2,1)} %get-tuple-element.47), channel_id=1, source_target_pairs={{0,2},{1,3},{2,0},{3,1},{4,6},{5,7},{6,4},{7,5},{8,10},{9,11},{10,... | collective-permute-start | bytes 442376 | tf_op jit(solution)/shard_map/ppermute | solution.py:696
  5.8 9.1 %collective-permute-start.2 = (bf16[3,64,384]{2,1,0:T(8,128)(2,1)}, bf16[3,64,384]{2,1,0:T(8,128)(2,1)S(1)}, u32[]{:S(2)}, u32[]{:S(2)}) collective-permute-start(bf16[3,64,384]{2,1,0:T(8,128)(2,1)} %get-tuple-element.48), channel_id=1, source_target_pairs={{0,3},{1,2},{2,1},{3,0},{4,7},{5,6},{6,5},{7,4},{8,11},{9,10},{10,... | collective-permute-start | bytes 442376 | tf_op jit(solution)/shard_map/ppermute | solution.py:696
  6.8 24.7 %all-to-all-start = ((bf16[8,112,384]{2,1,0:T(8,128)(2,1)}), bf16[8,112,384]{2,1,0:T(8,128)(2,1)S(1)}, u32[]{:S(2)}, u32[]{:S(2)}) async-start(bf16[8,112,384]{2,1,0:T(8,128)(2,1)} %shard_map.137), calls=%async_computation | async-start | bytes 1376256 | tf_op jit(solution)/shard_map/all_to_all | solution.py:692
  13.3 5.9 %collective-permute-start.3 = (bf16[2,64,384]{2,1,0:T(8,128)(2,1)S(1)}, bf16[2,64,384]{2,1,0:T(8,128)(2,1)S(1)}, u32[]{:S(2)}, u32[]{:S(2)}) collective-permute-start(bf16[2,64,384]{2,1,0:T(8,128)(2,1)S(1)} %get-tuple-element.51), channel_id=1, source_target_pairs={{0,2},{1,3},{2,0},{3,1},{4,6},{5,7},{6,4},{7,5},{8,10},{9,11},{10,... | collective-permute-start | bytes 294920 | tf_op jit(solution)/shard_map/ppermute | solution.py:696
  14.9 5.1 %collective-permute-start.4 = (bf16[2,64,384]{2,1,0:T(8,128)(2,1)S(1)}, bf16[2,64,384]{2,1,0:T(8,128)(2,1)S(1)}, u32[]{:S(2)}, u32[]{:S(2)}) collective-permute-start(bf16[2,64,384]{2,1,0:T(8,128)(2,1)S(1)} %get-tuple-element.52), channel_id=1, source_target_pairs={{0,3},{1,2},{2,1},{3,0},{4,7},{5,6},{6,5},{7,4},{8,11},{9,10},{10,... | collective-permute-start | bytes 294920 | tf_op jit(solution)/shard_map/ppermute | solution.py:696
  20.0 7.2 %collective-permute-start.6 = (bf16[4,64,384]{2,1,0:T(8,128)(2,1)S(1)}, bf16[4,64,384]{2,1,0:T(8,128)(2,1)S(1)}, u32[]{:S(2)}, u32[]{:S(2)}) collective-permute-start(bf16[4,64,384]{2,1,0:T(8,128)(2,1)S(1)} %shard_map.139.refs_0_), channel_id=1, source_target_pairs={{0,2},{1,3},{2,0},{3,1},{4,6},{5,7},{6,4},{7,5},{8,10},{9,11},{10,... | collective-permute-start | bytes 589832 | tf_op jit(solution)/shard_map/ppermute | solution.py:696
  20.9 8.2 %collective-permute-start.8 = (bf16[2,2,64,384]{3,2,1,0:T(8,128)(2,1)S(1)}, bf16[2,2,64,384]{3,2,1,0:T(8,128)(2,1)S(1)}, u32[]{:S(2)}, u32[]{:S(2)}) collective-permute-start(bf16[2,2,64,384]{3,2,1,0:T(8,128)(2,1)S(1)} %get-tuple-element.54), channel_id=1, source_target_pairs={{0,1},{1,0},{2,3},{3,2},{4,5},{5,4},{6,7},{7,6},{8,9},{9,8},{10,11... | collective-permute-start | bytes 589832 | tf_op jit(solution)/shard_map/ppermute | solution.py:696
  21.6 7.5 %collective-permute-start.5 = (bf16[4,64,384]{2,1,0:T(8,128)(2,1)S(1)}, bf16[4,64,384]{2,1,0:T(8,128)(2,1)S(1)}, u32[]{:S(2)}, u32[]{:S(2)}) collective-permute-start(bf16[4,64,384]{2,1,0:T(8,128)(2,1)S(1)} %shard_map.139.refs_0_), channel_id=1, source_target_pairs={{0,1},{1,0},{2,3},{3,2},{4,5},{5,4},{6,7},{7,6},{8,9},{9,8},{10,11... | collective-permute-start | bytes 589832 | tf_op jit(solution)/shard_map/ppermute | solution.py:696
  27.2 9.0 %collective-permute-start.9 = (bf16[2,64,384]{2,1,0:T(8,128)(2,1)S(1)}, bf16[2,64,384]{2,1,0:T(8,128)(2,1)S(1)}, u32[]{:S(2)}, u32[]{:S(2)}) collective-permute-start(bf16[2,64,384]{2,1,0:T(8,128)(2,1)S(1)} %get-tuple-element.61), channel_id=1, source_target_pairs={{0,2},{1,3},{2,0},{3,1},{4,6},{5,7},{6,4},{7,5},{8,10},{9,11},{10,... | collective-permute-start | bytes 294920 | tf_op jit(solution)/shard_map/ppermute | solution.py:696
  28.8 7.5 %collective-permute-start.10 = (bf16[2,64,384]{2,1,0:T(8,128)(2,1)S(1)}, bf16[2,64,384]{2,1,0:T(8,128)(2,1)S(1)}, u32[]{:S(2)}, u32[]{:S(2)}) collective-permute-start(bf16[2,64,384]{2,1,0:T(8,128)(2,1)S(1)} %get-tuple-element.62), channel_id=1, source_target_pairs={{0,3},{1,2},{2,1},{3,0},{4,7},{5,6},{6,5},{7,4},{8,11},{9,10},{10,... | collective-permute-start | bytes 294920 | tf_op jit(solution)/shard_map/ppermute | solution.py:696
  34.6 6.8 %collective-permute-start.11 = (bf16[2,128,384]{2,1,0:T(8,128)(2,1)S(1)}, bf16[2,128,384]{2,1,0:T(8,128)(2,1)S(1)}, u32[]{:S(2)}, u32[]{:S(2)}) collective-permute-start(bf16[2,128,384]{2,1,0:T(8,128)(2,1)S(1)} %get-tuple-element.67), channel_id=1, source_target_pairs={{0,2},{1,3},{2,0},{3,1},{4,6},{5,7},{6,4},{7,5},{8,10},{9,11},{10,... | collective-permute-start | bytes 589832 | tf_op jit(solution)/shard_map/ppermute | solution.py:696
  41.5 2.2 %collective-permute-start.12 = (bf16[2,256,384]{2,1,0:T(8,128)(2,1)S(1)}, bf16[2,256,384]{2,1,0:T(8,128)(2,1)S(1)}, u32[]{:S(2)}, u32[]{:S(2)}) collective-permute-start(bf16[2,256,384]{2,1,0:T(8,128)(2,1)S(1)} %shard_map.143), channel_id=1, source_target_pairs={{0,1},{1,0},{2,3},{3,2},{4,5},{5,4},{6,7},{7,6},{8,9},{9,8},{10,11... | collective-permute-start | bytes 1179656 | tf_op jit(solution)/shard_map/ppermute | solution.py:696
  42.2 10.5 %collective-permute-start.19 = (bf16[4,112,384]{2,1,0:T(8,128)(2,1)S(1)}, bf16[4,112,384]{2,1,0:T(8,128)(2,1)S(1)}, u32[]{:S(2)}, u32[]{:S(2)}) collective-permute-start(bf16[4,112,384]{2,1,0:T(8,128)(2,1)S(1)} %slice.33), channel_id=1, source_target_pairs={{0,4},{4,0},{8,12},{12,8},{16,20},{20,16},{24,28},{28,24},{1,5},{5... | collective-permute-start | bytes 1032200 | tf_op jit(solution)/shard_map/ppermute | solution.py:688
  43.8 9.0 %collective-permute-start.13 = (bf16[256,384]{1,0:T(8,128)(2,1)S(1)}, bf16[256,384]{1,0:T(8,128)(2,1)S(1)}, u32[]{:S(2)}, u32[]{:S(2)}) collective-permute-start(bf16[256,384]{1,0:T(8,128)(2,1)S(1)} %shard_map.144.refs_1_), channel_id=1, source_target_pairs={{0,2},{1,3},{2,0},{3,1},{4,6},{5,7},{6,4},{7,5},{8,10},{9,11},{10,... | collective-permute-start | bytes 589832 | tf_op jit(solution)/shard_map/ppermute | solution.py:696
  44.5 11.4 %collective-permute-start.15 = (bf16[2,128,384]{2,1,0:T(8,128)(2,1)S(1)}, bf16[2,128,384]{2,1,0:T(8,128)(2,1)S(1)}, u32[]{:S(2)}, u32[]{:S(2)}) collective-permute-start(bf16[2,128,384]{2,1,0:T(8,128)(2,1)S(1)} %shard_map.146), channel_id=1, source_target_pairs={{0,2},{1,3},{2,0},{3,1},{4,6},{5,7},{6,4},{7,5},{8,10},{9,11},{10,... | collective-permute-start | bytes 589832 | tf_op jit(solution)/shard_map/ppermute | solution.py:696
  52.9 6.1 %collective-permute-start.20 = (bf16[2,112,384]{2,1,0:T(8,128)(2,1)S(1)}, bf16[2,112,384]{2,1,0:T(8,128)(2,1)S(1)}, u32[]{:S(2)}, u32[]{:S(2)}) collective-permute-start(bf16[2,112,384]{2,1,0:T(8,128)(2,1)S(1)} %slice.35), channel_id=1, source_target_pairs={{0,8},{4,12},{8,0},{12,4},{16,24},{20,28},{24,16},{28,20},{1,9},{5... | collective-permute-start | bytes 516104 | tf_op jit(solution)/shard_map/ppermute | solution.py:688
  56.0 6.2 %collective-permute-start.16 = (bf16[3,64,384]{2,1,0:T(8,128)(2,1)S(1)}, bf16[3,64,384]{2,1,0:T(8,128)(2,1)S(1)}, u32[]{:S(2)}, u32[]{:S(2)}) collective-permute-start(bf16[3,64,384]{2,1,0:T(8,128)(2,1)S(1)} %shard_map.147), channel_id=1, source_target_pairs={{0,2},{1,3},{2,0},{3,1},{4,6},{5,7},{6,4},{7,5},{8,10},{9,11},{10,... | collective-permute-start | bytes 442376 | tf_op jit(solution)/shard_map/ppermute | solution.py:696
  59.0 6.3 %collective-permute-start.21 = (bf16[112,384]{1,0:T(8,128)(2,1)S(1)}, bf16[112,384]{1,0:T(8,128)(2,1)S(1)}, u32[]{:S(2)}, u32[]{:S(2)}) collective-permute-start(bf16[112,384]{1,0:T(8,128)(2,1)S(1)} %slice_bitcast_fusion.1), channel_id=1, source_target_pairs={{0,16},{4,20},{8,24},{12,28},{16,0},{20,4},{24,8},{28,12},{1,17},{... | collective-permute-start | bytes 258056 | tf_op jit(solution)/shard_map/ppermute | solution.py:688
  59.5 6.5 %collective-permute-start.17 = (bf16[3,64,384]{2,1,0:T(8,128)(2,1)S(1)}, bf16[3,64,384]{2,1,0:T(8,128)(2,1)S(1)}, u32[]{:S(2)}, u32[]{:S(2)}) collective-permute-start(bf16[3,64,384]{2,1,0:T(8,128)(2,1)S(1)} %get-tuple-element.72), channel_id=1, source_target_pairs={{0,3},{1,2},{2,1},{3,0},{4,7},{5,6},{6,5},{7,4},{8,11},{9,10},{10,... | collective-permute-start | bytes 442376 | tf_op jit(solution)/shard_map/ppermute | solution.py:696
  62.2 3.8 %collective-permute-start.18 = (bf16[4,128,384]{2,1,0:T(8,128)(2,1)S(1)}, bf16[4,128,384]{2,1,0:T(8,128)(2,1)S(1)}, u32[]{:S(2)}, u32[]{:S(2)}) collective-permute-start(bf16[4,128,384]{2,1,0:T(8,128)(2,1)S(1)} %shard_map.148), channel_id=1, source_target_pairs={{0,1},{1,0},{2,3},{3,2},{4,5},{5,4},{6,7},{7,6},{8,9},{9,8},{10,11... | collective-permute-start | bytes 1179656 | tf_op jit(solution)/shard_map/ppermute | solution.py:696
  66.0 3.4 %collective-permute-start.24 = (f32[16,384]{1,0:T(8,128)S(1)}, f32[16,384]{1,0:T(8,128)S(1)}, u32[]{:S(2)}, u32[]{:S(2)}) collective-permute-start(f32[16,384]{1,0:T(8,128)S(1)} %shard_map.153.refs_0_), channel_id=1, source_target_pairs={{0,3},{1,2},{2,1},{3,0},{4,7},{5,6},{6,5},{7,4},{8,11},{9,10},{10,... | collective-permute-start | bytes 73736 | tf_op jit(solution)/shard_map/ppermute | solution.py:696
  66.0 3.9 %collective-permute-start.23 = (f32[16,384]{1,0:T(8,128)S(1)}, f32[16,384]{1,0:T(8,128)S(1)}, u32[]{:S(2)}, u32[]{:S(2)}) collective-permute-start(f32[16,384]{1,0:T(8,128)S(1)} %shard_map.153.refs_0_), channel_id=1, source_target_pairs={{0,2},{1,3},{2,0},{3,1},{4,6},{5,7},{6,4},{7,5},{8,10},{9,11},{10,... | collective-permute-start | bytes 73736 | tf_op jit(solution)/shard_map/ppermute | solution.py:696
  67.3 2.6 %collective-permute-start.22 = (f32[16,384]{1,0:T(8,128)S(1)}, f32[16,384]{1,0:T(8,128)S(1)}, u32[]{:S(2)}, u32[]{:S(2)}) collective-permute-start(f32[16,384]{1,0:T(8,128)S(1)} %shard_map.153.refs_0_), channel_id=1, source_target_pairs={{0,1},{1,0},{2,3},{3,2},{4,5},{5,4},{6,7},{7,6},{8,9},{9,8},{10,11... | collective-permute-start | bytes 73736 | tf_op jit(solution)/shard_map/ppermute | solution.py:696
  (10 other events, 30.8 us)

commit v7 on v6

--- a/solution.py
+++ b/solution.py
@@ -371,24 +371,35 @@
     high = jnp.concatenate(
         [taps[TAP_PAD // 2 :], jnp.zeros((TAP_PAD - TAPS, taps.shape[1]), jnp.float32)], axis=0
     )
-    joined = jnp.concatenate([taps[: TAP_PAD // 2], high], axis=1).astype(jnp.bfloat16)
-    for target in range(N_DP):
-        out_ref[target, 0:entries] = panel_ref[...]
-        out_ref[target, entries:] = joined
+    out_ref[0, 0:entries] = panel_ref[...]
+    joined = jnp.concatenate([taps[: TAP_PAD // 2], high], axis=1)
+    out_ref[0, entries:] = joined.astype(jnp.bfloat16)
 
 
 def pack_channels(frame_ref, grad_ref, awaited_ref, *rest):
-    frame_outs, grad_outs, beside_ref, own_ref, sem = rest[:2], rest[2:4], *rest[4:]
+    across_ref, grad_outs, beside_ref, own_ref, sem = rest[0], rest[1:3], *rest[3:]
     width = frame_ref.shape[2] // N_CTX
+    frames = frame_ref.shape[1]
     place = lax.axis_index("ctx")
     pairs = []
-    for slot, (ref, outs) in enumerate(((frame_ref, frame_outs), (grad_ref, grad_outs))):
-        targets = [own_ref.at[slot], beside_ref.at[slot], outs[0], outs[1]]
+    for slot, ref in enumerate((frame_ref, grad_ref)):
         for apart in (2, 3, 1, 0):
             cols = columns((place ^ apart) * width, width)
             for utt in range(2):
-                pairs.append((ref.at[utt, :, cols], targets[apart].at[utt]))
+                rows = slice(utt * frames, (utt + 1) * frames)
+                if apart < 2:
+                    target = (own_ref, beside_ref)[apart].at[slot, rows]
+                elif slot == 0:
+                    target = across_ref.at[apart - 2, rows]
+                else:
+                    target = grad_outs[apart - 2].at[rows]
+                pairs.append((ref.at[utt, :, cols], target))
     run_copies(pairs, sem)
+
+
+def make_sides(beside_ref, across_ref, out_ref):
+    out_ref[0:2] = beside_ref[...]
+    out_ref[2] = across_ref[1]
 
 
 def unpack(*refs):
@@ -429,41 +440,50 @@
     return low.astype(jnp.bfloat16), (1.0 - low).astype(jnp.bfloat16)
 
 
+def weights_of(length_ref, key_pair, query_pair, mask, frames):
+    place = lax.axis_index("ctx")
+    rows = key_pair.shape[0]
+    frame = lax.broadcasted_iota(jnp.int32, (rows, rows), 0) ^ (place * frames)
+    scores = dot_tt(key_pair, query_pair * mask, 1, 1) * HEAD_DIM ** (-0.5)
+    scores = jnp.where(frame < length_ref[half_of(place)], scores, masked_score)
+    powers = jnp.exp(scores - jnp.max(scores, axis=0, keepdims=True))
+    total = jnp.sum(powers, axis=0, keepdims=True)
+    return (powers * (1.0 / total)).astype(jnp.bfloat16)
+
+
 def attend(length_ref, *refs):
-    ins, attended_ref, weight_ref = refs[:N_CTX], refs[N_CTX], refs[N_CTX + 1]
+    ins, attended_ref = refs[:N_CTX], refs[N_CTX]
     frames, half = ins[0].shape[1], ins[0].shape[2]
-    rows = N_CTX * frames
-    place = lax.axis_index("ctx")
-    length = length_ref[half_of(place)]
     query, key, value = (head_parts(ins, slot) for slot in range(3))
-    masks = half_masks(rows)
-    frame = lax.broadcasted_iota(jnp.int32, (rows, rows), 0) ^ (place * frames)
-    real = frame < length
+    masks = half_masks(N_CTX * frames)
     for pair in range(half // LANES):
         cols = slice(pair * LANES, (pair + 1) * LANES)
-        key_pair, value_pair = key[:, cols], value[:, cols]
         parts = []
         for side in range(2):
-            scores = dot_tt(key_pair, query[:, cols] * masks[side], 1, 1) * HEAD_DIM ** (-0.5)
-            scores = jnp.where(real, scores, masked_score)
-            largest = jnp.max(scores, axis=0, keepdims=True)
-            powers = jnp.exp(scores - largest)
-            total = jnp.sum(powers, axis=0, keepdims=True)
-            low = (powers * (1.0 / total)).astype(jnp.bfloat16)
-            weight_ref[2 * pair + side] = low
-            mixed = dot_tt(value_pair, low, 0, 0)
+            low = weights_of(length_ref, key[:, cols], query[:, cols], masks[side], frames)
+            mixed = dot_tt(value[:, cols], low, 0, 0)
             parts.append(mixed[side * HEAD_DIM : (side + 1) * HEAD_DIM])
         joined = jnp.concatenate(parts, axis=0).T.astype(jnp.bfloat16)
         attended_ref[:, :, cols] = joined.reshape(N_CTX, frames, LANES)
 
 
-def side_blocks(slot, refs):
-    return refs[0].at[slot], refs[1].at[slot], refs[2], refs[3]
-
-
-def forward(length_ref, weight_ref, *refs):
-    attended_refs, frame_refs = refs[:N_CTX], side_blocks(0, refs[N_CTX : 2 * N_CTX])
-    out_refs, refs = refs[2 * N_CTX : 2 * N_CTX + 3], refs[2 * N_CTX + 3 :]
+def weigh(length_ref, *refs):
+    ins, weight_ref = refs[:N_CTX], refs[N_CTX + 1]
+    frames, half = ins[0].shape[1], ins[0].shape[2]
+    query, key = (head_parts(ins, slot) for slot in range(2))
+    masks = half_masks(N_CTX * frames)
+    for pair in range(half // LANES):
+        cols = slice(pair * LANES, (pair + 1) * LANES)
+        for side in range(2):
+            weight_ref[2 * pair + side] = weights_of(
+                length_ref, key[:, cols], query[:, cols], masks[side], frames
+            )
+
+
+def forward(length_ref, near_ref, other_ref, *refs):
+    attended_refs, refs = refs[:N_CTX], refs[N_CTX:]
+    own_ref, beside_ref, across_ref = refs[:3]
+    out_refs, refs = refs[3:6], refs[6:]
     whole_ref, rows_ref, taps_ref, total_ref, masked_ref = refs[:5]
     hidden_ref, frame_ref, result_ref = refs[5:]
     frames, half = attended_refs[0].shape[1], attended_refs[0].shape[2]
@@ -478,13 +498,19 @@
         cols = columns((source & 1) * half, half)
         for block in range(N_CTX):
             whole_ref[half_of(source), block ^ source, :, cols] = attended_refs[apart][block]
-        frame_ref[source] = frame_refs[apart][...]
-    for part in range(N_DP):
-        rows_ref[part * entries : (part + 1) * entries] = weight_ref[part, 0:entries]
-    pieces = []
-    for part in range(2):
-        block = weight_ref[2 * place + part, entries:].astype(jnp.float32)
-        pieces.append(jnp.concatenate([block[:, :own], block[:, own:]], axis=0))
+        block = (own_ref, beside_ref, across_ref, beside_ref)[apart][(0, 0, 0, 2)[apart]]
+        frame_ref[source] = block.reshape(frame_ref.shape[1:])
+    group = lax.axis_index("dp")
+    for slot, apart in enumerate((0, 4, 2, 6)):
+        for odd, ref in enumerate((near_ref, other_ref)):
+            first = pl.multiple_of((group ^ (apart + odd)) * entries, entries)
+            rows_ref[pl.ds(first, entries)] = ref[slot, 0:entries]
+    apart = place ^ half_of(group)
+    slot = ((apart & 1) << 1) | half_of(apart)
+    odd = (group & 1) == 1
+    blocks = [ref[slot, entries:].astype(jnp.float32) for ref in (near_ref, other_ref)]
+    blocks = (jnp.where(odd, blocks[1], blocks[0]), jnp.where(odd, blocks[0], blocks[1]))
+    pieces = [jnp.concatenate([block[:, :own], block[:, own:]], axis=0) for block in blocks]
     taps = jnp.concatenate(pieces, axis=1)
     for chunk in range(chunks):
         for tap in range(TAPS):
@@ -530,7 +556,8 @@
 
 def backward(length_ref, total_ref, masked_ref, taps_ref, rows_ref, *refs):
     own_ref, beside_ref = refs[:2]
-    side_refs, refs = side_blocks(1, refs[2 : 2 + N_CTX]), refs[2 + N_CTX :]
+    own_sides_ref, beside_sides_ref, grad_across_ref, grad_diagonal_ref = refs[2:6]
+    refs = refs[6:]
     own_pair_ref, beside_pair_ref, across_ref = refs[:3]
     grad_ref, keep_ref, send_ref, sums_ref = refs[3:7]
     side_ref, result_ref, cotangent_ref, tap_sum_ref = refs[7:]
@@ -540,8 +567,9 @@
     chunks = width // LANES
     half = rows_ref.shape[0] // 2
     place = lax.axis_index("ctx")
+    blocks = (own_sides_ref[1], beside_sides_ref[1], grad_across_ref[...], grad_diagonal_ref[...])
     for apart in range(N_CTX):
-        side_ref[place ^ apart] = side_refs[apart][...]
+        side_ref[place ^ apart] = blocks[apart].reshape(side_ref.shape[1:])
     tap_sum_ref[...] = jnp.zeros_like(tap_sum_ref)
     edge = jnp.zeros((2 * chunks, 16, LANES), jnp.float32)
     cotangent_ref[:, 0:16, :] = edge
@@ -725,36 +753,38 @@
         room=63,
     )(queries, key_proj, value_proj)
     packed = traded(blocks)
-    (shards,) = call_kernel(
+    (shard,) = call_kernel(
         pack_weights,
-        (shape((N_DP, entries + TAP_PAD // 2, width), low),),
+        (shape((1, entries + TAP_PAD // 2, width), low),),
         ["vmem"] * 2 + ["any"],
     )(out_weight.T, conv_weight, packed[1])
-    shards = dealt(shards)
+    for bit in (4, 2):
+        shard = jnp.concatenate([shard, swapped(shard, bit)], axis=0)
+    other_shard = swapped(shard, 1)
     pair_block = shape((2, utts, frames, width), low)
-    *sides, beside_sides, own_sides = call_kernel(
+    side_block = shape((utts * frames, width), low)
+    double_block = shape((2, utts * frames, width), low)
+    frame_across, grad_across, grad_diagonal, beside_sides, own_sides = call_kernel(
         pack_channels,
-        (channel_block,) * 4 + (pair_block,) * 2,
+        (double_block,) + (side_block,) * 2 + (double_block,) * 2,
         ["hbm"] * 2 + ["any"],
         scratch=[dma((4 * N_CTX,))],
     )(frame_input, grad_output, packed[2])
-    frame_across, frame_diagonal = crossed(sides[0], 2), crossed(sides[1], 3)
+    frame_across = crossed(frame_across, 2)
+    (beside_sides,) = call_kernel(
+        make_sides, (shape((3, utts * frames, width), low),), ["vmem"] * 2
+    )(beside_sides, frame_across)
     beside_sides = crossed(beside_sides, 1)
-    attended, weights = call_kernel(
+    (attended,) = call_kernel(
         attend,
-        (
-            shape((N_CTX, frames, half), low),
-            shape((half // HEAD_DIM, rows, rows), low),
-        ),
+        (shape((N_CTX, frames, half), low),),
         ["smem"] + ["vmem"] * N_CTX,
-        micros=3.0,
     )(lengths, *packed)
-    (attended,) = gate([attended], frame_across, frame_diagonal, micros=20.0)
+    (attended,) = gate([attended], frame_across)
     across = crossed(attended, 2)
     beside = crossed(attended, 1)
     diagonal = crossed(across, 1)
-    grad_across, grad_diagonal = crossed(sides[2], 2), crossed(sides[3], 3)
-    frame_blocks = (own_sides, beside_sides, frame_across, frame_diagonal)
+    grad_across, grad_diagonal = crossed(grad_across, 2), crossed(grad_diagonal, 3)
     forward_out = call_kernel(
         forward,
         (channel_block,) * 2
@@ -766,14 +796,25 @@
             shape((utts * chunks, rows, LANES), f32),
             shape((utts * chunks, rows + 32, LANES), f32),
         ),
-        ["smem"] + ["vmem"] * (1 + 2 * N_CTX),
+        ["smem"] + ["vmem"] * (5 + N_CTX),
         scratch=[
             pltpu.VMEM((utts * chunks, rows, LANES), f32),
             pltpu.VMEM((N_CTX, utts, frames, width), low),
             pltpu.VMEM((N_CTX, utts, frames, width), low),
         ],
         micros=3.2,
-    )(lengths, shards, attended, beside, across, diagonal, *frame_blocks)
+    )(
+        lengths,
+        shard,
+        other_shard,
+        attended,
+        beside,
+        across,
+        diagonal,
+        own_sides,
+        beside_sides,
+        frame_across,
+    )
     output_across = crossed(forward_out[2], 2)
     whole, weight_rows, taps, totals, masked = forward_out[3:]
     grad_blocks = gate([grad_across, grad_diagonal], totals, micros=10.0)
@@ -800,10 +841,10 @@
     grad_hidden, keep, send, sums = backward_out[3:]
     (send,) = gate([send], output_across)
     came = crossed(send, 1)
-    (far,) = call_kernel(
+    (relayed,) = call_kernel(
         relay, (shape((rows, half), low),), ["vmem"] * 2, micros=0.2
     )(keep, came)
-    (input_across,) = gate([backward_out[2]], far)
+    (input_across,) = gate([backward_out[2]], relayed)
     (panels,) = call_kernel(
         make_panels,
         (shape((N_DP, entries + TAP_PAD // 2, width), low),),
@@ -818,8 +859,12 @@
             (came,) = gate([came], *awaited)
         return (slots[:count].astype(f32) + came.astype(f32)).astype(low)
 
-    far, input_across = crossed(far, 2), crossed(input_across, 2)
-    panels = halved(panels, 1, far)
+    far, input_across = crossed(relayed, 2), crossed(input_across, 2)
+    (weights,) = call_kernel(
+        weigh,
+        (shape((half // HEAD_DIM, rows, rows), low),),
+        ["smem"] + ["vmem"] * N_CTX + ["any"],
+    )(lengths, *packed, relayed)
     back_blocks = call_kernel(
         attend_back,
         (head_block,) * N_CTX,
@@ -837,6 +882,7 @@
     )(backward_out[1], output_across, input_across, grad_blocks[2])
     beside_pair = crossed(beside_pair, 1)
 
+    panels = halved(panels, 1, back_blocks[0])
     panels = halved(panels, 2, grad_blocks[1])
     total = panels[0].astype(f32) + swapped(panels[1], 4).astype(f32)
     grad_out_weight = total[:entries].T

time: 70.9 us -> 71.9 us (1.014)
  starting transfers between devices: 23.4 us -> 29.3 us
  waiting for transfers between devices: 24.2 us -> 20.9 us
  local copies, waits for them, and re-layouts: 2.77 us -> 0.77 us
    ppermute x3 -> x6, starting transfers between devices: 2.55 us -> 11.1 us  [swapped(): return lax.ppermute(array, 'dp', [(i, i ^ bit) for i in range(N_DP)])]
    all_to_all x1 -> x0, starting transfers between devices: 6.2 us -> none  [dealt(): return lax.all_to_all(slots, 'dp', 0, 0, tiled=True)]
    ppermute x22 -> x21, starting transfers between devices: 14.7 us -> 18.2 us  [crossed(): return lax.ppermute(array, 'ctx', [(i, i ^ apart) for i in range(N_CTX)])]
    ppermute x3 -> x6, waiting for transfers between devices: 11.5 us -> 8.99 us  [swapped(): return lax.ppermute(array, 'dp', [(i, i ^ bit) for i in range(N_DP)])]
    all_to_all x1 -> x0, waiting for transfers between devices: 2.44 us -> none  [dealt(): return lax.all_to_all(slots, 'dp', 0, 0, tiled=True)]
    unnamed x16 -> x12, local copies, waits for them, and re-layouts: 2.03 us -> 0.03 us
    ppermute x22 -> x21, waiting for transfers between devices: 10.3 us -> 11.9 us  [crossed(): return lax.ppermute(array, 'ctx', [(i, i ^ apart) for i in range(N_CTX)])]
    pallas_call x3 -> x5, Pallas kernels: 4 us -> 4.41 us  [the longest x1 2.77 us: per_device(): call_kernel(attend, (shape((N_CTX, frames, half), low),), ['smem'] + ['vm...]
  transfers between devices with their start and end apart: 26 -> 27, of which waited for: 10 -> 13; matrix products, arithmetic and copies ran while one was open for 1% -> 1% of each run, Pallas kernels for 23% -> 24%
where the time goes in v7:
time: 71.9 us; the launch traced here: 71.7 us
  starting transfers between devices  29.3 us (41%)
  waiting for transfers between devices  20.9 us (29%)
  Pallas kernels  19.6 us (27%)
  between operations  0.89 us (1%)
  local copies, waits for them, and re-layouts  0.77 us (1%)
    ppermute x21, starting transfers between devices, crossed(): return lax.ppermute(array, 'ctx', [(i, i ^ apart) for i in range(N_CTX)])  18.2 us
    ppermute x21, waiting for transfers between devices, crossed(): return lax.ppermute(array, 'ctx', [(i, i ^ apart) for i in range(N_CTX)])  11.9 us
    ppermute x6, starting transfers between devices, swapped(): return lax.ppermute(array, 'dp', [(i, i ^ bit) for i in range(N_DP)])  11.1 us
    ppermute x6, waiting for transfers between devices, swapped(): return lax.ppermute(array, 'dp', [(i, i ^ bit) for i in range(N_DP)])  8.99 us
    pallas_call x1, Pallas kernels, per_device(): call_kernel(backward, (pair_block,) * 2 + (shape((2, utts * frames, width...  5.24 us
    pallas_call x1, Pallas kernels, per_device(): call_kernel(forward, (channel_block,) * 2 + (shape((2, utts * frames, wid...  3.2 us
    pallas_call x1, Pallas kernels, per_device(): call_kernel(attend, (shape((N_CTX, frames, half), low),), ['smem'] + ['vm...  2.77 us
    pallas_call x1, Pallas kernels, per_device(): call_kernel(pack_heads, (head_block,) * N_CTX, ['hbm'] * 3, scratch=[dma(...  2.01 us
  transfers between devices with their start and end apart: 27, of which 13 were waited for; matrix products, arithmetic and copies ran while one was open for 1% of the time, Pallas kernels for 24%

profile of v7, /device:TPU:0, one launch (start us, length us, event | category | flops | bytes accessed | tf_op | source)
XLA Modules:
  0.0 71.7 jit_solution(3091715083480769348)
XLA Ops:
  0.7 2.0 %shard_map.135 = (bf16[3,64,384]{2,1,0:T(8,128)(2,1)}, bf16[3,64,384]{2,1,0:T(8,128)(2,1)}, bf16[3,64,384]{2,1,0:T(8,128)(2,1)}, bf16[3,64,384]{2,1,0:T(8,128)(2,1)}) custom-call(bf16[2,64,768]{2,1,0:T(8,128)(2,1)} %query_ref.1, bf16[2,64,768]{2,1,0:T(8,128)(2,1)} %key_ref.1, bf16[2,64,768]{2,1,0:T(8,128)(2,1)} %value_ref.1), custom_call_target="tpu_custom_call" | custom-call | flops 1150000000 | tf_op jit(solution)/shard_map/pallas_call | solution.py:748
  3.2 2.6 %collective-permute-start.1 = (bf16[3,64,384]{2,1,0:T(8,128)(2,1)}, bf16[3,64,384]{2,1,0:T(8,128)(2,1)S(1)}, u32[]{:S(2)}, u32[]{:S(2)}) collective-permute-start(bf16[3,64,384]{2,1,0:T(8,128)(2,1)} %get-tuple-element.44), channel_id=1, source_target_pairs={{0,2},{1,3},{2,0},{3,1},{4,6},{5,7},{6,4},{7,5},{8,10},{9,11},{10,... | collective-permute-start | bytes 442376 | tf_op jit(solution)/shard_map/ppermute | solution.py:724
  5.9 2.8 %collective-permute-start.3 = (bf16[1,112,384]{2,1,0:T(8,128)(2,1)S(1)}, bf16[1,112,384]{2,1,0:T(8,128)(2,1)S(1)}, u32[]{:S(2)}, u32[]{:S(2)}) collective-permute-start(bf16[1,112,384]{2,1,0:T(8,128)(2,1)S(1)} %shard_map.136), channel_id=1, source_target_pairs={{0,16},{4,20},{8,24},{12,28},{16,0},{20,4},{24,8},{28,12},{1,17},{... | collective-permute-start | bytes 258056 | tf_op jit(solution)/shard_map/ppermute | solution.py:716
  8.8 1.9 %collective-permute-done.1.refs_2_.awaited_ref = bf16[3,64,384]{2,1,0:T(8,128)(2,1)S(1)} collective-permute-done((bf16[3,64,384]{2,1,0:T(8,128)(2,1)}, bf16[3,64,384]{2,1,0:T(8,128)(2,1)S(1)}, u32[]{:S(2)}, u32[]{:S(2)}) %collective-permute-start.1) | collective-permute-done | bytes 147488 | tf_op jit(solution)/shard_map/ppermute | solution.py:724
  11.0 2.0 %collective-permute-start.6 = (bf16[2,128,384]{2,1,0:T(8,128)(2,1)S(1)}, bf16[2,128,384]{2,1,0:T(8,128)(2,1)S(1)}, u32[]{:S(2)}, u32[]{:S(2)}) collective-permute-start(bf16[2,128,384]{2,1,0:T(8,128)(2,1)S(1)} %get-tuple-element.46), channel_id=1, source_target_pairs={{0,2},{1,3},{2,0},{3,1},{4,6},{5,7},{6,4},{7,5},{8,10},{9,11},{10,... | collective-permute-start | bytes 589832 | tf_op jit(solution)/shard_map/ppermute | solution.py:724
  14.7 2.8 %shard_map.137.refs_0_ = bf16[4,64,384]{2,1,0:T(8,128)(2,1)S(1)} custom-call(s32[2]{0:T(128)S(1)} %copy-done.4, bf16[3,64,384]{2,1,0:T(8,128)(2,1)S(1)} %copy-done.5, bf16[3,64,384]{2,1,0:T(8,128)(2,1)S(1)} %collective-permute-done.awaited_ref.refs_1_, bf16[3,64,384]{2,1,0:T(8,128)(2,1)S(1)} %collective-permute-done.1.refs_2_.awaited_ref, ...), custom_call_target="tpu_custom_call" | custom-call | flops 1150000000 | tf_op jit(solution)/shard_map/pallas_call | solution.py:778
  17.8 1.8 %collective-permute-start.8 = (bf16[4,64,384]{2,1,0:T(8,128)(2,1)S(1)}, bf16[4,64,384]{2,1,0:T(8,128)(2,1)S(1)}, u32[]{:S(2)}, u32[]{:S(2)}) collective-permute-start(bf16[4,64,384]{2,1,0:T(8,128)(2,1)S(1)} %shard_map.139.refs_0_), channel_id=1, source_target_pairs={{0,2},{1,3},{2,0},{3,1},{4,6},{5,7},{6,4},{7,5},{8,10},{9,11},{10,... | collective-permute-start | bytes 589832 | tf_op jit(solution)/shard_map/ppermute | solution.py:724
  19.8 1.4 %collective-permute-start.5 = (bf16[4,112,384]{2,1,0:T(8,128)(2,1)S(1)}, bf16[4,112,384]{2,1,0:T(8,128)(2,1)S(1)}, u32[]{:S(2)}, u32[]{:S(2)}) collective-permute-start(bf16[4,112,384]{2,1,0:T(8,128)(2,1)S(1)} %pad_maximum_fusion.near_ref), channel_id=1, source_target_pairs={{0,4},{4,0},{8,12},{12,8},{16,20},{20,16},{24,28},{28,24},{1,5},{5... | collective-permute-start | bytes 1032200 | tf_op jit(solution)/shard_map/ppermute | solution.py:716
  21.9 2.1 %collective-permute-done.8.refs_2_ = bf16[4,64,384]{2,1,0:T(8,128)(2,1)S(1)} collective-permute-done((bf16[4,64,384]{2,1,0:T(8,128)(2,1)S(1)}, bf16[4,64,384]{2,1,0:T(8,128)(2,1)S(1)}, u32[]{:S(2)}, u32[]{:S(2)}) %collective-permute-start.8) | collective-permute-done | bytes 196640 | tf_op jit(solution)/shard_map/ppermute | solution.py:724
  23.9 1.5 %collective-permute-start.11 = (bf16[128,384]{1,0:T(8,128)(2,1)S(1)}, bf16[128,384]{1,0:T(8,128)(2,1)S(1)}, u32[]{:S(2)}, u32[]{:S(2)}) collective-permute-start(bf16[128,384]{1,0:T(8,128)(2,1)S(1)} %get-tuple-element.55), channel_id=1, source_target_pairs={{0,2},{1,3},{2,0},{3,1},{4,6},{5,7},{6,4},{7,5},{8,10},{9,11},{10,... | collective-permute-start | bytes 294920 | tf_op jit(solution)/shard_map/ppermute | solution.py:724
  25.8 2.9 %collective-permute-done.5.other_ref = bf16[4,112,384]{2,1,0:T(8,128)(2,1)S(1)} collective-permute-done((bf16[4,112,384]{2,1,0:T(8,128)(2,1)S(1)}, bf16[4,112,384]{2,1,0:T(8,128)(2,1)S(1)}, u32[]{:S(2)}, u32[]{:S(2)}) %collective-permute-start.5) | collective-permute-done | bytes 344096 | tf_op jit(solution)/shard_map/ppermute | solution.py:716
  28.7 3.2 %shard_map.141 = (bf16[2,64,384]{2,1,0:T(8,128)(2,1)S(1)}, bf16[2,64,384]{2,1,0:T(8,128)(2,1)S(1)}, bf16[2,128,384]{2,1,0:T(8,128)(2,1)S(1)}, bf16[2,4,64,768]{3...) custom-call(s32[2]{0:T(128)S(1)} %copy-done.4, ...), custom_call_target="tpu_custom_call" | custom-call | flops 3680000000 | tf_op jit(solution)/shard_map/pallas_call | solution.py:788
  33.1 5.2 %shard_map.143 = (bf16[2,2,64,384]{3,2,1,0:T(8,128)(2,1)S(1)}, bf16[2,2,64,384]{3,2,1,0:T(8,128)(2,1)S(1)}, bf16[2,128,384]{2,1,0:T(8,128)(2,1)S(1)}, bf16[2,256...) custom-call(s32[2]{0:T(128)S(1)} %copy-done.4, ...), custom_call_target="tpu_custom_call" | custom-call | flops 5980000256 | tf_op jit(solution)/shard_map/pallas_call | solution.py:822
  38.4 1.7 %collective-permute-done.14.came_ref = bf16[2,256,384]{2,1,0:T(8,128)(2,1)S(1)} collective-permute-done((bf16[2,256,384]{2,1,0:T(8,128)(2,1)S(1)}, bf16[2,256,384]{2,1,0:T(8,128)(2,1)S(1)}, u32[]{:S(2)}, u32[]{:S(2)}) %collective-permute-start.14) | collective-permute-done | bytes 393248 | tf_op jit(solution)/shard_map/ppermute | solution.py:724
  45.8 2.2 %collective-permute-done.15.far_ref = bf16[256,384]{1,0:T(8,128)(2,1)S(1)} collective-permute-done((bf16[256,384]{1,0:T(8,128)(2,1)S(1)}, bf16[256,384]{1,0:T(8,128)(2,1)S(1)}, u32[]{:S(2)}, u32[]{:S(2)}) %collective-permute-start.15) | collective-permute-done | bytes 196640 | tf_op jit(solution)/shard_map/ppermute | solution.py:724
  48.0 1.9 %shard_map.147 = (bf16[3,64,384]{2,1,0:T(8,128)(2,1)S(1)}, bf16[3,64,384]{2,1,0:T(8,128)(2,1)S(1)}, bf16[3,64,384]{2,1,0:T(8,128)(2,1)S(1)}, bf16[3,64,384]{2,1,0:T(8,128)(2,1)S(1)}) custom-call(bf16[6,256,256]{2,1,0:T(8,128)(2,1)S(1)} %shard_map.146.weight_ref, bf16[2,256,384]{2,1,0:T(8,128)(2,1)S(1)} %get-tuple-element.59.keep_ref, ...), custom_call_target="tpu_custom_call" | custom-call | flops 2529999872 | tf_op jit(solution)/shard_map/pallas_call | solution.py:868
  50.0 1.8 %collective-permute-done.21.refs_0_ = bf16[4,112,384]{2,1,0:T(8,128)(2,1)S(1)} collective-permute-done((bf16[4,112,384]{2,1,0:T(8,128)(2,1)S(1)}, bf16[4,112,384]{2,1,0:T(8,128)(2,1)S(1)}, u32[]{:S(2)}, u32[]{:S(2)}) %collective-permute-start.21) | collective-permute-done | bytes 344096 | tf_op jit(solution)/shard_map/ppermute | solution.py:716
  53.1 1.7 %collective-permute-start.18 = (bf16[3,64,384]{2,1,0:T(8,128)(2,1)S(1)}, bf16[3,64,384]{2,1,0:T(8,128)(2,1)S(1)}, u32[]{:S(2)}, u32[]{:S(2)}) collective-permute-start(bf16[3,64,384]{2,1,0:T(8,128)(2,1)S(1)} %shard_map.149), channel_id=1, source_target_pairs={{0,2},{1,3},{2,0},{3,1},{4,6},{5,7},{6,4},{7,5},{8,10},{9,11},{10,... | collective-permute-start | bytes 442376 | tf_op jit(solution)/shard_map/ppermute | solution.py:724
  54.8 2.6 %collective-permute-done.22.refs_0_ = bf16[2,112,384]{2,1,0:T(8,128)(2,1)S(1)} collective-permute-done((bf16[2,112,384]{2,1,0:T(8,128)(2,1)S(1)}, bf16[2,112,384]{2,1,0:T(8,128)(2,1)S(1)}, u32[]{:S(2)}, u32[]{:S(2)}) %collective-permute-start.22) | collective-permute-done | bytes 172064 | tf_op jit(solution)/shard_map/ppermute | solution.py:716
  57.4 3.4 %collective-permute-start.23 = (bf16[112,384]{1,0:T(8,128)(2,1)S(1)}, bf16[112,384]{1,0:T(8,128)(2,1)S(1)}, u32[]{:S(2)}, u32[]{:S(2)}) collective-permute-start(bf16[112,384]{1,0:T(8,128)(2,1)S(1)} %slice_bitcast_fusion.1), channel_id=1, source_target_pairs={{0,16},{4,20},{8,24},{12,28},{16,0},{20,4},{24,8},{28,12},{1,17},{... | collective-permute-start | bytes 258056 | tf_op jit(solution)/shard_map/ppermute | solution.py:716
  60.9 1.7 %collective-permute-start.20 = (bf16[4,128,384]{2,1,0:T(8,128)(2,1)S(1)}, bf16[4,128,384]{2,1,0:T(8,128)(2,1)S(1)}, u32[]{:S(2)}, u32[]{:S(2)}) collective-permute-start(bf16[4,128,384]{2,1,0:T(8,128)(2,1)S(1)} %shard_map.150), channel_id=1, source_target_pairs={{0,1},{1,0},{2,3},{3,2},{4,5},{5,4},{6,7},{7,6},{8,9},{9,8},{10,11... | collective-permute-start | bytes 1179656 | tf_op jit(solution)/shard_map/ppermute | solution.py:724
  64.0 2.9 %collective-permute-done.19.refs_3_.refs_1_ = bf16[3,64,384]{2,1,0:T(8,128)(2,1)S(1)} collective-permute-done((bf16[3,64,384]{2,1,0:T(8,128)(2,1)S(1)}, bf16[3,64,384]{2,1,0:T(8,128)(2,1)S(1)}, u32[]{:S(2)}, u32[]{:S(2)}) %collective-permute-start.19) | collective-permute-done | bytes 147488 | tf_op jit(solution)/shard_map/ppermute | solution.py:724
  67.0 1.7 %collective-permute-start.25 = (f32[16,384]{1,0:T(8,128)S(1)}, f32[16,384]{1,0:T(8,128)S(1)}, u32[]{:S(2)}, u32[]{:S(2)}) collective-permute-start(f32[16,384]{1,0:T(8,128)S(1)} %shard_map.155.refs_0_), channel_id=1, source_target_pairs={{0,2},{1,3},{2,0},{3,1},{4,6},{5,7},{6,4},{7,5},{8,10},{9,11},{10,... | collective-permute-start | bytes 73736 | tf_op jit(solution)/shard_map/ppermute | solution.py:724
  68.8 1.4 %shard_map.151 = (bf16[2,64,768]{2,1,0:T(8,128)(2,1)}, bf16[2,64,768]{2,1,0:T(8,128)(2,1)}, bf16[2,64,768]{2,1,0:T(8,128)(2,1)}, bf16[2,64,1536]{2,1,0:T(8,128)(2,1)}, bf16[2,64,1536]{2,1,0:T(8,128)(2,1)}) custom-call(bf16[3,64,384]{2,1,0:T(8,128)(2,1)S(1)} %get-tuple-element.62.refs_0_.refs_1_, bf16[3,64,384]{2,1,0:T(8,128)(2,1)S(1)} %collective-permute-done.16.refs_1_, ...), custom_call_target="tpu_custom_call" | custom-call | flops 1150000000 | tf_op jit(solution)/shard_map/pallas_call | solution.py:896
  (74 shorter events, 15.6 us)
Async XLA Ops:
  2.7 3.2 %collective-permute-start = (bf16[3,64,384]{2,1,0:T(8,128)(2,1)}, bf16[3,64,384]{2,1,0:T(8,128)(2,1)S(1)}, u32[]{:S(2)}, u32[]{:S(2)}) collective-permute-start(bf16[3,64,384]{2,1,0:T(8,128)(2,1)} %get-tuple-element.43), channel_id=1, source_target_pairs={{0,1},{1,0},{2,3},{3,2},{4,5},{5,4},{6,7},{7,6},{8,9},{9,8},{10,11... | collective-permute-start | bytes 442376 | tf_op jit(solution)/shard_map/ppermute | solution.py:724
  3.2 7.5 %collective-permute-start.1 = (bf16[3,64,384]{2,1,0:T(8,128)(2,1)}, bf16[3,64,384]{2,1,0:T(8,128)(2,1)S(1)}, u32[]{:S(2)}, u32[]{:S(2)}) collective-permute-start(bf16[3,64,384]{2,1,0:T(8,128)(2,1)} %get-tuple-element.44), channel_id=1, source_target_pairs={{0,2},{1,3},{2,0},{3,1},{4,6},{5,7},{6,4},{7,5},{8,10},{9,11},{10,... | collective-permute-start | bytes 442376 | tf_op jit(solution)/shard_map/ppermute | solution.py:724
  5.8 8.9 %collective-permute-start.2 = (bf16[3,64,384]{2,1,0:T(8,128)(2,1)}, bf16[3,64,384]{2,1,0:T(8,128)(2,1)S(1)}, u32[]{:S(2)}, u32[]{:S(2)}) collective-permute-start(bf16[3,64,384]{2,1,0:T(8,128)(2,1)} %get-tuple-element.45), channel_id=1, source_target_pairs={{0,3},{1,2},{2,1},{3,0},{4,7},{5,6},{6,5},{7,4},{8,11},{9,10},{10,... | collective-permute-start | bytes 442376 | tf_op jit(solution)/shard_map/ppermute | solution.py:724
  5.9 7.7 %collective-permute-start.3 = (bf16[1,112,384]{2,1,0:T(8,128)(2,1)S(1)}, bf16[1,112,384]{2,1,0:T(8,128)(2,1)S(1)}, u32[]{:S(2)}, u32[]{:S(2)}) collective-permute-start(bf16[1,112,384]{2,1,0:T(8,128)(2,1)S(1)} %shard_map.136), channel_id=1, source_target_pairs={{0,16},{4,20},{8,24},{12,28},{16,0},{20,4},{24,8},{28,12},{1,17},{... | collective-permute-start | bytes 258056 | tf_op jit(solution)/shard_map/ppermute | solution.py:716
  11.0 6.8 %collective-permute-start.6 = (bf16[2,128,384]{2,1,0:T(8,128)(2,1)S(1)}, bf16[2,128,384]{2,1,0:T(8,128)(2,1)S(1)}, u32[]{:S(2)}, u32[]{:S(2)}) collective-permute-start(bf16[2,128,384]{2,1,0:T(8,128)(2,1)S(1)} %get-tuple-element.46), channel_id=1, source_target_pairs={{0,2},{1,3},{2,0},{3,1},{4,6},{5,7},{6,4},{7,5},{8,10},{9,11},{10,... | collective-permute-start | bytes 589832 | tf_op jit(solution)/shard_map/ppermute | solution.py:724
  13.7 6.1 %collective-permute-start.4 = (bf16[2,112,384]{2,1,0:T(8,128)(2,1)S(1)}, bf16[2,112,384]{2,1,0:T(8,128)(2,1)S(1)}, u32[]{:S(2)}, u32[]{:S(2)}) collective-permute-start(bf16[2,112,384]{2,1,0:T(8,128)(2,1)S(1)} %pad_maximum_fusion.1), channel_id=1, source_target_pairs={{0,8},{4,12},{8,0},{12,4},{16,24},{20,28},{24,16},{28,20},{1,9},{5... | collective-permute-start | bytes 516104 | tf_op jit(solution)/shard_map/ppermute | solution.py:716
  17.8 6.2 %collective-permute-start.8 = (bf16[4,64,384]{2,1,0:T(8,128)(2,1)S(1)}, bf16[4,64,384]{2,1,0:T(8,128)(2,1)S(1)}, u32[]{:S(2)}, u32[]{:S(2)}) collective-permute-start(bf16[4,64,384]{2,1,0:T(8,128)(2,1)S(1)} %shard_map.139.refs_0_), channel_id=1, source_target_pairs={{0,2},{1,3},{2,0},{3,1},{4,6},{5,7},{6,4},{7,5},{8,10},{9,11},{10,... | collective-permute-start | bytes 589832 | tf_op jit(solution)/shard_map/ppermute | solution.py:724
  19.8 8.9 %collective-permute-start.5 = (bf16[4,112,384]{2,1,0:T(8,128)(2,1)S(1)}, bf16[4,112,384]{2,1,0:T(8,128)(2,1)S(1)}, u32[]{:S(2)}, u32[]{:S(2)}) collective-permute-start(bf16[4,112,384]{2,1,0:T(8,128)(2,1)S(1)} %pad_maximum_fusion.near_ref), channel_id=1, source_target_pairs={{0,4},{4,0},{8,12},{12,8},{16,20},{20,16},{24,28},{28,24},{1,5},{5... | collective-permute-start | bytes 1032200 | tf_op jit(solution)/shard_map/ppermute | solution.py:716
  21.3 4.5 %collective-permute-start.10 = (bf16[3,128,384]{2,1,0:T(8,128)(2,1)S(1)}, bf16[3,128,384]{2,1,0:T(8,128)(2,1)S(1)}, u32[]{:S(2)}, u32[]{:S(2)}) collective-permute-start(bf16[3,128,384]{2,1,0:T(8,128)(2,1)S(1)} %shard_map.140), channel_id=1, source_target_pairs={{0,1},{1,0},{2,3},{3,2},{4,5},{5,4},{6,7},{7,6},{8,9},{9,8},{10,11... | collective-permute-start | bytes 884744 | tf_op jit(solution)/shard_map/ppermute | solution.py:724
  21.4 4.1 %collective-permute-start.7 = (bf16[4,64,384]{2,1,0:T(8,128)(2,1)S(1)}, bf16[4,64,384]{2,1,0:T(8,128)(2,1)S(1)}, u32[]{:S(2)}, u32[]{:S(2)}) collective-permute-start(bf16[4,64,384]{2,1,0:T(8,128)(2,1)S(1)} %shard_map.139.refs_0_), channel_id=1, source_target_pairs={{0,1},{1,0},{2,3},{3,2},{4,5},{5,4},{6,7},{7,6},{8,9},{9,8},{10,11... | collective-permute-start | bytes 589832 | tf_op jit(solution)/shard_map/ppermute | solution.py:724
  23.9 9.2 %collective-permute-start.11 = (bf16[128,384]{1,0:T(8,128)(2,1)S(1)}, bf16[128,384]{1,0:T(8,128)(2,1)S(1)}, u32[]{:S(2)}, u32[]{:S(2)}) collective-permute-start(bf16[128,384]{1,0:T(8,128)(2,1)S(1)} %get-tuple-element.55), channel_id=1, source_target_pairs={{0,2},{1,3},{2,0},{3,1},{4,6},{5,7},{6,4},{7,5},{8,10},{9,11},{10,... | collective-permute-start | bytes 294920 | tf_op jit(solution)/shard_map/ppermute | solution.py:724
  25.4 7.7 %collective-permute-start.12 = (bf16[128,384]{1,0:T(8,128)(2,1)S(1)}, bf16[128,384]{1,0:T(8,128)(2,1)S(1)}, u32[]{:S(2)}, u32[]{:S(2)}) collective-permute-start(bf16[128,384]{1,0:T(8,128)(2,1)S(1)} %get-tuple-element.56), channel_id=1, source_target_pairs={{0,3},{1,2},{2,1},{3,0},{4,7},{5,6},{6,5},{7,4},{8,11},{9,10},{10,... | collective-permute-start | bytes 294920 | tf_op jit(solution)/shard_map/ppermute | solution.py:724
  32.0 6.4 %collective-permute-start.13 = (bf16[2,128,384]{2,1,0:T(8,128)(2,1)S(1)}, bf16[2,128,384]{2,1,0:T(8,128)(2,1)S(1)}, u32[]{:S(2)}, u32[]{:S(2)}) collective-permute-start(bf16[2,128,384]{2,1,0:T(8,128)(2,1)S(1)} %get-tuple-element.61), channel_id=1, source_target_pairs={{0,2},{1,3},{2,0},{3,1},{4,6},{5,7},{6,4},{7,5},{8,10},{9,11},{10,... | collective-permute-start | bytes 589832 | tf_op jit(solution)/shard_map/ppermute | solution.py:724
  40.2 7.8 %collective-permute-start.15 = (bf16[256,384]{1,0:T(8,128)(2,1)S(1)}, bf16[256,384]{1,0:T(8,128)(2,1)S(1)}, u32[]{:S(2)}, u32[]{:S(2)}) collective-permute-start(bf16[256,384]{1,0:T(8,128)(2,1)S(1)} %shard_map.145.refs_4_.refs_1_), channel_id=1, source_target_pairs={{0,2},{1,3},{2,0},{3,1},{4,6},{5,7},{6,4},{7,5},{8,10},{9,11},{10,... | collective-permute-start | bytes 589832 | tf_op jit(solution)/shard_map/ppermute | solution.py:724
  41.9 9.9 %collective-permute-start.21 = (bf16[4,112,384]{2,1,0:T(8,128)(2,1)S(1)}, bf16[4,112,384]{2,1,0:T(8,128)(2,1)S(1)}, u32[]{:S(2)}, u32[]{:S(2)}) collective-permute-start(bf16[4,112,384]{2,1,0:T(8,128)(2,1)S(1)} %slice.33), channel_id=1, source_target_pairs={{0,4},{4,0},{8,12},{12,8},{16,20},{20,16},{24,28},{28,24},{1,5},{5... | collective-permute-start | bytes 1032200 | tf_op jit(solution)/shard_map/ppermute | solution.py:716
  43.2 10.0 %collective-permute-start.17 = (bf16[2,128,384]{2,1,0:T(8,128)(2,1)S(1)}, bf16[2,128,384]{2,1,0:T(8,128)(2,1)S(1)}, u32[]{:S(2)}, u32[]{:S(2)}) collective-permute-start(bf16[2,128,384]{2,1,0:T(8,128)(2,1)S(1)} %shard_map.148), channel_id=1, source_target_pairs={{0,2},{1,3},{2,0},{3,1},{4,6},{5,7},{6,4},{7,5},{8,10},{9,11},{10,... | collective-permute-start | bytes 589832 | tf_op jit(solution)/shard_map/ppermute | solution.py:724
  51.9 5.5 %collective-permute-start.22 = (bf16[2,112,384]{2,1,0:T(8,128)(2,1)S(1)}, bf16[2,112,384]{2,1,0:T(8,128)(2,1)S(1)}, u32[]{:S(2)}, u32[]{:S(2)}) collective-permute-start(bf16[2,112,384]{2,1,0:T(8,128)(2,1)S(1)} %slice.35), channel_id=1, source_target_pairs={{0,8},{4,12},{8,0},{12,4},{16,24},{20,28},{24,16},{28,20},{1,9},{5... | collective-permute-start | bytes 516104 | tf_op jit(solution)/shard_map/ppermute | solution.py:716
  53.1 7.7 %collective-permute-start.18 = (bf16[3,64,384]{2,1,0:T(8,128)(2,1)S(1)}, bf16[3,64,384]{2,1,0:T(8,128)(2,1)S(1)}, u32[]{:S(2)}, u32[]{:S(2)}) collective-permute-start(bf16[3,64,384]{2,1,0:T(8,128)(2,1)S(1)} %shard_map.149), channel_id=1, source_target_pairs={{0,2},{1,3},{2,0},{3,1},{4,6},{5,7},{6,4},{7,5},{8,10},{9,11},{10,... | collective-permute-start | bytes 442376 | tf_op jit(solution)/shard_map/ppermute | solution.py:724
  57.4 5.9 %collective-permute-start.23 = (bf16[112,384]{1,0:T(8,128)(2,1)S(1)}, bf16[112,384]{1,0:T(8,128)(2,1)S(1)}, u32[]{:S(2)}, u32[]{:S(2)}) collective-permute-start(bf16[112,384]{1,0:T(8,128)(2,1)S(1)} %slice_bitcast_fusion.1), channel_id=1, source_target_pairs={{0,16},{4,20},{8,24},{12,28},{16,0},{20,4},{24,8},{28,12},{1,17},{... | collective-permute-start | bytes 258056 | tf_op jit(solution)/shard_map/ppermute | solution.py:716
  60.8 6.1 %collective-permute-start.19 = (bf16[3,64,384]{2,1,0:T(8,128)(2,1)S(1)}, bf16[3,64,384]{2,1,0:T(8,128)(2,1)S(1)}, u32[]{:S(2)}, u32[]{:S(2)}) collective-permute-start(bf16[3,64,384]{2,1,0:T(8,128)(2,1)S(1)} %get-tuple-element.66), channel_id=1, source_target_pairs={{0,3},{1,2},{2,1},{3,0},{4,7},{5,6},{6,5},{7,4},{8,11},{9,10},{10,... | collective-permute-start | bytes 442376 | tf_op jit(solution)/shard_map/ppermute | solution.py:724
  60.9 6.1 %collective-permute-start.20 = (bf16[4,128,384]{2,1,0:T(8,128)(2,1)S(1)}, bf16[4,128,384]{2,1,0:T(8,128)(2,1)S(1)}, u32[]{:S(2)}, u32[]{:S(2)}) collective-permute-start(bf16[4,128,384]{2,1,0:T(8,128)(2,1)S(1)} %shard_map.150), channel_id=1, source_target_pairs={{0,1},{1,0},{2,3},{3,2},{4,5},{5,4},{6,7},{7,6},{8,9},{9,8},{10,11... | collective-permute-start | bytes 1179656 | tf_op jit(solution)/shard_map/ppermute | solution.py:724
  67.0 3.3 %collective-permute-start.26 = (f32[16,384]{1,0:T(8,128)S(1)}, f32[16,384]{1,0:T(8,128)S(1)}, u32[]{:S(2)}, u32[]{:S(2)}) collective-permute-start(f32[16,384]{1,0:T(8,128)S(1)} %shard_map.155.refs_0_), channel_id=1, source_target_pairs={{0,3},{1,2},{2,1},{3,0},{4,7},{5,6},{6,5},{7,4},{8,11},{9,10},{10,... | collective-permute-start | bytes 73736 | tf_op jit(solution)/shard_map/ppermute | solution.py:724
  67.0 4.1 %collective-permute-start.25 = (f32[16,384]{1,0:T(8,128)S(1)}, f32[16,384]{1,0:T(8,128)S(1)}, u32[]{:S(2)}, u32[]{:S(2)}) collective-permute-start(f32[16,384]{1,0:T(8,128)S(1)} %shard_map.155.refs_0_), channel_id=1, source_target_pairs={{0,2},{1,3},{2,0},{3,1},{4,6},{5,7},{6,4},{7,5},{8,10},{9,11},{10,... | collective-permute-start | bytes 73736 | tf_op jit(solution)/shard_map/ppermute | solution.py:724
  68.7 2.3 %collective-permute-start.24 = (f32[16,384]{1,0:T(8,128)S(1)}, f32[16,384]{1,0:T(8,128)S(1)}, u32[]{:S(2)}, u32[]{:S(2)}) collective-permute-start(f32[16,384]{1,0:T(8,128)S(1)} %shard_map.155.refs_0_), channel_id=1, source_target_pairs={{0,1},{1,0},{2,3},{3,2},{4,5},{5,4},{6,7},{7,6},{8,9},{9,8},{10,11... | collective-permute-start | bytes 73736 | tf_op jit(solution)/shard_map/ppermute | solution.py:724
  (9 other events, 30.1 us)

commit v8 on v7

--- a/solution.py
+++ b/solution.py
@@ -554,13 +554,13 @@
         out_refs[2][apart] = result_ref[place ^ (2 + apart)].reshape(2 * frames, width)
 
 
-def backward(length_ref, total_ref, masked_ref, taps_ref, rows_ref, *refs):
+def backward(length_ref, total_ref, taps_ref, rows_ref, *refs):
     own_ref, beside_ref = refs[:2]
     own_sides_ref, beside_sides_ref, grad_across_ref, grad_diagonal_ref = refs[2:6]
     refs = refs[6:]
     own_pair_ref, beside_pair_ref, across_ref = refs[:3]
-    grad_ref, keep_ref, send_ref, sums_ref = refs[3:7]
-    side_ref, result_ref, cotangent_ref, tap_sum_ref = refs[7:]
+    grad_ref, keep_ref, send_ref, cotangent_ref = refs[3:7]
+    side_ref, result_ref = refs[7:]
     own_pair_ref[0], beside_pair_ref[0] = own_ref[...], beside_ref[...]
     utts, frames, width = own_ref.shape
     rows = N_CTX * frames
@@ -570,7 +570,6 @@
     blocks = (own_sides_ref[1], beside_sides_ref[1], grad_across_ref[...], grad_diagonal_ref[...])
     for apart in range(N_CTX):
         side_ref[place ^ apart] = blocks[apart].reshape(side_ref.shape[1:])
-    tap_sum_ref[...] = jnp.zeros_like(tap_sum_ref)
     edge = jnp.zeros((2 * chunks, 16, LANES), jnp.float32)
     cotangent_ref[:, 0:16, :] = edge
     cotangent_ref[:, 16 + rows : 32 + rows, :] = edge
@@ -591,12 +590,10 @@
         for block in range(N_CTX):
             base = block * frames
             total = jnp.zeros(shape, jnp.float32)
-            held = masked_ref[step, 16 + base : 16 + base + frames, :].reshape(shape)
             for tap in range(TAPS):
                 first = base + 16 + REACH - tap
                 piece = cotangent_ref[step, first : first + frames, :].reshape(shape)
                 total += taps_ref[chunk, tap][None] * piece
-                tap_sum_ref[chunk, tap] += jnp.sum(held * piece, axis=0)
             place_of = base + lax.broadcasted_iota(jnp.int32, (frames, LANES), 0)
             total = jnp.where(place_of < length, total.reshape(frames, LANES), 0.0)
             incoming = side_ref[block, utt, :, cols].astype(jnp.float32)
@@ -606,17 +603,6 @@
         return carry
 
     lax.fori_loop(0, 2 * chunks, convolve, 0)
-    sums = [
-        jnp.concatenate(
-            [
-                jnp.sum(tap_sum_ref[chunk, tap], axis=0, keepdims=True)
-                for tap in range(TAP_PAD)
-            ],
-            axis=0,
-        )
-        for chunk in range(chunks)
-    ]
-    sums_ref[...] = jnp.concatenate(sums, axis=1)
     for apart in range(N_CTX):
         mine = result_ref[place ^ apart]
         if apart < 2:
@@ -636,10 +622,48 @@
             ref[apart // 2, pl.ds(first, frames), :] = mixed[block * frames : (block + 1) * frames]
 
 
-def make_panels(whole_ref, grad_ref, sums_ref, panel_ref):
+def make_taps(masked_ref, cotangent_ref, awaited_ref, keep_ref, send_ref, tap_sum_ref):
+    steps, rows, chunks = masked_ref.shape[0], masked_ref.shape[1] - 32, tap_sum_ref.shape[0]
+    block = 64
+    shape = (block // 8, 8, LANES)
+    tap_sum_ref[...] = jnp.zeros_like(tap_sum_ref)
+
+    def correlate(step, carry):
+        chunk = step % chunks
+        for base in range(0, rows, block):
+            held = masked_ref[step, 16 + base : 16 + base + block, :].reshape(shape)
+            for tap in range(TAPS):
+                first = base + 16 + REACH - tap
+                piece = cotangent_ref[step, first : first + block, :].reshape(shape)
+                tap_sum_ref[chunk, tap] += jnp.sum(held * piece, axis=0)
+        return carry
+
+    lax.fori_loop(0, steps, correlate, 0)
+    sums = [
+        jnp.concatenate(
+            [
+                jnp.sum(tap_sum_ref[chunk, tap], axis=0, keepdims=True)
+                for tap in range(TAP_PAD)
+            ],
+            axis=0,
+        )
+        for chunk in range(chunks)
+    ]
+    sums = jnp.concatenate(sums, axis=1)
+    own = sums.shape[1] // 2
+    halves = [
+        jnp.concatenate([part[: TAP_PAD // 2], part[TAP_PAD // 2 :]], axis=1)
+        for part in (sums[:, :own], sums[:, own:])
+    ]
+    odd = (lax.axis_index("dp") & 1) == 1
+    keep_ref[...] = jnp.where(odd, halves[1], halves[0])
+    send_ref[...] = jnp.where(odd, halves[0], halves[1])
+
+
+def make_panels(whole_ref, grad_ref, panel_ref):
     rows, half = grad_ref.shape[1], whole_ref.shape[3] // 2
     entries = 2 * half // N_DP
-    group, place = lax.axis_index("dp"), lax.axis_index("ctx")
+    group = lax.axis_index("dp")
     for side in range(2):
         panel = 0.0
         for utt in range(2):
@@ -647,15 +671,28 @@
             panel += dot_tt(mixed, grad_ref[utt], 0, 0)
         panel = panel.astype(jnp.bfloat16)
         for part in range(N_DP // 2):
-            panel_ref[slot_of(side * N_DP // 2 + part, group), 0:entries] = panel[
+            panel_ref[slot_of(side * N_DP // 2 + part, group)] = panel[
                 part * entries : (part + 1) * entries
             ]
-    panel_ref[:, entries:, :] = jnp.zeros((N_DP, TAP_PAD // 2, half), jnp.bfloat16)
-    own = half // 2
-    for part in range(2):
-        mine = sums_ref[:, part * own : (part + 1) * own]
-        mine = jnp.concatenate([mine[: TAP_PAD // 2], mine[TAP_PAD // 2 :]], axis=1)
-        panel_ref[slot_of(2 * place + part, group), entries:, :] = mine.astype(jnp.bfloat16)
+
+
+def join(panel_ref, came_ref, tap_ref, tap_came_ref, awaited_ref, keep_ref, send_ref):
+    entries = panel_ref.shape[1]
+    group, place = lax.axis_index("dp"), lax.axis_index("ctx")
+    taps = (tap_ref[...] + tap_came_ref[...]).astype(jnp.bfloat16)
+    none = jnp.zeros_like(taps)
+    for slot in range(N_DP // 2):
+        ref = (keep_ref, send_ref)[slot // 2]
+        total = panel_ref[slot].astype(jnp.float32) + came_ref[slot].astype(jnp.float32)
+        ref[slot % 2, 0:entries] = total.astype(jnp.bfloat16)
+        ref[slot % 2, entries:] = none
+    mine = slot_of(2 * place, group & 6)
+    for slot in range(N_DP // 2):
+        ref = (keep_ref, send_ref)[slot // 2]
+
+        @pl.when(mine == slot)
+        def _(ref=ref, slot=slot):
+            ref[slot % 2, entries:] = taps
 
 
 def pick_taps(*refs):
@@ -672,7 +709,8 @@
     out_ref[...] = total.astype(jnp.bfloat16)
 
 
-def make_pair(pair_ref, output_ref, input_ref, awaited_ref, out_ref):
+def make_pair(pair_ref, output_ref, input_ref, *refs):
+    out_ref = refs[-1]
     for slot in range(2):
         out_ref[slot] = pair_ref[slot].reshape(out_ref.shape[1:])
     out_ref[2] = output_ref[1]
@@ -680,7 +718,7 @@
 
 
 def attend_back(weight_ref, keep_ref, came_ref, far_ref, *refs):
-    ins, out_refs = refs[:N_CTX], refs[N_CTX:]
+    ins, out_refs = refs[:N_CTX], refs[N_CTX + 1 :]
     frames, half = ins[0].shape[1], ins[0].shape[2]
     rows = N_CTX * frames
     query, key, value = (head_parts(ins, slot) for slot in range(3))
@@ -827,18 +865,16 @@
             shape((utts, rows, width), low),
             shape((2, rows, half), low),
             shape((2, rows, half), low),
-            shape((TAP_PAD, width), f32),
+            shape((utts * chunks, rows + 32, LANES), f32),
         ),
-        ["smem"] + ["vmem"] * (6 + N_CTX),
+        ["smem"] + ["vmem"] * (5 + N_CTX),
         scratch=[
             pltpu.VMEM((N_CTX, utts, frames, width), low),
             pltpu.VMEM((N_CTX, utts, frames, width), low),
-            pltpu.VMEM((utts * chunks, rows + 32, LANES), f32),
-            pltpu.VMEM((chunks, TAP_PAD, 8, LANES), f32),
         ],
         micros=5.2,
-    )(lengths, totals, masked, taps, weight_rows, *forward_out[:2], *grad_blocks)
-    grad_hidden, keep, send, sums = backward_out[3:]
+    )(lengths, totals, taps, weight_rows, *forward_out[:2], *grad_blocks)
+    grad_hidden, keep, send, cotangents = backward_out[3:]
     (send,) = gate([send], output_across)
     came = crossed(send, 1)
     (relayed,) = call_kernel(
@@ -847,18 +883,19 @@
     (input_across,) = gate([backward_out[2]], relayed)
     (panels,) = call_kernel(
         make_panels,
-        (shape((N_DP, entries + TAP_PAD // 2, width), low),),
-        ["vmem"] * 3,
+        (shape((N_DP, entries, width), low),),
+        ["vmem"] * 2,
         micros=0.7,
-    )(whole, grad_hidden, sums)
-
-    def halved(slots, bit, *awaited):
-        count = slots.shape[0] // 2
-        came = swapped(slots[count:], bit)
-        if awaited:
-            (came,) = gate([came], *awaited)
-        return (slots[:count].astype(f32) + came.astype(f32)).astype(low)
-
+    )(whole, grad_hidden)
+    panels_came = swapped(panels[4:], 1)
+    tap_block = shape((TAP_PAD // 2, width), f32)
+    tap_keep, tap_send = call_kernel(
+        make_taps,
+        (tap_block,) * 2,
+        ["vmem"] * 2 + ["any"],
+        scratch=[pltpu.VMEM((chunks, TAP_PAD, 8, LANES), f32)],
+    )(masked, cotangents, relayed)
+    taps_came = swapped(tap_send, 1)
     far, input_across = crossed(relayed, 2), crossed(input_across, 2)
     (weights,) = call_kernel(
         weigh,
@@ -868,25 +905,29 @@
     back_blocks = call_kernel(
         attend_back,
         (head_block,) * N_CTX,
-        ["vmem"] * (4 + N_CTX),
+        ["vmem"] * (4 + N_CTX) + ["any"],
         micros=2.2,
-    )(weights, keep, came, far, *packed)
+    )(weights, keep, came, far, *packed, taps_came)
     (across_block,) = gate([back_blocks[2]], input_across)
     grad_blocks = traded([*back_blocks[:2], across_block, back_blocks[3]])
     own_pair = backward_out[0]
     (beside_pair,) = call_kernel(
         make_pair,
         (shape((4, utts * frames, width), low),),
-        ["vmem"] * 3 + ["any"],
+        ["vmem"] * 3 + ["any"] * 3,
         micros=0.2,
-    )(backward_out[1], output_across, input_across, grad_blocks[2])
+    )(backward_out[1], output_across, input_across, *grad_blocks[1:])
     beside_pair = crossed(beside_pair, 1)
 
-    panels = halved(panels, 1, back_blocks[0])
-    panels = halved(panels, 2, grad_blocks[1])
+    kept, sent = call_kernel(
+        join,
+        (shape((2, entries + TAP_PAD // 2, width), low),) * 2,
+        ["vmem"] * 4 + ["any"],
+    )(panels[:4], panels_came, tap_keep, taps_came, back_blocks[0])
+    panels = (kept.astype(f32) + swapped(sent, 2).astype(f32)).astype(low)
     total = panels[0].astype(f32) + swapped(panels[1], 4).astype(f32)
     grad_out_weight = total[:entries].T
-    (tap_sums,) = gate([total[entries:]], grad_blocks[3], beside_pair)
+    (tap_sums,) = gate([total[entries:]], beside_pair)
     (grad_taps,) = call_kernel(
         pick_taps,
         (shape(conv_weight.shape, f32),),

time: 71.9 us -> 68.2 us (0.949)
  waiting for transfers between devices: 20.9 us -> 17 us
    ppermute x21, waiting for transfers between devices: 11.9 us -> 5.87 us  [crossed(): return lax.ppermute(array, 'ctx', [(i, i ^ apart) for i in range(N_CTX)])]
    pallas_call x2 -> x4, Pallas kernels: 2.57 us -> 4.74 us  [the longest x1 2.08 us: per_device(): call_kernel(make_taps, (tap_block,) * 2, ['vmem'] * 2 + ['any'], scratch=...]
    ppermute x6 -> x7, waiting for transfers between devices: 8.99 us -> 11.1 us  [swapped(): return lax.ppermute(array, 'dp', [(i, i ^ bit) for i in range(N_DP)])]
    pallas_call x1, Pallas kernels: 5.24 us -> 3.58 us  [per_device(): call_kernel(backward, (pair_block,) * 2 + (shape((2, utts * frames, width...]
    ppermute x21, starting transfers between devices: 18.2 us -> 16.7 us  [crossed(): return lax.ppermute(array, 'ctx', [(i, i ^ apart) for i in range(N_CTX)])]
    ppermute x6 -> x7, starting transfers between devices: 11.1 us -> 12.1 us  [swapped(): return lax.ppermute(array, 'dp', [(i, i ^ bit) for i in range(N_DP)])]
  transfers between devices with their start and end apart: 27 -> 28, of which waited for: 13 -> 12; matrix products, arithmetic and copies ran while one was open for 1% -> 1% of each run, Pallas kernels for 24% -> 26%
where the time goes in v8:
time: 68.2 us; the launch traced here: 67.8 us
  starting transfers between devices  28.8 us (42%)
  Pallas kernels  20.2 us (30%)
  waiting for transfers between devices  17 us (25%)
  between operations  0.87 us (1%)
  local copies, waits for them, and re-layouts  0.78 us (1%)
    ppermute x21, starting transfers between devices, crossed(): return lax.ppermute(array, 'ctx', [(i, i ^ apart) for i in range(N_CTX)])  16.7 us
    ppermute x7, starting transfers between devices, swapped(): return lax.ppermute(array, 'dp', [(i, i ^ bit) for i in range(N_DP)])  12.1 us
    ppermute x7, waiting for transfers between devices, swapped(): return lax.ppermute(array, 'dp', [(i, i ^ bit) for i in range(N_DP)])  11.1 us
    ppermute x21, waiting for transfers between devices, crossed(): return lax.ppermute(array, 'ctx', [(i, i ^ apart) for i in range(N_CTX)])  5.87 us
    pallas_call x1, Pallas kernels, per_device(): call_kernel(backward, (pair_block,) * 2 + (shape((2, utts * frames, width...  3.58 us
    pallas_call x1, Pallas kernels, per_device(): call_kernel(forward, (channel_block,) * 2 + (shape((2, utts * frames, wid...  3.22 us
    pallas_call x1, Pallas kernels, per_device(): call_kernel(attend, (shape((N_CTX, frames, half), low),), ['smem'] + ['vm...  2.77 us
    pallas_call x1, Pallas kernels, per_device(): call_kernel(make_taps, (tap_block,) * 2, ['vmem'] * 2 + ['any'], scratch=...  2.08 us
  transfers between devices with their start and end apart: 28, of which 12 were waited for; matrix products, arithmetic and copies ran while one was open for 1% of the time, Pallas kernels for 26%

profile of v8, /device:TPU:0, one launch (start us, length us, event | category | flops | bytes accessed | tf_op | source)
XLA Modules:
  0.0 67.8 jit_solution(3891288280923673131)
XLA Ops:
  0.7 2.0 %shard_map.135 = (bf16[3,64,384]{2,1,0:T(8,128)(2,1)}, bf16[3,64,384]{2,1,0:T(8,128)(2,1)}, bf16[3,64,384]{2,1,0:T(8,128)(2,1)}, bf16[3,64,384]{2,1,0:T(8,128)(2,1)}) custom-call(bf16[2,64,768]{2,1,0:T(8,128)(2,1)} %query_ref.1, bf16[2,64,768]{2,1,0:T(8,128)(2,1)} %key_ref.1, bf16[2,64,768]{2,1,0:T(8,128)(2,1)} %value_ref.1), custom_call_target="tpu_custom_call" | custom-call | flops 1150000000 | tf_op jit(solution)/shard_map/pallas_call | solution.py:786
  3.2 2.6 %collective-permute-start.1 = (bf16[3,64,384]{2,1,0:T(8,128)(2,1)}, bf16[3,64,384]{2,1,0:T(8,128)(2,1)S(1)}, u32[]{:S(2)}, u32[]{:S(2)}) collective-permute-start(bf16[3,64,384]{2,1,0:T(8,128)(2,1)} %get-tuple-element.48), channel_id=1, source_target_pairs={{0,2},{1,3},{2,0},{3,1},{4,6},{5,7},{6,4},{7,5},{8,10},{9,11},{10,... | collective-permute-start | bytes 442376 | tf_op jit(solution)/shard_map/ppermute | solution.py:762
  5.9 2.8 %collective-permute-start.3 = (bf16[1,112,384]{2,1,0:T(8,128)(2,1)S(1)}, bf16[1,112,384]{2,1,0:T(8,128)(2,1)S(1)}, u32[]{:S(2)}, u32[]{:S(2)}) collective-permute-start(bf16[1,112,384]{2,1,0:T(8,128)(2,1)S(1)} %shard_map.136), channel_id=1, source_target_pairs={{0,16},{4,20},{8,24},{12,28},{16,0},{20,4},{24,8},{28,12},{1,17},{... | collective-permute-start | bytes 258056 | tf_op jit(solution)/shard_map/ppermute | solution.py:754
  8.8 1.9 %collective-permute-done.1.refs_2_.awaited_ref = bf16[3,64,384]{2,1,0:T(8,128)(2,1)S(1)} collective-permute-done((bf16[3,64,384]{2,1,0:T(8,128)(2,1)}, bf16[3,64,384]{2,1,0:T(8,128)(2,1)S(1)}, u32[]{:S(2)}, u32[]{:S(2)}) %collective-permute-start.1) | collective-permute-done | bytes 147488 | tf_op jit(solution)/shard_map/ppermute | solution.py:762
  11.0 2.0 %collective-permute-start.6 = (bf16[2,128,384]{2,1,0:T(8,128)(2,1)S(1)}, bf16[2,128,384]{2,1,0:T(8,128)(2,1)S(1)}, u32[]{:S(2)}, u32[]{:S(2)}) collective-permute-start(bf16[2,128,384]{2,1,0:T(8,128)(2,1)S(1)} %get-tuple-element.50), channel_id=1, source_target_pairs={{0,2},{1,3},{2,0},{3,1},{4,6},{5,7},{6,4},{7,5},{8,10},{9,11},{10,... | collective-permute-start | bytes 589832 | tf_op jit(solution)/shard_map/ppermute | solution.py:762
  14.7 2.8 %shard_map.137.refs_0_ = bf16[4,64,384]{2,1,0:T(8,128)(2,1)S(1)} custom-call(s32[2]{0:T(128)S(1)} %copy-done.4, bf16[3,64,384]{2,1,0:T(8,128)(2,1)S(1)} %copy-done.5, bf16[3,64,384]{2,1,0:T(8,128)(2,1)S(1)} %collective-permute-done.awaited_ref.refs_1_, bf16[3,64,384]{2,1,0:T(8,128)(2,1)S(1)} %collective-permute-done.1.refs_2_.awaited_ref, ...), custom_call_target="tpu_custom_call" | custom-call | flops 1150000000 | tf_op jit(solution)/shard_map/pallas_call | solution.py:816
  17.8 1.8 %collective-permute-start.8 = (bf16[4,64,384]{2,1,0:T(8,128)(2,1)S(1)}, bf16[4,64,384]{2,1,0:T(8,128)(2,1)S(1)}, u32[]{:S(2)}, u32[]{:S(2)}) collective-permute-start(bf16[4,64,384]{2,1,0:T(8,128)(2,1)S(1)} %shard_map.139.refs_0_), channel_id=1, source_target_pairs={{0,2},{1,3},{2,0},{3,1},{4,6},{5,7},{6,4},{7,5},{8,10},{9,11},{10,... | collective-permute-start | bytes 589832 | tf_op jit(solution)/shard_map/ppermute | solution.py:762
  19.8 1.4 %collective-permute-start.5 = (bf16[4,112,384]{2,1,0:T(8,128)(2,1)S(1)}, bf16[4,112,384]{2,1,0:T(8,128)(2,1)S(1)}, u32[]{:S(2)}, u32[]{:S(2)}) collective-permute-start(bf16[4,112,384]{2,1,0:T(8,128)(2,1)S(1)} %pad_maximum_fusion.near_ref), channel_id=1, source_target_pairs={{0,4},{4,0},{8,12},{12,8},{16,20},{20,16},{24,28},{28,24},{1,5},{5... | collective-permute-start | bytes 1032200 | tf_op jit(solution)/shard_map/ppermute | solution.py:754
  21.9 2.1 %collective-permute-done.8.refs_2_ = bf16[4,64,384]{2,1,0:T(8,128)(2,1)S(1)} collective-permute-done((bf16[4,64,384]{2,1,0:T(8,128)(2,1)S(1)}, bf16[4,64,384]{2,1,0:T(8,128)(2,1)S(1)}, u32[]{:S(2)}, u32[]{:S(2)}) %collective-permute-start.8) | collective-permute-done | bytes 196640 | tf_op jit(solution)/shard_map/ppermute | solution.py:762
  23.9 1.5 %collective-permute-start.11 = (bf16[128,384]{1,0:T(8,128)(2,1)S(1)}, bf16[128,384]{1,0:T(8,128)(2,1)S(1)}, u32[]{:S(2)}, u32[]{:S(2)}) collective-permute-start(bf16[128,384]{1,0:T(8,128)(2,1)S(1)} %get-tuple-element.58), channel_id=1, source_target_pairs={{0,2},{1,3},{2,0},{3,1},{4,6},{5,7},{6,4},{7,5},{8,10},{9,11},{10,... | collective-permute-start | bytes 294920 | tf_op jit(solution)/shard_map/ppermute | solution.py:762
  25.8 2.9 %collective-permute-done.5.other_ref = bf16[4,112,384]{2,1,0:T(8,128)(2,1)S(1)} collective-permute-done((bf16[4,112,384]{2,1,0:T(8,128)(2,1)S(1)}, bf16[4,112,384]{2,1,0:T(8,128)(2,1)S(1)}, u32[]{:S(2)}, u32[]{:S(2)}) %collective-permute-start.5) | collective-permute-done | bytes 344096 | tf_op jit(solution)/shard_map/ppermute | solution.py:754
  28.7 3.2 %shard_map.141 = (bf16[2,64,384]{2,1,0:T(8,128)(2,1)S(1)}, bf16[2,64,384]{2,1,0:T(8,128)(2,1)S(1)}, bf16[2,128,384]{2,1,0:T(8,128)(2,1)S(1)}, bf16[2,4,64,768]{3...) custom-call(s32[2]{0:T(128)S(1)} %copy-done.4, ...), custom_call_target="tpu_custom_call" | custom-call | flops 3680000000 | tf_op jit(solution)/shard_map/pallas_call | solution.py:826
  33.1 3.6 %shard_map.143 = (bf16[2,2,64,384]{3,2,1,0:T(8,128)(2,1)S(1)}, bf16[2,2,64,384]{3,2,1,0:T(8,128)(2,1)S(1)}, bf16[2,128,384]{2,1,0:T(8,128)(2,1)S(1)}, bf16[2,256...) custom-call(s32[2]{0:T(128)S(1)} %copy-done.4, ...), custom_call_target="tpu_custom_call" | custom-call | flops 5980000256 | tf_op jit(solution)/shard_map/pallas_call | solution.py:860
  38.4 1.3 %collective-permute-start.22 = (bf16[4,96,384]{2,1,0:T(8,128)(2,1)S(1)}, bf16[4,96,384]{2,1,0:T(8,128)(2,1)S(1)}, u32[]{:S(2)}, u32[]{:S(2)}) collective-permute-start(bf16[4,96,384]{2,1,0:T(8,128)(2,1)S(1)} %get-tuple-element.85), channel_id=1, source_target_pairs={{0,4},{4,0},{8,12},{12,8},{16,20},{20,16},{24,28},{28,24},{1,5},{5... | collective-permute-start | bytes 884744 | tf_op jit(solution)/shard_map/ppermute | solution.py:754
  39.7 1.5 %collective-permute-start.15 = (bf16[256,384]{1,0:T(8,128)(2,1)S(1)}, bf16[256,384]{1,0:T(8,128)(2,1)S(1)}, u32[]{:S(2)}, u32[]{:S(2)}) collective-permute-start(bf16[256,384]{1,0:T(8,128)(2,1)S(1)} %shard_map.145.refs_4_.awaited_ref.refs_1_), channel_id=1, source_target_pairs={{0,2},{1,3},{2,0},{3,1},{4,6},{5,7},{6,4},{7,5},{8,10},{9,11},{10,... | collective-permute-start | bytes 589832 | tf_op jit(solution)/shard_map/ppermute | solution.py:762
  41.2 2.1 %shard_map.147 = (f32[16,384]{1,0:T(8,128)S(1)}, f32[16,384]{1,0:T(8,128)S(1)}) custom-call(f32[6,288,128]{2,1,0:T(8,128)S(1)} %get-tuple-element.65.masked_ref, f32[6,288,128]{2,1,0:T(8,128)S(1)} %get-tuple-element.66.cotangent_ref, bf16[256,384]{1,0:T(8,128)(2,1)S(1)} %shard_map.145.refs_4_.awaited_ref.refs_1_), custom_call_target="tpu_custom_call" | custom-call | flops 1150000000 | tf_op jit(solution)/shard_map/pallas_call | solution.py:892
  46.2 2.2 %collective-permute-done.16.refs_4_.tap_came_ref = f32[16,384]{1,0:T(8,128)S(1)} collective-permute-done((f32[16,384]{1,0:T(8,128)S(1)}, f32[16,384]{1,0:T(8,128)S(1)}, u32[]{:S(2)}, u32[]{:S(2)}) %collective-permute-start.16) | collective-permute-done | bytes 24608 | tf_op jit(solution)/shard_map/ppermute | solution.py:754
  48.4 2.0 %shard_map.148 = (bf16[3,64,384]{2,1,0:T(8,128)(2,1)S(1)}, bf16[3,64,384]{2,1,0:T(8,128)(2,1)S(1)}, bf16[3,64,384]{2,1,0:T(8,128)(2,1)S(1)}, bf16[3,64,384]{2,1,0:T(8,128)(2,1)S(1)}) custom-call(bf16[6,256,256]{2,1,0:T(8,128)(2,1)S(1)} %shard_map.146.weight_ref, bf16[2,256,384]{2,1,0:T(8,128)(2,1)S(1)} %get-tuple-element.62.keep_ref, ...), custom_call_target="tpu_custom_call" | custom-call | flops 2529999872 | tf_op jit(solution)/shard_map/pallas_call | solution.py:905
  51.7 1.7 %collective-permute-start.19 = (bf16[3,64,384]{2,1,0:T(8,128)(2,1)S(1)}, bf16[3,64,384]{2,1,0:T(8,128)(2,1)S(1)}, u32[]{:S(2)}, u32[]{:S(2)}) collective-permute-start(bf16[3,64,384]{2,1,0:T(8,128)(2,1)S(1)} %shard_map.150), channel_id=1, source_target_pairs={{0,2},{1,3},{2,0},{3,1},{4,6},{5,7},{6,4},{7,5},{8,10},{9,11},{10,... | collective-permute-start | bytes 442376 | tf_op jit(solution)/shard_map/ppermute | solution.py:762
  53.9 2.7 %collective-permute-done.23 = bf16[2,112,384]{2,1,0:T(8,128)(2,1)S(1)} collective-permute-done((bf16[2,112,384]{2,1,0:T(8,128)(2,1)S(1)}, bf16[2,112,384]{2,1,0:T(8,128)(2,1)S(1)}, u32[]{:S(2)}, u32[]{:S(2)}) %collective-permute-start.23) | collective-permute-done | bytes 172064 | tf_op jit(solution)/shard_map/ppermute | solution.py:754
  56.6 3.4 %collective-permute-start.24 = (bf16[112,384]{1,0:T(8,128)(2,1)S(1)}, bf16[112,384]{1,0:T(8,128)(2,1)S(1)}, u32[]{:S(2)}, u32[]{:S(2)}) collective-permute-start(bf16[112,384]{1,0:T(8,128)(2,1)S(1)} %slice_bitcast_fusion.1), channel_id=1, source_target_pairs={{0,16},{4,20},{8,24},{12,28},{16,0},{20,4},{24,8},{28,12},{1,17},{... | collective-permute-start | bytes 258056 | tf_op jit(solution)/shard_map/ppermute | solution.py:754
  60.2 2.3 %collective-permute-done.24 = bf16[112,384]{1,0:T(8,128)(2,1)S(1)} collective-permute-done((bf16[112,384]{1,0:T(8,128)(2,1)S(1)}, bf16[112,384]{1,0:T(8,128)(2,1)S(1)}, u32[]{:S(2)}, u32[]{:S(2)}) %collective-permute-start.24) | collective-permute-done | bytes 86048 | tf_op jit(solution)/shard_map/ppermute | solution.py:754
  63.2 1.5 %collective-permute-start.26 = (f32[16,384]{1,0:T(8,128)S(1)}, f32[16,384]{1,0:T(8,128)S(1)}, u32[]{:S(2)}, u32[]{:S(2)}) collective-permute-start(f32[16,384]{1,0:T(8,128)S(1)} %shard_map.155.refs_0_), channel_id=1, source_target_pairs={{0,2},{1,3},{2,0},{3,1},{4,6},{5,7},{6,4},{7,5},{8,10},{9,11},{10,... | collective-permute-start | bytes 73736 | tf_op jit(solution)/shard_map/ppermute | solution.py:762
  65.1 1.4 %shard_map.152 = (bf16[2,64,768]{2,1,0:T(8,128)(2,1)}, bf16[2,64,768]{2,1,0:T(8,128)(2,1)}, bf16[2,64,768]{2,1,0:T(8,128)(2,1)}, bf16[2,64,1536]{2,1,0:T(8,128)(2,1)}, bf16[2,64,1536]{2,1,0:T(8,128)(2,1)}) custom-call(bf16[3,64,384]{2,1,0:T(8,128)(2,1)S(1)} %get-tuple-element.68.refs_0_.awaited_ref, ...), custom_call_target="tpu_custom_call" | custom-call | flops 1150000000 | tf_op jit(solution)/shard_map/pallas_call | solution.py:937
  (74 shorter events, 14.3 us)
Async XLA Ops:
  2.7 3.2 %collective-permute-start = (bf16[3,64,384]{2,1,0:T(8,128)(2,1)}, bf16[3,64,384]{2,1,0:T(8,128)(2,1)S(1)}, u32[]{:S(2)}, u32[]{:S(2)}) collective-permute-start(bf16[3,64,384]{2,1,0:T(8,128)(2,1)} %get-tuple-element.47), channel_id=1, source_target_pairs={{0,1},{1,0},{2,3},{3,2},{4,5},{5,4},{6,7},{7,6},{8,9},{9,8},{10,11... | collective-permute-start | bytes 442376 | tf_op jit(solution)/shard_map/ppermute | solution.py:762
  3.2 7.5 %collective-permute-start.1 = (bf16[3,64,384]{2,1,0:T(8,128)(2,1)}, bf16[3,64,384]{2,1,0:T(8,128)(2,1)S(1)}, u32[]{:S(2)}, u32[]{:S(2)}) collective-permute-start(bf16[3,64,384]{2,1,0:T(8,128)(2,1)} %get-tuple-element.48), channel_id=1, source_target_pairs={{0,2},{1,3},{2,0},{3,1},{4,6},{5,7},{6,4},{7,5},{8,10},{9,11},{10,... | collective-permute-start | bytes 442376 | tf_op jit(solution)/shard_map/ppermute | solution.py:762
  5.8 8.9 %collective-permute-start.2 = (bf16[3,64,384]{2,1,0:T(8,128)(2,1)}, bf16[3,64,384]{2,1,0:T(8,128)(2,1)S(1)}, u32[]{:S(2)}, u32[]{:S(2)}) collective-permute-start(bf16[3,64,384]{2,1,0:T(8,128)(2,1)} %get-tuple-element.49), channel_id=1, source_target_pairs={{0,3},{1,2},{2,1},{3,0},{4,7},{5,6},{6,5},{7,4},{8,11},{9,10},{10,... | collective-permute-start | bytes 442376 | tf_op jit(solution)/shard_map/ppermute | solution.py:762
  5.9 7.7 %collective-permute-start.3 = (bf16[1,112,384]{2,1,0:T(8,128)(2,1)S(1)}, bf16[1,112,384]{2,1,0:T(8,128)(2,1)S(1)}, u32[]{:S(2)}, u32[]{:S(2)}) collective-permute-start(bf16[1,112,384]{2,1,0:T(8,128)(2,1)S(1)} %shard_map.136), channel_id=1, source_target_pairs={{0,16},{4,20},{8,24},{12,28},{16,0},{20,4},{24,8},{28,12},{1,17},{... | collective-permute-start | bytes 258056 | tf_op jit(solution)/shard_map/ppermute | solution.py:754
  11.0 6.8 %collective-permute-start.6 = (bf16[2,128,384]{2,1,0:T(8,128)(2,1)S(1)}, bf16[2,128,384]{2,1,0:T(8,128)(2,1)S(1)}, u32[]{:S(2)}, u32[]{:S(2)}) collective-permute-start(bf16[2,128,384]{2,1,0:T(8,128)(2,1)S(1)} %get-tuple-element.50), channel_id=1, source_target_pairs={{0,2},{1,3},{2,0},{3,1},{4,6},{5,7},{6,4},{7,5},{8,10},{9,11},{10,... | collective-permute-start | bytes 589832 | tf_op jit(solution)/shard_map/ppermute | solution.py:762
  13.7 6.1 %collective-permute-start.4 = (bf16[2,112,384]{2,1,0:T(8,128)(2,1)S(1)}, bf16[2,112,384]{2,1,0:T(8,128)(2,1)S(1)}, u32[]{:S(2)}, u32[]{:S(2)}) collective-permute-start(bf16[2,112,384]{2,1,0:T(8,128)(2,1)S(1)} %pad_maximum_fusion.1), channel_id=1, source_target_pairs={{0,8},{4,12},{8,0},{12,4},{16,24},{20,28},{24,16},{28,20},{1,9},{5... | collective-permute-start | bytes 516104 | tf_op jit(solution)/shard_map/ppermute | solution.py:754
  17.8 6.2 %collective-permute-start.8 = (bf16[4,64,384]{2,1,0:T(8,128)(2,1)S(1)}, bf16[4,64,384]{2,1,0:T(8,128)(2,1)S(1)}, u32[]{:S(2)}, u32[]{:S(2)}) collective-permute-start(bf16[4,64,384]{2,1,0:T(8,128)(2,1)S(1)} %shard_map.139.refs_0_), channel_id=1, source_target_pairs={{0,2},{1,3},{2,0},{3,1},{4,6},{5,7},{6,4},{7,5},{8,10},{9,11},{10,... | collective-permute-start | bytes 589832 | tf_op jit(solution)/shard_map/ppermute | solution.py:762
  19.8 8.9 %collective-permute-start.5 = (bf16[4,112,384]{2,1,0:T(8,128)(2,1)S(1)}, bf16[4,112,384]{2,1,0:T(8,128)(2,1)S(1)}, u32[]{:S(2)}, u32[]{:S(2)}) collective-permute-start(bf16[4,112,384]{2,1,0:T(8,128)(2,1)S(1)} %pad_maximum_fusion.near_ref), channel_id=1, source_target_pairs={{0,4},{4,0},{8,12},{12,8},{16,20},{20,16},{24,28},{28,24},{1,5},{5... | collective-permute-start | bytes 1032200 | tf_op jit(solution)/shard_map/ppermute | solution.py:754
  21.3 4.5 %collective-permute-start.10 = (bf16[3,128,384]{2,1,0:T(8,128)(2,1)S(1)}, bf16[3,128,384]{2,1,0:T(8,128)(2,1)S(1)}, u32[]{:S(2)}, u32[]{:S(2)}) collective-permute-start(bf16[3,128,384]{2,1,0:T(8,128)(2,1)S(1)} %shard_map.140), channel_id=1, source_target_pairs={{0,1},{1,0},{2,3},{3,2},{4,5},{5,4},{6,7},{7,6},{8,9},{9,8},{10,11... | collective-permute-start | bytes 884744 | tf_op jit(solution)/shard_map/ppermute | solution.py:762
  21.4 4.1 %collective-permute-start.7 = (bf16[4,64,384]{2,1,0:T(8,128)(2,1)S(1)}, bf16[4,64,384]{2,1,0:T(8,128)(2,1)S(1)}, u32[]{:S(2)}, u32[]{:S(2)}) collective-permute-start(bf16[4,64,384]{2,1,0:T(8,128)(2,1)S(1)} %shard_map.139.refs_0_), channel_id=1, source_target_pairs={{0,1},{1,0},{2,3},{3,2},{4,5},{5,4},{6,7},{7,6},{8,9},{9,8},{10,11... | collective-permute-start | bytes 589832 | tf_op jit(solution)/shard_map/ppermute | solution.py:762
  23.9 9.2 %collective-permute-start.11 = (bf16[128,384]{1,0:T(8,128)(2,1)S(1)}, bf16[128,384]{1,0:T(8,128)(2,1)S(1)}, u32[]{:S(2)}, u32[]{:S(2)}) collective-permute-start(bf16[128,384]{1,0:T(8,128)(2,1)S(1)} %get-tuple-element.58), channel_id=1, source_target_pairs={{0,2},{1,3},{2,0},{3,1},{4,6},{5,7},{6,4},{7,5},{8,10},{9,11},{10,... | collective-permute-start | bytes 294920 | tf_op jit(solution)/shard_map/ppermute | solution.py:762
  25.4 7.7 %collective-permute-start.12 = (bf16[128,384]{1,0:T(8,128)(2,1)S(1)}, bf16[128,384]{1,0:T(8,128)(2,1)S(1)}, u32[]{:S(2)}, u32[]{:S(2)}) collective-permute-start(bf16[128,384]{1,0:T(8,128)(2,1)S(1)} %get-tuple-element.59), channel_id=1, source_target_pairs={{0,3},{1,2},{2,1},{3,0},{4,7},{5,6},{6,5},{7,4},{8,11},{9,10},{10,... | collective-permute-start | bytes 294920 | tf_op jit(solution)/shard_map/ppermute | solution.py:762
  32.0 5.7 %collective-permute-start.13 = (bf16[2,128,384]{2,1,0:T(8,128)(2,1)S(1)}, bf16[2,128,384]{2,1,0:T(8,128)(2,1)S(1)}, u32[]{:S(2)}, u32[]{:S(2)}) collective-permute-start(bf16[2,128,384]{2,1,0:T(8,128)(2,1)S(1)} %get-tuple-element.64), channel_id=1, source_target_pairs={{0,2},{1,3},{2,0},{3,1},{4,6},{5,7},{6,4},{7,5},{8,10},{9,11},{10,... | collective-permute-start | bytes 589832 | tf_op jit(solution)/shard_map/ppermute | solution.py:762
  38.4 12.0 %collective-permute-start.22 = (bf16[4,96,384]{2,1,0:T(8,128)(2,1)S(1)}, bf16[4,96,384]{2,1,0:T(8,128)(2,1)S(1)}, u32[]{:S(2)}, u32[]{:S(2)}) collective-permute-start(bf16[4,96,384]{2,1,0:T(8,128)(2,1)S(1)} %get-tuple-element.85), channel_id=1, source_target_pairs={{0,4},{4,0},{8,12},{12,8},{16,20},{20,16},{24,28},{28,24},{1,5},{5... | collective-permute-start | bytes 884744 | tf_op jit(solution)/shard_map/ppermute | solution.py:754
  39.7 8.7 %collective-permute-start.15 = (bf16[256,384]{1,0:T(8,128)(2,1)S(1)}, bf16[256,384]{1,0:T(8,128)(2,1)S(1)}, u32[]{:S(2)}, u32[]{:S(2)}) collective-permute-start(bf16[256,384]{1,0:T(8,128)(2,1)S(1)} %shard_map.145.refs_4_.awaited_ref.refs_1_), channel_id=1, source_target_pairs={{0,2},{1,3},{2,0},{3,1},{4,6},{5,7},{6,4},{7,5},{8,10},{9,11},{10,... | collective-permute-start | bytes 589832 | tf_op jit(solution)/shard_map/ppermute | solution.py:762
  43.3 5.1 %collective-permute-start.16 = (f32[16,384]{1,0:T(8,128)S(1)}, f32[16,384]{1,0:T(8,128)S(1)}, u32[]{:S(2)}, u32[]{:S(2)}) collective-permute-start(f32[16,384]{1,0:T(8,128)S(1)} %get-tuple-element.67), channel_id=1, source_target_pairs={{0,4},{4,0},{8,12},{12,8},{16,20},{20,16},{24,28},{28,24},{1,5},{5... | collective-permute-start | bytes 73736 | tf_op jit(solution)/shard_map/ppermute | solution.py:754
  44.3 7.4 %collective-permute-start.18 = (bf16[2,128,384]{2,1,0:T(8,128)(2,1)S(1)}, bf16[2,128,384]{2,1,0:T(8,128)(2,1)S(1)}, u32[]{:S(2)}, u32[]{:S(2)}) collective-permute-start(bf16[2,128,384]{2,1,0:T(8,128)(2,1)S(1)} %shard_map.149), channel_id=1, source_target_pairs={{0,2},{1,3},{2,0},{3,1},{4,6},{5,7},{6,4},{7,5},{8,10},{9,11},{10,... | collective-permute-start | bytes 589832 | tf_op jit(solution)/shard_map/ppermute | solution.py:762
  50.5 6.1 %collective-permute-start.23 = (bf16[2,112,384]{2,1,0:T(8,128)(2,1)S(1)}, bf16[2,112,384]{2,1,0:T(8,128)(2,1)S(1)}, u32[]{:S(2)}, u32[]{:S(2)}) collective-permute-start(bf16[2,112,384]{2,1,0:T(8,128)(2,1)S(1)} %get-tuple-element.84), channel_id=1, source_target_pairs={{0,8},{4,12},{8,0},{12,4},{16,24},{20,28},{24,16},{28,20},{1,9},{5... | collective-permute-start | bytes 516104 | tf_op jit(solution)/shard_map/ppermute | solution.py:754
  51.7 8.3 %collective-permute-start.19 = (bf16[3,64,384]{2,1,0:T(8,128)(2,1)S(1)}, bf16[3,64,384]{2,1,0:T(8,128)(2,1)S(1)}, u32[]{:S(2)}, u32[]{:S(2)}) collective-permute-start(bf16[3,64,384]{2,1,0:T(8,128)(2,1)S(1)} %shard_map.150), channel_id=1, source_target_pairs={{0,2},{1,3},{2,0},{3,1},{4,6},{5,7},{6,4},{7,5},{8,10},{9,11},{10,... | collective-permute-start | bytes 442376 | tf_op jit(solution)/shard_map/ppermute | solution.py:762
  53.4 6.6 %collective-permute-start.17 = (bf16[3,64,384]{2,1,0:T(8,128)(2,1)S(1)}, bf16[3,64,384]{2,1,0:T(8,128)(2,1)S(1)}, u32[]{:S(2)}, u32[]{:S(2)}) collective-permute-start(bf16[3,64,384]{2,1,0:T(8,128)(2,1)S(1)} %get-tuple-element.69), channel_id=1, source_target_pairs={{0,1},{1,0},{2,3},{3,2},{4,5},{5,4},{6,7},{7,6},{8,9},{9,8},{10,11... | collective-permute-start | bytes 442376 | tf_op jit(solution)/shard_map/ppermute | solution.py:762
  53.4 6.6 %collective-permute-start.20 = (bf16[3,64,384]{2,1,0:T(8,128)(2,1)S(1)}, bf16[3,64,384]{2,1,0:T(8,128)(2,1)S(1)}, u32[]{:S(2)}, u32[]{:S(2)}) collective-permute-start(bf16[3,64,384]{2,1,0:T(8,128)(2,1)S(1)} %get-tuple-element.72), channel_id=1, source_target_pairs={{0,3},{1,2},{2,1},{3,0},{4,7},{5,6},{6,5},{7,4},{8,11},{9,10},{10,... | collective-permute-start | bytes 442376 | tf_op jit(solution)/shard_map/ppermute | solution.py:762
  56.6 5.9 %collective-permute-start.24 = (bf16[112,384]{1,0:T(8,128)(2,1)S(1)}, bf16[112,384]{1,0:T(8,128)(2,1)S(1)}, u32[]{:S(2)}, u32[]{:S(2)}) collective-permute-start(bf16[112,384]{1,0:T(8,128)(2,1)S(1)} %slice_bitcast_fusion.1), channel_id=1, source_target_pairs={{0,16},{4,20},{8,24},{12,28},{16,0},{20,4},{24,8},{28,12},{1,17},{... | collective-permute-start | bytes 258056 | tf_op jit(solution)/shard_map/ppermute | solution.py:754
  63.2 3.5 %collective-permute-start.27 = (f32[16,384]{1,0:T(8,128)S(1)}, f32[16,384]{1,0:T(8,128)S(1)}, u32[]{:S(2)}, u32[]{:S(2)}) collective-permute-start(f32[16,384]{1,0:T(8,128)S(1)} %shard_map.155.refs_0_), channel_id=1, source_target_pairs={{0,3},{1,2},{2,1},{3,0},{4,7},{5,6},{6,5},{7,4},{8,11},{9,10},{10,... | collective-permute-start | bytes 73736 | tf_op jit(solution)/shard_map/ppermute | solution.py:762
  63.2 3.9 %collective-permute-start.26 = (f32[16,384]{1,0:T(8,128)S(1)}, f32[16,384]{1,0:T(8,128)S(1)}, u32[]{:S(2)}, u32[]{:S(2)}) collective-permute-start(f32[16,384]{1,0:T(8,128)S(1)} %shard_map.155.refs_0_), channel_id=1, source_target_pairs={{0,2},{1,3},{2,0},{3,1},{4,6},{5,7},{6,4},{7,5},{8,10},{9,11},{10,... | collective-permute-start | bytes 73736 | tf_op jit(solution)/shard_map/ppermute | solution.py:762
  (10 other events, 34.1 us)

commit v9 on v8

--- a/solution.py
+++ b/solution.py
@@ -376,6 +376,19 @@
     out_ref[0, entries:] = joined.astype(jnp.bfloat16)
 
 
+def pack_near(held_ref, came_ref, out_ref):
+    entries = held_ref.shape[1] - TAP_PAD // 2
+    for slot in range(2):
+        for half, ref in enumerate((held_ref, came_ref)):
+            first = (2 * half + slot) * entries
+            out_ref[first : first + entries, :] = ref[slot, 0:entries]
+    apart = lax.axis_index("ctx") ^ half_of(lax.axis_index("dp"))
+    slot = half_of(apart)
+    taps = [ref[slot, entries:].astype(jnp.float32) for ref in (held_ref, came_ref)]
+    taps = jnp.where((apart & 1) == 1, taps[1], taps[0])
+    out_ref[4 * entries :, :] = taps.astype(jnp.bfloat16)
+
+
 def pack_channels(frame_ref, grad_ref, awaited_ref, *rest):
     across_ref, grad_outs, beside_ref, own_ref, sem = rest[0], rest[1:3], *rest[3:]
     width = frame_ref.shape[2] // N_CTX
@@ -504,11 +517,9 @@
     for slot, apart in enumerate((0, 4, 2, 6)):
         for odd, ref in enumerate((near_ref, other_ref)):
             first = pl.multiple_of((group ^ (apart + odd)) * entries, entries)
-            rows_ref[pl.ds(first, entries)] = ref[slot, 0:entries]
-    apart = place ^ half_of(group)
-    slot = ((apart & 1) << 1) | half_of(apart)
+            rows_ref[pl.ds(first, entries)] = ref[slot * entries : (slot + 1) * entries]
     odd = (group & 1) == 1
-    blocks = [ref[slot, entries:].astype(jnp.float32) for ref in (near_ref, other_ref)]
+    blocks = [ref[4 * entries :].astype(jnp.float32) for ref in (near_ref, other_ref)]
     blocks = (jnp.where(odd, blocks[1], blocks[0]), jnp.where(odd, blocks[0], blocks[1]))
     pieces = [jnp.concatenate([block[:, :own], block[:, own:]], axis=0) for block in blocks]
     taps = jnp.concatenate(pieces, axis=1)
@@ -695,8 +706,19 @@
             ref[slot % 2, entries:] = taps
 
 
+def mark(*refs):
+    refs[-1][...] = jnp.zeros_like(refs[-1])
+
+
+def finish(kept_ref, came_ref, awaited_ref, panel_ref, taps_ref):
+    entries = panel_ref.shape[0]
+    total = kept_ref[0].astype(jnp.float32) + came_ref[...].astype(jnp.float32)
+    panel_ref[...] = total[:entries]
+    taps_ref[...] = total[entries:]
+
+
 def pick_taps(*refs):
-    ins, held_ref, out_ref = refs[:N_CTX], refs[N_CTX + 1], refs[N_CTX]
+    ins, out_ref, held_ref = refs[:N_CTX], refs[N_CTX + 1], refs[N_CTX + 2]
     own = ins[0].shape[1] // 2
     for apart in range(N_CTX):
         held_ref[apart] = ins[apart][...]
@@ -796,8 +818,10 @@
         (shape((1, entries + TAP_PAD // 2, width), low),),
         ["vmem"] * 2 + ["any"],
     )(out_weight.T, conv_weight, packed[1])
-    for bit in (4, 2):
-        shard = jnp.concatenate([shard, swapped(shard, bit)], axis=0)
+    shard = jnp.concatenate([shard, swapped(shard, 4)], axis=0)
+    (shard,) = call_kernel(
+        pack_near, (shape((4 * entries + TAP_PAD // 2, width), low),), ["vmem"] * 2
+    )(shard, swapped(shard, 2))
     other_shard = swapped(shard, 1)
     pair_block = shape((2, utts, frames, width), low)
     side_block = shape((utts * frames, width), low)
@@ -914,9 +938,9 @@
     (beside_pair,) = call_kernel(
         make_pair,
         (shape((4, utts * frames, width), low),),
-        ["vmem"] * 3 + ["any"] * 3,
+        ["vmem"] * 3 + ["any"],
         micros=0.2,
-    )(backward_out[1], output_across, input_across, *grad_blocks[1:])
+    )(backward_out[1], output_across, input_across, grad_blocks[1])
     beside_pair = crossed(beside_pair, 1)
 
     kept, sent = call_kernel(
@@ -925,15 +949,13 @@
         ["vmem"] * 4 + ["any"],
     )(panels[:4], panels_came, tap_keep, taps_came, back_blocks[0])
     panels = (kept.astype(f32) + swapped(sent, 2).astype(f32)).astype(low)
-    total = panels[0].astype(f32) + swapped(panels[1], 4).astype(f32)
-    grad_out_weight = total[:entries].T
-    (tap_sums,) = gate([total[entries:]], beside_pair)
-    (grad_taps,) = call_kernel(
-        pick_taps,
-        (shape(conv_weight.shape, f32),),
-        ["vmem"] * N_CTX,
-        scratch=[pltpu.VMEM((N_CTX, TAP_PAD // 2, width), f32)],
-    )(*traded([tap_sums] * N_CTX))
+    (arrived,) = call_kernel(mark, (shape((8, LANES), f32),), ["any"] * 2)(*grad_blocks[2:])
+    panel_total, tap_sums = call_kernel(
+        finish,
+        (shape((entries, width), f32), shape((TAP_PAD // 2, width), f32)),
+        ["vmem"] * 2 + ["any"],
+    )(panels, swapped(panels[1], 4), arrived)
+    grad_out_weight = panel_total.T
     unpacked = call_kernel(
         unpack,
         (shape((utts, frames, inner), low),) * 3 + (shape((utts, frames, wide), low),) * 2,
@@ -948,6 +970,12 @@
         output_across,
         input_across,
     )
+    (grad_taps,) = call_kernel(
+        pick_taps,
+        (shape(conv_weight.shape, f32),),
+        ["vmem"] * N_CTX + ["any"],
+        scratch=[pltpu.VMEM((N_CTX, TAP_PAD // 2, width), f32)],
+    )(*traded([tap_sums] * N_CTX), unpacked[0])
     grad_queries, grad_keys, grad_values, block_output, grad_input = unpacked
     return (
         block_output,

time: 68.2 us -> 68.3 us (level)
  waiting for transfers between devices: 17 us -> 16.2 us
  Pallas kernels: 20.2 us -> 20.9 us
    ppermute x7, waiting for transfers between devices: 11.1 us -> 9.65 us  [swapped(): return lax.ppermute(array, 'dp', [(i, i ^ bit) for i in range(N_DP)])]
    unnamed x12 -> x14, local copies, waits for them, and re-layouts: 0.03 us -> 0.96 us
    ppermute x21, waiting for transfers between devices: 5.87 us -> 6.59 us  [crossed(): return lax.ppermute(array, 'ctx', [(i, i ^ apart) for i in range(N_CTX)])]
    pallas_call x0 -> x3, Pallas kernels: none -> 0.71 us  [the longest x1 0.68 us: per_device(): call_kernel(finish, (shape((entries, width), f32), shape((TAP_PAD // 2, w...]
  transfers between devices with their start and end apart: 28 -> 28, of which waited for: 12 -> 13; matrix products, arithmetic and copies ran while one was open for 1% -> 0% of each run, Pallas kernels for 26% -> 27%
where the time goes in v9:
time: 68.3 us; the launch traced here: 67.9 us
  starting transfers between devices  28.8 us (42%)
  Pallas kernels  20.9 us (31%)
  waiting for transfers between devices  16.2 us (24%)
  local copies, waits for them, and re-layouts  1.03 us (2%)
  between operations  0.85 us (1%)
    ppermute x21, starting transfers between devices, crossed(): return lax.ppermute(array, 'ctx', [(i, i ^ apart) for i in range(N_CTX)])  16.7 us
    ppermute x7, starting transfers between devices, swapped(): return lax.ppermute(array, 'dp', [(i, i ^ bit) for i in range(N_DP)])  12.1 us
    ppermute x7, waiting for transfers between devices, swapped(): return lax.ppermute(array, 'dp', [(i, i ^ bit) for i in range(N_DP)])  9.65 us
    ppermute x21, waiting for transfers between devices, crossed(): return lax.ppermute(array, 'ctx', [(i, i ^ apart) for i in range(N_CTX)])  6.59 us
    pallas_call x1, Pallas kernels, per_device(): call_kernel(backward, (pair_block,) * 2 + (shape((2, utts * frames, width...  3.58 us
    pallas_call x1, Pallas kernels, per_device(): call_kernel(forward, (channel_block,) * 2 + (shape((2, utts * frames, wid...  3.22 us
    pallas_call x1, Pallas kernels, per_device(): call_kernel(attend, (shape((N_CTX, frames, half), low),), ['smem'] + ['vm...  2.77 us
    pallas_call x1, Pallas kernels, per_device(): call_kernel(make_taps, (tap_block,) * 2, ['vmem'] * 2 + ['any'], scratch=...  2.08 us
  transfers between devices with their start and end apart: 28, of which 13 were waited for; matrix products, arithmetic and copies ran while one was open for 0% of the time, Pallas kernels for 27%

profile of v9, /device:TPU:0, one launch (start us, length us, event | category | flops | bytes accessed | tf_op | source)
XLA Modules:
  0.0 67.9 jit_solution(12627557411209470773)
XLA Ops:
  0.7 2.0 %shard_map.135 = (bf16[3,64,384]{2,1,0:T(8,128)(2,1)}, bf16[3,64,384]{2,1,0:T(8,128)(2,1)}, bf16[3,64,384]{2,1,0:T(8,128)(2,1)}, bf16[3,64,384]{2,1,0:T(8,128)(2,1)}) custom-call(bf16[2,64,768]{2,1,0:T(8,128)(2,1)} %query_ref.1, bf16[2,64,768]{2,1,0:T(8,128)(2,1)} %key_ref.1, bf16[2,64,768]{2,1,0:T(8,128)(2,1)} %value_ref.1), custom_call_target="tpu_custom_call" | custom-call | flops 1150000000 | tf_op jit(solution)/shard_map/pallas_call | solution.py:808
  3.2 2.6 %collective-permute-start.1 = (bf16[3,64,384]{2,1,0:T(8,128)(2,1)}, bf16[3,64,384]{2,1,0:T(8,128)(2,1)S(1)}, u32[]{:S(2)}, u32[]{:S(2)}) collective-permute-start(bf16[3,64,384]{2,1,0:T(8,128)(2,1)} %get-tuple-element.50), channel_id=1, source_target_pairs={{0,2},{1,3},{2,0},{3,1},{4,6},{5,7},{6,4},{7,5},{8,10},{9,11},{10,... | collective-permute-start | bytes 442376 | tf_op jit(solution)/shard_map/ppermute | solution.py:784
  5.9 2.8 %collective-permute-start.3 = (bf16[1,112,384]{2,1,0:T(8,128)(2,1)S(1)}, bf16[1,112,384]{2,1,0:T(8,128)(2,1)S(1)}, u32[]{:S(2)}, u32[]{:S(2)}) collective-permute-start(bf16[1,112,384]{2,1,0:T(8,128)(2,1)S(1)} %shard_map.136), channel_id=1, source_target_pairs={{0,16},{4,20},{8,24},{12,28},{16,0},{20,4},{24,8},{28,12},{1,17},{... | collective-permute-start | bytes 258056 | tf_op jit(solution)/shard_map/ppermute | solution.py:776
  8.8 1.9 %collective-permute-done.1.refs_2_.awaited_ref = bf16[3,64,384]{2,1,0:T(8,128)(2,1)S(1)} collective-permute-done((bf16[3,64,384]{2,1,0:T(8,128)(2,1)}, bf16[3,64,384]{2,1,0:T(8,128)(2,1)S(1)}, u32[]{:S(2)}, u32[]{:S(2)}) %collective-permute-start.1) | collective-permute-done | bytes 147488 | tf_op jit(solution)/shard_map/ppermute | solution.py:784
  11.0 2.0 %collective-permute-start.6 = (bf16[2,128,384]{2,1,0:T(8,128)(2,1)S(1)}, bf16[2,128,384]{2,1,0:T(8,128)(2,1)S(1)}, u32[]{:S(2)}, u32[]{:S(2)}) collective-permute-start(bf16[2,128,384]{2,1,0:T(8,128)(2,1)S(1)} %get-tuple-element.52), channel_id=1, source_target_pairs={{0,2},{1,3},{2,0},{3,1},{4,6},{5,7},{6,4},{7,5},{8,10},{9,11},{10,... | collective-permute-start | bytes 589832 | tf_op jit(solution)/shard_map/ppermute | solution.py:784
  14.7 2.8 %shard_map.138.refs_0_ = bf16[4,64,384]{2,1,0:T(8,128)(2,1)S(1)} custom-call(s32[2]{0:T(128)S(1)} %copy-done.4, bf16[3,64,384]{2,1,0:T(8,128)(2,1)S(1)} %copy-done.6, bf16[3,64,384]{2,1,0:T(8,128)(2,1)S(1)} %collective-permute-done.awaited_ref.refs_1_, bf16[3,64,384]{2,1,0:T(8,128)(2,1)S(1)} %collective-permute-done.1.refs_2_.awaited_ref, ...), custom_call_target="tpu_custom_call" | custom-call | flops 1150000000 | tf_op jit(solution)/shard_map/pallas_call | solution.py:840
  17.8 1.8 %collective-permute-start.8 = (bf16[4,64,384]{2,1,0:T(8,128)(2,1)S(1)}, bf16[4,64,384]{2,1,0:T(8,128)(2,1)S(1)}, u32[]{:S(2)}, u32[]{:S(2)}) collective-permute-start(bf16[4,64,384]{2,1,0:T(8,128)(2,1)S(1)} %shard_map.140.refs_0_), channel_id=1, source_target_pairs={{0,2},{1,3},{2,0},{3,1},{4,6},{5,7},{6,4},{7,5},{8,10},{9,11},{10,... | collective-permute-start | bytes 589832 | tf_op jit(solution)/shard_map/ppermute | solution.py:784
  19.8 1.4 %collective-permute-start.5 = (bf16[400,384]{1,0:T(8,128)(2,1)S(1)}, bf16[400,384]{1,0:T(8,128)(2,1)S(1)}, u32[]{:S(2)}, u32[]{:S(2)}) collective-permute-start(bf16[400,384]{1,0:T(8,128)(2,1)S(1)} %shard_map.137.near_ref), channel_id=1, source_target_pairs={{0,4},{4,0},{8,12},{12,8},{16,20},{20,16},{24,28},{28,24},{1,5},{5... | collective-permute-start | bytes 921608 | tf_op jit(solution)/shard_map/ppermute | solution.py:776
  21.9 2.1 %collective-permute-done.8.refs_2_ = bf16[4,64,384]{2,1,0:T(8,128)(2,1)S(1)} collective-permute-done((bf16[4,64,384]{2,1,0:T(8,128)(2,1)S(1)}, bf16[4,64,384]{2,1,0:T(8,128)(2,1)S(1)}, u32[]{:S(2)}, u32[]{:S(2)}) %collective-permute-start.8) | collective-permute-done | bytes 196640 | tf_op jit(solution)/shard_map/ppermute | solution.py:784
  23.9 1.5 %collective-permute-start.11 = (bf16[128,384]{1,0:T(8,128)(2,1)S(1)}, bf16[128,384]{1,0:T(8,128)(2,1)S(1)}, u32[]{:S(2)}, u32[]{:S(2)}) collective-permute-start(bf16[128,384]{1,0:T(8,128)(2,1)S(1)} %get-tuple-element.60), channel_id=1, source_target_pairs={{0,2},{1,3},{2,0},{3,1},{4,6},{5,7},{6,4},{7,5},{8,10},{9,11},{10,... | collective-permute-start | bytes 294920 | tf_op jit(solution)/shard_map/ppermute | solution.py:784
  25.8 2.1 %collective-permute-done.5.other_ref = bf16[400,384]{1,0:T(8,128)(2,1)S(1)} collective-permute-done((bf16[400,384]{1,0:T(8,128)(2,1)S(1)}, bf16[400,384]{1,0:T(8,128)(2,1)S(1)}, u32[]{:S(2)}, u32[]{:S(2)}) %collective-permute-start.5) | collective-permute-done | bytes 307232 | tf_op jit(solution)/shard_map/ppermute | solution.py:776
  27.9 3.2 %shard_map.142 = (bf16[2,64,384]{2,1,0:T(8,128)(2,1)S(1)}, bf16[2,64,384]{2,1,0:T(8,128)(2,1)S(1)}, bf16[2,128,384]{2,1,0:T(8,128)(2,1)S(1)}, bf16[2,4,64,768]{3...) custom-call(s32[2]{0:T(128)S(1)} %copy-done.4, ...), custom_call_target="tpu_custom_call" | custom-call | flops 3680000000 | tf_op jit(solution)/shard_map/pallas_call | solution.py:850
  32.3 3.6 %shard_map.144 = (bf16[2,2,64,384]{3,2,1,0:T(8,128)(2,1)S(1)}, bf16[2,2,64,384]{3,2,1,0:T(8,128)(2,1)S(1)}, bf16[2,128,384]{2,1,0:T(8,128)(2,1)S(1)}, bf16[2,256...) custom-call(s32[2]{0:T(128)S(1)} %copy-done.4, ...), custom_call_target="tpu_custom_call" | custom-call | flops 5980000256 | tf_op jit(solution)/shard_map/pallas_call | solution.py:884
  37.6 1.3 %collective-permute-start.22 = (bf16[4,96,384]{2,1,0:T(8,128)(2,1)S(1)}, bf16[4,96,384]{2,1,0:T(8,128)(2,1)S(1)}, u32[]{:S(2)}, u32[]{:S(2)}) collective-permute-start(bf16[4,96,384]{2,1,0:T(8,128)(2,1)S(1)} %get-tuple-element.89), channel_id=1, source_target_pairs={{0,4},{4,0},{8,12},{12,8},{16,20},{20,16},{24,28},{28,24},{1,5},{5... | collective-permute-start | bytes 884744 | tf_op jit(solution)/shard_map/ppermute | solution.py:776
  38.9 1.5 %collective-permute-start.15 = (bf16[256,384]{1,0:T(8,128)(2,1)S(1)}, bf16[256,384]{1,0:T(8,128)(2,1)S(1)}, u32[]{:S(2)}, u32[]{:S(2)}) collective-permute-start(bf16[256,384]{1,0:T(8,128)(2,1)S(1)} %shard_map.146.refs_4_.awaited_ref.refs_1_), channel_id=1, source_target_pairs={{0,2},{1,3},{2,0},{3,1},{4,6},{5,7},{6,4},{7,5},{8,10},{9,11},{10,... | collective-permute-start | bytes 589832 | tf_op jit(solution)/shard_map/ppermute | solution.py:784
  40.4 2.1 %shard_map.148 = (f32[16,384]{1,0:T(8,128)S(1)}, f32[16,384]{1,0:T(8,128)S(1)}) custom-call(f32[6,288,128]{2,1,0:T(8,128)S(1)} %get-tuple-element.67.masked_ref, f32[6,288,128]{2,1,0:T(8,128)S(1)} %get-tuple-element.68.cotangent_ref, bf16[256,384]{1,0:T(8,128)(2,1)S(1)} %shard_map.146.refs_4_.awaited_ref.refs_1_), custom_call_target="tpu_custom_call" | custom-call | flops 1150000000 | tf_op jit(solution)/shard_map/pallas_call | solution.py:916
  45.4 2.2 %collective-permute-done.16.refs_4_.tap_came_ref = f32[16,384]{1,0:T(8,128)S(1)} collective-permute-done((f32[16,384]{1,0:T(8,128)S(1)}, f32[16,384]{1,0:T(8,128)S(1)}, u32[]{:S(2)}, u32[]{:S(2)}) %collective-permute-start.16) | collective-permute-done | bytes 24608 | tf_op jit(solution)/shard_map/ppermute | solution.py:776
  47.6 2.0 %shard_map.149 = (bf16[3,64,384]{2,1,0:T(8,128)(2,1)S(1)}, bf16[3,64,384]{2,1,0:T(8,128)(2,1)S(1)}, bf16[3,64,384]{2,1,0:T(8,128)(2,1)S(1)}, bf16[3,64,384]{2,1,0:T(8,128)(2,1)S(1)}) custom-call(bf16[6,256,256]{2,1,0:T(8,128)(2,1)S(1)} %shard_map.147.weight_ref, bf16[2,256,384]{2,1,0:T(8,128)(2,1)S(1)} %get-tuple-element.64.keep_ref, ...), custom_call_target="tpu_custom_call" | custom-call | flops 2529999872 | tf_op jit(solution)/shard_map/pallas_call | solution.py:929
  50.9 1.7 %collective-permute-start.19 = (bf16[3,64,384]{2,1,0:T(8,128)(2,1)S(1)}, bf16[3,64,384]{2,1,0:T(8,128)(2,1)S(1)}, u32[]{:S(2)}, u32[]{:S(2)}) collective-permute-start(bf16[3,64,384]{2,1,0:T(8,128)(2,1)S(1)} %shard_map.151), channel_id=1, source_target_pairs={{0,2},{1,3},{2,0},{3,1},{4,6},{5,7},{6,4},{7,5},{8,10},{9,11},{10,... | collective-permute-start | bytes 442376 | tf_op jit(solution)/shard_map/ppermute | solution.py:784
  53.2 2.6 %collective-permute-done.23 = bf16[2,112,384]{2,1,0:T(8,128)(2,1)S(1)} collective-permute-done((bf16[2,112,384]{2,1,0:T(8,128)(2,1)S(1)}, bf16[2,112,384]{2,1,0:T(8,128)(2,1)S(1)}, u32[]{:S(2)}, u32[]{:S(2)}) %collective-permute-start.23) | collective-permute-done | bytes 172064 | tf_op jit(solution)/shard_map/ppermute | solution.py:776
  55.8 3.4 %collective-permute-start.24 = (bf16[112,384]{1,0:T(8,128)(2,1)S(1)}, bf16[112,384]{1,0:T(8,128)(2,1)S(1)}, u32[]{:S(2)}, u32[]{:S(2)}) collective-permute-start(bf16[112,384]{1,0:T(8,128)(2,1)S(1)} %slice_bitcast_fusion), channel_id=1, source_target_pairs={{0,16},{4,20},{8,24},{12,28},{16,0},{20,4},{24,8},{28,12},{1,17},{... | collective-permute-start | bytes 258056 | tf_op jit(solution)/shard_map/ppermute | solution.py:776
  60.0 1.8 %collective-permute-done.24.came_ref = bf16[112,384]{1,0:T(8,128)(2,1)S(1)} collective-permute-done((bf16[112,384]{1,0:T(8,128)(2,1)S(1)}, bf16[112,384]{1,0:T(8,128)(2,1)S(1)}, u32[]{:S(2)}, u32[]{:S(2)}) %collective-permute-start.24) | collective-permute-done | bytes 86048 | tf_op jit(solution)/shard_map/ppermute | solution.py:776
  62.4 1.5 %collective-permute-start.26 = (f32[16,384]{1,0:T(8,128)S(1)}, f32[16,384]{1,0:T(8,128)S(1)}, u32[]{:S(2)}, u32[]{:S(2)}) collective-permute-start(f32[16,384]{1,0:T(8,128)S(1)} %get-tuple-element.88.refs_0_), channel_id=1, source_target_pairs={{0,2},{1,3},{2,0},{3,1},{4,6},{5,7},{6,4},{7,5},{8,10},{9,11},{10,... | collective-permute-start | bytes 73736 | tf_op jit(solution)/shard_map/ppermute | solution.py:784
  64.3 1.4 %shard_map.153 = (bf16[2,64,768]{2,1,0:T(8,128)(2,1)}, bf16[2,64,768]{2,1,0:T(8,128)(2,1)}, bf16[2,64,768]{2,1,0:T(8,128)(2,1)}, bf16[2,64,1536]{2,1,0:T(8,128)(2,1)}, bf16[2,64,1536]{2,1,0:T(8,128)(2,1)}) custom-call(bf16[3,64,384]{2,1,0:T(8,128)(2,1)S(1)} %get-tuple-element.70.refs_0_.awaited_ref, ...), custom_call_target="tpu_custom_call" | custom-call | flops 1150000000 | tf_op jit(solution)/shard_map/pallas_call | solution.py:959
  (74 shorter events, 15.9 us)
Async XLA Ops:
  3.2 7.5 %collective-permute-start.1 = (bf16[3,64,384]{2,1,0:T(8,128)(2,1)}, bf16[3,64,384]{2,1,0:T(8,128)(2,1)S(1)}, u32[]{:S(2)}, u32[]{:S(2)}) collective-permute-start(bf16[3,64,384]{2,1,0:T(8,128)(2,1)} %get-tuple-element.50), channel_id=1, source_target_pairs={{0,2},{1,3},{2,0},{3,1},{4,6},{5,7},{6,4},{7,5},{8,10},{9,11},{10,... | collective-permute-start | bytes 442376 | tf_op jit(solution)/shard_map/ppermute | solution.py:784
  5.8 8.9 %collective-permute-start.2 = (bf16[3,64,384]{2,1,0:T(8,128)(2,1)}, bf16[3,64,384]{2,1,0:T(8,128)(2,1)S(1)}, u32[]{:S(2)}, u32[]{:S(2)}) collective-permute-start(bf16[3,64,384]{2,1,0:T(8,128)(2,1)} %get-tuple-element.51), channel_id=1, source_target_pairs={{0,3},{1,2},{2,1},{3,0},{4,7},{5,6},{6,5},{7,4},{8,11},{9,10},{10,... | collective-permute-start | bytes 442376 | tf_op jit(solution)/shard_map/ppermute | solution.py:784
  5.9 7.7 %collective-permute-start.3 = (bf16[1,112,384]{2,1,0:T(8,128)(2,1)S(1)}, bf16[1,112,384]{2,1,0:T(8,128)(2,1)S(1)}, u32[]{:S(2)}, u32[]{:S(2)}) collective-permute-start(bf16[1,112,384]{2,1,0:T(8,128)(2,1)S(1)} %shard_map.136), channel_id=1, source_target_pairs={{0,16},{4,20},{8,24},{12,28},{16,0},{20,4},{24,8},{28,12},{1,17},{... | collective-permute-start | bytes 258056 | tf_op jit(solution)/shard_map/ppermute | solution.py:776
  11.0 6.8 %collective-permute-start.6 = (bf16[2,128,384]{2,1,0:T(8,128)(2,1)S(1)}, bf16[2,128,384]{2,1,0:T(8,128)(2,1)S(1)}, u32[]{:S(2)}, u32[]{:S(2)}) collective-permute-start(bf16[2,128,384]{2,1,0:T(8,128)(2,1)S(1)} %get-tuple-element.52), channel_id=1, source_target_pairs={{0,2},{1,3},{2,0},{3,1},{4,6},{5,7},{6,4},{7,5},{8,10},{9,11},{10,... | collective-permute-start | bytes 589832 | tf_op jit(solution)/shard_map/ppermute | solution.py:784
  13.7 6.1 %collective-permute-start.4 = (bf16[2,112,384]{2,1,0:T(8,128)(2,1)S(1)}, bf16[2,112,384]{2,1,0:T(8,128)(2,1)S(1)}, u32[]{:S(2)}, u32[]{:S(2)}) collective-permute-start(bf16[2,112,384]{2,1,0:T(8,128)(2,1)S(1)} %pad_maximum_fusion.held_ref), channel_id=1, source_target_pairs={{0,8},{4,12},{8,0},{12,4},{16,24},{20,28},{24,16},{28,20},{1,9},{5... | collective-permute-start | bytes 516104 | tf_op jit(solution)/shard_map/ppermute | solution.py:776
  17.8 6.2 %collective-permute-start.8 = (bf16[4,64,384]{2,1,0:T(8,128)(2,1)S(1)}, bf16[4,64,384]{2,1,0:T(8,128)(2,1)S(1)}, u32[]{:S(2)}, u32[]{:S(2)}) collective-permute-start(bf16[4,64,384]{2,1,0:T(8,128)(2,1)S(1)} %shard_map.140.refs_0_), channel_id=1, source_target_pairs={{0,2},{1,3},{2,0},{3,1},{4,6},{5,7},{6,4},{7,5},{8,10},{9,11},{10,... | collective-permute-start | bytes 589832 | tf_op jit(solution)/shard_map/ppermute | solution.py:784
  19.8 8.1 %collective-permute-start.5 = (bf16[400,384]{1,0:T(8,128)(2,1)S(1)}, bf16[400,384]{1,0:T(8,128)(2,1)S(1)}, u32[]{:S(2)}, u32[]{:S(2)}) collective-permute-start(bf16[400,384]{1,0:T(8,128)(2,1)S(1)} %shard_map.137.near_ref), channel_id=1, source_target_pairs={{0,4},{4,0},{8,12},{12,8},{16,20},{20,16},{24,28},{28,24},{1,5},{5... | collective-permute-start | bytes 921608 | tf_op jit(solution)/shard_map/ppermute | solution.py:776
  21.3 4.5 %collective-permute-start.10 = (bf16[3,128,384]{2,1,0:T(8,128)(2,1)S(1)}, bf16[3,128,384]{2,1,0:T(8,128)(2,1)S(1)}, u32[]{:S(2)}, u32[]{:S(2)}) collective-permute-start(bf16[3,128,384]{2,1,0:T(8,128)(2,1)S(1)} %shard_map.141), channel_id=1, source_target_pairs={{0,1},{1,0},{2,3},{3,2},{4,5},{5,4},{6,7},{7,6},{8,9},{9,8},{10,11... | collective-permute-start | bytes 884744 | tf_op jit(solution)/shard_map/ppermute | solution.py:784
  21.4 4.1 %collective-permute-start.7 = (bf16[4,64,384]{2,1,0:T(8,128)(2,1)S(1)}, bf16[4,64,384]{2,1,0:T(8,128)(2,1)S(1)}, u32[]{:S(2)}, u32[]{:S(2)}) collective-permute-start(bf16[4,64,384]{2,1,0:T(8,128)(2,1)S(1)} %shard_map.140.refs_0_), channel_id=1, source_target_pairs={{0,1},{1,0},{2,3},{3,2},{4,5},{5,4},{6,7},{7,6},{8,9},{9,8},{10,11... | collective-permute-start | bytes 589832 | tf_op jit(solution)/shard_map/ppermute | solution.py:784
  23.9 4.0 %collective-permute-start.9 = (bf16[4,64,384]{2,1,0:T(8,128)(2,1)S(1)}, bf16[4,64,384]{2,1,0:T(8,128)(2,1)S(1)}, u32[]{:S(2)}, u32[]{:S(2)}) collective-permute-start(bf16[4,64,384]{2,1,0:T(8,128)(2,1)S(1)} %collective-permute-done.8.refs_2_), channel_id=1, source_target_pairs={{0,1},{1,0},{2,3},{3,2},{4,5},{5,4},{6,7},{7,6},{8,9},{9,8},{10,11... | collective-permute-start | bytes 589832 | tf_op jit(solution)/shard_map/ppermute | solution.py:784
  23.9 8.4 %collective-permute-start.11 = (bf16[128,384]{1,0:T(8,128)(2,1)S(1)}, bf16[128,384]{1,0:T(8,128)(2,1)S(1)}, u32[]{:S(2)}, u32[]{:S(2)}) collective-permute-start(bf16[128,384]{1,0:T(8,128)(2,1)S(1)} %get-tuple-element.60), channel_id=1, source_target_pairs={{0,2},{1,3},{2,0},{3,1},{4,6},{5,7},{6,4},{7,5},{8,10},{9,11},{10,... | collective-permute-start | bytes 294920 | tf_op jit(solution)/shard_map/ppermute | solution.py:784
  25.4 6.9 %collective-permute-start.12 = (bf16[128,384]{1,0:T(8,128)(2,1)S(1)}, bf16[128,384]{1,0:T(8,128)(2,1)S(1)}, u32[]{:S(2)}, u32[]{:S(2)}) collective-permute-start(bf16[128,384]{1,0:T(8,128)(2,1)S(1)} %get-tuple-element.61), channel_id=1, source_target_pairs={{0,3},{1,2},{2,1},{3,0},{4,7},{5,6},{6,5},{7,4},{8,11},{9,10},{10,... | collective-permute-start | bytes 294920 | tf_op jit(solution)/shard_map/ppermute | solution.py:784
  31.2 5.7 %collective-permute-start.13 = (bf16[2,128,384]{2,1,0:T(8,128)(2,1)S(1)}, bf16[2,128,384]{2,1,0:T(8,128)(2,1)S(1)}, u32[]{:S(2)}, u32[]{:S(2)}) collective-permute-start(bf16[2,128,384]{2,1,0:T(8,128)(2,1)S(1)} %get-tuple-element.66), channel_id=1, source_target_pairs={{0,2},{1,3},{2,0},{3,1},{4,6},{5,7},{6,4},{7,5},{8,10},{9,11},{10,... | collective-permute-start | bytes 589832 | tf_op jit(solution)/shard_map/ppermute | solution.py:784
  37.6 12.0 %collective-permute-start.22 = (bf16[4,96,384]{2,1,0:T(8,128)(2,1)S(1)}, bf16[4,96,384]{2,1,0:T(8,128)(2,1)S(1)}, u32[]{:S(2)}, u32[]{:S(2)}) collective-permute-start(bf16[4,96,384]{2,1,0:T(8,128)(2,1)S(1)} %get-tuple-element.89), channel_id=1, source_target_pairs={{0,4},{4,0},{8,12},{12,8},{16,20},{20,16},{24,28},{28,24},{1,5},{5... | collective-permute-start | bytes 884744 | tf_op jit(solution)/shard_map/ppermute | solution.py:776
  38.9 8.7 %collective-permute-start.15 = (bf16[256,384]{1,0:T(8,128)(2,1)S(1)}, bf16[256,384]{1,0:T(8,128)(2,1)S(1)}, u32[]{:S(2)}, u32[]{:S(2)}) collective-permute-start(bf16[256,384]{1,0:T(8,128)(2,1)S(1)} %shard_map.146.refs_4_.awaited_ref.refs_1_), channel_id=1, source_target_pairs={{0,2},{1,3},{2,0},{3,1},{4,6},{5,7},{6,4},{7,5},{8,10},{9,11},{10,... | collective-permute-start | bytes 589832 | tf_op jit(solution)/shard_map/ppermute | solution.py:784
  42.5 5.1 %collective-permute-start.16 = (f32[16,384]{1,0:T(8,128)S(1)}, f32[16,384]{1,0:T(8,128)S(1)}, u32[]{:S(2)}, u32[]{:S(2)}) collective-permute-start(f32[16,384]{1,0:T(8,128)S(1)} %get-tuple-element.69), channel_id=1, source_target_pairs={{0,4},{4,0},{8,12},{12,8},{16,20},{20,16},{24,28},{28,24},{1,5},{5... | collective-permute-start | bytes 73736 | tf_op jit(solution)/shard_map/ppermute | solution.py:776
  43.5 7.4 %collective-permute-start.18 = (bf16[2,128,384]{2,1,0:T(8,128)(2,1)S(1)}, bf16[2,128,384]{2,1,0:T(8,128)(2,1)S(1)}, u32[]{:S(2)}, u32[]{:S(2)}) collective-permute-start(bf16[2,128,384]{2,1,0:T(8,128)(2,1)S(1)} %shard_map.150), channel_id=1, source_target_pairs={{0,2},{1,3},{2,0},{3,1},{4,6},{5,7},{6,4},{7,5},{8,10},{9,11},{10,... | collective-permute-start | bytes 589832 | tf_op jit(solution)/shard_map/ppermute | solution.py:784
  49.7 6.1 %collective-permute-start.23 = (bf16[2,112,384]{2,1,0:T(8,128)(2,1)S(1)}, bf16[2,112,384]{2,1,0:T(8,128)(2,1)S(1)}, u32[]{:S(2)}, u32[]{:S(2)}) collective-permute-start(bf16[2,112,384]{2,1,0:T(8,128)(2,1)S(1)} %get-tuple-element.86), channel_id=1, source_target_pairs={{0,8},{4,12},{8,0},{12,4},{16,24},{20,28},{24,16},{28,20},{1,9},{5... | collective-permute-start | bytes 516104 | tf_op jit(solution)/shard_map/ppermute | solution.py:776
  50.9 8.3 %collective-permute-start.19 = (bf16[3,64,384]{2,1,0:T(8,128)(2,1)S(1)}, bf16[3,64,384]{2,1,0:T(8,128)(2,1)S(1)}, u32[]{:S(2)}, u32[]{:S(2)}) collective-permute-start(bf16[3,64,384]{2,1,0:T(8,128)(2,1)S(1)} %shard_map.151), channel_id=1, source_target_pairs={{0,2},{1,3},{2,0},{3,1},{4,6},{5,7},{6,4},{7,5},{8,10},{9,11},{10,... | collective-permute-start | bytes 442376 | tf_op jit(solution)/shard_map/ppermute | solution.py:784
  52.6 7.3 %collective-permute-start.20 = (bf16[3,64,384]{2,1,0:T(8,128)(2,1)S(1)}, bf16[3,64,384]{2,1,0:T(8,128)(2,1)S(1)}, u32[]{:S(2)}, u32[]{:S(2)}) collective-permute-start(bf16[3,64,384]{2,1,0:T(8,128)(2,1)S(1)} %get-tuple-element.74), channel_id=1, source_target_pairs={{0,3},{1,2},{2,1},{3,0},{4,7},{5,6},{6,5},{7,4},{8,11},{9,10},{10,... | collective-permute-start | bytes 442376 | tf_op jit(solution)/shard_map/ppermute | solution.py:784
  52.8 11.4 %collective-permute-start.21 = (bf16[4,128,384]{2,1,0:T(8,128)(2,1)S(1)}, bf16[4,128,384]{2,1,0:T(8,128)(2,1)S(1)}, u32[]{:S(2)}, u32[]{:S(2)}) collective-permute-start(bf16[4,128,384]{2,1,0:T(8,128)(2,1)S(1)} %shard_map.152), channel_id=1, source_target_pairs={{0,1},{1,0},{2,3},{3,2},{4,5},{5,4},{6,7},{7,6},{8,9},{9,8},{10,11... | collective-permute-start | bytes 1179656 | tf_op jit(solution)/shard_map/ppermute | solution.py:784
  55.8 5.9 %collective-permute-start.24 = (bf16[112,384]{1,0:T(8,128)(2,1)S(1)}, bf16[112,384]{1,0:T(8,128)(2,1)S(1)}, u32[]{:S(2)}, u32[]{:S(2)}) collective-permute-start(bf16[112,384]{1,0:T(8,128)(2,1)S(1)} %slice_bitcast_fusion), channel_id=1, source_target_pairs={{0,16},{4,20},{8,24},{12,28},{16,0},{20,4},{24,8},{28,12},{1,17},{... | collective-permute-start | bytes 258056 | tf_op jit(solution)/shard_map/ppermute | solution.py:776
  62.4 3.5 %collective-permute-start.27 = (f32[16,384]{1,0:T(8,128)S(1)}, f32[16,384]{1,0:T(8,128)S(1)}, u32[]{:S(2)}, u32[]{:S(2)}) collective-permute-start(f32[16,384]{1,0:T(8,128)S(1)} %get-tuple-element.88.refs_0_), channel_id=1, source_target_pairs={{0,3},{1,2},{2,1},{3,0},{4,7},{5,6},{6,5},{7,4},{8,11},{9,10},{10,... | collective-permute-start | bytes 73736 | tf_op jit(solution)/shard_map/ppermute | solution.py:784
  62.4 3.9 %collective-permute-start.26 = (f32[16,384]{1,0:T(8,128)S(1)}, f32[16,384]{1,0:T(8,128)S(1)}, u32[]{:S(2)}, u32[]{:S(2)}) collective-permute-start(f32[16,384]{1,0:T(8,128)S(1)} %get-tuple-element.88.refs_0_), channel_id=1, source_target_pairs={{0,2},{1,3},{2,0},{3,1},{4,6},{5,7},{6,4},{7,5},{8,10},{9,11},{10,... | collective-permute-start | bytes 73736 | tf_op jit(solution)/shard_map/ppermute | solution.py:784
  (11 other events, 35.0 us)

commit v10 on v9

--- a/solution.py
+++ b/solution.py
@@ -418,7 +418,8 @@
 def unpack(*refs):
     ins, refs = refs[:N_CTX], refs[N_CTX:]
     own_ref, beside_ref, output_ref, input_ref = refs[:4]
-    heads, channels, sem = refs[4:7], refs[7:9], refs[9]
+    heads, channels, token_ref, sem = refs[4:7], refs[7:9], refs[9], refs[10]
+    token_ref[...] = jnp.zeros_like(token_ref)
     half, width = ins[0].shape[2], own_ref.shape[3]
     frames = own_ref.shape[2]
     place = lax.axis_index("ctx")
@@ -931,7 +932,7 @@
         (head_block,) * N_CTX,
         ["vmem"] * (4 + N_CTX) + ["any"],
         micros=2.2,
-    )(weights, keep, came, far, *packed, taps_came)
+    )(weights, keep, came, far, *packed, tap_keep)
     (across_block,) = gate([back_blocks[2]], input_across)
     grad_blocks = traded([*back_blocks[:2], across_block, back_blocks[3]])
     own_pair = backward_out[0]
@@ -958,9 +959,11 @@
     grad_out_weight = panel_total.T
     unpacked = call_kernel(
         unpack,
-        (shape((utts, frames, inner), low),) * 3 + (shape((utts, frames, wide), low),) * 2,
+        (shape((utts, frames, inner), low),) * 3
+        + (shape((utts, frames, wide), low),) * 2
+        + (shape((8, LANES), f32),),
         ["any"] * (N_CTX + 4),
-        ["hbm"] * 5,
+        ["hbm"] * 5 + ["vmem"],
         [dma((7 * N_CTX + 4 * N_CTX,))],
         micros=1.0,
     )(
@@ -975,8 +978,8 @@
         (shape(conv_weight.shape, f32),),
         ["vmem"] * N_CTX + ["any"],
         scratch=[pltpu.VMEM((N_CTX, TAP_PAD // 2, width), f32)],
-    )(*traded([tap_sums] * N_CTX), unpacked[0])
-    grad_queries, grad_keys, grad_values, block_output, grad_input = unpacked
+    )(*traded([tap_sums] * N_CTX), unpacked[5])
+    grad_queries, grad_keys, grad_values, block_output, grad_input = unpacked[:5]
     return (
         block_output,
         grad_input,

time: 68.3 us -> 66.8 us (0.978)
  local copies, waits for them, and re-layouts: 1.03 us -> 0.11 us
  waiting for transfers between devices: 16.2 us -> 15.4 us
    ppermute x7, waiting for transfers between devices: 9.65 us -> 5.17 us  [swapped(): return lax.ppermute(array, 'dp', [(i, i ^ bit) for i in range(N_DP)])]
    ppermute x21, waiting for transfers between devices: 6.59 us -> 10.2 us  [crossed(): return lax.ppermute(array, 'ctx', [(i, i ^ apart) for i in range(N_CTX)])]
    unnamed x14 -> x12, local copies, waits for them, and re-layouts: 0.96 us -> 0.03 us
where the time goes in v10:
time: 66.8 us; the launch traced here: 66.7 us
  starting transfers between devices  29.3 us (44%)
  Pallas kernels  20.9 us (31%)
  waiting for transfers between devices  15.4 us (23%)
  between operations  0.86 us (1%)
    ppermute x21, starting transfers between devices, crossed(): return lax.ppermute(array, 'ctx', [(i, i ^ apart) for i in range(N_CTX)])  16.8 us
    ppermute x7, starting transfers between devices, swapped(): return lax.ppermute(array, 'dp', [(i, i ^ bit) for i in range(N_DP)])  12.5 us
    ppermute x21, waiting for transfers between devices, crossed(): return lax.ppermute(array, 'ctx', [(i, i ^ apart) for i in range(N_CTX)])  10.2 us
    ppermute x7, waiting for transfers between devices, swapped(): return lax.ppermute(array, 'dp', [(i, i ^ bit) for i in range(N_DP)])  5.17 us
    pallas_call x1, Pallas kernels, per_device(): call_kernel(backward, (pair_block,) * 2 + (shape((2, utts * frames, width...  3.58 us
    pallas_call x1, Pallas kernels, per_device(): call_kernel(forward, (channel_block,) * 2 + (shape((2, utts * frames, wid...  3.22 us
    pallas_call x1, Pallas kernels, per_device(): call_kernel(attend, (shape((N_CTX, frames, half), low),), ['smem'] + ['vm...  2.77 us
    pallas_call x1, Pallas kernels, per_device(): call_kernel(make_taps, (tap_block,) * 2, ['vmem'] * 2 + ['any'], scratch=...  2.08 us
  transfers between devices with their start and end apart: 28, of which 13 were waited for; matrix products, arithmetic and copies ran while one was open for 0% of the time, Pallas kernels for 27%

profile of v10, /device:TPU:0, one launch (start us, length us, event | category | flops | bytes accessed | tf_op | source)
XLA Modules:
  0.0 66.7 jit_solution(2736321025395057364)
XLA Ops:
  0.7 2.0 %shard_map.135 = (bf16[3,64,384]{2,1,0:T(8,128)(2,1)}, bf16[3,64,384]{2,1,0:T(8,128)(2,1)}, bf16[3,64,384]{2,1,0:T(8,128)(2,1)}, bf16[3,64,384]{2,1,0:T(8,128)(2,1)}) custom-call(bf16[2,64,768]{2,1,0:T(8,128)(2,1)} %query_ref.1, bf16[2,64,768]{2,1,0:T(8,128)(2,1)} %key_ref.1, bf16[2,64,768]{2,1,0:T(8,128)(2,1)} %value_ref.1), custom_call_target="tpu_custom_call" | custom-call | flops 1150000000 | tf_op jit(solution)/shard_map/pallas_call | solution.py:809
  3.2 2.6 %collective-permute-start.1 = (bf16[3,64,384]{2,1,0:T(8,128)(2,1)}, bf16[3,64,384]{2,1,0:T(8,128)(2,1)S(1)}, u32[]{:S(2)}, u32[]{:S(2)}) collective-permute-start(bf16[3,64,384]{2,1,0:T(8,128)(2,1)} %get-tuple-element.51), channel_id=1, source_target_pairs={{0,2},{1,3},{2,0},{3,1},{4,6},{5,7},{6,4},{7,5},{8,10},{9,11},{10,... | collective-permute-start | bytes 442376 | tf_op jit(solution)/shard_map/ppermute | solution.py:785
  5.9 2.8 %collective-permute-start.3 = (bf16[1,112,384]{2,1,0:T(8,128)(2,1)S(1)}, bf16[1,112,384]{2,1,0:T(8,128)(2,1)S(1)}, u32[]{:S(2)}, u32[]{:S(2)}) collective-permute-start(bf16[1,112,384]{2,1,0:T(8,128)(2,1)S(1)} %shard_map.136), channel_id=1, source_target_pairs={{0,16},{4,20},{8,24},{12,28},{16,0},{20,4},{24,8},{28,12},{1,17},{... | collective-permute-start | bytes 258056 | tf_op jit(solution)/shard_map/ppermute | solution.py:777
  8.8 1.9 %collective-permute-done.1.refs_2_.awaited_ref = bf16[3,64,384]{2,1,0:T(8,128)(2,1)S(1)} collective-permute-done((bf16[3,64,384]{2,1,0:T(8,128)(2,1)}, bf16[3,64,384]{2,1,0:T(8,128)(2,1)S(1)}, u32[]{:S(2)}, u32[]{:S(2)}) %collective-permute-start.1) | collective-permute-done | bytes 147488 | tf_op jit(solution)/shard_map/ppermute | solution.py:785
  11.0 2.0 %collective-permute-start.6 = (bf16[2,128,384]{2,1,0:T(8,128)(2,1)S(1)}, bf16[2,128,384]{2,1,0:T(8,128)(2,1)S(1)}, u32[]{:S(2)}, u32[]{:S(2)}) collective-permute-start(bf16[2,128,384]{2,1,0:T(8,128)(2,1)S(1)} %get-tuple-element.53), channel_id=1, source_target_pairs={{0,2},{1,3},{2,0},{3,1},{4,6},{5,7},{6,4},{7,5},{8,10},{9,11},{10,... | collective-permute-start | bytes 589832 | tf_op jit(solution)/shard_map/ppermute | solution.py:785
  14.7 2.8 %shard_map.138.refs_0_ = bf16[4,64,384]{2,1,0:T(8,128)(2,1)S(1)} custom-call(s32[2]{0:T(128)S(1)} %copy-done.4, bf16[3,64,384]{2,1,0:T(8,128)(2,1)S(1)} %copy-done.5, bf16[3,64,384]{2,1,0:T(8,128)(2,1)S(1)} %collective-permute-done.awaited_ref.refs_1_, bf16[3,64,384]{2,1,0:T(8,128)(2,1)S(1)} %collective-permute-done.1.refs_2_.awaited_ref, ...), custom_call_target="tpu_custom_call" | custom-call | flops 1150000000 | tf_op jit(solution)/shard_map/pallas_call | solution.py:841
  17.8 1.8 %collective-permute-start.8 = (bf16[4,64,384]{2,1,0:T(8,128)(2,1)S(1)}, bf16[4,64,384]{2,1,0:T(8,128)(2,1)S(1)}, u32[]{:S(2)}, u32[]{:S(2)}) collective-permute-start(bf16[4,64,384]{2,1,0:T(8,128)(2,1)S(1)} %shard_map.140.refs_0_), channel_id=1, source_target_pairs={{0,2},{1,3},{2,0},{3,1},{4,6},{5,7},{6,4},{7,5},{8,10},{9,11},{10,... | collective-permute-start | bytes 589832 | tf_op jit(solution)/shard_map/ppermute | solution.py:785
  19.8 1.4 %collective-permute-start.5 = (bf16[400,384]{1,0:T(8,128)(2,1)S(1)}, bf16[400,384]{1,0:T(8,128)(2,1)S(1)}, u32[]{:S(2)}, u32[]{:S(2)}) collective-permute-start(bf16[400,384]{1,0:T(8,128)(2,1)S(1)} %shard_map.137.near_ref), channel_id=1, source_target_pairs={{0,4},{4,0},{8,12},{12,8},{16,20},{20,16},{24,28},{28,24},{1,5},{5... | collective-permute-start | bytes 921608 | tf_op jit(solution)/shard_map/ppermute | solution.py:777
  21.9 2.1 %collective-permute-done.8.refs_2_ = bf16[4,64,384]{2,1,0:T(8,128)(2,1)S(1)} collective-permute-done((bf16[4,64,384]{2,1,0:T(8,128)(2,1)S(1)}, bf16[4,64,384]{2,1,0:T(8,128)(2,1)S(1)}, u32[]{:S(2)}, u32[]{:S(2)}) %collective-permute-start.8) | collective-permute-done | bytes 196640 | tf_op jit(solution)/shard_map/ppermute | solution.py:785
  23.9 1.5 %collective-permute-start.11 = (bf16[128,384]{1,0:T(8,128)(2,1)S(1)}, bf16[128,384]{1,0:T(8,128)(2,1)S(1)}, u32[]{:S(2)}, u32[]{:S(2)}) collective-permute-start(bf16[128,384]{1,0:T(8,128)(2,1)S(1)} %get-tuple-element.61), channel_id=1, source_target_pairs={{0,2},{1,3},{2,0},{3,1},{4,6},{5,7},{6,4},{7,5},{8,10},{9,11},{10,... | collective-permute-start | bytes 294920 | tf_op jit(solution)/shard_map/ppermute | solution.py:785
  25.8 2.1 %collective-permute-done.5.other_ref = bf16[400,384]{1,0:T(8,128)(2,1)S(1)} collective-permute-done((bf16[400,384]{1,0:T(8,128)(2,1)S(1)}, bf16[400,384]{1,0:T(8,128)(2,1)S(1)}, u32[]{:S(2)}, u32[]{:S(2)}) %collective-permute-start.5) | collective-permute-done | bytes 307232 | tf_op jit(solution)/shard_map/ppermute | solution.py:777
  27.9 3.2 %shard_map.142 = (bf16[2,64,384]{2,1,0:T(8,128)(2,1)S(1)}, bf16[2,64,384]{2,1,0:T(8,128)(2,1)S(1)}, bf16[2,128,384]{2,1,0:T(8,128)(2,1)S(1)}, bf16[2,4,64,768]{3...) custom-call(s32[2]{0:T(128)S(1)} %copy-done.4, ...), custom_call_target="tpu_custom_call" | custom-call | flops 3680000000 | tf_op jit(solution)/shard_map/pallas_call | solution.py:851
  32.3 3.6 %shard_map.144 = (bf16[2,2,64,384]{3,2,1,0:T(8,128)(2,1)S(1)}, bf16[2,2,64,384]{3,2,1,0:T(8,128)(2,1)S(1)}, bf16[2,128,384]{2,1,0:T(8,128)(2,1)S(1)}, bf16[2,256...) custom-call(s32[2]{0:T(128)S(1)} %copy-done.4, ...), custom_call_target="tpu_custom_call" | custom-call | flops 5980000256 | tf_op jit(solution)/shard_map/pallas_call | solution.py:885
  37.6 1.3 %collective-permute-start.21 = (bf16[4,96,384]{2,1,0:T(8,128)(2,1)S(1)}, bf16[4,96,384]{2,1,0:T(8,128)(2,1)S(1)}, u32[]{:S(2)}, u32[]{:S(2)}) collective-permute-start(bf16[4,96,384]{2,1,0:T(8,128)(2,1)S(1)} %get-tuple-element.91), channel_id=1, source_target_pairs={{0,4},{4,0},{8,12},{12,8},{16,20},{20,16},{24,28},{28,24},{1,5},{5... | collective-permute-start | bytes 884744 | tf_op jit(solution)/shard_map/ppermute | solution.py:777
  38.9 1.5 %collective-permute-start.15 = (bf16[256,384]{1,0:T(8,128)(2,1)S(1)}, bf16[256,384]{1,0:T(8,128)(2,1)S(1)}, u32[]{:S(2)}, u32[]{:S(2)}) collective-permute-start(bf16[256,384]{1,0:T(8,128)(2,1)S(1)} %shard_map.146.refs_4_.awaited_ref.refs_1_), channel_id=1, source_target_pairs={{0,2},{1,3},{2,0},{3,1},{4,6},{5,7},{6,4},{7,5},{8,10},{9,11},{10,... | collective-permute-start | bytes 589832 | tf_op jit(solution)/shard_map/ppermute | solution.py:785
  40.4 2.1 %shard_map.148 = (f32[16,384]{1,0:T(8,128)S(1)}, f32[16,384]{1,0:T(8,128)S(1)}) custom-call(f32[6,288,128]{2,1,0:T(8,128)S(1)} %get-tuple-element.68.masked_ref, f32[6,288,128]{2,1,0:T(8,128)S(1)} %get-tuple-element.69.cotangent_ref, bf16[256,384]{1,0:T(8,128)(2,1)S(1)} %shard_map.146.refs_4_.awaited_ref.refs_1_), custom_call_target="tpu_custom_call" | custom-call | flops 1150000000 | tf_op jit(solution)/shard_map/pallas_call | solution.py:917
  46.3 2.0 %shard_map.149 = (bf16[3,64,384]{2,1,0:T(8,128)(2,1)S(1)}, bf16[3,64,384]{2,1,0:T(8,128)(2,1)S(1)}, bf16[3,64,384]{2,1,0:T(8,128)(2,1)S(1)}, bf16[3,64,384]{2,1,0:T(8,128)(2,1)S(1)}) custom-call(bf16[6,256,256]{2,1,0:T(8,128)(2,1)S(1)} %shard_map.147.weight_ref, bf16[2,256,384]{2,1,0:T(8,128)(2,1)S(1)} %get-tuple-element.65.keep_ref, ...), custom_call_target="tpu_custom_call" | custom-call | flops 2529999872 | tf_op jit(solution)/shard_map/pallas_call | solution.py:930
  48.4 1.3 %collective-permute-start.23 = (bf16[2,112,384]{2,1,0:T(8,128)(2,1)S(1)}, bf16[2,112,384]{2,1,0:T(8,128)(2,1)S(1)}, u32[]{:S(2)}, u32[]{:S(2)}) collective-permute-start(bf16[2,112,384]{2,1,0:T(8,128)(2,1)S(1)} %get-tuple-element.87), channel_id=1, source_target_pairs={{0,8},{4,12},{8,0},{12,4},{16,24},{20,28},{24,16},{28,20},{1,9},{5... | collective-permute-start | bytes 516104 | tf_op jit(solution)/shard_map/ppermute | solution.py:777
  50.2 1.8 %collective-permute-start.18 = (bf16[3,64,384]{2,1,0:T(8,128)(2,1)S(1)}, bf16[3,64,384]{2,1,0:T(8,128)(2,1)S(1)}, u32[]{:S(2)}, u32[]{:S(2)}) collective-permute-start(bf16[3,64,384]{2,1,0:T(8,128)(2,1)S(1)} %shard_map.151), channel_id=1, source_target_pairs={{0,2},{1,3},{2,0},{3,1},{4,6},{5,7},{6,4},{7,5},{8,10},{9,11},{10,... | collective-permute-start | bytes 442376 | tf_op jit(solution)/shard_map/ppermute | solution.py:785
  52.5 1.4 %collective-permute-done.23 = bf16[2,112,384]{2,1,0:T(8,128)(2,1)S(1)} collective-permute-done((bf16[2,112,384]{2,1,0:T(8,128)(2,1)S(1)}, bf16[2,112,384]{2,1,0:T(8,128)(2,1)S(1)}, u32[]{:S(2)}, u32[]{:S(2)}) %collective-permute-start.23) | collective-permute-done | bytes 172064 | tf_op jit(solution)/shard_map/ppermute | solution.py:777
  53.9 3.7 %collective-permute-start.24 = (bf16[112,384]{1,0:T(8,128)(2,1)S(1)}, bf16[112,384]{1,0:T(8,128)(2,1)S(1)}, u32[]{:S(2)}, u32[]{:S(2)}) collective-permute-start(bf16[112,384]{1,0:T(8,128)(2,1)S(1)} %slice_bitcast_fusion), channel_id=1, source_target_pairs={{0,16},{4,20},{8,24},{12,28},{16,0},{20,4},{24,8},{28,12},{1,17},{... | collective-permute-start | bytes 258056 | tf_op jit(solution)/shard_map/ppermute | solution.py:777
  57.7 1.7 %collective-permute-done.19.refs_3_.refs_1_ = bf16[3,64,384]{2,1,0:T(8,128)(2,1)S(1)} collective-permute-done((bf16[3,64,384]{2,1,0:T(8,128)(2,1)S(1)}, bf16[3,64,384]{2,1,0:T(8,128)(2,1)S(1)}, u32[]{:S(2)}, u32[]{:S(2)}) %collective-permute-start.19) | collective-permute-done | bytes 147488 | tf_op jit(solution)/shard_map/ppermute | solution.py:785
  62.8 1.4 %shard_map.153 = (bf16[2,64,768]{2,1,0:T(8,128)(2,1)}, bf16[2,64,768]{2,1,0:T(8,128)(2,1)}, bf16[2,64,768]{2,1,0:T(8,128)(2,1)}, bf16[2,64,1536]{2,1,0:T(8,128)(...) custom-call(bf16[3,64,384]{2,1,0:T(8,128)(2,1)S(1)} %get-tuple-element.71.refs_0_.awaited_ref, ...), custom_call_target="tpu_custom_call" | custom-call | flops 1150000000 | tf_op jit(solution)/shard_map/pallas_call | solution.py:960
  64.3 1.7 %collective-permute-done.26.refs_2_ = f32[16,384]{1,0:T(8,128)S(1)} collective-permute-done((f32[16,384]{1,0:T(8,128)S(1)}, f32[16,384]{1,0:T(8,128)S(1)}, u32[]{:S(2)}, u32[]{:S(2)}) %collective-permute-start.26) | collective-permute-done | bytes 24608 | tf_op jit(solution)/shard_map/ppermute | solution.py:785
  (72 shorter events, 16.3 us)
Async XLA Ops:
  3.2 7.5 %collective-permute-start.1 = (bf16[3,64,384]{2,1,0:T(8,128)(2,1)}, bf16[3,64,384]{2,1,0:T(8,128)(2,1)S(1)}, u32[]{:S(2)}, u32[]{:S(2)}) collective-permute-start(bf16[3,64,384]{2,1,0:T(8,128)(2,1)} %get-tuple-element.51), channel_id=1, source_target_pairs={{0,2},{1,3},{2,0},{3,1},{4,6},{5,7},{6,4},{7,5},{8,10},{9,11},{10,... | collective-permute-start | bytes 442376 | tf_op jit(solution)/shard_map/ppermute | solution.py:785
  5.8 8.9 %collective-permute-start.2 = (bf16[3,64,384]{2,1,0:T(8,128)(2,1)}, bf16[3,64,384]{2,1,0:T(8,128)(2,1)S(1)}, u32[]{:S(2)}, u32[]{:S(2)}) collective-permute-start(bf16[3,64,384]{2,1,0:T(8,128)(2,1)} %get-tuple-element.52), channel_id=1, source_target_pairs={{0,3},{1,2},{2,1},{3,0},{4,7},{5,6},{6,5},{7,4},{8,11},{9,10},{10,... | collective-permute-start | bytes 442376 | tf_op jit(solution)/shard_map/ppermute | solution.py:785
  5.9 7.7 %collective-permute-start.3 = (bf16[1,112,384]{2,1,0:T(8,128)(2,1)S(1)}, bf16[1,112,384]{2,1,0:T(8,128)(2,1)S(1)}, u32[]{:S(2)}, u32[]{:S(2)}) collective-permute-start(bf16[1,112,384]{2,1,0:T(8,128)(2,1)S(1)} %shard_map.136), channel_id=1, source_target_pairs={{0,16},{4,20},{8,24},{12,28},{16,0},{20,4},{24,8},{28,12},{1,17},{... | collective-permute-start | bytes 258056 | tf_op jit(solution)/shard_map/ppermute | solution.py:777
  11.0 6.8 %collective-permute-start.6 = (bf16[2,128,384]{2,1,0:T(8,128)(2,1)S(1)}, bf16[2,128,384]{2,1,0:T(8,128)(2,1)S(1)}, u32[]{:S(2)}, u32[]{:S(2)}) collective-permute-start(bf16[2,128,384]{2,1,0:T(8,128)(2,1)S(1)} %get-tuple-element.53), channel_id=1, source_target_pairs={{0,2},{1,3},{2,0},{3,1},{4,6},{5,7},{6,4},{7,5},{8,10},{9,11},{10,... | collective-permute-start | bytes 589832 | tf_op jit(solution)/shard_map/ppermute | solution.py:785
  13.7 6.1 %collective-permute-start.4 = (bf16[2,112,384]{2,1,0:T(8,128)(2,1)S(1)}, bf16[2,112,384]{2,1,0:T(8,128)(2,1)S(1)}, u32[]{:S(2)}, u32[]{:S(2)}) collective-permute-start(bf16[2,112,384]{2,1,0:T(8,128)(2,1)S(1)} %pad_maximum_fusion.held_ref), channel_id=1, source_target_pairs={{0,8},{4,12},{8,0},{12,4},{16,24},{20,28},{24,16},{28,20},{1,9},{5... | collective-permute-start | bytes 516104 | tf_op jit(solution)/shard_map/ppermute | solution.py:777
  17.8 6.2 %collective-permute-start.8 = (bf16[4,64,384]{2,1,0:T(8,128)(2,1)S(1)}, bf16[4,64,384]{2,1,0:T(8,128)(2,1)S(1)}, u32[]{:S(2)}, u32[]{:S(2)}) collective-permute-start(bf16[4,64,384]{2,1,0:T(8,128)(2,1)S(1)} %shard_map.140.refs_0_), channel_id=1, source_target_pairs={{0,2},{1,3},{2,0},{3,1},{4,6},{5,7},{6,4},{7,5},{8,10},{9,11},{10,... | collective-permute-start | bytes 589832 | tf_op jit(solution)/shard_map/ppermute | solution.py:785
  19.8 8.1 %collective-permute-start.5 = (bf16[400,384]{1,0:T(8,128)(2,1)S(1)}, bf16[400,384]{1,0:T(8,128)(2,1)S(1)}, u32[]{:S(2)}, u32[]{:S(2)}) collective-permute-start(bf16[400,384]{1,0:T(8,128)(2,1)S(1)} %shard_map.137.near_ref), channel_id=1, source_target_pairs={{0,4},{4,0},{8,12},{12,8},{16,20},{20,16},{24,28},{28,24},{1,5},{5... | collective-permute-start | bytes 921608 | tf_op jit(solution)/shard_map/ppermute | solution.py:777
  21.3 4.5 %collective-permute-start.10 = (bf16[3,128,384]{2,1,0:T(8,128)(2,1)S(1)}, bf16[3,128,384]{2,1,0:T(8,128)(2,1)S(1)}, u32[]{:S(2)}, u32[]{:S(2)}) collective-permute-start(bf16[3,128,384]{2,1,0:T(8,128)(2,1)S(1)} %shard_map.141), channel_id=1, source_target_pairs={{0,1},{1,0},{2,3},{3,2},{4,5},{5,4},{6,7},{7,6},{8,9},{9,8},{10,11... | collective-permute-start | bytes 884744 | tf_op jit(solution)/shard_map/ppermute | solution.py:785
  21.4 4.1 %collective-permute-start.7 = (bf16[4,64,384]{2,1,0:T(8,128)(2,1)S(1)}, bf16[4,64,384]{2,1,0:T(8,128)(2,1)S(1)}, u32[]{:S(2)}, u32[]{:S(2)}) collective-permute-start(bf16[4,64,384]{2,1,0:T(8,128)(2,1)S(1)} %shard_map.140.refs_0_), channel_id=1, source_target_pairs={{0,1},{1,0},{2,3},{3,2},{4,5},{5,4},{6,7},{7,6},{8,9},{9,8},{10,11... | collective-permute-start | bytes 589832 | tf_op jit(solution)/shard_map/ppermute | solution.py:785
  23.9 4.0 %collective-permute-start.9 = (bf16[4,64,384]{2,1,0:T(8,128)(2,1)S(1)}, bf16[4,64,384]{2,1,0:T(8,128)(2,1)S(1)}, u32[]{:S(2)}, u32[]{:S(2)}) collective-permute-start(bf16[4,64,384]{2,1,0:T(8,128)(2,1)S(1)} %collective-permute-done.8.refs_2_), channel_id=1, source_target_pairs={{0,1},{1,0},{2,3},{3,2},{4,5},{5,4},{6,7},{7,6},{8,9},{9,8},{10,11... | collective-permute-start | bytes 589832 | tf_op jit(solution)/shard_map/ppermute | solution.py:785
  23.9 8.4 %collective-permute-start.11 = (bf16[128,384]{1,0:T(8,128)(2,1)S(1)}, bf16[128,384]{1,0:T(8,128)(2,1)S(1)}, u32[]{:S(2)}, u32[]{:S(2)}) collective-permute-start(bf16[128,384]{1,0:T(8,128)(2,1)S(1)} %get-tuple-element.61), channel_id=1, source_target_pairs={{0,2},{1,3},{2,0},{3,1},{4,6},{5,7},{6,4},{7,5},{8,10},{9,11},{10,... | collective-permute-start | bytes 294920 | tf_op jit(solution)/shard_map/ppermute | solution.py:785
  25.4 6.9 %collective-permute-start.12 = (bf16[128,384]{1,0:T(8,128)(2,1)S(1)}, bf16[128,384]{1,0:T(8,128)(2,1)S(1)}, u32[]{:S(2)}, u32[]{:S(2)}) collective-permute-start(bf16[128,384]{1,0:T(8,128)(2,1)S(1)} %get-tuple-element.62), channel_id=1, source_target_pairs={{0,3},{1,2},{2,1},{3,0},{4,7},{5,6},{6,5},{7,4},{8,11},{9,10},{10,... | collective-permute-start | bytes 294920 | tf_op jit(solution)/shard_map/ppermute | solution.py:785
  31.2 5.7 %collective-permute-start.13 = (bf16[2,128,384]{2,1,0:T(8,128)(2,1)S(1)}, bf16[2,128,384]{2,1,0:T(8,128)(2,1)S(1)}, u32[]{:S(2)}, u32[]{:S(2)}) collective-permute-start(bf16[2,128,384]{2,1,0:T(8,128)(2,1)S(1)} %get-tuple-element.67), channel_id=1, source_target_pairs={{0,2},{1,3},{2,0},{3,1},{4,6},{5,7},{6,4},{7,5},{8,10},{9,11},{10,... | collective-permute-start | bytes 589832 | tf_op jit(solution)/shard_map/ppermute | solution.py:785
  37.6 10.7 %collective-permute-start.21 = (bf16[4,96,384]{2,1,0:T(8,128)(2,1)S(1)}, bf16[4,96,384]{2,1,0:T(8,128)(2,1)S(1)}, u32[]{:S(2)}, u32[]{:S(2)}) collective-permute-start(bf16[4,96,384]{2,1,0:T(8,128)(2,1)S(1)} %get-tuple-element.91), channel_id=1, source_target_pairs={{0,4},{4,0},{8,12},{12,8},{16,20},{20,16},{24,28},{28,24},{1,5},{5... | collective-permute-start | bytes 884744 | tf_op jit(solution)/shard_map/ppermute | solution.py:777
  38.9 7.4 %collective-permute-start.15 = (bf16[256,384]{1,0:T(8,128)(2,1)S(1)}, bf16[256,384]{1,0:T(8,128)(2,1)S(1)}, u32[]{:S(2)}, u32[]{:S(2)}) collective-permute-start(bf16[256,384]{1,0:T(8,128)(2,1)S(1)} %shard_map.146.refs_4_.awaited_ref.refs_1_), channel_id=1, source_target_pairs={{0,2},{1,3},{2,0},{3,1},{4,6},{5,7},{6,4},{7,5},{8,10},{9,11},{10,... | collective-permute-start | bytes 589832 | tf_op jit(solution)/shard_map/ppermute | solution.py:785
  42.5 5.8 %collective-permute-start.22 = (f32[16,384]{1,0:T(8,128)S(1)}, f32[16,384]{1,0:T(8,128)S(1)}, u32[]{:S(2)}, u32[]{:S(2)}) collective-permute-start(f32[16,384]{1,0:T(8,128)S(1)} %get-tuple-element.85), channel_id=1, source_target_pairs={{0,4},{4,0},{8,12},{12,8},{16,20},{20,16},{24,28},{28,24},{1,5},{5... | collective-permute-start | bytes 73736 | tf_op jit(solution)/shard_map/ppermute | solution.py:777
  43.5 6.7 %collective-permute-start.17 = (bf16[2,128,384]{2,1,0:T(8,128)(2,1)S(1)}, bf16[2,128,384]{2,1,0:T(8,128)(2,1)S(1)}, u32[]{:S(2)}, u32[]{:S(2)}) collective-permute-start(bf16[2,128,384]{2,1,0:T(8,128)(2,1)S(1)} %shard_map.150), channel_id=1, source_target_pairs={{0,2},{1,3},{2,0},{3,1},{4,6},{5,7},{6,4},{7,5},{8,10},{9,11},{10,... | collective-permute-start | bytes 589832 | tf_op jit(solution)/shard_map/ppermute | solution.py:785
  48.4 5.5 %collective-permute-start.23 = (bf16[2,112,384]{2,1,0:T(8,128)(2,1)S(1)}, bf16[2,112,384]{2,1,0:T(8,128)(2,1)S(1)}, u32[]{:S(2)}, u32[]{:S(2)}) collective-permute-start(bf16[2,112,384]{2,1,0:T(8,128)(2,1)S(1)} %get-tuple-element.87), channel_id=1, source_target_pairs={{0,8},{4,12},{8,0},{12,4},{16,24},{20,28},{24,16},{28,20},{1,9},{5... | collective-permute-start | bytes 516104 | tf_op jit(solution)/shard_map/ppermute | solution.py:777
  50.2 7.4 %collective-permute-start.18 = (bf16[3,64,384]{2,1,0:T(8,128)(2,1)S(1)}, bf16[3,64,384]{2,1,0:T(8,128)(2,1)S(1)}, u32[]{:S(2)}, u32[]{:S(2)}) collective-permute-start(bf16[3,64,384]{2,1,0:T(8,128)(2,1)S(1)} %shard_map.151), channel_id=1, source_target_pairs={{0,2},{1,3},{2,0},{3,1},{4,6},{5,7},{6,4},{7,5},{8,10},{9,11},{10,... | collective-permute-start | bytes 442376 | tf_op jit(solution)/shard_map/ppermute | solution.py:785
  52.0 7.4 %collective-permute-start.19 = (bf16[3,64,384]{2,1,0:T(8,128)(2,1)S(1)}, bf16[3,64,384]{2,1,0:T(8,128)(2,1)S(1)}, u32[]{:S(2)}, u32[]{:S(2)}) collective-permute-start(bf16[3,64,384]{2,1,0:T(8,128)(2,1)S(1)} %get-tuple-element.75), channel_id=1, source_target_pairs={{0,3},{1,2},{2,1},{3,0},{4,7},{5,6},{6,5},{7,4},{8,11},{9,10},{10,... | collective-permute-start | bytes 442376 | tf_op jit(solution)/shard_map/ppermute | solution.py:785
  52.2 10.6 %collective-permute-start.20 = (bf16[4,128,384]{2,1,0:T(8,128)(2,1)S(1)}, bf16[4,128,384]{2,1,0:T(8,128)(2,1)S(1)}, u32[]{:S(2)}, u32[]{:S(2)}) collective-permute-start(bf16[4,128,384]{2,1,0:T(8,128)(2,1)S(1)} %shard_map.152), channel_id=1, source_target_pairs={{0,1},{1,0},{2,3},{3,2},{4,5},{5,4},{6,7},{7,6},{8,9},{9,8},{10,11... | collective-permute-start | bytes 1179656 | tf_op jit(solution)/shard_map/ppermute | solution.py:785
  53.9 6.2 %collective-permute-start.24 = (bf16[112,384]{1,0:T(8,128)(2,1)S(1)}, bf16[112,384]{1,0:T(8,128)(2,1)S(1)}, u32[]{:S(2)}, u32[]{:S(2)}) collective-permute-start(bf16[112,384]{1,0:T(8,128)(2,1)S(1)} %slice_bitcast_fusion), channel_id=1, source_target_pairs={{0,16},{4,20},{8,24},{12,28},{16,0},{20,4},{24,8},{28,12},{1,17},{... | collective-permute-start | bytes 258056 | tf_op jit(solution)/shard_map/ppermute | solution.py:777
  60.8 3.5 %collective-permute-start.27 = (f32[16,384]{1,0:T(8,128)S(1)}, f32[16,384]{1,0:T(8,128)S(1)}, u32[]{:S(2)}, u32[]{:S(2)}) collective-permute-start(f32[16,384]{1,0:T(8,128)S(1)} %get-tuple-element.89.refs_0_), channel_id=1, source_target_pairs={{0,3},{1,2},{2,1},{3,0},{4,7},{5,6},{6,5},{7,4},{8,11},{9,10},{10,... | collective-permute-start | bytes 73736 | tf_op jit(solution)/shard_map/ppermute | solution.py:785
  61.9 4.1 %collective-permute-start.26 = (f32[16,384]{1,0:T(8,128)S(1)}, f32[16,384]{1,0:T(8,128)S(1)}, u32[]{:S(2)}, u32[]{:S(2)}) collective-permute-start(f32[16,384]{1,0:T(8,128)S(1)} %get-tuple-element.89.refs_0_), channel_id=1, source_target_pairs={{0,2},{1,3},{2,0},{3,1},{4,6},{5,7},{6,4},{7,5},{8,10},{9,11},{10,... | collective-permute-start | bytes 73736 | tf_op jit(solution)/shard_map/ppermute | solution.py:785
  (10 other events, 35.6 us)

commit v11 on v10

--- a/solution.py
+++ b/solution.py
@@ -418,8 +418,8 @@
 def unpack(*refs):
     ins, refs = refs[:N_CTX], refs[N_CTX:]
     own_ref, beside_ref, output_ref, input_ref = refs[:4]
-    heads, channels, token_ref, sem = refs[4:7], refs[7:9], refs[9], refs[10]
-    token_ref[...] = jnp.zeros_like(token_ref)
+    taps, heads, channels, taps_ref = refs[4:8], refs[8:11], refs[11:13], refs[13]
+    held_ref, picked_ref, sem = refs[14:]
     half, width = ins[0].shape[2], own_ref.shape[3]
     frames = own_ref.shape[2]
     place = lax.axis_index("ctx")
@@ -441,7 +441,16 @@
             for apart, block in enumerate(blocks):
                 cols = columns((place ^ apart) * width, width)
                 pairs.append((block, ref.at[utt, :, cols]))
-    run_copies(pairs, sem)
+    start_copies(pairs, sem)
+    for apart in range(N_CTX):
+        held_ref[apart] = taps[apart][...]
+    mine = held_ref[place ^ half_of(lax.axis_index("dp"))]
+    side = mine.shape[1] // 2
+    picked_ref[...] = jnp.concatenate([mine[:, :side], mine[:, side:]], axis=0)[:TAPS]
+    last = pltpu.make_async_copy(picked_ref, taps_ref, sem.at[len(pairs)])
+    last.start()
+    wait_copies(pairs, sem)
+    last.wait()
 
 
 def head_parts(refs, slot):
@@ -711,20 +720,10 @@
     refs[-1][...] = jnp.zeros_like(refs[-1])
 
 
-def finish(kept_ref, came_ref, awaited_ref, panel_ref, taps_ref):
-    entries = panel_ref.shape[0]
-    total = kept_ref[0].astype(jnp.float32) + came_ref[...].astype(jnp.float32)
-    panel_ref[...] = total[:entries]
-    taps_ref[...] = total[entries:]
-
-
-def pick_taps(*refs):
-    ins, out_ref, held_ref = refs[:N_CTX], refs[N_CTX + 1], refs[N_CTX + 2]
-    own = ins[0].shape[1] // 2
-    for apart in range(N_CTX):
-        held_ref[apart] = ins[apart][...]
-    mine = held_ref[lax.axis_index("ctx") ^ half_of(lax.axis_index("dp"))]
-    out_ref[...] = jnp.concatenate([mine[:, :own], mine[:, own:]], axis=0)[:TAPS]
+def finish(kept_ref, came_ref, awaited_ref, taps_ref):
+    entries = kept_ref.shape[1] - TAP_PAD // 2
+    total = kept_ref[0, entries:].astype(jnp.float32)
+    taps_ref[...] = total + came_ref[entries:].astype(jnp.float32)
 
 
 def relay(keep_ref, came_ref, out_ref):
@@ -951,20 +950,25 @@
     )(panels[:4], panels_came, tap_keep, taps_came, back_blocks[0])
     panels = (kept.astype(f32) + swapped(sent, 2).astype(f32)).astype(low)
     (arrived,) = call_kernel(mark, (shape((8, LANES), f32),), ["any"] * 2)(*grad_blocks[2:])
-    panel_total, tap_sums = call_kernel(
-        finish,
-        (shape((entries, width), f32), shape((TAP_PAD // 2, width), f32)),
-        ["vmem"] * 2 + ["any"],
-    )(panels, swapped(panels[1], 4), arrived)
-    grad_out_weight = panel_total.T
-    unpacked = call_kernel(
+    panels_last = swapped(panels[1], 4)
+    (tap_sums,) = call_kernel(
+        finish, (shape((TAP_PAD // 2, width), f32),), ["vmem"] * 2 + ["any"]
+    )(panels, panels_last, arrived)
+    total = panels[0].astype(f32) + panels_last.astype(f32)
+    grad_out_weight = total[:entries].T
+    tap_blocks = traded([tap_sums] * N_CTX)
+    grad_queries, grad_keys, grad_values, block_output, grad_input, grad_taps = call_kernel(
         unpack,
         (shape((utts, frames, inner), low),) * 3
         + (shape((utts, frames, wide), low),) * 2
-        + (shape((8, LANES), f32),),
-        ["any"] * (N_CTX + 4),
-        ["hbm"] * 5 + ["vmem"],
-        [dma((7 * N_CTX + 4 * N_CTX,))],
+        + (shape(conv_weight.shape, f32),),
+        ["any"] * (N_CTX + 4) + ["vmem"] * N_CTX,
+        ["hbm"] * 6,
+        [
+            pltpu.VMEM((N_CTX, TAP_PAD // 2, width), f32),
+            pltpu.VMEM(conv_weight.shape, f32),
+            dma((7 * N_CTX + 1,)),
+        ],
         micros=1.0,
     )(
         *grad_blocks,
@@ -972,14 +976,8 @@
         beside_pair,
         output_across,
         input_across,
-    )
-    (grad_taps,) = call_kernel(
-        pick_taps,
-        (shape(conv_weight.shape, f32),),
-        ["vmem"] * N_CTX + ["any"],
-        scratch=[pltpu.VMEM((N_CTX, TAP_PAD // 2, width), f32)],
-    )(*traded([tap_sums] * N_CTX), unpacked[5])
-    grad_queries, grad_keys, grad_values, block_output, grad_input = unpacked[:5]
+        *tap_blocks,
+    )
     return (
         block_output,
         grad_input,

time: 66.8 us -> 66.8 us (level)
  Pallas kernels: 20.9 us -> 19.4 us
  waiting for transfers between devices: 15.4 us -> 16.2 us
  other arithmetic: 0.07 us -> 0.74 us
    pallas_call x2 -> x1, Pallas kernels: 1.38 us -> 0.01 us  [per_device(): call_kernel(finish, (shape((TAP_PAD // 2, width), f32),), ['vmem'] * 2 +...]
    ppermute x21, waiting for transfers between devices: 10.2 us -> 11 us  [crossed(): return lax.ppermute(array, 'ctx', [(i, i ^ apart) for i in range(N_CTX)])]
    transpose x0 -> x1, other arithmetic: none -> 0.68 us  [per_device(): grad_out_weight = total[:entries].T]
  transfers between devices with their start and end apart: 28 -> 28, of which waited for: 13 -> 14; matrix products, arithmetic and copies ran while one was open for 0% -> 1% of each run, Pallas kernels for 27% -> 24%
where the time goes in v11:
time: 66.8 us; the launch traced here: 66.6 us
  starting transfers between devices  29.3 us (44%)
  Pallas kernels  19.4 us (29%)
  waiting for transfers between devices  16.2 us (24%)
  between operations  0.85 us (1%)
  other arithmetic  0.74 us (1%)
    ppermute x21, starting transfers between devices, crossed(): return lax.ppermute(array, 'ctx', [(i, i ^ apart) for i in range(N_CTX)])  16.8 us
    ppermute x7, starting transfers between devices, swapped(): return lax.ppermute(array, 'dp', [(i, i ^ bit) for i in range(N_DP)])  12.5 us
    ppermute x21, waiting for transfers between devices, crossed(): return lax.ppermute(array, 'ctx', [(i, i ^ apart) for i in range(N_CTX)])  11 us
    ppermute x7, waiting for transfers between devices, swapped(): return lax.ppermute(array, 'dp', [(i, i ^ bit) for i in range(N_DP)])  5.18 us
    pallas_call x1, Pallas kernels, per_device(): call_kernel(backward, (pair_block,) * 2 + (shape((2, utts * frames, width...  3.58 us
    pallas_call x1, Pallas kernels, per_device(): call_kernel(forward, (channel_block,) * 2 + (shape((2, utts * frames, wid...  3.22 us
    pallas_call x1, Pallas kernels, per_device(): call_kernel(attend, (shape((N_CTX, frames, half), low),), ['smem'] + ['vm...  2.77 us
    pallas_call x1, Pallas kernels, per_device(): call_kernel(make_taps, (tap_block,) * 2, ['vmem'] * 2 + ['any'], scratch=...  2.08 us
  transfers between devices with their start and end apart: 28, of which 14 were waited for; matrix products, arithmetic and copies ran while one was open for 1% of the time, Pallas kernels for 24%

profile of v11, /device:TPU:0, one launch (start us, length us, event | category | flops | bytes accessed | tf_op | source)
XLA Modules:
  0.0 66.6 jit_solution(16060753992447381113)
XLA Ops:
  0.7 2.0 %shard_map.135 = (bf16[3,64,384]{2,1,0:T(8,128)(2,1)}, bf16[3,64,384]{2,1,0:T(8,128)(2,1)}, bf16[3,64,384]{2,1,0:T(8,128)(2,1)}, bf16[3,64,384]{2,1,0:T(8,128)(2,1)}) custom-call(bf16[2,64,768]{2,1,0:T(8,128)(2,1)} %query_ref.1, bf16[2,64,768]{2,1,0:T(8,128)(2,1)} %key_ref.1, bf16[2,64,768]{2,1,0:T(8,128)(2,1)} %value_ref.1), custom_call_target="tpu_custom_call" | custom-call | flops 1150000000 | tf_op jit(solution)/shard_map/pallas_call | solution.py:808
  3.2 2.6 %collective-permute-start.1 = (bf16[3,64,384]{2,1,0:T(8,128)(2,1)}, bf16[3,64,384]{2,1,0:T(8,128)(2,1)S(1)}, u32[]{:S(2)}, u32[]{:S(2)}) collective-permute-start(bf16[3,64,384]{2,1,0:T(8,128)(2,1)} %get-tuple-element.49), channel_id=1, source_target_pairs={{0,2},{1,3},{2,0},{3,1},{4,6},{5,7},{6,4},{7,5},{8,10},{9,11},{10,... | collective-permute-start | bytes 442376 | tf_op jit(solution)/shard_map/ppermute | solution.py:784
  5.9 2.8 %collective-permute-start.3 = (bf16[1,112,384]{2,1,0:T(8,128)(2,1)S(1)}, bf16[1,112,384]{2,1,0:T(8,128)(2,1)S(1)}, u32[]{:S(2)}, u32[]{:S(2)}) collective-permute-start(bf16[1,112,384]{2,1,0:T(8,128)(2,1)S(1)} %shard_map.136), channel_id=1, source_target_pairs={{0,16},{4,20},{8,24},{12,28},{16,0},{20,4},{24,8},{28,12},{1,17},{... | collective-permute-start | bytes 258056 | tf_op jit(solution)/shard_map/ppermute | solution.py:776
  8.8 1.9 %collective-permute-done.1.refs_2_.awaited_ref = bf16[3,64,384]{2,1,0:T(8,128)(2,1)S(1)} collective-permute-done((bf16[3,64,384]{2,1,0:T(8,128)(2,1)}, bf16[3,64,384]{2,1,0:T(8,128)(2,1)S(1)}, u32[]{:S(2)}, u32[]{:S(2)}) %collective-permute-start.1) | collective-permute-done | bytes 147488 | tf_op jit(solution)/shard_map/ppermute | solution.py:784
  11.0 2.0 %collective-permute-start.6 = (bf16[2,128,384]{2,1,0:T(8,128)(2,1)S(1)}, bf16[2,128,384]{2,1,0:T(8,128)(2,1)S(1)}, u32[]{:S(2)}, u32[]{:S(2)}) collective-permute-start(bf16[2,128,384]{2,1,0:T(8,128)(2,1)S(1)} %get-tuple-element.51), channel_id=1, source_target_pairs={{0,2},{1,3},{2,0},{3,1},{4,6},{5,7},{6,4},{7,5},{8,10},{9,11},{10,... | collective-permute-start | bytes 589832 | tf_op jit(solution)/shard_map/ppermute | solution.py:784
  14.7 2.8 %shard_map.138.refs_0_ = bf16[4,64,384]{2,1,0:T(8,128)(2,1)S(1)} custom-call(s32[2]{0:T(128)S(1)} %copy-done.4, bf16[3,64,384]{2,1,0:T(8,128)(2,1)S(1)} %copy-done.5, bf16[3,64,384]{2,1,0:T(8,128)(2,1)S(1)} %collective-permute-done.awaited_ref.refs_1_, bf16[3,64,384]{2,1,0:T(8,128)(2,1)S(1)} %collective-permute-done.1.refs_2_.awaited_ref, ...), custom_call_target="tpu_custom_call" | custom-call | flops 1150000000 | tf_op jit(solution)/shard_map/pallas_call | solution.py:840
  17.8 1.8 %collective-permute-start.8 = (bf16[4,64,384]{2,1,0:T(8,128)(2,1)S(1)}, bf16[4,64,384]{2,1,0:T(8,128)(2,1)S(1)}, u32[]{:S(2)}, u32[]{:S(2)}) collective-permute-start(bf16[4,64,384]{2,1,0:T(8,128)(2,1)S(1)} %shard_map.140.refs_0_), channel_id=1, source_target_pairs={{0,2},{1,3},{2,0},{3,1},{4,6},{5,7},{6,4},{7,5},{8,10},{9,11},{10,... | collective-permute-start | bytes 589832 | tf_op jit(solution)/shard_map/ppermute | solution.py:784
  19.8 1.4 %collective-permute-start.5 = (bf16[400,384]{1,0:T(8,128)(2,1)S(1)}, bf16[400,384]{1,0:T(8,128)(2,1)S(1)}, u32[]{:S(2)}, u32[]{:S(2)}) collective-permute-start(bf16[400,384]{1,0:T(8,128)(2,1)S(1)} %shard_map.137.near_ref), channel_id=1, source_target_pairs={{0,4},{4,0},{8,12},{12,8},{16,20},{20,16},{24,28},{28,24},{1,5},{5... | collective-permute-start | bytes 921608 | tf_op jit(solution)/shard_map/ppermute | solution.py:776
  21.9 2.1 %collective-permute-done.8.refs_2_ = bf16[4,64,384]{2,1,0:T(8,128)(2,1)S(1)} collective-permute-done((bf16[4,64,384]{2,1,0:T(8,128)(2,1)S(1)}, bf16[4,64,384]{2,1,0:T(8,128)(2,1)S(1)}, u32[]{:S(2)}, u32[]{:S(2)}) %collective-permute-start.8) | collective-permute-done | bytes 196640 | tf_op jit(solution)/shard_map/ppermute | solution.py:784
  23.9 1.5 %collective-permute-start.11 = (bf16[128,384]{1,0:T(8,128)(2,1)S(1)}, bf16[128,384]{1,0:T(8,128)(2,1)S(1)}, u32[]{:S(2)}, u32[]{:S(2)}) collective-permute-start(bf16[128,384]{1,0:T(8,128)(2,1)S(1)} %get-tuple-element.59), channel_id=1, source_target_pairs={{0,2},{1,3},{2,0},{3,1},{4,6},{5,7},{6,4},{7,5},{8,10},{9,11},{10,... | collective-permute-start | bytes 294920 | tf_op jit(solution)/shard_map/ppermute | solution.py:784
  25.8 2.1 %collective-permute-done.5.other_ref = bf16[400,384]{1,0:T(8,128)(2,1)S(1)} collective-permute-done((bf16[400,384]{1,0:T(8,128)(2,1)S(1)}, bf16[400,384]{1,0:T(8,128)(2,1)S(1)}, u32[]{:S(2)}, u32[]{:S(2)}) %collective-permute-start.5) | collective-permute-done | bytes 307232 | tf_op jit(solution)/shard_map/ppermute | solution.py:776
  27.9 3.2 %shard_map.142 = (bf16[2,64,384]{2,1,0:T(8,128)(2,1)S(1)}, bf16[2,64,384]{2,1,0:T(8,128)(2,1)S(1)}, bf16[2,128,384]{2,1,0:T(8,128)(2,1)S(1)}, bf16[2,4,64,768]{3...) custom-call(s32[2]{0:T(128)S(1)} %copy-done.4, ...), custom_call_target="tpu_custom_call" | custom-call | flops 3680000000 | tf_op jit(solution)/shard_map/pallas_call | solution.py:850
  32.3 3.6 %shard_map.144 = (bf16[2,2,64,384]{3,2,1,0:T(8,128)(2,1)S(1)}, bf16[2,2,64,384]{3,2,1,0:T(8,128)(2,1)S(1)}, bf16[2,128,384]{2,1,0:T(8,128)(2,1)S(1)}, bf16[2,256...) custom-call(s32[2]{0:T(128)S(1)} %copy-done.4, ...), custom_call_target="tpu_custom_call" | custom-call | flops 5980000256 | tf_op jit(solution)/shard_map/pallas_call | solution.py:884
  37.6 1.3 %collective-permute-start.21 = (bf16[4,96,384]{2,1,0:T(8,128)(2,1)S(1)}, bf16[4,96,384]{2,1,0:T(8,128)(2,1)S(1)}, u32[]{:S(2)}, u32[]{:S(2)}) collective-permute-start(bf16[4,96,384]{2,1,0:T(8,128)(2,1)S(1)} %get-tuple-element.87), channel_id=1, source_target_pairs={{0,4},{4,0},{8,12},{12,8},{16,20},{20,16},{24,28},{28,24},{1,5},{5... | collective-permute-start | bytes 884744 | tf_op jit(solution)/shard_map/ppermute | solution.py:776
  38.9 1.5 %collective-permute-start.15 = (bf16[256,384]{1,0:T(8,128)(2,1)S(1)}, bf16[256,384]{1,0:T(8,128)(2,1)S(1)}, u32[]{:S(2)}, u32[]{:S(2)}) collective-permute-start(bf16[256,384]{1,0:T(8,128)(2,1)S(1)} %shard_map.146.refs_4_.awaited_ref.refs_1_), channel_id=1, source_target_pairs={{0,2},{1,3},{2,0},{3,1},{4,6},{5,7},{6,4},{7,5},{8,10},{9,11},{10,... | collective-permute-start | bytes 589832 | tf_op jit(solution)/shard_map/ppermute | solution.py:784
  40.4 2.1 %shard_map.148 = (f32[16,384]{1,0:T(8,128)S(1)}, f32[16,384]{1,0:T(8,128)S(1)}) custom-call(f32[6,288,128]{2,1,0:T(8,128)S(1)} %get-tuple-element.66.masked_ref, f32[6,288,128]{2,1,0:T(8,128)S(1)} %get-tuple-element.67.cotangent_ref, bf16[256,384]{1,0:T(8,128)(2,1)S(1)} %shard_map.146.refs_4_.awaited_ref.refs_1_), custom_call_target="tpu_custom_call" | custom-call | flops 1150000000 | tf_op jit(solution)/shard_map/pallas_call | solution.py:916
  46.3 2.0 %shard_map.149 = (bf16[3,64,384]{2,1,0:T(8,128)(2,1)S(1)}, bf16[3,64,384]{2,1,0:T(8,128)(2,1)S(1)}, bf16[3,64,384]{2,1,0:T(8,128)(2,1)S(1)}, bf16[3,64,384]{2,1,0:T(8,128)(2,1)S(1)}) custom-call(bf16[6,256,256]{2,1,0:T(8,128)(2,1)S(1)} %shard_map.147.weight_ref, bf16[2,256,384]{2,1,0:T(8,128)(2,1)S(1)} %get-tuple-element.63.keep_ref, ...), custom_call_target="tpu_custom_call" | custom-call | flops 2529999872 | tf_op jit(solution)/shard_map/pallas_call | solution.py:929
  48.4 1.3 %collective-permute-start.23 = (bf16[2,112,384]{2,1,0:T(8,128)(2,1)S(1)}, bf16[2,112,384]{2,1,0:T(8,128)(2,1)S(1)}, u32[]{:S(2)}, u32[]{:S(2)}) collective-permute-start(bf16[2,112,384]{2,1,0:T(8,128)(2,1)S(1)} %get-tuple-element.80), channel_id=1, source_target_pairs={{0,8},{4,12},{8,0},{12,4},{16,24},{20,28},{24,16},{28,20},{1,9},{5... | collective-permute-start | bytes 516104 | tf_op jit(solution)/shard_map/ppermute | solution.py:776
  50.2 1.8 %collective-permute-start.18 = (bf16[3,64,384]{2,1,0:T(8,128)(2,1)S(1)}, bf16[3,64,384]{2,1,0:T(8,128)(2,1)S(1)}, u32[]{:S(2)}, u32[]{:S(2)}) collective-permute-start(bf16[3,64,384]{2,1,0:T(8,128)(2,1)S(1)} %shard_map.151), channel_id=1, source_target_pairs={{0,2},{1,3},{2,0},{3,1},{4,6},{5,7},{6,4},{7,5},{8,10},{9,11},{10,... | collective-permute-start | bytes 442376 | tf_op jit(solution)/shard_map/ppermute | solution.py:784
  52.5 1.4 %collective-permute-done.23 = bf16[2,112,384]{2,1,0:T(8,128)(2,1)S(1)} collective-permute-done((bf16[2,112,384]{2,1,0:T(8,128)(2,1)S(1)}, bf16[2,112,384]{2,1,0:T(8,128)(2,1)S(1)}, u32[]{:S(2)}, u32[]{:S(2)}) %collective-permute-start.23) | collective-permute-done | bytes 172064 | tf_op jit(solution)/shard_map/ppermute | solution.py:776
  53.9 3.7 %collective-permute-start.24 = (bf16[112,384]{1,0:T(8,128)(2,1)S(1)}, bf16[112,384]{1,0:T(8,128)(2,1)S(1)}, u32[]{:S(2)}, u32[]{:S(2)}) collective-permute-start(bf16[112,384]{1,0:T(8,128)(2,1)S(1)} %get-tuple-element.90), channel_id=1, source_target_pairs={{0,16},{4,20},{8,24},{12,28},{16,0},{20,4},{24,8},{28,12},{1,17},{... | collective-permute-start | bytes 258056 | tf_op jit(solution)/shard_map/ppermute | solution.py:776
  57.7 1.7 %collective-permute-done.19.refs_1_.refs_3_ = bf16[3,64,384]{2,1,0:T(8,128)(2,1)S(1)} collective-permute-done((bf16[3,64,384]{2,1,0:T(8,128)(2,1)S(1)}, bf16[3,64,384]{2,1,0:T(8,128)(2,1)S(1)}, u32[]{:S(2)}, u32[]{:S(2)}) %collective-permute-start.19) | collective-permute-done | bytes 147488 | tf_op jit(solution)/shard_map/ppermute | solution.py:784
  63.4 1.9 %collective-permute-done.26.refs_10_ = f32[16,384]{1,0:T(8,128)S(1)} collective-permute-done((f32[16,384]{1,0:T(8,128)S(1)}, f32[16,384]{1,0:T(8,128)S(1)}, u32[]{:S(2)}, u32[]{:S(2)}) %collective-permute-start.26) | collective-permute-done | bytes 24608 | tf_op jit(solution)/shard_map/ppermute | solution.py:784
  65.3 1.3 %shard_map.157 = (bf16[2,64,768]{2,1,0:T(8,128)(2,1)}, bf16[2,64,768]{2,1,0:T(8,128)(2,1)}, bf16[2,64,768]{2,1,0:T(8,128)(2,1)}, bf16[2,64,1536]{2,1,0:T(8,128)(...) custom-call(bf16[3,64,384]{2,1,0:T(8,128)(2,1)S(1)} %get-tuple-element.69.awaited_ref.refs_0_, ...), custom_call_target="tpu_custom_call" | custom-call | flops 1150000000 | tf_op jit(solution)/shard_map/pallas_call | solution.py:960
  (72 shorter events, 16.1 us)
Async XLA Ops:
  3.2 7.5 %collective-permute-start.1 = (bf16[3,64,384]{2,1,0:T(8,128)(2,1)}, bf16[3,64,384]{2,1,0:T(8,128)(2,1)S(1)}, u32[]{:S(2)}, u32[]{:S(2)}) collective-permute-start(bf16[3,64,384]{2,1,0:T(8,128)(2,1)} %get-tuple-element.49), channel_id=1, source_target_pairs={{0,2},{1,3},{2,0},{3,1},{4,6},{5,7},{6,4},{7,5},{8,10},{9,11},{10,... | collective-permute-start | bytes 442376 | tf_op jit(solution)/shard_map/ppermute | solution.py:784
  5.8 8.9 %collective-permute-start.2 = (bf16[3,64,384]{2,1,0:T(8,128)(2,1)}, bf16[3,64,384]{2,1,0:T(8,128)(2,1)S(1)}, u32[]{:S(2)}, u32[]{:S(2)}) collective-permute-start(bf16[3,64,384]{2,1,0:T(8,128)(2,1)} %get-tuple-element.50), channel_id=1, source_target_pairs={{0,3},{1,2},{2,1},{3,0},{4,7},{5,6},{6,5},{7,4},{8,11},{9,10},{10,... | collective-permute-start | bytes 442376 | tf_op jit(solution)/shard_map/ppermute | solution.py:784
  5.9 7.7 %collective-permute-start.3 = (bf16[1,112,384]{2,1,0:T(8,128)(2,1)S(1)}, bf16[1,112,384]{2,1,0:T(8,128)(2,1)S(1)}, u32[]{:S(2)}, u32[]{:S(2)}) collective-permute-start(bf16[1,112,384]{2,1,0:T(8,128)(2,1)S(1)} %shard_map.136), channel_id=1, source_target_pairs={{0,16},{4,20},{8,24},{12,28},{16,0},{20,4},{24,8},{28,12},{1,17},{... | collective-permute-start | bytes 258056 | tf_op jit(solution)/shard_map/ppermute | solution.py:776
  11.0 6.8 %collective-permute-start.6 = (bf16[2,128,384]{2,1,0:T(8,128)(2,1)S(1)}, bf16[2,128,384]{2,1,0:T(8,128)(2,1)S(1)}, u32[]{:S(2)}, u32[]{:S(2)}) collective-permute-start(bf16[2,128,384]{2,1,0:T(8,128)(2,1)S(1)} %get-tuple-element.51), channel_id=1, source_target_pairs={{0,2},{1,3},{2,0},{3,1},{4,6},{5,7},{6,4},{7,5},{8,10},{9,11},{10,... | collective-permute-start | bytes 589832 | tf_op jit(solution)/shard_map/ppermute | solution.py:784
  13.7 6.1 %collective-permute-start.4 = (bf16[2,112,384]{2,1,0:T(8,128)(2,1)S(1)}, bf16[2,112,384]{2,1,0:T(8,128)(2,1)S(1)}, u32[]{:S(2)}, u32[]{:S(2)}) collective-permute-start(bf16[2,112,384]{2,1,0:T(8,128)(2,1)S(1)} %pad_maximum_fusion.held_ref), channel_id=1, source_target_pairs={{0,8},{4,12},{8,0},{12,4},{16,24},{20,28},{24,16},{28,20},{1,9},{5... | collective-permute-start | bytes 516104 | tf_op jit(solution)/shard_map/ppermute | solution.py:776
  17.8 6.2 %collective-permute-start.8 = (bf16[4,64,384]{2,1,0:T(8,128)(2,1)S(1)}, bf16[4,64,384]{2,1,0:T(8,128)(2,1)S(1)}, u32[]{:S(2)}, u32[]{:S(2)}) collective-permute-start(bf16[4,64,384]{2,1,0:T(8,128)(2,1)S(1)} %shard_map.140.refs_0_), channel_id=1, source_target_pairs={{0,2},{1,3},{2,0},{3,1},{4,6},{5,7},{6,4},{7,5},{8,10},{9,11},{10,... | collective-permute-start | bytes 589832 | tf_op jit(solution)/shard_map/ppermute | solution.py:784
  19.8 8.1 %collective-permute-start.5 = (bf16[400,384]{1,0:T(8,128)(2,1)S(1)}, bf16[400,384]{1,0:T(8,128)(2,1)S(1)}, u32[]{:S(2)}, u32[]{:S(2)}) collective-permute-start(bf16[400,384]{1,0:T(8,128)(2,1)S(1)} %shard_map.137.near_ref), channel_id=1, source_target_pairs={{0,4},{4,0},{8,12},{12,8},{16,20},{20,16},{24,28},{28,24},{1,5},{5... | collective-permute-start | bytes 921608 | tf_op jit(solution)/shard_map/ppermute | solution.py:776
  21.3 4.5 %collective-permute-start.10 = (bf16[3,128,384]{2,1,0:T(8,128)(2,1)S(1)}, bf16[3,128,384]{2,1,0:T(8,128)(2,1)S(1)}, u32[]{:S(2)}, u32[]{:S(2)}) collective-permute-start(bf16[3,128,384]{2,1,0:T(8,128)(2,1)S(1)} %shard_map.141), channel_id=1, source_target_pairs={{0,1},{1,0},{2,3},{3,2},{4,5},{5,4},{6,7},{7,6},{8,9},{9,8},{10,11... | collective-permute-start | bytes 884744 | tf_op jit(solution)/shard_map/ppermute | solution.py:784
  21.4 4.1 %collective-permute-start.7 = (bf16[4,64,384]{2,1,0:T(8,128)(2,1)S(1)}, bf16[4,64,384]{2,1,0:T(8,128)(2,1)S(1)}, u32[]{:S(2)}, u32[]{:S(2)}) collective-permute-start(bf16[4,64,384]{2,1,0:T(8,128)(2,1)S(1)} %shard_map.140.refs_0_), channel_id=1, source_target_pairs={{0,1},{1,0},{2,3},{3,2},{4,5},{5,4},{6,7},{7,6},{8,9},{9,8},{10,11... | collective-permute-start | bytes 589832 | tf_op jit(solution)/shard_map/ppermute | solution.py:784
  23.9 4.0 %collective-permute-start.9 = (bf16[4,64,384]{2,1,0:T(8,128)(2,1)S(1)}, bf16[4,64,384]{2,1,0:T(8,128)(2,1)S(1)}, u32[]{:S(2)}, u32[]{:S(2)}) collective-permute-start(bf16[4,64,384]{2,1,0:T(8,128)(2,1)S(1)} %collective-permute-done.8.refs_2_), channel_id=1, source_target_pairs={{0,1},{1,0},{2,3},{3,2},{4,5},{5,4},{6,7},{7,6},{8,9},{9,8},{10,11... | collective-permute-start | bytes 589832 | tf_op jit(solution)/shard_map/ppermute | solution.py:784
  23.9 8.4 %collective-permute-start.11 = (bf16[128,384]{1,0:T(8,128)(2,1)S(1)}, bf16[128,384]{1,0:T(8,128)(2,1)S(1)}, u32[]{:S(2)}, u32[]{:S(2)}) collective-permute-start(bf16[128,384]{1,0:T(8,128)(2,1)S(1)} %get-tuple-element.59), channel_id=1, source_target_pairs={{0,2},{1,3},{2,0},{3,1},{4,6},{5,7},{6,4},{7,5},{8,10},{9,11},{10,... | collective-permute-start | bytes 294920 | tf_op jit(solution)/shard_map/ppermute | solution.py:784
  25.4 6.9 %collective-permute-start.12 = (bf16[128,384]{1,0:T(8,128)(2,1)S(1)}, bf16[128,384]{1,0:T(8,128)(2,1)S(1)}, u32[]{:S(2)}, u32[]{:S(2)}) collective-permute-start(bf16[128,384]{1,0:T(8,128)(2,1)S(1)} %get-tuple-element.60), channel_id=1, source_target_pairs={{0,3},{1,2},{2,1},{3,0},{4,7},{5,6},{6,5},{7,4},{8,11},{9,10},{10,... | collective-permute-start | bytes 294920 | tf_op jit(solution)/shard_map/ppermute | solution.py:784
  31.2 5.7 %collective-permute-start.13 = (bf16[2,128,384]{2,1,0:T(8,128)(2,1)S(1)}, bf16[2,128,384]{2,1,0:T(8,128)(2,1)S(1)}, u32[]{:S(2)}, u32[]{:S(2)}) collective-permute-start(bf16[2,128,384]{2,1,0:T(8,128)(2,1)S(1)} %get-tuple-element.65), channel_id=1, source_target_pairs={{0,2},{1,3},{2,0},{3,1},{4,6},{5,7},{6,4},{7,5},{8,10},{9,11},{10,... | collective-permute-start | bytes 589832 | tf_op jit(solution)/shard_map/ppermute | solution.py:784
  37.6 10.7 %collective-permute-start.21 = (bf16[4,96,384]{2,1,0:T(8,128)(2,1)S(1)}, bf16[4,96,384]{2,1,0:T(8,128)(2,1)S(1)}, u32[]{:S(2)}, u32[]{:S(2)}) collective-permute-start(bf16[4,96,384]{2,1,0:T(8,128)(2,1)S(1)} %get-tuple-element.87), channel_id=1, source_target_pairs={{0,4},{4,0},{8,12},{12,8},{16,20},{20,16},{24,28},{28,24},{1,5},{5... | collective-permute-start | bytes 884744 | tf_op jit(solution)/shard_map/ppermute | solution.py:776
  38.9 7.4 %collective-permute-start.15 = (bf16[256,384]{1,0:T(8,128)(2,1)S(1)}, bf16[256,384]{1,0:T(8,128)(2,1)S(1)}, u32[]{:S(2)}, u32[]{:S(2)}) collective-permute-start(bf16[256,384]{1,0:T(8,128)(2,1)S(1)} %shard_map.146.refs_4_.awaited_ref.refs_1_), channel_id=1, source_target_pairs={{0,2},{1,3},{2,0},{3,1},{4,6},{5,7},{6,4},{7,5},{8,10},{9,11},{10,... | collective-permute-start | bytes 589832 | tf_op jit(solution)/shard_map/ppermute | solution.py:784
  42.5 5.8 %collective-permute-start.22 = (f32[16,384]{1,0:T(8,128)S(1)}, f32[16,384]{1,0:T(8,128)S(1)}, u32[]{:S(2)}, u32[]{:S(2)}) collective-permute-start(f32[16,384]{1,0:T(8,128)S(1)} %get-tuple-element.78), channel_id=1, source_target_pairs={{0,4},{4,0},{8,12},{12,8},{16,20},{20,16},{24,28},{28,24},{1,5},{5... | collective-permute-start | bytes 73736 | tf_op jit(solution)/shard_map/ppermute | solution.py:776
  43.5 6.7 %collective-permute-start.17 = (bf16[2,128,384]{2,1,0:T(8,128)(2,1)S(1)}, bf16[2,128,384]{2,1,0:T(8,128)(2,1)S(1)}, u32[]{:S(2)}, u32[]{:S(2)}) collective-permute-start(bf16[2,128,384]{2,1,0:T(8,128)(2,1)S(1)} %shard_map.150), channel_id=1, source_target_pairs={{0,2},{1,3},{2,0},{3,1},{4,6},{5,7},{6,4},{7,5},{8,10},{9,11},{10,... | collective-permute-start | bytes 589832 | tf_op jit(solution)/shard_map/ppermute | solution.py:784
  48.4 5.5 %collective-permute-start.23 = (bf16[2,112,384]{2,1,0:T(8,128)(2,1)S(1)}, bf16[2,112,384]{2,1,0:T(8,128)(2,1)S(1)}, u32[]{:S(2)}, u32[]{:S(2)}) collective-permute-start(bf16[2,112,384]{2,1,0:T(8,128)(2,1)S(1)} %get-tuple-element.80), channel_id=1, source_target_pairs={{0,8},{4,12},{8,0},{12,4},{16,24},{20,28},{24,16},{28,20},{1,9},{5... | collective-permute-start | bytes 516104 | tf_op jit(solution)/shard_map/ppermute | solution.py:776
  50.2 7.4 %collective-permute-start.18 = (bf16[3,64,384]{2,1,0:T(8,128)(2,1)S(1)}, bf16[3,64,384]{2,1,0:T(8,128)(2,1)S(1)}, u32[]{:S(2)}, u32[]{:S(2)}) collective-permute-start(bf16[3,64,384]{2,1,0:T(8,128)(2,1)S(1)} %shard_map.151), channel_id=1, source_target_pairs={{0,2},{1,3},{2,0},{3,1},{4,6},{5,7},{6,4},{7,5},{8,10},{9,11},{10,... | collective-permute-start | bytes 442376 | tf_op jit(solution)/shard_map/ppermute | solution.py:784
  52.0 7.4 %collective-permute-start.19 = (bf16[3,64,384]{2,1,0:T(8,128)(2,1)S(1)}, bf16[3,64,384]{2,1,0:T(8,128)(2,1)S(1)}, u32[]{:S(2)}, u32[]{:S(2)}) collective-permute-start(bf16[3,64,384]{2,1,0:T(8,128)(2,1)S(1)} %get-tuple-element.73), channel_id=1, source_target_pairs={{0,3},{1,2},{2,1},{3,0},{4,7},{5,6},{6,5},{7,4},{8,11},{9,10},{10,... | collective-permute-start | bytes 442376 | tf_op jit(solution)/shard_map/ppermute | solution.py:784
  52.2 13.1 %collective-permute-start.20 = (bf16[4,128,384]{2,1,0:T(8,128)(2,1)S(1)}, bf16[4,128,384]{2,1,0:T(8,128)(2,1)S(1)}, u32[]{:S(2)}, u32[]{:S(2)}) collective-permute-start(bf16[4,128,384]{2,1,0:T(8,128)(2,1)S(1)} %shard_map.152), channel_id=1, source_target_pairs={{0,1},{1,0},{2,3},{3,2},{4,5},{5,4},{6,7},{7,6},{8,9},{9,8},{10,11... | collective-permute-start | bytes 1179656 | tf_op jit(solution)/shard_map/ppermute | solution.py:784
  53.9 6.2 %collective-permute-start.24 = (bf16[112,384]{1,0:T(8,128)(2,1)S(1)}, bf16[112,384]{1,0:T(8,128)(2,1)S(1)}, u32[]{:S(2)}, u32[]{:S(2)}) collective-permute-start(bf16[112,384]{1,0:T(8,128)(2,1)S(1)} %get-tuple-element.90), channel_id=1, source_target_pairs={{0,16},{4,20},{8,24},{12,28},{16,0},{20,4},{24,8},{28,12},{1,17},{... | collective-permute-start | bytes 258056 | tf_op jit(solution)/shard_map/ppermute | solution.py:776
  60.1 3.3 %collective-permute-start.27 = (f32[16,384]{1,0:T(8,128)S(1)}, f32[16,384]{1,0:T(8,128)S(1)}, u32[]{:S(2)}, u32[]{:S(2)}) collective-permute-start(f32[16,384]{1,0:T(8,128)S(1)} %shard_map.156.refs_8_), channel_id=1, source_target_pairs={{0,3},{1,2},{2,1},{3,0},{4,7},{5,6},{6,5},{7,4},{8,11},{9,10},{10,... | collective-permute-start | bytes 73736 | tf_op jit(solution)/shard_map/ppermute | solution.py:784
  61.3 4.0 %collective-permute-start.26 = (f32[16,384]{1,0:T(8,128)S(1)}, f32[16,384]{1,0:T(8,128)S(1)}, u32[]{:S(2)}, u32[]{:S(2)}) collective-permute-start(f32[16,384]{1,0:T(8,128)S(1)} %shard_map.156.refs_8_), channel_id=1, source_target_pairs={{0,2},{1,3},{2,0},{3,1},{4,6},{5,7},{6,4},{7,5},{8,10},{9,11},{10,... | collective-permute-start | bytes 73736 | tf_op jit(solution)/shard_map/ppermute | solution.py:784
  (10 other events, 35.5 us)

commit v12 on v11

--- a/solution.py
+++ b/solution.py
@@ -697,23 +697,25 @@
             ]
 
 
-def join(panel_ref, came_ref, tap_ref, tap_came_ref, awaited_ref, keep_ref, send_ref):
+def join(panel_ref, came_ref, tap_ref, tap_came_ref, awaited_ref, *refs):
+    first_refs, second_refs = refs[0:2], refs[2:4]
+    split = first_refs[0].shape[1]
     entries = panel_ref.shape[1]
-    group, place = lax.axis_index("dp"), lax.axis_index("ctx")
+    place = lax.axis_index("ctx")
     taps = (tap_ref[...] + tap_came_ref[...]).astype(jnp.bfloat16)
     none = jnp.zeros_like(taps)
-    for slot in range(N_DP // 2):
-        ref = (keep_ref, send_ref)[slot // 2]
+    mine = place ^ half_of(lax.axis_index("dp"))
+    for slot, apart in enumerate((0, 2, 1, 3)):
         total = panel_ref[slot].astype(jnp.float32) + came_ref[slot].astype(jnp.float32)
-        ref[slot % 2, 0:entries] = total.astype(jnp.bfloat16)
-        ref[slot % 2, entries:] = none
-    mine = slot_of(2 * place, group & 6)
-    for slot in range(N_DP // 2):
-        ref = (keep_ref, send_ref)[slot // 2]
-
-        @pl.when(mine == slot)
-        def _(ref=ref, slot=slot):
-            ref[slot % 2, entries:] = taps
+        total = total.astype(jnp.bfloat16)
+        first_refs[apart // 2][apart & 1] = total[:split]
+        ref, number = second_refs[apart & 1], apart // 2
+        ref[number, 0 : entries - split] = total[split:]
+        ref[number, entries - split :] = none
+
+        @pl.when(mine == apart)
+        def _(ref=ref, number=number):
+            ref[number, entries - split :] = taps
 
 
 def mark(*refs):
@@ -943,19 +945,30 @@
     )(backward_out[1], output_across, input_across, grad_blocks[1])
     beside_pair = crossed(beside_pair, 1)
 
-    kept, sent = call_kernel(
+    split = entries // 2
+    first_kept, first_sent, second_kept, second_sent = call_kernel(
         join,
-        (shape((2, entries + TAP_PAD // 2, width), low),) * 2,
+        (shape((2, split, width), low),) * 2
+        + (shape((2, entries - split + TAP_PAD // 2, width), low),) * 2,
         ["vmem"] * 4 + ["any"],
     )(panels[:4], panels_came, tap_keep, taps_came, back_blocks[0])
-    panels = (kept.astype(f32) + swapped(sent, 2).astype(f32)).astype(low)
+    (first_sent,) = gate([first_sent], grad_blocks[1])
+    second_came, first_came = swapped(second_sent, 2), swapped(first_sent, 4)
+    second = (second_kept.astype(f32) + second_came.astype(f32)).astype(low)
+    first = (first_kept.astype(f32) + first_came.astype(f32)).astype(low)
+    second_last, first_last = swapped(second[1], 4), swapped(first[1], 2)
     (arrived,) = call_kernel(mark, (shape((8, LANES), f32),), ["any"] * 2)(*grad_blocks[2:])
-    panels_last = swapped(panels[1], 4)
     (tap_sums,) = call_kernel(
         finish, (shape((TAP_PAD // 2, width), f32),), ["vmem"] * 2 + ["any"]
-    )(panels, panels_last, arrived)
-    total = panels[0].astype(f32) + panels_last.astype(f32)
-    grad_out_weight = total[:entries].T
+    )(second, second_last, arrived)
+    total = jnp.concatenate(
+        [
+            first[0].astype(f32) + first_last.astype(f32),
+            (second[0].astype(f32) + second_last.astype(f32))[: entries - split],
+        ],
+        axis=0,
+    )
+    grad_out_weight = total.T
     tap_blocks = traded([tap_sums] * N_CTX)
     grad_queries, grad_keys, grad_values, block_output, grad_input, grad_taps = call_kernel(
         unpack,

time: 66.8 us -> 68.6 us (1.027)
  starting transfers between devices: 29.3 us -> 32.2 us
  waiting for transfers between devices: 16.2 us -> 15.1 us
    ppermute x21, waiting for transfers between devices: 11 us -> 8.17 us  [crossed(): return lax.ppermute(array, 'ctx', [(i, i ^ apart) for i in range(N_CTX)])]
    ppermute x7 -> x9, starting transfers between devices: 12.5 us -> 14.9 us  [swapped(): return lax.ppermute(array, 'dp', [(i, i ^ bit) for i in range(N_DP)])]
    ppermute x7 -> x9, waiting for transfers between devices: 5.18 us -> 6.93 us  [swapped(): return lax.ppermute(array, 'dp', [(i, i ^ bit) for i in range(N_DP)])]
  transfers between devices with their start and end apart: 28 -> 30, of which waited for: 14 -> 14; matrix products, arithmetic and copies ran while one was open for 1% -> 1% of each run, Pallas kernels for 24% -> 23%
where the time goes in v12:
time: 68.6 us; the launch traced here: 68.5 us
  starting transfers between devices  32.2 us (47%)
  Pallas kernels  19.4 us (28%)
  waiting for transfers between devices  15.1 us (22%)
  between operations  0.88 us (1%)
  other arithmetic  0.76 us (1%)
    ppermute x21, starting transfers between devices, crossed(): return lax.ppermute(array, 'ctx', [(i, i ^ apart) for i in range(N_CTX)])  17.3 us
    ppermute x9, starting transfers between devices, swapped(): return lax.ppermute(array, 'dp', [(i, i ^ bit) for i in range(N_DP)])  14.9 us
    ppermute x21, waiting for transfers between devices, crossed(): return lax.ppermute(array, 'ctx', [(i, i ^ apart) for i in range(N_CTX)])  8.17 us
    ppermute x9, waiting for transfers between devices, swapped(): return lax.ppermute(array, 'dp', [(i, i ^ bit) for i in range(N_DP)])  6.93 us
    pallas_call x1, Pallas kernels, per_device(): call_kernel(backward, (pair_block,) * 2 + (shape((2, utts * frames, width...  3.58 us
    pallas_call x1, Pallas kernels, per_device(): call_kernel(forward, (channel_block,) * 2 + (shape((2, utts * frames, wid...  3.22 us
    pallas_call x1, Pallas kernels, per_device(): call_kernel(attend, (shape((N_CTX, frames, half), low),), ['smem'] + ['vm...  2.77 us
    pallas_call x1, Pallas kernels, per_device(): call_kernel(make_taps, (tap_block,) * 2, ['vmem'] * 2 + ['any'], scratch=...  2.08 us
  transfers between devices with their start and end apart: 30, of which 14 were waited for; matrix products, arithmetic and copies ran while one was open for 1% of the time, Pallas kernels for 23%

profile of v12, /device:TPU:0, one launch (start us, length us, event | category | flops | bytes accessed | tf_op | source)
XLA Modules:
  0.0 68.5 jit_solution(5971461928524560736)
XLA Ops:
  0.7 2.0 %shard_map.135 = (bf16[3,64,384]{2,1,0:T(8,128)(2,1)}, bf16[3,64,384]{2,1,0:T(8,128)(2,1)}, bf16[3,64,384]{2,1,0:T(8,128)(2,1)}, bf16[3,64,384]{2,1,0:T(8,128)(2,1)}) custom-call(bf16[2,64,768]{2,1,0:T(8,128)(2,1)} %query_ref.1, bf16[2,64,768]{2,1,0:T(8,128)(2,1)} %key_ref.1, bf16[2,64,768]{2,1,0:T(8,128)(2,1)} %value_ref.1), custom_call_target="tpu_custom_call" | custom-call | flops 1150000000 | tf_op jit(solution)/shard_map/pallas_call | solution.py:810
  3.2 2.6 %collective-permute-start.1 = (bf16[3,64,384]{2,1,0:T(8,128)(2,1)}, bf16[3,64,384]{2,1,0:T(8,128)(2,1)S(1)}, u32[]{:S(2)}, u32[]{:S(2)}) collective-permute-start(bf16[3,64,384]{2,1,0:T(8,128)(2,1)} %get-tuple-element.51), channel_id=1, source_target_pairs={{0,2},{1,3},{2,0},{3,1},{4,6},{5,7},{6,4},{7,5},{8,10},{9,11},{10,... | collective-permute-start | bytes 442376 | tf_op jit(solution)/shard_map/ppermute | solution.py:786
  5.9 2.8 %collective-permute-start.3 = (bf16[1,112,384]{2,1,0:T(8,128)(2,1)S(1)}, bf16[1,112,384]{2,1,0:T(8,128)(2,1)S(1)}, u32[]{:S(2)}, u32[]{:S(2)}) collective-permute-start(bf16[1,112,384]{2,1,0:T(8,128)(2,1)S(1)} %shard_map.136), channel_id=1, source_target_pairs={{0,16},{4,20},{8,24},{12,28},{16,0},{20,4},{24,8},{28,12},{1,17},{... | collective-permute-start | bytes 258056 | tf_op jit(solution)/shard_map/ppermute | solution.py:778
  8.8 1.9 %collective-permute-done.1.refs_2_.awaited_ref = bf16[3,64,384]{2,1,0:T(8,128)(2,1)S(1)} collective-permute-done((bf16[3,64,384]{2,1,0:T(8,128)(2,1)}, bf16[3,64,384]{2,1,0:T(8,128)(2,1)S(1)}, u32[]{:S(2)}, u32[]{:S(2)}) %collective-permute-start.1) | collective-permute-done | bytes 147488 | tf_op jit(solution)/shard_map/ppermute | solution.py:786
  11.0 2.0 %collective-permute-start.6 = (bf16[2,128,384]{2,1,0:T(8,128)(2,1)S(1)}, bf16[2,128,384]{2,1,0:T(8,128)(2,1)S(1)}, u32[]{:S(2)}, u32[]{:S(2)}) collective-permute-start(bf16[2,128,384]{2,1,0:T(8,128)(2,1)S(1)} %get-tuple-element.53), channel_id=1, source_target_pairs={{0,2},{1,3},{2,0},{3,1},{4,6},{5,7},{6,4},{7,5},{8,10},{9,11},{10,... | collective-permute-start | bytes 589832 | tf_op jit(solution)/shard_map/ppermute | solution.py:786
  14.7 2.8 %shard_map.138.refs_0_ = bf16[4,64,384]{2,1,0:T(8,128)(2,1)S(1)} custom-call(s32[2]{0:T(128)S(1)} %copy-done.4, bf16[3,64,384]{2,1,0:T(8,128)(2,1)S(1)} %copy-done.5, bf16[3,64,384]{2,1,0:T(8,128)(2,1)S(1)} %collective-permute-done.awaited_ref.refs_1_, bf16[3,64,384]{2,1,0:T(8,128)(2,1)S(1)} %collective-permute-done.1.refs_2_.awaited_ref, ...), custom_call_target="tpu_custom_call" | custom-call | flops 1150000000 | tf_op jit(solution)/shard_map/pallas_call | solution.py:842
  17.8 1.8 %collective-permute-start.8 = (bf16[4,64,384]{2,1,0:T(8,128)(2,1)S(1)}, bf16[4,64,384]{2,1,0:T(8,128)(2,1)S(1)}, u32[]{:S(2)}, u32[]{:S(2)}) collective-permute-start(bf16[4,64,384]{2,1,0:T(8,128)(2,1)S(1)} %shard_map.140.refs_0_), channel_id=1, source_target_pairs={{0,2},{1,3},{2,0},{3,1},{4,6},{5,7},{6,4},{7,5},{8,10},{9,11},{10,... | collective-permute-start | bytes 589832 | tf_op jit(solution)/shard_map/ppermute | solution.py:786
  19.8 1.4 %collective-permute-start.5 = (bf16[400,384]{1,0:T(8,128)(2,1)S(1)}, bf16[400,384]{1,0:T(8,128)(2,1)S(1)}, u32[]{:S(2)}, u32[]{:S(2)}) collective-permute-start(bf16[400,384]{1,0:T(8,128)(2,1)S(1)} %shard_map.137.near_ref), channel_id=1, source_target_pairs={{0,4},{4,0},{8,12},{12,8},{16,20},{20,16},{24,28},{28,24},{1,5},{5... | collective-permute-start | bytes 921608 | tf_op jit(solution)/shard_map/ppermute | solution.py:778
  21.9 2.1 %collective-permute-done.8.refs_2_ = bf16[4,64,384]{2,1,0:T(8,128)(2,1)S(1)} collective-permute-done((bf16[4,64,384]{2,1,0:T(8,128)(2,1)S(1)}, bf16[4,64,384]{2,1,0:T(8,128)(2,1)S(1)}, u32[]{:S(2)}, u32[]{:S(2)}) %collective-permute-start.8) | collective-permute-done | bytes 196640 | tf_op jit(solution)/shard_map/ppermute | solution.py:786
  23.9 1.5 %collective-permute-start.11 = (bf16[128,384]{1,0:T(8,128)(2,1)S(1)}, bf16[128,384]{1,0:T(8,128)(2,1)S(1)}, u32[]{:S(2)}, u32[]{:S(2)}) collective-permute-start(bf16[128,384]{1,0:T(8,128)(2,1)S(1)} %get-tuple-element.61), channel_id=1, source_target_pairs={{0,2},{1,3},{2,0},{3,1},{4,6},{5,7},{6,4},{7,5},{8,10},{9,11},{10,... | collective-permute-start | bytes 294920 | tf_op jit(solution)/shard_map/ppermute | solution.py:786
  25.8 2.1 %collective-permute-done.5.other_ref = bf16[400,384]{1,0:T(8,128)(2,1)S(1)} collective-permute-done((bf16[400,384]{1,0:T(8,128)(2,1)S(1)}, bf16[400,384]{1,0:T(8,128)(2,1)S(1)}, u32[]{:S(2)}, u32[]{:S(2)}) %collective-permute-start.5) | collective-permute-done | bytes 307232 | tf_op jit(solution)/shard_map/ppermute | solution.py:778
  27.9 3.2 %shard_map.142 = (bf16[2,64,384]{2,1,0:T(8,128)(2,1)S(1)}, bf16[2,64,384]{2,1,0:T(8,128)(2,1)S(1)}, bf16[2,128,384]{2,1,0:T(8,128)(2,1)S(1)}, bf16[2,4,64,768]{3...) custom-call(s32[2]{0:T(128)S(1)} %copy-done.4, ...), custom_call_target="tpu_custom_call" | custom-call | flops 3680000000 | tf_op jit(solution)/shard_map/pallas_call | solution.py:852
  32.3 3.6 %shard_map.144 = (bf16[2,2,64,384]{3,2,1,0:T(8,128)(2,1)S(1)}, bf16[2,2,64,384]{3,2,1,0:T(8,128)(2,1)S(1)}, bf16[2,128,384]{2,1,0:T(8,128)(2,1)S(1)}, bf16[2,256...) custom-call(s32[2]{0:T(128)S(1)} %copy-done.4, ...), custom_call_target="tpu_custom_call" | custom-call | flops 5980000256 | tf_op jit(solution)/shard_map/pallas_call | solution.py:886
  37.6 1.3 %collective-permute-start.21 = (bf16[4,96,384]{2,1,0:T(8,128)(2,1)S(1)}, bf16[4,96,384]{2,1,0:T(8,128)(2,1)S(1)}, u32[]{:S(2)}, u32[]{:S(2)}) collective-permute-start(bf16[4,96,384]{2,1,0:T(8,128)(2,1)S(1)} %get-tuple-element.91), channel_id=1, source_target_pairs={{0,4},{4,0},{8,12},{12,8},{16,20},{20,16},{24,28},{28,24},{1,5},{5... | collective-permute-start | bytes 884744 | tf_op jit(solution)/shard_map/ppermute | solution.py:778
  38.9 1.5 %collective-permute-start.15 = (bf16[256,384]{1,0:T(8,128)(2,1)S(1)}, bf16[256,384]{1,0:T(8,128)(2,1)S(1)}, u32[]{:S(2)}, u32[]{:S(2)}) collective-permute-start(bf16[256,384]{1,0:T(8,128)(2,1)S(1)} %shard_map.146.refs_4_.awaited_ref.refs_1_), channel_id=1, source_target_pairs={{0,2},{1,3},{2,0},{3,1},{4,6},{5,7},{6,4},{7,5},{8,10},{9,11},{10,... | collective-permute-start | bytes 589832 | tf_op jit(solution)/shard_map/ppermute | solution.py:786
  40.4 2.1 %shard_map.148 = (f32[16,384]{1,0:T(8,128)S(1)}, f32[16,384]{1,0:T(8,128)S(1)}) custom-call(f32[6,288,128]{2,1,0:T(8,128)S(1)} %get-tuple-element.68.masked_ref, f32[6,288,128]{2,1,0:T(8,128)S(1)} %get-tuple-element.69.cotangent_ref, bf16[256,384]{1,0:T(8,128)(2,1)S(1)} %shard_map.146.refs_4_.awaited_ref.refs_1_), custom_call_target="tpu_custom_call" | custom-call | flops 1150000000 | tf_op jit(solution)/shard_map/pallas_call | solution.py:918
  46.3 2.0 %shard_map.149 = (bf16[3,64,384]{2,1,0:T(8,128)(2,1)S(1)}, bf16[3,64,384]{2,1,0:T(8,128)(2,1)S(1)}, bf16[3,64,384]{2,1,0:T(8,128)(2,1)S(1)}, bf16[3,64,384]{2,1,0:T(8,128)(2,1)S(1)}) custom-call(bf16[6,256,256]{2,1,0:T(8,128)(2,1)S(1)} %shard_map.147.weight_ref, bf16[2,256,384]{2,1,0:T(8,128)(2,1)S(1)} %get-tuple-element.65.keep_ref, ...), custom_call_target="tpu_custom_call" | custom-call | flops 2529999872 | tf_op jit(solution)/shard_map/pallas_call | solution.py:931
  48.4 1.3 %collective-permute-start.23 = (bf16[2,64,384]{2,1,0:T(8,128)(2,1)S(1)}, bf16[2,64,384]{2,1,0:T(8,128)(2,1)S(1)}, u32[]{:S(2)}, u32[]{:S(2)}) collective-permute-start(bf16[2,64,384]{2,1,0:T(8,128)(2,1)S(1)} %get-tuple-element.82), channel_id=1, source_target_pairs={{0,8},{4,12},{8,0},{12,4},{16,24},{20,28},{24,16},{28,20},{1,9},{5... | collective-permute-start | bytes 294920 | tf_op jit(solution)/shard_map/ppermute | solution.py:778
  50.2 1.8 %collective-permute-start.18 = (bf16[3,64,384]{2,1,0:T(8,128)(2,1)S(1)}, bf16[3,64,384]{2,1,0:T(8,128)(2,1)S(1)}, u32[]{:S(2)}, u32[]{:S(2)}) collective-permute-start(bf16[3,64,384]{2,1,0:T(8,128)(2,1)S(1)} %shard_map.151), channel_id=1, source_target_pairs={{0,2},{1,3},{2,0},{3,1},{4,6},{5,7},{6,4},{7,5},{8,10},{9,11},{10,... | collective-permute-start | bytes 442376 | tf_op jit(solution)/shard_map/ppermute | solution.py:786
  53.1 3.6 %collective-permute-start.24 = (bf16[64,384]{1,0:T(8,128)(2,1)S(1)}, bf16[64,384]{1,0:T(8,128)(2,1)S(1)}, u32[]{:S(2)}, u32[]{:S(2)}) collective-permute-start(bf16[64,384]{1,0:T(8,128)(2,1)S(1)} %get-tuple-element.94), channel_id=1, source_target_pairs={{0,16},{4,20},{8,24},{12,28},{16,0},{20,4},{24,8},{28,12},{1,17},{... | collective-permute-start | bytes 147464 | tf_op jit(solution)/shard_map/ppermute | solution.py:778
  56.9 1.3 %collective-permute-done.19.refs_1_.refs_3_ = bf16[3,64,384]{2,1,0:T(8,128)(2,1)S(1)} collective-permute-done((bf16[3,64,384]{2,1,0:T(8,128)(2,1)S(1)}, bf16[3,64,384]{2,1,0:T(8,128)(2,1)S(1)}, u32[]{:S(2)}, u32[]{:S(2)}) %collective-permute-start.19) | collective-permute-done | bytes 147488 | tf_op jit(solution)/shard_map/ppermute | solution.py:786
  62.1 2.4 %collective-permute-start.29 = (bf16[48,384]{1,0:T(8,128)(2,1)S(1)}, bf16[48,384]{1,0:T(8,128)(2,1)S(1)}, u32[]{:S(2)}, u32[]{:S(2)}) collective-permute-start(bf16[48,384]{1,0:T(8,128)(2,1)S(1)} %slice_bitcast_fusion.2), channel_id=1, source_target_pairs={{0,8},{4,12},{8,0},{12,4},{16,24},{20,28},{24,16},{28,20},{1,9},{5... | collective-permute-start | bytes 110600 | tf_op jit(solution)/shard_map/ppermute | solution.py:778
  64.5 1.9 %collective-permute-done.29 = bf16[48,384]{1,0:T(8,128)(2,1)S(1)} collective-permute-done((bf16[48,384]{1,0:T(8,128)(2,1)S(1)}, bf16[48,384]{1,0:T(8,128)(2,1)S(1)}, u32[]{:S(2)}, u32[]{:S(2)}) %collective-permute-start.29) | collective-permute-done | bytes 36896 | tf_op jit(solution)/shard_map/ppermute | solution.py:778
  67.1 1.3 %shard_map.157 = (bf16[2,64,768]{2,1,0:T(8,128)(2,1)}, bf16[2,64,768]{2,1,0:T(8,128)(2,1)}, bf16[2,64,768]{2,1,0:T(8,128)(2,1)}, bf16[2,64,1536]{2,1,0:T(8,128)(...) custom-call(bf16[3,64,384]{2,1,0:T(8,128)(2,1)S(1)} %get-tuple-element.71.awaited_ref.refs_0_, ...), custom_call_target="tpu_custom_call" | custom-call | flops 1150000000 | tf_op jit(solution)/shard_map/pallas_call | solution.py:973
  (81 shorter events, 17.4 us)
Async XLA Ops:
  3.2 7.5 %collective-permute-start.1 = (bf16[3,64,384]{2,1,0:T(8,128)(2,1)}, bf16[3,64,384]{2,1,0:T(8,128)(2,1)S(1)}, u32[]{:S(2)}, u32[]{:S(2)}) collective-permute-start(bf16[3,64,384]{2,1,0:T(8,128)(2,1)} %get-tuple-element.51), channel_id=1, source_target_pairs={{0,2},{1,3},{2,0},{3,1},{4,6},{5,7},{6,4},{7,5},{8,10},{9,11},{10,... | collective-permute-start | bytes 442376 | tf_op jit(solution)/shard_map/ppermute | solution.py:786
  5.8 8.9 %collective-permute-start.2 = (bf16[3,64,384]{2,1,0:T(8,128)(2,1)}, bf16[3,64,384]{2,1,0:T(8,128)(2,1)S(1)}, u32[]{:S(2)}, u32[]{:S(2)}) collective-permute-start(bf16[3,64,384]{2,1,0:T(8,128)(2,1)} %get-tuple-element.52), channel_id=1, source_target_pairs={{0,3},{1,2},{2,1},{3,0},{4,7},{5,6},{6,5},{7,4},{8,11},{9,10},{10,... | collective-permute-start | bytes 442376 | tf_op jit(solution)/shard_map/ppermute | solution.py:786
  5.9 7.7 %collective-permute-start.3 = (bf16[1,112,384]{2,1,0:T(8,128)(2,1)S(1)}, bf16[1,112,384]{2,1,0:T(8,128)(2,1)S(1)}, u32[]{:S(2)}, u32[]{:S(2)}) collective-permute-start(bf16[1,112,384]{2,1,0:T(8,128)(2,1)S(1)} %shard_map.136), channel_id=1, source_target_pairs={{0,16},{4,20},{8,24},{12,28},{16,0},{20,4},{24,8},{28,12},{1,17},{... | collective-permute-start | bytes 258056 | tf_op jit(solution)/shard_map/ppermute | solution.py:778
  11.0 6.8 %collective-permute-start.6 = (bf16[2,128,384]{2,1,0:T(8,128)(2,1)S(1)}, bf16[2,128,384]{2,1,0:T(8,128)(2,1)S(1)}, u32[]{:S(2)}, u32[]{:S(2)}) collective-permute-start(bf16[2,128,384]{2,1,0:T(8,128)(2,1)S(1)} %get-tuple-element.53), channel_id=1, source_target_pairs={{0,2},{1,3},{2,0},{3,1},{4,6},{5,7},{6,4},{7,5},{8,10},{9,11},{10,... | collective-permute-start | bytes 589832 | tf_op jit(solution)/shard_map/ppermute | solution.py:786
  13.7 6.1 %collective-permute-start.4 = (bf16[2,112,384]{2,1,0:T(8,128)(2,1)S(1)}, bf16[2,112,384]{2,1,0:T(8,128)(2,1)S(1)}, u32[]{:S(2)}, u32[]{:S(2)}) collective-permute-start(bf16[2,112,384]{2,1,0:T(8,128)(2,1)S(1)} %pad_maximum_fusion.held_ref), channel_id=1, source_target_pairs={{0,8},{4,12},{8,0},{12,4},{16,24},{20,28},{24,16},{28,20},{1,9},{5... | collective-permute-start | bytes 516104 | tf_op jit(solution)/shard_map/ppermute | solution.py:778
  17.8 6.2 %collective-permute-start.8 = (bf16[4,64,384]{2,1,0:T(8,128)(2,1)S(1)}, bf16[4,64,384]{2,1,0:T(8,128)(2,1)S(1)}, u32[]{:S(2)}, u32[]{:S(2)}) collective-permute-start(bf16[4,64,384]{2,1,0:T(8,128)(2,1)S(1)} %shard_map.140.refs_0_), channel_id=1, source_target_pairs={{0,2},{1,3},{2,0},{3,1},{4,6},{5,7},{6,4},{7,5},{8,10},{9,11},{10,... | collective-permute-start | bytes 589832 | tf_op jit(solution)/shard_map/ppermute | solution.py:786
  19.8 8.1 %collective-permute-start.5 = (bf16[400,384]{1,0:T(8,128)(2,1)S(1)}, bf16[400,384]{1,0:T(8,128)(2,1)S(1)}, u32[]{:S(2)}, u32[]{:S(2)}) collective-permute-start(bf16[400,384]{1,0:T(8,128)(2,1)S(1)} %shard_map.137.near_ref), channel_id=1, source_target_pairs={{0,4},{4,0},{8,12},{12,8},{16,20},{20,16},{24,28},{28,24},{1,5},{5... | collective-permute-start | bytes 921608 | tf_op jit(solution)/shard_map/ppermute | solution.py:778
  23.9 8.4 %collective-permute-start.11 = (bf16[128,384]{1,0:T(8,128)(2,1)S(1)}, bf16[128,384]{1,0:T(8,128)(2,1)S(1)}, u32[]{:S(2)}, u32[]{:S(2)}) collective-permute-start(bf16[128,384]{1,0:T(8,128)(2,1)S(1)} %get-tuple-element.61), channel_id=1, source_target_pairs={{0,2},{1,3},{2,0},{3,1},{4,6},{5,7},{6,4},{7,5},{8,10},{9,11},{10,... | collective-permute-start | bytes 294920 | tf_op jit(solution)/shard_map/ppermute | solution.py:786
  25.4 6.9 %collective-permute-start.12 = (bf16[128,384]{1,0:T(8,128)(2,1)S(1)}, bf16[128,384]{1,0:T(8,128)(2,1)S(1)}, u32[]{:S(2)}, u32[]{:S(2)}) collective-permute-start(bf16[128,384]{1,0:T(8,128)(2,1)S(1)} %get-tuple-element.62), channel_id=1, source_target_pairs={{0,3},{1,2},{2,1},{3,0},{4,7},{5,6},{6,5},{7,4},{8,11},{9,10},{10,... | collective-permute-start | bytes 294920 | tf_op jit(solution)/shard_map/ppermute | solution.py:786
  31.2 5.7 %collective-permute-start.13 = (bf16[2,128,384]{2,1,0:T(8,128)(2,1)S(1)}, bf16[2,128,384]{2,1,0:T(8,128)(2,1)S(1)}, u32[]{:S(2)}, u32[]{:S(2)}) collective-permute-start(bf16[2,128,384]{2,1,0:T(8,128)(2,1)S(1)} %get-tuple-element.67), channel_id=1, source_target_pairs={{0,2},{1,3},{2,0},{3,1},{4,6},{5,7},{6,4},{7,5},{8,10},{9,11},{10,... | collective-permute-start | bytes 589832 | tf_op jit(solution)/shard_map/ppermute | solution.py:786
  37.6 10.7 %collective-permute-start.21 = (bf16[4,96,384]{2,1,0:T(8,128)(2,1)S(1)}, bf16[4,96,384]{2,1,0:T(8,128)(2,1)S(1)}, u32[]{:S(2)}, u32[]{:S(2)}) collective-permute-start(bf16[4,96,384]{2,1,0:T(8,128)(2,1)S(1)} %get-tuple-element.91), channel_id=1, source_target_pairs={{0,4},{4,0},{8,12},{12,8},{16,20},{20,16},{24,28},{28,24},{1,5},{5... | collective-permute-start | bytes 884744 | tf_op jit(solution)/shard_map/ppermute | solution.py:778
  38.9 7.4 %collective-permute-start.15 = (bf16[256,384]{1,0:T(8,128)(2,1)S(1)}, bf16[256,384]{1,0:T(8,128)(2,1)S(1)}, u32[]{:S(2)}, u32[]{:S(2)}) collective-permute-start(bf16[256,384]{1,0:T(8,128)(2,1)S(1)} %shard_map.146.refs_4_.awaited_ref.refs_1_), channel_id=1, source_target_pairs={{0,2},{1,3},{2,0},{3,1},{4,6},{5,7},{6,4},{7,5},{8,10},{9,11},{10,... | collective-permute-start | bytes 589832 | tf_op jit(solution)/shard_map/ppermute | solution.py:786
  42.5 5.8 %collective-permute-start.22 = (f32[16,384]{1,0:T(8,128)S(1)}, f32[16,384]{1,0:T(8,128)S(1)}, u32[]{:S(2)}, u32[]{:S(2)}) collective-permute-start(f32[16,384]{1,0:T(8,128)S(1)} %get-tuple-element.80), channel_id=1, source_target_pairs={{0,4},{4,0},{8,12},{12,8},{16,20},{20,16},{24,28},{28,24},{1,5},{5... | collective-permute-start | bytes 73736 | tf_op jit(solution)/shard_map/ppermute | solution.py:778
  43.5 6.7 %collective-permute-start.17 = (bf16[2,128,384]{2,1,0:T(8,128)(2,1)S(1)}, bf16[2,128,384]{2,1,0:T(8,128)(2,1)S(1)}, u32[]{:S(2)}, u32[]{:S(2)}) collective-permute-start(bf16[2,128,384]{2,1,0:T(8,128)(2,1)S(1)} %shard_map.150), channel_id=1, source_target_pairs={{0,2},{1,3},{2,0},{3,1},{4,6},{5,7},{6,4},{7,5},{8,10},{9,11},{10,... | collective-permute-start | bytes 589832 | tf_op jit(solution)/shard_map/ppermute | solution.py:786
  48.4 4.7 %collective-permute-start.23 = (bf16[2,64,384]{2,1,0:T(8,128)(2,1)S(1)}, bf16[2,64,384]{2,1,0:T(8,128)(2,1)S(1)}, u32[]{:S(2)}, u32[]{:S(2)}) collective-permute-start(bf16[2,64,384]{2,1,0:T(8,128)(2,1)S(1)} %get-tuple-element.82), channel_id=1, source_target_pairs={{0,8},{4,12},{8,0},{12,4},{16,24},{20,28},{24,16},{28,20},{1,9},{5... | collective-permute-start | bytes 294920 | tf_op jit(solution)/shard_map/ppermute | solution.py:778
  50.2 6.6 %collective-permute-start.18 = (bf16[3,64,384]{2,1,0:T(8,128)(2,1)S(1)}, bf16[3,64,384]{2,1,0:T(8,128)(2,1)S(1)}, u32[]{:S(2)}, u32[]{:S(2)}) collective-permute-start(bf16[3,64,384]{2,1,0:T(8,128)(2,1)S(1)} %shard_map.151), channel_id=1, source_target_pairs={{0,2},{1,3},{2,0},{3,1},{4,6},{5,7},{6,4},{7,5},{8,10},{9,11},{10,... | collective-permute-start | bytes 442376 | tf_op jit(solution)/shard_map/ppermute | solution.py:786
  52.0 4.7 %collective-permute-start.16 = (bf16[3,64,384]{2,1,0:T(8,128)(2,1)S(1)}, bf16[3,64,384]{2,1,0:T(8,128)(2,1)S(1)}, u32[]{:S(2)}, u32[]{:S(2)}) collective-permute-start(bf16[3,64,384]{2,1,0:T(8,128)(2,1)S(1)} %get-tuple-element.72), channel_id=1, source_target_pairs={{0,1},{1,0},{2,3},{3,2},{4,5},{5,4},{6,7},{7,6},{8,9},{9,8},{10,11... | collective-permute-start | bytes 442376 | tf_op jit(solution)/shard_map/ppermute | solution.py:786
  52.0 6.2 %collective-permute-start.19 = (bf16[3,64,384]{2,1,0:T(8,128)(2,1)S(1)}, bf16[3,64,384]{2,1,0:T(8,128)(2,1)S(1)}, u32[]{:S(2)}, u32[]{:S(2)}) collective-permute-start(bf16[3,64,384]{2,1,0:T(8,128)(2,1)S(1)} %get-tuple-element.75), channel_id=1, source_target_pairs={{0,3},{1,2},{2,1},{3,0},{4,7},{5,6},{6,5},{7,4},{8,11},{9,10},{10,... | collective-permute-start | bytes 442376 | tf_op jit(solution)/shard_map/ppermute | solution.py:786
  53.1 5.8 %collective-permute-start.24 = (bf16[64,384]{1,0:T(8,128)(2,1)S(1)}, bf16[64,384]{1,0:T(8,128)(2,1)S(1)}, u32[]{:S(2)}, u32[]{:S(2)}) collective-permute-start(bf16[64,384]{1,0:T(8,128)(2,1)S(1)} %get-tuple-element.94), channel_id=1, source_target_pairs={{0,16},{4,20},{8,24},{12,28},{16,0},{20,4},{24,8},{28,12},{1,17},{... | collective-permute-start | bytes 147464 | tf_op jit(solution)/shard_map/ppermute | solution.py:778
  56.8 5.3 %collective-permute-start.28 = (bf16[2,48,384]{2,1,0:T(8,128)(2,1)S(1)}, bf16[2,48,384]{2,1,0:T(8,128)(2,1)S(1)}, u32[]{:S(2)}, u32[]{:S(2)}) collective-permute-start(bf16[2,48,384]{2,1,0:T(8,128)(2,1)S(1)} %shard_map.158), channel_id=1, source_target_pairs={{0,16},{4,20},{8,24},{12,28},{16,0},{20,4},{24,8},{28,12},{1,17},{... | collective-permute-start | bytes 221192 | tf_op jit(solution)/shard_map/ppermute | solution.py:778
  58.9 8.2 %collective-permute-start.27 = (f32[16,384]{1,0:T(8,128)S(1)}, f32[16,384]{1,0:T(8,128)S(1)}, u32[]{:S(2)}, u32[]{:S(2)}) collective-permute-start(f32[16,384]{1,0:T(8,128)S(1)} %shard_map.156.refs_8_), channel_id=1, source_target_pairs={{0,3},{1,2},{2,1},{3,0},{4,7},{5,6},{6,5},{7,4},{8,11},{9,10},{10,... | collective-permute-start | bytes 73736 | tf_op jit(solution)/shard_map/ppermute | solution.py:786
  59.7 7.4 %collective-permute-start.26 = (f32[16,384]{1,0:T(8,128)S(1)}, f32[16,384]{1,0:T(8,128)S(1)}, u32[]{:S(2)}, u32[]{:S(2)}) collective-permute-start(f32[16,384]{1,0:T(8,128)S(1)} %shard_map.156.refs_8_), channel_id=1, source_target_pairs={{0,2},{1,3},{2,0},{3,1},{4,6},{5,7},{6,4},{7,5},{8,10},{9,11},{10,... | collective-permute-start | bytes 73736 | tf_op jit(solution)/shard_map/ppermute | solution.py:786
  60.9 6.2 %collective-permute-start.25 = (f32[16,384]{1,0:T(8,128)S(1)}, f32[16,384]{1,0:T(8,128)S(1)}, u32[]{:S(2)}, u32[]{:S(2)}) collective-permute-start(f32[16,384]{1,0:T(8,128)S(1)} %shard_map.156.refs_8_), channel_id=1, source_target_pairs={{0,1},{1,0},{2,3},{3,2},{4,5},{5,4},{6,7},{7,6},{8,9},{9,8},{10,11... | collective-permute-start | bytes 73736 | tf_op jit(solution)/shard_map/ppermute | solution.py:786
  61.0 6.1 %collective-permute-start.20 = (bf16[4,128,384]{2,1,0:T(8,128)(2,1)S(1)}, bf16[4,128,384]{2,1,0:T(8,128)(2,1)S(1)}, u32[]{:S(2)}, u32[]{:S(2)}) collective-permute-start(bf16[4,128,384]{2,1,0:T(8,128)(2,1)S(1)} %shard_map.152), channel_id=1, source_target_pairs={{0,1},{1,0},{2,3},{3,2},{4,5},{5,4},{6,7},{7,6},{8,9},{9,8},{10,11... | collective-permute-start | bytes 1179656 | tf_op jit(solution)/shard_map/ppermute | solution.py:786
  (12 other events, 46.8 us)

commit v13 on v11

--- a/solution.py
+++ b/solution.py
@@ -721,9 +721,8 @@
 
 
 def finish(kept_ref, came_ref, awaited_ref, taps_ref):
-    entries = kept_ref.shape[1] - TAP_PAD // 2
-    total = kept_ref[0, entries:].astype(jnp.float32)
-    taps_ref[...] = total + came_ref[entries:].astype(jnp.float32)
+    first = kept_ref.shape[1] - TAP_PAD // 2
+    taps_ref[...] = kept_ref[0, first:].astype(jnp.float32) + came_ref[...].astype(jnp.float32)
 
 
 def relay(keep_ref, came_ref, out_ref):
@@ -949,13 +948,15 @@
         ["vmem"] * 4 + ["any"],
     )(panels[:4], panels_came, tap_keep, taps_came, back_blocks[0])
     panels = (kept.astype(f32) + swapped(sent, 2).astype(f32)).astype(low)
-    (arrived,) = call_kernel(mark, (shape((8, LANES), f32),), ["any"] * 2)(*grad_blocks[2:])
-    panels_last = swapped(panels[1], 4)
+    taps_last = swapped(panels[1, entries:], 4)
+    panels_last = swapped(panels[1, :entries], 4)
+    (arrived,) = call_kernel(mark, (shape((8, LANES), f32),), ["any"] * 3)(
+        *grad_blocks[2:], taps_last
+    )
     (tap_sums,) = call_kernel(
         finish, (shape((TAP_PAD // 2, width), f32),), ["vmem"] * 2 + ["any"]
-    )(panels, panels_last, arrived)
-    total = panels[0].astype(f32) + panels_last.astype(f32)
-    grad_out_weight = total[:entries].T
+    )(panels, taps_last, arrived)
+    grad_out_weight = (panels[0, :entries].astype(f32) + panels_last.astype(f32)).T
     tap_blocks = traded([tap_sums] * N_CTX)
     grad_queries, grad_keys, grad_values, block_output, grad_input, grad_taps = call_kernel(
         unpack,

time: 66.8 us -> 66.4 us (level)
    ppermute x21, waiting for transfers between devices: 11 us -> 9.7 us  [crossed(): return lax.ppermute(array, 'ctx', [(i, i ^ apart) for i in range(N_CTX)])]
    ppermute x7 -> x8, waiting for transfers between devices: 5.18 us -> 6 us  [swapped(): return lax.ppermute(array, 'dp', [(i, i ^ bit) for i in range(N_DP)])]
    ppermute x7 -> x8, starting transfers between devices: 12.5 us -> 12.6 us  [swapped(): return lax.ppermute(array, 'dp', [(i, i ^ bit) for i in range(N_DP)])]
  transfers between devices with their start and end apart: 28 -> 29, of which waited for: 14 -> 13; matrix products, arithmetic and copies ran while one was open for 1% -> 1% of each run, Pallas kernels for 24% -> 24%
where the time goes in v13:
time: 66.4 us; the launch traced here: 66.2 us
  starting transfers between devices  29.4 us (44%)
  Pallas kernels  19.4 us (29%)
  waiting for transfers between devices  15.7 us (24%)
  between operations  0.86 us (1%)
  other arithmetic  0.75 us (1%)
    ppermute x21, starting transfers between devices, crossed(): return lax.ppermute(array, 'ctx', [(i, i ^ apart) for i in range(N_CTX)])  16.8 us
    ppermute x8, starting transfers between devices, swapped(): return lax.ppermute(array, 'dp', [(i, i ^ bit) for i in range(N_DP)])  12.6 us
    ppermute x21, waiting for transfers between devices, crossed(): return lax.ppermute(array, 'ctx', [(i, i ^ apart) for i in range(N_CTX)])  9.7 us
    ppermute x8, waiting for transfers between devices, swapped(): return lax.ppermute(array, 'dp', [(i, i ^ bit) for i in range(N_DP)])  6 us
    pallas_call x1, Pallas kernels, per_device(): call_kernel(backward, (pair_block,) * 2 + (shape((2, utts * frames, width...  3.58 us
    pallas_call x1, Pallas kernels, per_device(): call_kernel(forward, (channel_block,) * 2 + (shape((2, utts * frames, wid...  3.22 us
    pallas_call x1, Pallas kernels, per_device(): call_kernel(attend, (shape((N_CTX, frames, half), low),), ['smem'] + ['vm...  2.77 us
    pallas_call x1, Pallas kernels, per_device(): call_kernel(make_taps, (tap_block,) * 2, ['vmem'] * 2 + ['any'], scratch=...  2.08 us
  transfers between devices with their start and end apart: 29, of which 13 were waited for; matrix products, arithmetic and copies ran while one was open for 1% of the time, Pallas kernels for 24%

profile of v13, /device:TPU:0, one launch (start us, length us, event | category | flops | bytes accessed | tf_op | source)
XLA Modules:
  0.0 66.2 jit_solution(10457725743778408299)
XLA Ops:
  0.7 2.0 %shard_map.135 = (bf16[3,64,384]{2,1,0:T(8,128)(2,1)}, bf16[3,64,384]{2,1,0:T(8,128)(2,1)}, bf16[3,64,384]{2,1,0:T(8,128)(2,1)}, bf16[3,64,384]{2,1,0:T(8,128)(2,1)}) custom-call(bf16[2,64,768]{2,1,0:T(8,128)(2,1)} %query_ref.1, bf16[2,64,768]{2,1,0:T(8,128)(2,1)} %key_ref.1, bf16[2,64,768]{2,1,0:T(8,128)(2,1)} %value_ref.1), custom_call_target="tpu_custom_call" | custom-call | flops 1150000000 | tf_op jit(solution)/shard_map/pallas_call | solution.py:807
  3.2 2.6 %collective-permute-start.1 = (bf16[3,64,384]{2,1,0:T(8,128)(2,1)}, bf16[3,64,384]{2,1,0:T(8,128)(2,1)S(1)}, u32[]{:S(2)}, u32[]{:S(2)}) collective-permute-start(bf16[3,64,384]{2,1,0:T(8,128)(2,1)} %get-tuple-element.49), channel_id=1, source_target_pairs={{0,2},{1,3},{2,0},{3,1},{4,6},{5,7},{6,4},{7,5},{8,10},{9,11},{10,... | collective-permute-start | bytes 442376 | tf_op jit(solution)/shard_map/ppermute | solution.py:783
  5.9 2.8 %collective-permute-start.3 = (bf16[1,112,384]{2,1,0:T(8,128)(2,1)S(1)}, bf16[1,112,384]{2,1,0:T(8,128)(2,1)S(1)}, u32[]{:S(2)}, u32[]{:S(2)}) collective-permute-start(bf16[1,112,384]{2,1,0:T(8,128)(2,1)S(1)} %shard_map.136), channel_id=1, source_target_pairs={{0,16},{4,20},{8,24},{12,28},{16,0},{20,4},{24,8},{28,12},{1,17},{... | collective-permute-start | bytes 258056 | tf_op jit(solution)/shard_map/ppermute | solution.py:775
  8.8 1.9 %collective-permute-done.1.refs_2_.awaited_ref = bf16[3,64,384]{2,1,0:T(8,128)(2,1)S(1)} collective-permute-done((bf16[3,64,384]{2,1,0:T(8,128)(2,1)}, bf16[3,64,384]{2,1,0:T(8,128)(2,1)S(1)}, u32[]{:S(2)}, u32[]{:S(2)}) %collective-permute-start.1) | collective-permute-done | bytes 147488 | tf_op jit(solution)/shard_map/ppermute | solution.py:783
  11.0 2.0 %collective-permute-start.6 = (bf16[2,128,384]{2,1,0:T(8,128)(2,1)S(1)}, bf16[2,128,384]{2,1,0:T(8,128)(2,1)S(1)}, u32[]{:S(2)}, u32[]{:S(2)}) collective-permute-start(bf16[2,128,384]{2,1,0:T(8,128)(2,1)S(1)} %get-tuple-element.51), channel_id=1, source_target_pairs={{0,2},{1,3},{2,0},{3,1},{4,6},{5,7},{6,4},{7,5},{8,10},{9,11},{10,... | collective-permute-start | bytes 589832 | tf_op jit(solution)/shard_map/ppermute | solution.py:783
  14.7 2.8 %shard_map.138.refs_0_ = bf16[4,64,384]{2,1,0:T(8,128)(2,1)S(1)} custom-call(s32[2]{0:T(128)S(1)} %copy-done.4, bf16[3,64,384]{2,1,0:T(8,128)(2,1)S(1)} %copy-done.5, bf16[3,64,384]{2,1,0:T(8,128)(2,1)S(1)} %collective-permute-done.awaited_ref.refs_1_, bf16[3,64,384]{2,1,0:T(8,128)(2,1)S(1)} %collective-permute-done.1.refs_2_.awaited_ref, ...), custom_call_target="tpu_custom_call" | custom-call | flops 1150000000 | tf_op jit(solution)/shard_map/pallas_call | solution.py:839
  17.8 1.8 %collective-permute-start.8 = (bf16[4,64,384]{2,1,0:T(8,128)(2,1)S(1)}, bf16[4,64,384]{2,1,0:T(8,128)(2,1)S(1)}, u32[]{:S(2)}, u32[]{:S(2)}) collective-permute-start(bf16[4,64,384]{2,1,0:T(8,128)(2,1)S(1)} %shard_map.140.refs_0_), channel_id=1, source_target_pairs={{0,2},{1,3},{2,0},{3,1},{4,6},{5,7},{6,4},{7,5},{8,10},{9,11},{10,... | collective-permute-start | bytes 589832 | tf_op jit(solution)/shard_map/ppermute | solution.py:783
  19.8 1.4 %collective-permute-start.5 = (bf16[400,384]{1,0:T(8,128)(2,1)S(1)}, bf16[400,384]{1,0:T(8,128)(2,1)S(1)}, u32[]{:S(2)}, u32[]{:S(2)}) collective-permute-start(bf16[400,384]{1,0:T(8,128)(2,1)S(1)} %shard_map.137.near_ref), channel_id=1, source_target_pairs={{0,4},{4,0},{8,12},{12,8},{16,20},{20,16},{24,28},{28,24},{1,5},{5... | collective-permute-start | bytes 921608 | tf_op jit(solution)/shard_map/ppermute | solution.py:775
  21.9 2.1 %collective-permute-done.8.refs_2_ = bf16[4,64,384]{2,1,0:T(8,128)(2,1)S(1)} collective-permute-done((bf16[4,64,384]{2,1,0:T(8,128)(2,1)S(1)}, bf16[4,64,384]{2,1,0:T(8,128)(2,1)S(1)}, u32[]{:S(2)}, u32[]{:S(2)}) %collective-permute-start.8) | collective-permute-done | bytes 196640 | tf_op jit(solution)/shard_map/ppermute | solution.py:783
  23.9 1.5 %collective-permute-start.11 = (bf16[128,384]{1,0:T(8,128)(2,1)S(1)}, bf16[128,384]{1,0:T(8,128)(2,1)S(1)}, u32[]{:S(2)}, u32[]{:S(2)}) collective-permute-start(bf16[128,384]{1,0:T(8,128)(2,1)S(1)} %get-tuple-element.59), channel_id=1, source_target_pairs={{0,2},{1,3},{2,0},{3,1},{4,6},{5,7},{6,4},{7,5},{8,10},{9,11},{10,... | collective-permute-start | bytes 294920 | tf_op jit(solution)/shard_map/ppermute | solution.py:783
  25.8 2.1 %collective-permute-done.5.other_ref = bf16[400,384]{1,0:T(8,128)(2,1)S(1)} collective-permute-done((bf16[400,384]{1,0:T(8,128)(2,1)S(1)}, bf16[400,384]{1,0:T(8,128)(2,1)S(1)}, u32[]{:S(2)}, u32[]{:S(2)}) %collective-permute-start.5) | collective-permute-done | bytes 307232 | tf_op jit(solution)/shard_map/ppermute | solution.py:775
  27.9 3.2 %shard_map.142 = (bf16[2,64,384]{2,1,0:T(8,128)(2,1)S(1)}, bf16[2,64,384]{2,1,0:T(8,128)(2,1)S(1)}, bf16[2,128,384]{2,1,0:T(8,128)(2,1)S(1)}, bf16[2,4,64,768]{3...) custom-call(s32[2]{0:T(128)S(1)} %copy-done.4, ...), custom_call_target="tpu_custom_call" | custom-call | flops 3680000000 | tf_op jit(solution)/shard_map/pallas_call | solution.py:849
  32.3 3.6 %shard_map.144 = (bf16[2,2,64,384]{3,2,1,0:T(8,128)(2,1)S(1)}, bf16[2,2,64,384]{3,2,1,0:T(8,128)(2,1)S(1)}, bf16[2,128,384]{2,1,0:T(8,128)(2,1)S(1)}, bf16[2,256...) custom-call(s32[2]{0:T(128)S(1)} %copy-done.4, ...), custom_call_target="tpu_custom_call" | custom-call | flops 5980000256 | tf_op jit(solution)/shard_map/pallas_call | solution.py:883
  38.9 1.5 %collective-permute-start.15 = (bf16[256,384]{1,0:T(8,128)(2,1)S(1)}, bf16[256,384]{1,0:T(8,128)(2,1)S(1)}, u32[]{:S(2)}, u32[]{:S(2)}) collective-permute-start(bf16[256,384]{1,0:T(8,128)(2,1)S(1)} %shard_map.146.refs_4_.awaited_ref.refs_1_), channel_id=1, source_target_pairs={{0,2},{1,3},{2,0},{3,1},{4,6},{5,7},{6,4},{7,5},{8,10},{9,11},{10,... | collective-permute-start | bytes 589832 | tf_op jit(solution)/shard_map/ppermute | solution.py:783
  40.4 2.1 %shard_map.148 = (f32[16,384]{1,0:T(8,128)S(1)}, f32[16,384]{1,0:T(8,128)S(1)}) custom-call(f32[6,288,128]{2,1,0:T(8,128)S(1)} %get-tuple-element.66.masked_ref, f32[6,288,128]{2,1,0:T(8,128)S(1)} %get-tuple-element.67.cotangent_ref, bf16[256,384]{1,0:T(8,128)(2,1)S(1)} %shard_map.146.refs_4_.awaited_ref.refs_1_), custom_call_target="tpu_custom_call" | custom-call | flops 1150000000 | tf_op jit(solution)/shard_map/pallas_call | solution.py:915
  46.3 2.0 %shard_map.149 = (bf16[3,64,384]{2,1,0:T(8,128)(2,1)S(1)}, bf16[3,64,384]{2,1,0:T(8,128)(2,1)S(1)}, bf16[3,64,384]{2,1,0:T(8,128)(2,1)S(1)}, bf16[3,64,384]{2,1,0:T(8,128)(2,1)S(1)}) custom-call(bf16[6,256,256]{2,1,0:T(8,128)(2,1)S(1)} %shard_map.147.weight_ref, bf16[2,256,384]{2,1,0:T(8,128)(2,1)S(1)} %get-tuple-element.63.keep_ref, ...), custom_call_target="tpu_custom_call" | custom-call | flops 2529999872 | tf_op jit(solution)/shard_map/pallas_call | solution.py:928
  48.4 1.3 %collective-permute-start.23 = (bf16[2,112,384]{2,1,0:T(8,128)(2,1)S(1)}, bf16[2,112,384]{2,1,0:T(8,128)(2,1)S(1)}, u32[]{:S(2)}, u32[]{:S(2)}) collective-permute-start(bf16[2,112,384]{2,1,0:T(8,128)(2,1)S(1)} %get-tuple-element.80), channel_id=1, source_target_pairs={{0,8},{4,12},{8,0},{12,4},{16,24},{20,28},{24,16},{28,20},{1,9},{5... | collective-permute-start | bytes 516104 | tf_op jit(solution)/shard_map/ppermute | solution.py:775
  50.2 1.8 %collective-permute-start.18 = (bf16[3,64,384]{2,1,0:T(8,128)(2,1)S(1)}, bf16[3,64,384]{2,1,0:T(8,128)(2,1)S(1)}, u32[]{:S(2)}, u32[]{:S(2)}) collective-permute-start(bf16[3,64,384]{2,1,0:T(8,128)(2,1)S(1)} %shard_map.151), channel_id=1, source_target_pairs={{0,2},{1,3},{2,0},{3,1},{4,6},{5,7},{6,4},{7,5},{8,10},{9,11},{10,... | collective-permute-start | bytes 442376 | tf_op jit(solution)/shard_map/ppermute | solution.py:783
  52.5 1.4 %collective-permute-done.23 = bf16[2,112,384]{2,1,0:T(8,128)(2,1)S(1)} collective-permute-done((bf16[2,112,384]{2,1,0:T(8,128)(2,1)S(1)}, bf16[2,112,384]{2,1,0:T(8,128)(2,1)S(1)}, u32[]{:S(2)}, u32[]{:S(2)}) %collective-permute-start.23) | collective-permute-done | bytes 172064 | tf_op jit(solution)/shard_map/ppermute | solution.py:775
  53.9 3.7 %collective-permute-start.24 = (bf16[16,384]{1,0:T(8,128)(2,1)S(1)}, bf16[16,384]{1,0:T(8,128)(2,1)S(1)}, u32[]{:S(2)}, u32[]{:S(2)}) collective-permute-start(bf16[16,384]{1,0:T(8,128)(2,1)S(1)} %slice_bitcast_fusion.2), channel_id=1, source_target_pairs={{0,16},{4,20},{8,24},{12,28},{16,0},{20,4},{24,8},{28,12},{1,17},{... | collective-permute-start | bytes 36872 | tf_op jit(solution)/shard_map/ppermute | solution.py:775
  57.7 1.7 %collective-permute-done.19.refs_1_.refs_3_ = bf16[3,64,384]{2,1,0:T(8,128)(2,1)S(1)} collective-permute-done((bf16[3,64,384]{2,1,0:T(8,128)(2,1)S(1)}, bf16[3,64,384]{2,1,0:T(8,128)(2,1)S(1)}, u32[]{:S(2)}, u32[]{:S(2)}) %collective-permute-start.19) | collective-permute-done | bytes 147488 | tf_op jit(solution)/shard_map/ppermute | solution.py:783
  59.4 1.6 %collective-permute-start.27 = (f32[16,384]{1,0:T(8,128)S(1)}, f32[16,384]{1,0:T(8,128)S(1)}, u32[]{:S(2)}, u32[]{:S(2)}) collective-permute-start(f32[16,384]{1,0:T(8,128)S(1)} %shard_map.156.refs_8_), channel_id=1, source_target_pairs={{0,3},{1,2},{2,1},{3,0},{4,7},{5,6},{6,5},{7,4},{8,11},{9,10},{10,... | collective-permute-start | bytes 73736 | tf_op jit(solution)/shard_map/ppermute | solution.py:783
  61.4 1.5 %collective-permute-done.28 = bf16[96,384]{1,0:T(8,128)(2,1)S(1)} collective-permute-done((bf16[96,384]{1,0:T(8,128)(2,1)S(1)}, bf16[96,384]{1,0:T(8,128)(2,1)S(1)}, u32[]{:S(2)}, u32[]{:S(2)}) %collective-permute-start.28) | collective-permute-done | bytes 73760 | tf_op jit(solution)/shard_map/ppermute | solution.py:775
  64.9 1.3 %shard_map.157 = (bf16[2,64,768]{2,1,0:T(8,128)(2,1)}, bf16[2,64,768]{2,1,0:T(8,128)(2,1)}, bf16[2,64,768]{2,1,0:T(8,128)(2,1)}, bf16[2,64,1536]{2,1,0:T(8,128)(...) custom-call(bf16[3,64,384]{2,1,0:T(8,128)(2,1)S(1)} %get-tuple-element.69.awaited_ref.refs_0_, ...), custom_call_target="tpu_custom_call" | custom-call | flops 1150000000 | tf_op jit(solution)/shard_map/pallas_call | solution.py:961
  (75 shorter events, 15.8 us)
Async XLA Ops:
  3.2 7.5 %collective-permute-start.1 = (bf16[3,64,384]{2,1,0:T(8,128)(2,1)}, bf16[3,64,384]{2,1,0:T(8,128)(2,1)S(1)}, u32[]{:S(2)}, u32[]{:S(2)}) collective-permute-start(bf16[3,64,384]{2,1,0:T(8,128)(2,1)} %get-tuple-element.49), channel_id=1, source_target_pairs={{0,2},{1,3},{2,0},{3,1},{4,6},{5,7},{6,4},{7,5},{8,10},{9,11},{10,... | collective-permute-start | bytes 442376 | tf_op jit(solution)/shard_map/ppermute | solution.py:783
  5.8 8.9 %collective-permute-start.2 = (bf16[3,64,384]{2,1,0:T(8,128)(2,1)}, bf16[3,64,384]{2,1,0:T(8,128)(2,1)S(1)}, u32[]{:S(2)}, u32[]{:S(2)}) collective-permute-start(bf16[3,64,384]{2,1,0:T(8,128)(2,1)} %get-tuple-element.50), channel_id=1, source_target_pairs={{0,3},{1,2},{2,1},{3,0},{4,7},{5,6},{6,5},{7,4},{8,11},{9,10},{10,... | collective-permute-start | bytes 442376 | tf_op jit(solution)/shard_map/ppermute | solution.py:783
  5.9 7.7 %collective-permute-start.3 = (bf16[1,112,384]{2,1,0:T(8,128)(2,1)S(1)}, bf16[1,112,384]{2,1,0:T(8,128)(2,1)S(1)}, u32[]{:S(2)}, u32[]{:S(2)}) collective-permute-start(bf16[1,112,384]{2,1,0:T(8,128)(2,1)S(1)} %shard_map.136), channel_id=1, source_target_pairs={{0,16},{4,20},{8,24},{12,28},{16,0},{20,4},{24,8},{28,12},{1,17},{... | collective-permute-start | bytes 258056 | tf_op jit(solution)/shard_map/ppermute | solution.py:775
  11.0 6.8 %collective-permute-start.6 = (bf16[2,128,384]{2,1,0:T(8,128)(2,1)S(1)}, bf16[2,128,384]{2,1,0:T(8,128)(2,1)S(1)}, u32[]{:S(2)}, u32[]{:S(2)}) collective-permute-start(bf16[2,128,384]{2,1,0:T(8,128)(2,1)S(1)} %get-tuple-element.51), channel_id=1, source_target_pairs={{0,2},{1,3},{2,0},{3,1},{4,6},{5,7},{6,4},{7,5},{8,10},{9,11},{10,... | collective-permute-start | bytes 589832 | tf_op jit(solution)/shard_map/ppermute | solution.py:783
  13.7 6.1 %collective-permute-start.4 = (bf16[2,112,384]{2,1,0:T(8,128)(2,1)S(1)}, bf16[2,112,384]{2,1,0:T(8,128)(2,1)S(1)}, u32[]{:S(2)}, u32[]{:S(2)}) collective-permute-start(bf16[2,112,384]{2,1,0:T(8,128)(2,1)S(1)} %pad_maximum_fusion.held_ref), channel_id=1, source_target_pairs={{0,8},{4,12},{8,0},{12,4},{16,24},{20,28},{24,16},{28,20},{1,9},{5... | collective-permute-start | bytes 516104 | tf_op jit(solution)/shard_map/ppermute | solution.py:775
  17.8 6.2 %collective-permute-start.8 = (bf16[4,64,384]{2,1,0:T(8,128)(2,1)S(1)}, bf16[4,64,384]{2,1,0:T(8,128)(2,1)S(1)}, u32[]{:S(2)}, u32[]{:S(2)}) collective-permute-start(bf16[4,64,384]{2,1,0:T(8,128)(2,1)S(1)} %shard_map.140.refs_0_), channel_id=1, source_target_pairs={{0,2},{1,3},{2,0},{3,1},{4,6},{5,7},{6,4},{7,5},{8,10},{9,11},{10,... | collective-permute-start | bytes 589832 | tf_op jit(solution)/shard_map/ppermute | solution.py:783
  19.8 8.1 %collective-permute-start.5 = (bf16[400,384]{1,0:T(8,128)(2,1)S(1)}, bf16[400,384]{1,0:T(8,128)(2,1)S(1)}, u32[]{:S(2)}, u32[]{:S(2)}) collective-permute-start(bf16[400,384]{1,0:T(8,128)(2,1)S(1)} %shard_map.137.near_ref), channel_id=1, source_target_pairs={{0,4},{4,0},{8,12},{12,8},{16,20},{20,16},{24,28},{28,24},{1,5},{5... | collective-permute-start | bytes 921608 | tf_op jit(solution)/shard_map/ppermute | solution.py:775
  21.3 4.5 %collective-permute-start.10 = (bf16[3,128,384]{2,1,0:T(8,128)(2,1)S(1)}, bf16[3,128,384]{2,1,0:T(8,128)(2,1)S(1)}, u32[]{:S(2)}, u32[]{:S(2)}) collective-permute-start(bf16[3,128,384]{2,1,0:T(8,128)(2,1)S(1)} %shard_map.141), channel_id=1, source_target_pairs={{0,1},{1,0},{2,3},{3,2},{4,5},{5,4},{6,7},{7,6},{8,9},{9,8},{10,11... | collective-permute-start | bytes 884744 | tf_op jit(solution)/shard_map/ppermute | solution.py:783
  21.4 4.1 %collective-permute-start.7 = (bf16[4,64,384]{2,1,0:T(8,128)(2,1)S(1)}, bf16[4,64,384]{2,1,0:T(8,128)(2,1)S(1)}, u32[]{:S(2)}, u32[]{:S(2)}) collective-permute-start(bf16[4,64,384]{2,1,0:T(8,128)(2,1)S(1)} %shard_map.140.refs_0_), channel_id=1, source_target_pairs={{0,1},{1,0},{2,3},{3,2},{4,5},{5,4},{6,7},{7,6},{8,9},{9,8},{10,11... | collective-permute-start | bytes 589832 | tf_op jit(solution)/shard_map/ppermute | solution.py:783
  23.9 4.0 %collective-permute-start.9 = (bf16[4,64,384]{2,1,0:T(8,128)(2,1)S(1)}, bf16[4,64,384]{2,1,0:T(8,128)(2,1)S(1)}, u32[]{:S(2)}, u32[]{:S(2)}) collective-permute-start(bf16[4,64,384]{2,1,0:T(8,128)(2,1)S(1)} %collective-permute-done.8.refs_2_), channel_id=1, source_target_pairs={{0,1},{1,0},{2,3},{3,2},{4,5},{5,4},{6,7},{7,6},{8,9},{9,8},{10,11... | collective-permute-start | bytes 589832 | tf_op jit(solution)/shard_map/ppermute | solution.py:783
  23.9 8.4 %collective-permute-start.11 = (bf16[128,384]{1,0:T(8,128)(2,1)S(1)}, bf16[128,384]{1,0:T(8,128)(2,1)S(1)}, u32[]{:S(2)}, u32[]{:S(2)}) collective-permute-start(bf16[128,384]{1,0:T(8,128)(2,1)S(1)} %get-tuple-element.59), channel_id=1, source_target_pairs={{0,2},{1,3},{2,0},{3,1},{4,6},{5,7},{6,4},{7,5},{8,10},{9,11},{10,... | collective-permute-start | bytes 294920 | tf_op jit(solution)/shard_map/ppermute | solution.py:783
  25.4 6.9 %collective-permute-start.12 = (bf16[128,384]{1,0:T(8,128)(2,1)S(1)}, bf16[128,384]{1,0:T(8,128)(2,1)S(1)}, u32[]{:S(2)}, u32[]{:S(2)}) collective-permute-start(bf16[128,384]{1,0:T(8,128)(2,1)S(1)} %get-tuple-element.60), channel_id=1, source_target_pairs={{0,3},{1,2},{2,1},{3,0},{4,7},{5,6},{6,5},{7,4},{8,11},{9,10},{10,... | collective-permute-start | bytes 294920 | tf_op jit(solution)/shard_map/ppermute | solution.py:783
  31.2 5.7 %collective-permute-start.13 = (bf16[2,128,384]{2,1,0:T(8,128)(2,1)S(1)}, bf16[2,128,384]{2,1,0:T(8,128)(2,1)S(1)}, u32[]{:S(2)}, u32[]{:S(2)}) collective-permute-start(bf16[2,128,384]{2,1,0:T(8,128)(2,1)S(1)} %get-tuple-element.65), channel_id=1, source_target_pairs={{0,2},{1,3},{2,0},{3,1},{4,6},{5,7},{6,4},{7,5},{8,10},{9,11},{10,... | collective-permute-start | bytes 589832 | tf_op jit(solution)/shard_map/ppermute | solution.py:783
  37.6 10.7 %collective-permute-start.21 = (bf16[4,96,384]{2,1,0:T(8,128)(2,1)S(1)}, bf16[4,96,384]{2,1,0:T(8,128)(2,1)S(1)}, u32[]{:S(2)}, u32[]{:S(2)}) collective-permute-start(bf16[4,96,384]{2,1,0:T(8,128)(2,1)S(1)} %get-tuple-element.87), channel_id=1, source_target_pairs={{0,4},{4,0},{8,12},{12,8},{16,20},{20,16},{24,28},{28,24},{1,5},{5... | collective-permute-start | bytes 884744 | tf_op jit(solution)/shard_map/ppermute | solution.py:775
  38.9 7.4 %collective-permute-start.15 = (bf16[256,384]{1,0:T(8,128)(2,1)S(1)}, bf16[256,384]{1,0:T(8,128)(2,1)S(1)}, u32[]{:S(2)}, u32[]{:S(2)}) collective-permute-start(bf16[256,384]{1,0:T(8,128)(2,1)S(1)} %shard_map.146.refs_4_.awaited_ref.refs_1_), channel_id=1, source_target_pairs={{0,2},{1,3},{2,0},{3,1},{4,6},{5,7},{6,4},{7,5},{8,10},{9,11},{10,... | collective-permute-start | bytes 589832 | tf_op jit(solution)/shard_map/ppermute | solution.py:783
  42.5 5.8 %collective-permute-start.22 = (f32[16,384]{1,0:T(8,128)S(1)}, f32[16,384]{1,0:T(8,128)S(1)}, u32[]{:S(2)}, u32[]{:S(2)}) collective-permute-start(f32[16,384]{1,0:T(8,128)S(1)} %get-tuple-element.78), channel_id=1, source_target_pairs={{0,4},{4,0},{8,12},{12,8},{16,20},{20,16},{24,28},{28,24},{1,5},{5... | collective-permute-start | bytes 73736 | tf_op jit(solution)/shard_map/ppermute | solution.py:775
  43.5 6.7 %collective-permute-start.17 = (bf16[2,128,384]{2,1,0:T(8,128)(2,1)S(1)}, bf16[2,128,384]{2,1,0:T(8,128)(2,1)S(1)}, u32[]{:S(2)}, u32[]{:S(2)}) collective-permute-start(bf16[2,128,384]{2,1,0:T(8,128)(2,1)S(1)} %shard_map.150), channel_id=1, source_target_pairs={{0,2},{1,3},{2,0},{3,1},{4,6},{5,7},{6,4},{7,5},{8,10},{9,11},{10,... | collective-permute-start | bytes 589832 | tf_op jit(solution)/shard_map/ppermute | solution.py:783
  48.4 5.5 %collective-permute-start.23 = (bf16[2,112,384]{2,1,0:T(8,128)(2,1)S(1)}, bf16[2,112,384]{2,1,0:T(8,128)(2,1)S(1)}, u32[]{:S(2)}, u32[]{:S(2)}) collective-permute-start(bf16[2,112,384]{2,1,0:T(8,128)(2,1)S(1)} %get-tuple-element.80), channel_id=1, source_target_pairs={{0,8},{4,12},{8,0},{12,4},{16,24},{20,28},{24,16},{28,20},{1,9},{5... | collective-permute-start | bytes 516104 | tf_op jit(solution)/shard_map/ppermute | solution.py:775
  50.2 7.5 %collective-permute-start.18 = (bf16[3,64,384]{2,1,0:T(8,128)(2,1)S(1)}, bf16[3,64,384]{2,1,0:T(8,128)(2,1)S(1)}, u32[]{:S(2)}, u32[]{:S(2)}) collective-permute-start(bf16[3,64,384]{2,1,0:T(8,128)(2,1)S(1)} %shard_map.151), channel_id=1, source_target_pairs={{0,2},{1,3},{2,0},{3,1},{4,6},{5,7},{6,4},{7,5},{8,10},{9,11},{10,... | collective-permute-start | bytes 442376 | tf_op jit(solution)/shard_map/ppermute | solution.py:783
  52.0 7.4 %collective-permute-start.19 = (bf16[3,64,384]{2,1,0:T(8,128)(2,1)S(1)}, bf16[3,64,384]{2,1,0:T(8,128)(2,1)S(1)}, u32[]{:S(2)}, u32[]{:S(2)}) collective-permute-start(bf16[3,64,384]{2,1,0:T(8,128)(2,1)S(1)} %get-tuple-element.73), channel_id=1, source_target_pairs={{0,3},{1,2},{2,1},{3,0},{4,7},{5,6},{6,5},{7,4},{8,11},{9,10},{10,... | collective-permute-start | bytes 442376 | tf_op jit(solution)/shard_map/ppermute | solution.py:783
  52.2 12.7 %collective-permute-start.20 = (bf16[4,128,384]{2,1,0:T(8,128)(2,1)S(1)}, bf16[4,128,384]{2,1,0:T(8,128)(2,1)S(1)}, u32[]{:S(2)}, u32[]{:S(2)}) collective-permute-start(bf16[4,128,384]{2,1,0:T(8,128)(2,1)S(1)} %shard_map.152), channel_id=1, source_target_pairs={{0,1},{1,0},{2,3},{3,2},{4,5},{5,4},{6,7},{7,6},{8,9},{9,8},{10,11... | collective-permute-start | bytes 1179656 | tf_op jit(solution)/shard_map/ppermute | solution.py:783
  53.9 5.5 %collective-permute-start.24 = (bf16[16,384]{1,0:T(8,128)(2,1)S(1)}, bf16[16,384]{1,0:T(8,128)(2,1)S(1)}, u32[]{:S(2)}, u32[]{:S(2)}) collective-permute-start(bf16[16,384]{1,0:T(8,128)(2,1)S(1)} %slice_bitcast_fusion.2), channel_id=1, source_target_pairs={{0,16},{4,20},{8,24},{12,28},{16,0},{20,4},{24,8},{28,12},{1,17},{... | collective-permute-start | bytes 36872 | tf_op jit(solution)/shard_map/ppermute | solution.py:775
  57.7 5.3 %collective-permute-start.28 = (bf16[96,384]{1,0:T(8,128)(2,1)S(1)}, bf16[96,384]{1,0:T(8,128)(2,1)S(1)}, u32[]{:S(2)}, u32[]{:S(2)}) collective-permute-start(bf16[96,384]{1,0:T(8,128)(2,1)S(1)} %slice_bitcast_fusion), channel_id=1, source_target_pairs={{0,16},{4,20},{8,24},{12,28},{16,0},{20,4},{24,8},{28,12},{1,17},{... | collective-permute-start | bytes 221192 | tf_op jit(solution)/shard_map/ppermute | solution.py:775
  59.4 4.2 %collective-permute-start.27 = (f32[16,384]{1,0:T(8,128)S(1)}, f32[16,384]{1,0:T(8,128)S(1)}, u32[]{:S(2)}, u32[]{:S(2)}) collective-permute-start(f32[16,384]{1,0:T(8,128)S(1)} %shard_map.156.refs_8_), channel_id=1, source_target_pairs={{0,3},{1,2},{2,1},{3,0},{4,7},{5,6},{6,5},{7,4},{8,11},{9,10},{10,... | collective-permute-start | bytes 73736 | tf_op jit(solution)/shard_map/ppermute | solution.py:783
  (11 other events, 39.7 us)

commit v14 on v13

--- a/solution.py
+++ b/solution.py
@@ -816,7 +816,7 @@
         pack_weights,
         (shape((1, entries + TAP_PAD // 2, width), low),),
         ["vmem"] * 2 + ["any"],
-    )(out_weight.T, conv_weight, packed[1])
+    )(out_weight.T, conv_weight, blocks[1])
     shard = jnp.concatenate([shard, swapped(shard, 4)], axis=0)
     (shard,) = call_kernel(
         pack_near, (shape((4 * entries + TAP_PAD // 2, width), low),), ["vmem"] * 2

time: 66.4 us -> 69.6 us (1.048)
  waiting for transfers between devices: 15.7 us -> 18 us
  local copies, waits for them, and re-layouts: 0.11 us -> 1.01 us
    ppermute x21, waiting for transfers between devices: 9.7 us -> 14.1 us  [crossed(): return lax.ppermute(array, 'ctx', [(i, i ^ apart) for i in range(N_CTX)])]
    ppermute x8, waiting for transfers between devices: 6 us -> 3.92 us  [swapped(): return lax.ppermute(array, 'dp', [(i, i ^ bit) for i in range(N_DP)])]
    unnamed x12 -> x18, local copies, waits for them, and re-layouts: 0.03 us -> 0.94 us
    ppermute x21, starting transfers between devices: 16.8 us -> 16 us  [crossed(): return lax.ppermute(array, 'ctx', [(i, i ^ apart) for i in range(N_CTX)])]
    ppermute x8, starting transfers between devices: 12.6 us -> 13.4 us  [swapped(): return lax.ppermute(array, 'dp', [(i, i ^ bit) for i in range(N_DP)])]
  transfers between devices with their start and end apart: 29 -> 29, of which waited for: 13 -> 11; matrix products, arithmetic and copies ran while one was open for 1% -> 1% of each run, Pallas kernels for 24% -> 23%
where the time goes in v14:
time: 69.6 us; the launch traced here: 69.4 us
  starting transfers between devices  29.4 us (42%)
  Pallas kernels  19.4 us (28%)
  waiting for transfers between devices  18 us (26%)
  local copies, waits for them, and re-layouts  1.01 us (1%)
  between operations  0.88 us (1%)
  other arithmetic  0.75 us (1%)
    ppermute x21, starting transfers between devices, crossed(): return lax.ppermute(array, 'ctx', [(i, i ^ apart) for i in range(N_CTX)])  16 us
    ppermute x21, waiting for transfers between devices, crossed(): return lax.ppermute(array, 'ctx', [(i, i ^ apart) for i in range(N_CTX)])  14.1 us
    ppermute x8, starting transfers between devices, swapped(): return lax.ppermute(array, 'dp', [(i, i ^ bit) for i in range(N_DP)])  13.4 us
    ppermute x8, waiting for transfers between devices, swapped(): return lax.ppermute(array, 'dp', [(i, i ^ bit) for i in range(N_DP)])  3.92 us
    pallas_call x1, Pallas kernels, per_device(): call_kernel(backward, (pair_block,) * 2 + (shape((2, utts * frames, width...  3.58 us
    pallas_call x1, Pallas kernels, per_device(): call_kernel(forward, (channel_block,) * 2 + (shape((2, utts * frames, wid...  3.24 us
    pallas_call x1, Pallas kernels, per_device(): call_kernel(attend, (shape((N_CTX, frames, half), low),), ['smem'] + ['vm...  2.76 us
    pallas_call x1, Pallas kernels, per_device(): call_kernel(make_taps, (tap_block,) * 2, ['vmem'] * 2 + ['any'], scratch=...  2.08 us
  transfers between devices with their start and end apart: 29, of which 11 were waited for; matrix products, arithmetic and copies ran while one was open for 1% of the time, Pallas kernels for 23%

profile of v14, /device:TPU:0, one launch (start us, length us, event | category | flops | bytes accessed | tf_op | source)
XLA Modules:
  0.0 69.4 jit_solution(16245349612735456763)
XLA Ops:
  0.7 2.0 %shard_map.135 = (bf16[3,64,384]{2,1,0:T(8,128)(2,1)}, bf16[3,64,384]{2,1,0:T(8,128)(2,1)}, bf16[3,64,384]{2,1,0:T(8,128)(2,1)}, bf16[3,64,384]{2,1,0:T(8,128)(2,1)}) custom-call(bf16[2,64,768]{2,1,0:T(8,128)(2,1)} %query_ref.1, bf16[2,64,768]{2,1,0:T(8,128)(2,1)} %key_ref.1, bf16[2,64,768]{2,1,0:T(8,128)(2,1)} %value_ref.1), custom_call_target="tpu_custom_call" | custom-call | flops 1150000000 | tf_op jit(solution)/shard_map/pallas_call | solution.py:807
  3.7 4.0 %collective-permute-start.3 = (bf16[1,112,384]{2,1,0:T(8,128)(2,1)S(1)}, bf16[1,112,384]{2,1,0:T(8,128)(2,1)S(1)}, u32[]{:S(2)}, u32[]{:S(2)}) collective-permute-start(bf16[1,112,384]{2,1,0:T(8,128)(2,1)S(1)} %shard_map.136), channel_id=1, source_target_pairs={{0,16},{4,20},{8,24},{12,28},{16,0},{20,4},{24,8},{28,12},{1,17},{... | collective-permute-start | bytes 258056 | tf_op jit(solution)/shard_map/ppermute | solution.py:775
  7.7 1.5 %collective-permute-start.1 = (bf16[3,64,384]{2,1,0:T(8,128)(2,1)S(1)}, bf16[3,64,384]{2,1,0:T(8,128)(2,1)S(1)}, u32[]{:S(2)}, u32[]{:S(2)}) collective-permute-start(bf16[3,64,384]{2,1,0:T(8,128)(2,1)S(1)} %copy-done.8), channel_id=1, source_target_pairs={{0,2},{1,3},{2,0},{3,1},{4,6},{5,7},{6,4},{7,5},{8,10},{9,11},{10,... | collective-permute-start | bytes 442376 | tf_op jit(solution)/shard_map/ppermute | solution.py:783
  9.9 2.2 %collective-permute-done.3 = bf16[1,112,384]{2,1,0:T(8,128)(2,1)S(1)} collective-permute-done((bf16[1,112,384]{2,1,0:T(8,128)(2,1)S(1)}, bf16[1,112,384]{2,1,0:T(8,128)(2,1)S(1)}, u32[]{:S(2)}, u32[]{:S(2)}) %collective-permute-start.3) | collective-permute-done | bytes 86048 | tf_op jit(solution)/shard_map/ppermute | solution.py:775
  14.2 2.2 %collective-permute-start.6 = (bf16[2,128,384]{2,1,0:T(8,128)(2,1)S(1)}, bf16[2,128,384]{2,1,0:T(8,128)(2,1)S(1)}, u32[]{:S(2)}, u32[]{:S(2)}) collective-permute-start(bf16[2,128,384]{2,1,0:T(8,128)(2,1)S(1)} %get-tuple-element.51), channel_id=1, source_target_pairs={{0,2},{1,3},{2,0},{3,1},{4,6},{5,7},{6,4},{7,5},{8,10},{9,11},{10,... | collective-permute-start | bytes 589832 | tf_op jit(solution)/shard_map/ppermute | solution.py:783
  16.4 2.8 %shard_map.138.refs_0_ = bf16[4,64,384]{2,1,0:T(8,128)(2,1)S(1)} custom-call(s32[2]{0:T(128)S(1)} %copy-done.5, bf16[3,64,384]{2,1,0:T(8,128)(2,1)S(1)} %copy-done.6, bf16[3,64,384]{2,1,0:T(8,128)(2,1)S(1)} %collective-permute-done.refs_1_, bf16[3,64,384]{2,1,0:T(8,128)(2,1)S(1)} %collective-permute-done.1.refs_2_.awaited_ref, ...), custom_call_target="tpu_custom_call" | custom-call | flops 1150000000 | tf_op jit(solution)/shard_map/pallas_call | solution.py:839
  19.2 1.6 %collective-permute-start.5 = (bf16[400,384]{1,0:T(8,128)(2,1)S(1)}, bf16[400,384]{1,0:T(8,128)(2,1)S(1)}, u32[]{:S(2)}, u32[]{:S(2)}) collective-permute-start(bf16[400,384]{1,0:T(8,128)(2,1)S(1)} %shard_map.137.near_ref), channel_id=1, source_target_pairs={{0,4},{4,0},{8,12},{12,8},{16,20},{20,16},{24,28},{28,24},{1,5},{5... | collective-permute-start | bytes 921608 | tf_op jit(solution)/shard_map/ppermute | solution.py:775
  22.7 5.2 %collective-permute-done.8.refs_2_ = bf16[4,64,384]{2,1,0:T(8,128)(2,1)S(1)} collective-permute-done((bf16[4,64,384]{2,1,0:T(8,128)(2,1)S(1)}, bf16[4,64,384]{2,1,0:T(8,128)(2,1)S(1)}, u32[]{:S(2)}, u32[]{:S(2)}) %collective-permute-start.8) | collective-permute-done | bytes 196640 | tf_op jit(solution)/shard_map/ppermute | solution.py:783
  27.9 1.5 %collective-permute-start.11 = (bf16[128,384]{1,0:T(8,128)(2,1)S(1)}, bf16[128,384]{1,0:T(8,128)(2,1)S(1)}, u32[]{:S(2)}, u32[]{:S(2)}) collective-permute-start(bf16[128,384]{1,0:T(8,128)(2,1)S(1)} %get-tuple-element.59), channel_id=1, source_target_pairs={{0,2},{1,3},{2,0},{3,1},{4,6},{5,7},{6,4},{7,5},{8,10},{9,11},{10,... | collective-permute-start | bytes 294920 | tf_op jit(solution)/shard_map/ppermute | solution.py:783
  29.8 3.2 %shard_map.142 = (bf16[2,64,384]{2,1,0:T(8,128)(2,1)S(1)}, bf16[2,64,384]{2,1,0:T(8,128)(2,1)S(1)}, bf16[2,128,384]{2,1,0:T(8,128)(2,1)S(1)}, bf16[2,4,64,768]{3...) custom-call(s32[2]{0:T(128)S(1)} %copy-done.5, ...), custom_call_target="tpu_custom_call" | custom-call | flops 3680000000 | tf_op jit(solution)/shard_map/pallas_call | solution.py:849
  33.0 1.6 %collective-permute-start.13 = (bf16[2,128,384]{2,1,0:T(8,128)(2,1)S(1)}, bf16[2,128,384]{2,1,0:T(8,128)(2,1)S(1)}, u32[]{:S(2)}, u32[]{:S(2)}) collective-permute-start(bf16[2,128,384]{2,1,0:T(8,128)(2,1)S(1)} %get-tuple-element.65), channel_id=1, source_target_pairs={{0,2},{1,3},{2,0},{3,1},{4,6},{5,7},{6,4},{7,5},{8,10},{9,11},{10,... | collective-permute-start | bytes 589832 | tf_op jit(solution)/shard_map/ppermute | solution.py:783
  34.8 3.6 %shard_map.144 = (bf16[2,2,64,384]{3,2,1,0:T(8,128)(2,1)S(1)}, bf16[2,2,64,384]{3,2,1,0:T(8,128)(2,1)S(1)}, bf16[2,128,384]{2,1,0:T(8,128)(2,1)S(1)}, bf16[2,256...) custom-call(s32[2]{0:T(128)S(1)} %copy-done.5, ...), custom_call_target="tpu_custom_call" | custom-call | flops 5980000256 | tf_op jit(solution)/shard_map/pallas_call | solution.py:883
  38.4 1.8 %collective-permute-done.13.refs_1_.output_ref.refs_6_ = bf16[2,128,384]{2,1,0:T(8,128)(2,1)S(1)} collective-permute-done((bf16[2,128,384]{2,1,0:T(8,128)(2,1)S(1)}, bf16[2,128,384]{2,1,0:T(8,128)(2,1)S(1)}, u32[]{:S(2)}, u32[]{:S(2)}) %collective-permute-start.13) | collective-permute-done | bytes 196640 | tf_op jit(solution)/shard_map/ppermute | solution.py:783
  41.9 1.6 %collective-permute-start.15 = (bf16[256,384]{1,0:T(8,128)(2,1)S(1)}, bf16[256,384]{1,0:T(8,128)(2,1)S(1)}, u32[]{:S(2)}, u32[]{:S(2)}) collective-permute-start(bf16[256,384]{1,0:T(8,128)(2,1)S(1)} %shard_map.146.refs_4_.awaited_ref.refs_1_), channel_id=1, source_target_pairs={{0,2},{1,3},{2,0},{3,1},{4,6},{5,7},{6,4},{7,5},{8,10},{9,11},{10,... | collective-permute-start | bytes 589832 | tf_op jit(solution)/shard_map/ppermute | solution.py:783
  43.5 2.1 %shard_map.148 = (f32[16,384]{1,0:T(8,128)S(1)}, f32[16,384]{1,0:T(8,128)S(1)}) custom-call(f32[6,288,128]{2,1,0:T(8,128)S(1)} %get-tuple-element.66.masked_ref, f32[6,288,128]{2,1,0:T(8,128)S(1)} %get-tuple-element.67.cotangent_ref, bf16[256,384]{1,0:T(8,128)(2,1)S(1)} %shard_map.146.refs_4_.awaited_ref.refs_1_), custom_call_target="tpu_custom_call" | custom-call | flops 1150000000 | tf_op jit(solution)/shard_map/pallas_call | solution.py:915
  48.9 2.0 %shard_map.149 = (bf16[3,64,384]{2,1,0:T(8,128)(2,1)S(1)}, bf16[3,64,384]{2,1,0:T(8,128)(2,1)S(1)}, bf16[3,64,384]{2,1,0:T(8,128)(2,1)S(1)}, bf16[3,64,384]{2,1,0:T(8,128)(2,1)S(1)}) custom-call(bf16[6,256,256]{2,1,0:T(8,128)(2,1)S(1)} %shard_map.147.weight_ref, bf16[2,256,384]{2,1,0:T(8,128)(2,1)S(1)} %get-tuple-element.63.keep_ref, ...), custom_call_target="tpu_custom_call" | custom-call | flops 2529999872 | tf_op jit(solution)/shard_map/pallas_call | solution.py:928
  51.0 2.2 %collective-permute-start.23 = (bf16[2,112,384]{2,1,0:T(8,128)(2,1)S(1)}, bf16[2,112,384]{2,1,0:T(8,128)(2,1)S(1)}, u32[]{:S(2)}, u32[]{:S(2)}) collective-permute-start(bf16[2,112,384]{2,1,0:T(8,128)(2,1)S(1)} %get-tuple-element.80), channel_id=1, source_target_pairs={{0,8},{4,12},{8,0},{12,4},{16,24},{20,28},{24,16},{28,20},{1,9},{5... | collective-permute-start | bytes 516104 | tf_op jit(solution)/shard_map/ppermute | solution.py:775
  53.3 2.1 %collective-permute-start.18 = (bf16[3,64,384]{2,1,0:T(8,128)(2,1)S(1)}, bf16[3,64,384]{2,1,0:T(8,128)(2,1)S(1)}, u32[]{:S(2)}, u32[]{:S(2)}) collective-permute-start(bf16[3,64,384]{2,1,0:T(8,128)(2,1)S(1)} %shard_map.151), channel_id=1, source_target_pairs={{0,2},{1,3},{2,0},{3,1},{4,6},{5,7},{6,4},{7,5},{8,10},{9,11},{10,... | collective-permute-start | bytes 442376 | tf_op jit(solution)/shard_map/ppermute | solution.py:783
  55.7 1.7 %collective-permute-done.23 = bf16[2,112,384]{2,1,0:T(8,128)(2,1)S(1)} collective-permute-done((bf16[2,112,384]{2,1,0:T(8,128)(2,1)S(1)}, bf16[2,112,384]{2,1,0:T(8,128)(2,1)S(1)}, u32[]{:S(2)}, u32[]{:S(2)}) %collective-permute-start.23) | collective-permute-done | bytes 172064 | tf_op jit(solution)/shard_map/ppermute | solution.py:775
  58.5 2.0 %collective-permute-start.28 = (bf16[96,384]{1,0:T(8,128)(2,1)S(1)}, bf16[96,384]{1,0:T(8,128)(2,1)S(1)}, u32[]{:S(2)}, u32[]{:S(2)}) collective-permute-start(bf16[96,384]{1,0:T(8,128)(2,1)S(1)} %slice_bitcast_fusion), channel_id=1, source_target_pairs={{0,16},{4,20},{8,24},{12,28},{16,0},{20,4},{24,8},{28,12},{1,17},{... | collective-permute-start | bytes 221192 | tf_op jit(solution)/shard_map/ppermute | solution.py:775
  60.5 2.3 %collective-permute-done.19.refs_1_.refs_3_ = bf16[3,64,384]{2,1,0:T(8,128)(2,1)S(1)} collective-permute-done((bf16[3,64,384]{2,1,0:T(8,128)(2,1)S(1)}, bf16[3,64,384]{2,1,0:T(8,128)(2,1)S(1)}, u32[]{:S(2)}, u32[]{:S(2)}) %collective-permute-start.19) | collective-permute-done | bytes 147488 | tf_op jit(solution)/shard_map/ppermute | solution.py:783
  62.8 1.4 %collective-permute-start.27 = (f32[16,384]{1,0:T(8,128)S(1)}, f32[16,384]{1,0:T(8,128)S(1)}, u32[]{:S(2)}, u32[]{:S(2)}) collective-permute-start(f32[16,384]{1,0:T(8,128)S(1)} %shard_map.156.refs_8_), channel_id=1, source_target_pairs={{0,3},{1,2},{2,1},{3,0},{4,7},{5,6},{6,5},{7,4},{8,11},{9,10},{10,... | collective-permute-start | bytes 73736 | tf_op jit(solution)/shard_map/ppermute | solution.py:783
  66.1 1.9 %collective-permute-done.26.refs_10_ = f32[16,384]{1,0:T(8,128)S(1)} collective-permute-done((f32[16,384]{1,0:T(8,128)S(1)}, f32[16,384]{1,0:T(8,128)S(1)}, u32[]{:S(2)}, u32[]{:S(2)}) %collective-permute-start.26) | collective-permute-done | bytes 24608 | tf_op jit(solution)/shard_map/ppermute | solution.py:783
  68.1 1.3 %shard_map.157 = (bf16[2,64,768]{2,1,0:T(8,128)(2,1)}, bf16[2,64,768]{2,1,0:T(8,128)(2,1)}, bf16[2,64,768]{2,1,0:T(8,128)(2,1)}, bf16[2,64,1536]{2,1,0:T(8,128)(...) custom-call(bf16[3,64,384]{2,1,0:T(8,128)(2,1)S(1)} %get-tuple-element.69.awaited_ref.refs_0_, ...), custom_call_target="tpu_custom_call" | custom-call | flops 1150000000 | tf_op jit(solution)/shard_map/pallas_call | solution.py:961
  (81 shorter events, 14.8 us)
Async XLA Ops:
  3.7 8.4 %collective-permute-start.3 = (bf16[1,112,384]{2,1,0:T(8,128)(2,1)S(1)}, bf16[1,112,384]{2,1,0:T(8,128)(2,1)S(1)}, u32[]{:S(2)}, u32[]{:S(2)}) collective-permute-start(bf16[1,112,384]{2,1,0:T(8,128)(2,1)S(1)} %shard_map.136), channel_id=1, source_target_pairs={{0,16},{4,20},{8,24},{12,28},{16,0},{20,4},{24,8},{28,12},{1,17},{... | collective-permute-start | bytes 258056 | tf_op jit(solution)/shard_map/ppermute | solution.py:775
  7.7 6.1 %collective-permute-start.1 = (bf16[3,64,384]{2,1,0:T(8,128)(2,1)S(1)}, bf16[3,64,384]{2,1,0:T(8,128)(2,1)S(1)}, u32[]{:S(2)}, u32[]{:S(2)}) collective-permute-start(bf16[3,64,384]{2,1,0:T(8,128)(2,1)S(1)} %copy-done.8), channel_id=1, source_target_pairs={{0,2},{1,3},{2,0},{3,1},{4,6},{5,7},{6,4},{7,5},{8,10},{9,11},{10,... | collective-permute-start | bytes 442376 | tf_op jit(solution)/shard_map/ppermute | solution.py:783
  9.2 7.1 %collective-permute-start = (bf16[3,64,384]{2,1,0:T(8,128)(2,1)S(1)}, bf16[3,64,384]{2,1,0:T(8,128)(2,1)S(1)}, u32[]{:S(2)}, u32[]{:S(2)}) collective-permute-start(bf16[3,64,384]{2,1,0:T(8,128)(2,1)S(1)} %copy-done.2), channel_id=1, source_target_pairs={{0,1},{1,0},{2,3},{3,2},{4,5},{5,4},{6,7},{7,6},{8,9},{9,8},{10,11... | collective-permute-start | bytes 442376 | tf_op jit(solution)/shard_map/ppermute | solution.py:783
  9.2 7.1 %collective-permute-start.2 = (bf16[3,64,384]{2,1,0:T(8,128)(2,1)S(1)}, bf16[3,64,384]{2,1,0:T(8,128)(2,1)S(1)}, u32[]{:S(2)}, u32[]{:S(2)}) collective-permute-start(bf16[3,64,384]{2,1,0:T(8,128)(2,1)S(1)} %copy-done.7), channel_id=1, source_target_pairs={{0,3},{1,2},{2,1},{3,0},{4,7},{5,6},{6,5},{7,4},{8,11},{9,10},{10,... | collective-permute-start | bytes 442376 | tf_op jit(solution)/shard_map/ppermute | solution.py:783
  12.2 7.0 %collective-permute-start.4 = (bf16[2,112,384]{2,1,0:T(8,128)(2,1)S(1)}, bf16[2,112,384]{2,1,0:T(8,128)(2,1)S(1)}, u32[]{:S(2)}, u32[]{:S(2)}) collective-permute-start(bf16[2,112,384]{2,1,0:T(8,128)(2,1)S(1)} %pad_maximum_fusion.held_ref), channel_id=1, source_target_pairs={{0,8},{4,12},{8,0},{12,4},{16,24},{20,28},{24,16},{28,20},{1,9},{5... | collective-permute-start | bytes 516104 | tf_op jit(solution)/shard_map/ppermute | solution.py:775
  14.2 6.6 %collective-permute-start.6 = (bf16[2,128,384]{2,1,0:T(8,128)(2,1)S(1)}, bf16[2,128,384]{2,1,0:T(8,128)(2,1)S(1)}, u32[]{:S(2)}, u32[]{:S(2)}) collective-permute-start(bf16[2,128,384]{2,1,0:T(8,128)(2,1)S(1)} %get-tuple-element.51), channel_id=1, source_target_pairs={{0,2},{1,3},{2,0},{3,1},{4,6},{5,7},{6,4},{7,5},{8,10},{9,11},{10,... | collective-permute-start | bytes 589832 | tf_op jit(solution)/shard_map/ppermute | solution.py:783
  19.2 10.5 %collective-permute-start.5 = (bf16[400,384]{1,0:T(8,128)(2,1)S(1)}, bf16[400,384]{1,0:T(8,128)(2,1)S(1)}, u32[]{:S(2)}, u32[]{:S(2)}) collective-permute-start(bf16[400,384]{1,0:T(8,128)(2,1)S(1)} %shard_map.137.near_ref), channel_id=1, source_target_pairs={{0,4},{4,0},{8,12},{12,8},{16,20},{20,16},{24,28},{28,24},{1,5},{5... | collective-permute-start | bytes 921608 | tf_op jit(solution)/shard_map/ppermute | solution.py:775
  20.8 7.1 %collective-permute-start.8 = (bf16[4,64,384]{2,1,0:T(8,128)(2,1)S(1)}, bf16[4,64,384]{2,1,0:T(8,128)(2,1)S(1)}, u32[]{:S(2)}, u32[]{:S(2)}) collective-permute-start(bf16[4,64,384]{2,1,0:T(8,128)(2,1)S(1)} %shard_map.140.refs_0_), channel_id=1, source_target_pairs={{0,2},{1,3},{2,0},{3,1},{4,6},{5,7},{6,4},{7,5},{8,10},{9,11},{10,... | collective-permute-start | bytes 589832 | tf_op jit(solution)/shard_map/ppermute | solution.py:783
  22.1 7.7 %collective-permute-start.10 = (bf16[3,128,384]{2,1,0:T(8,128)(2,1)S(1)}, bf16[3,128,384]{2,1,0:T(8,128)(2,1)S(1)}, u32[]{:S(2)}, u32[]{:S(2)}) collective-permute-start(bf16[3,128,384]{2,1,0:T(8,128)(2,1)S(1)} %shard_map.141), channel_id=1, source_target_pairs={{0,1},{1,0},{2,3},{3,2},{4,5},{5,4},{6,7},{7,6},{8,9},{9,8},{10,11... | collective-permute-start | bytes 884744 | tf_op jit(solution)/shard_map/ppermute | solution.py:783
  22.4 7.0 %collective-permute-start.7 = (bf16[4,64,384]{2,1,0:T(8,128)(2,1)S(1)}, bf16[4,64,384]{2,1,0:T(8,128)(2,1)S(1)}, u32[]{:S(2)}, u32[]{:S(2)}) collective-permute-start(bf16[4,64,384]{2,1,0:T(8,128)(2,1)S(1)} %shard_map.140.refs_0_), channel_id=1, source_target_pairs={{0,1},{1,0},{2,3},{3,2},{4,5},{5,4},{6,7},{7,6},{8,9},{9,8},{10,11... | collective-permute-start | bytes 589832 | tf_op jit(solution)/shard_map/ppermute | solution.py:783
  27.9 6.7 %collective-permute-start.11 = (bf16[128,384]{1,0:T(8,128)(2,1)S(1)}, bf16[128,384]{1,0:T(8,128)(2,1)S(1)}, u32[]{:S(2)}, u32[]{:S(2)}) collective-permute-start(bf16[128,384]{1,0:T(8,128)(2,1)S(1)} %get-tuple-element.59), channel_id=1, source_target_pairs={{0,2},{1,3},{2,0},{3,1},{4,6},{5,7},{6,4},{7,5},{8,10},{9,11},{10,... | collective-permute-start | bytes 294920 | tf_op jit(solution)/shard_map/ppermute | solution.py:783
  29.4 5.4 %collective-permute-start.12 = (bf16[128,384]{1,0:T(8,128)(2,1)S(1)}, bf16[128,384]{1,0:T(8,128)(2,1)S(1)}, u32[]{:S(2)}, u32[]{:S(2)}) collective-permute-start(bf16[128,384]{1,0:T(8,128)(2,1)S(1)} %get-tuple-element.60), channel_id=1, source_target_pairs={{0,3},{1,2},{2,1},{3,0},{4,7},{5,6},{6,5},{7,4},{8,11},{9,10},{10,... | collective-permute-start | bytes 294920 | tf_op jit(solution)/shard_map/ppermute | solution.py:783
  33.0 7.2 %collective-permute-start.13 = (bf16[2,128,384]{2,1,0:T(8,128)(2,1)S(1)}, bf16[2,128,384]{2,1,0:T(8,128)(2,1)S(1)}, u32[]{:S(2)}, u32[]{:S(2)}) collective-permute-start(bf16[2,128,384]{2,1,0:T(8,128)(2,1)S(1)} %get-tuple-element.65), channel_id=1, source_target_pairs={{0,2},{1,3},{2,0},{3,1},{4,6},{5,7},{6,4},{7,5},{8,10},{9,11},{10,... | collective-permute-start | bytes 589832 | tf_op jit(solution)/shard_map/ppermute | solution.py:783
  40.8 10.1 %collective-permute-start.21 = (bf16[4,96,384]{2,1,0:T(8,128)(2,1)S(1)}, bf16[4,96,384]{2,1,0:T(8,128)(2,1)S(1)}, u32[]{:S(2)}, u32[]{:S(2)}) collective-permute-start(bf16[4,96,384]{2,1,0:T(8,128)(2,1)S(1)} %get-tuple-element.87), channel_id=1, source_target_pairs={{0,4},{4,0},{8,12},{12,8},{16,20},{20,16},{24,28},{28,24},{1,5},{5... | collective-permute-start | bytes 884744 | tf_op jit(solution)/shard_map/ppermute | solution.py:775
  41.9 7.0 %collective-permute-start.15 = (bf16[256,384]{1,0:T(8,128)(2,1)S(1)}, bf16[256,384]{1,0:T(8,128)(2,1)S(1)}, u32[]{:S(2)}, u32[]{:S(2)}) collective-permute-start(bf16[256,384]{1,0:T(8,128)(2,1)S(1)} %shard_map.146.refs_4_.awaited_ref.refs_1_), channel_id=1, source_target_pairs={{0,2},{1,3},{2,0},{3,1},{4,6},{5,7},{6,4},{7,5},{8,10},{9,11},{10,... | collective-permute-start | bytes 589832 | tf_op jit(solution)/shard_map/ppermute | solution.py:783
  45.6 5.4 %collective-permute-start.22 = (f32[16,384]{1,0:T(8,128)S(1)}, f32[16,384]{1,0:T(8,128)S(1)}, u32[]{:S(2)}, u32[]{:S(2)}) collective-permute-start(f32[16,384]{1,0:T(8,128)S(1)} %get-tuple-element.78), channel_id=1, source_target_pairs={{0,4},{4,0},{8,12},{12,8},{16,20},{20,16},{24,28},{28,24},{1,5},{5... | collective-permute-start | bytes 73736 | tf_op jit(solution)/shard_map/ppermute | solution.py:775
  46.7 6.6 %collective-permute-start.17 = (bf16[2,128,384]{2,1,0:T(8,128)(2,1)S(1)}, bf16[2,128,384]{2,1,0:T(8,128)(2,1)S(1)}, u32[]{:S(2)}, u32[]{:S(2)}) collective-permute-start(bf16[2,128,384]{2,1,0:T(8,128)(2,1)S(1)} %shard_map.150), channel_id=1, source_target_pairs={{0,2},{1,3},{2,0},{3,1},{4,6},{5,7},{6,4},{7,5},{8,10},{9,11},{10,... | collective-permute-start | bytes 589832 | tf_op jit(solution)/shard_map/ppermute | solution.py:783
  51.0 6.3 %collective-permute-start.23 = (bf16[2,112,384]{2,1,0:T(8,128)(2,1)S(1)}, bf16[2,112,384]{2,1,0:T(8,128)(2,1)S(1)}, u32[]{:S(2)}, u32[]{:S(2)}) collective-permute-start(bf16[2,112,384]{2,1,0:T(8,128)(2,1)S(1)} %get-tuple-element.80), channel_id=1, source_target_pairs={{0,8},{4,12},{8,0},{12,4},{16,24},{20,28},{24,16},{28,20},{1,9},{5... | collective-permute-start | bytes 516104 | tf_op jit(solution)/shard_map/ppermute | solution.py:775
  53.3 7.2 %collective-permute-start.18 = (bf16[3,64,384]{2,1,0:T(8,128)(2,1)S(1)}, bf16[3,64,384]{2,1,0:T(8,128)(2,1)S(1)}, u32[]{:S(2)}, u32[]{:S(2)}) collective-permute-start(bf16[3,64,384]{2,1,0:T(8,128)(2,1)S(1)} %shard_map.151), channel_id=1, source_target_pairs={{0,2},{1,3},{2,0},{3,1},{4,6},{5,7},{6,4},{7,5},{8,10},{9,11},{10,... | collective-permute-start | bytes 442376 | tf_op jit(solution)/shard_map/ppermute | solution.py:783
  55.3 7.5 %collective-permute-start.19 = (bf16[3,64,384]{2,1,0:T(8,128)(2,1)S(1)}, bf16[3,64,384]{2,1,0:T(8,128)(2,1)S(1)}, u32[]{:S(2)}, u32[]{:S(2)}) collective-permute-start(bf16[3,64,384]{2,1,0:T(8,128)(2,1)S(1)} %get-tuple-element.73), channel_id=1, source_target_pairs={{0,3},{1,2},{2,1},{3,0},{4,7},{5,6},{6,5},{7,4},{8,11},{9,10},{10,... | collective-permute-start | bytes 442376 | tf_op jit(solution)/shard_map/ppermute | solution.py:783
  55.5 12.6 %collective-permute-start.20 = (bf16[4,128,384]{2,1,0:T(8,128)(2,1)S(1)}, bf16[4,128,384]{2,1,0:T(8,128)(2,1)S(1)}, u32[]{:S(2)}, u32[]{:S(2)}) collective-permute-start(bf16[4,128,384]{2,1,0:T(8,128)(2,1)S(1)} %shard_map.152), channel_id=1, source_target_pairs={{0,1},{1,0},{2,3},{3,2},{4,5},{5,4},{6,7},{7,6},{8,9},{9,8},{10,11... | collective-permute-start | bytes 1179656 | tf_op jit(solution)/shard_map/ppermute | solution.py:783
  57.4 5.4 %collective-permute-start.24 = (bf16[16,384]{1,0:T(8,128)(2,1)S(1)}, bf16[16,384]{1,0:T(8,128)(2,1)S(1)}, u32[]{:S(2)}, u32[]{:S(2)}) collective-permute-start(bf16[16,384]{1,0:T(8,128)(2,1)S(1)} %slice_bitcast_fusion.2), channel_id=1, source_target_pairs={{0,16},{4,20},{8,24},{12,28},{16,0},{20,4},{24,8},{28,12},{1,17},{... | collective-permute-start | bytes 36872 | tf_op jit(solution)/shard_map/ppermute | solution.py:775
  58.5 6.3 %collective-permute-start.28 = (bf16[96,384]{1,0:T(8,128)(2,1)S(1)}, bf16[96,384]{1,0:T(8,128)(2,1)S(1)}, u32[]{:S(2)}, u32[]{:S(2)}) collective-permute-start(bf16[96,384]{1,0:T(8,128)(2,1)S(1)} %slice_bitcast_fusion), channel_id=1, source_target_pairs={{0,16},{4,20},{8,24},{12,28},{16,0},{20,4},{24,8},{28,12},{1,17},{... | collective-permute-start | bytes 221192 | tf_op jit(solution)/shard_map/ppermute | solution.py:775
  64.2 3.8 %collective-permute-start.26 = (f32[16,384]{1,0:T(8,128)S(1)}, f32[16,384]{1,0:T(8,128)S(1)}, u32[]{:S(2)}, u32[]{:S(2)}) collective-permute-start(f32[16,384]{1,0:T(8,128)S(1)} %shard_map.156.refs_8_), channel_id=1, source_target_pairs={{0,2},{1,3},{2,0},{3,1},{4,6},{5,7},{6,4},{7,5},{8,10},{9,11},{10,... | collective-permute-start | bytes 73736 | tf_op jit(solution)/shard_map/ppermute | solution.py:783
  (14 other events, 54.4 us)

commit v15 on v13

--- a/solution.py
+++ b/solution.py
@@ -467,7 +467,7 @@
     place = lax.axis_index("ctx")
     rows = key_pair.shape[0]
     frame = lax.broadcasted_iota(jnp.int32, (rows, rows), 0) ^ (place * frames)
-    scores = dot_tt(key_pair, query_pair * mask, 1, 1) * HEAD_DIM ** (-0.5)
+    scores = dot_tt(key_pair, query_pair * (mask * HEAD_DIM ** (-0.5)), 1, 1)
     scores = jnp.where(frame < length_ref[half_of(place)], scores, masked_score)
     powers = jnp.exp(scores - jnp.max(scores, axis=0, keepdims=True))
     total = jnp.sum(powers, axis=0, keepdims=True)

time: 66.4 us -> 66.4 us (level)
  no operation moved by 1% of the time
where the time goes in v15:
time: 66.4 us; the launch traced here: 66.2 us
  starting transfers between devices  29.4 us (44%)
  Pallas kernels  19.5 us (29%)
  waiting for transfers between devices  15.6 us (23%)
  between operations  0.86 us (1%)
  other arithmetic  0.75 us (1%)
    ppermute x21, starting transfers between devices, crossed(): return lax.ppermute(array, 'ctx', [(i, i ^ apart) for i in range(N_CTX)])  16.8 us
    ppermute x8, starting transfers between devices, swapped(): return lax.ppermute(array, 'dp', [(i, i ^ bit) for i in range(N_DP)])  12.6 us
    ppermute x21, waiting for transfers between devices, crossed(): return lax.ppermute(array, 'ctx', [(i, i ^ apart) for i in range(N_CTX)])  9.65 us
    ppermute x8, waiting for transfers between devices, swapped(): return lax.ppermute(array, 'dp', [(i, i ^ bit) for i in range(N_DP)])  6 us
    pallas_call x1, Pallas kernels, per_device(): call_kernel(backward, (pair_block,) * 2 + (shape((2, utts * frames, width...  3.58 us
    pallas_call x1, Pallas kernels, per_device(): call_kernel(forward, (channel_block,) * 2 + (shape((2, utts * frames, wid...  3.22 us
    pallas_call x1, Pallas kernels, per_device(): call_kernel(attend, (shape((N_CTX, frames, half), low),), ['smem'] + ['vm...  2.76 us
    pallas_call x1, Pallas kernels, per_device(): call_kernel(make_taps, (tap_block,) * 2, ['vmem'] * 2 + ['any'], scratch=...  2.08 us
  transfers between devices with their start and end apart: 29, of which 13 were waited for; matrix products, arithmetic and copies ran while one was open for 1% of the time, Pallas kernels for 24%

profile of v15, /device:TPU:0, one launch (start us, length us, event | category | flops | bytes accessed | tf_op | source)
XLA Modules:
  0.0 66.2 jit_solution(10793910364248803125)
XLA Ops:
  0.7 2.0 %shard_map.135 = (bf16[3,64,384]{2,1,0:T(8,128)(2,1)}, bf16[3,64,384]{2,1,0:T(8,128)(2,1)}, bf16[3,64,384]{2,1,0:T(8,128)(2,1)}, bf16[3,64,384]{2,1,0:T(8,128)(2,1)}) custom-call(bf16[2,64,768]{2,1,0:T(8,128)(2,1)} %query_ref.1, bf16[2,64,768]{2,1,0:T(8,128)(2,1)} %key_ref.1, bf16[2,64,768]{2,1,0:T(8,128)(2,1)} %value_ref.1), custom_call_target="tpu_custom_call" | custom-call | flops 1150000000 | tf_op jit(solution)/shard_map/pallas_call | solution.py:807
  3.2 2.6 %collective-permute-start.1 = (bf16[3,64,384]{2,1,0:T(8,128)(2,1)}, bf16[3,64,384]{2,1,0:T(8,128)(2,1)S(1)}, u32[]{:S(2)}, u32[]{:S(2)}) collective-permute-start(bf16[3,64,384]{2,1,0:T(8,128)(2,1)} %get-tuple-element.49), channel_id=1, source_target_pairs={{0,2},{1,3},{2,0},{3,1},{4,6},{5,7},{6,4},{7,5},{8,10},{9,11},{10,... | collective-permute-start | bytes 442376 | tf_op jit(solution)/shard_map/ppermute | solution.py:783
  5.9 2.8 %collective-permute-start.3 = (bf16[1,112,384]{2,1,0:T(8,128)(2,1)S(1)}, bf16[1,112,384]{2,1,0:T(8,128)(2,1)S(1)}, u32[]{:S(2)}, u32[]{:S(2)}) collective-permute-start(bf16[1,112,384]{2,1,0:T(8,128)(2,1)S(1)} %shard_map.136), channel_id=1, source_target_pairs={{0,16},{4,20},{8,24},{12,28},{16,0},{20,4},{24,8},{28,12},{1,17},{... | collective-permute-start | bytes 258056 | tf_op jit(solution)/shard_map/ppermute | solution.py:775
  8.8 1.9 %collective-permute-done.1.refs_2_.awaited_ref = bf16[3,64,384]{2,1,0:T(8,128)(2,1)S(1)} collective-permute-done((bf16[3,64,384]{2,1,0:T(8,128)(2,1)}, bf16[3,64,384]{2,1,0:T(8,128)(2,1)S(1)}, u32[]{:S(2)}, u32[]{:S(2)}) %collective-permute-start.1) | collective-permute-done | bytes 147488 | tf_op jit(solution)/shard_map/ppermute | solution.py:783
  11.0 2.0 %collective-permute-start.6 = (bf16[2,128,384]{2,1,0:T(8,128)(2,1)S(1)}, bf16[2,128,384]{2,1,0:T(8,128)(2,1)S(1)}, u32[]{:S(2)}, u32[]{:S(2)}) collective-permute-start(bf16[2,128,384]{2,1,0:T(8,128)(2,1)S(1)} %get-tuple-element.51), channel_id=1, source_target_pairs={{0,2},{1,3},{2,0},{3,1},{4,6},{5,7},{6,4},{7,5},{8,10},{9,11},{10,... | collective-permute-start | bytes 589832 | tf_op jit(solution)/shard_map/ppermute | solution.py:783
  14.7 2.8 %shard_map.138.refs_0_ = bf16[4,64,384]{2,1,0:T(8,128)(2,1)S(1)} custom-call(s32[2]{0:T(128)S(1)} %copy-done.4, bf16[3,64,384]{2,1,0:T(8,128)(2,1)S(1)} %copy-done.5, bf16[3,64,384]{2,1,0:T(8,128)(2,1)S(1)} %collective-permute-done.awaited_ref.refs_1_, bf16[3,64,384]{2,1,0:T(8,128)(2,1)S(1)} %collective-permute-done.1.refs_2_.awaited_ref, ...), custom_call_target="tpu_custom_call" | custom-call | flops 1150000000 | tf_op jit(solution)/shard_map/pallas_call | solution.py:839
  17.8 1.8 %collective-permute-start.8 = (bf16[4,64,384]{2,1,0:T(8,128)(2,1)S(1)}, bf16[4,64,384]{2,1,0:T(8,128)(2,1)S(1)}, u32[]{:S(2)}, u32[]{:S(2)}) collective-permute-start(bf16[4,64,384]{2,1,0:T(8,128)(2,1)S(1)} %shard_map.140.refs_0_), channel_id=1, source_target_pairs={{0,2},{1,3},{2,0},{3,1},{4,6},{5,7},{6,4},{7,5},{8,10},{9,11},{10,... | collective-permute-start | bytes 589832 | tf_op jit(solution)/shard_map/ppermute | solution.py:783
  19.8 1.4 %collective-permute-start.5 = (bf16[400,384]{1,0:T(8,128)(2,1)S(1)}, bf16[400,384]{1,0:T(8,128)(2,1)S(1)}, u32[]{:S(2)}, u32[]{:S(2)}) collective-permute-start(bf16[400,384]{1,0:T(8,128)(2,1)S(1)} %shard_map.137.near_ref), channel_id=1, source_target_pairs={{0,4},{4,0},{8,12},{12,8},{16,20},{20,16},{24,28},{28,24},{1,5},{5... | collective-permute-start | bytes 921608 | tf_op jit(solution)/shard_map/ppermute | solution.py:775
  21.9 2.1 %collective-permute-done.8.refs_2_ = bf16[4,64,384]{2,1,0:T(8,128)(2,1)S(1)} collective-permute-done((bf16[4,64,384]{2,1,0:T(8,128)(2,1)S(1)}, bf16[4,64,384]{2,1,0:T(8,128)(2,1)S(1)}, u32[]{:S(2)}, u32[]{:S(2)}) %collective-permute-start.8) | collective-permute-done | bytes 196640 | tf_op jit(solution)/shard_map/ppermute | solution.py:783
  23.9 1.5 %collective-permute-start.11 = (bf16[128,384]{1,0:T(8,128)(2,1)S(1)}, bf16[128,384]{1,0:T(8,128)(2,1)S(1)}, u32[]{:S(2)}, u32[]{:S(2)}) collective-permute-start(bf16[128,384]{1,0:T(8,128)(2,1)S(1)} %get-tuple-element.59), channel_id=1, source_target_pairs={{0,2},{1,3},{2,0},{3,1},{4,6},{5,7},{6,4},{7,5},{8,10},{9,11},{10,... | collective-permute-start | bytes 294920 | tf_op jit(solution)/shard_map/ppermute | solution.py:783
  25.8 2.1 %collective-permute-done.5.other_ref = bf16[400,384]{1,0:T(8,128)(2,1)S(1)} collective-permute-done((bf16[400,384]{1,0:T(8,128)(2,1)S(1)}, bf16[400,384]{1,0:T(8,128)(2,1)S(1)}, u32[]{:S(2)}, u32[]{:S(2)}) %collective-permute-start.5) | collective-permute-done | bytes 307232 | tf_op jit(solution)/shard_map/ppermute | solution.py:775
  27.9 3.2 %shard_map.142 = (bf16[2,64,384]{2,1,0:T(8,128)(2,1)S(1)}, bf16[2,64,384]{2,1,0:T(8,128)(2,1)S(1)}, bf16[2,128,384]{2,1,0:T(8,128)(2,1)S(1)}, bf16[2,4,64,768]{3...) custom-call(s32[2]{0:T(128)S(1)} %copy-done.4, ...), custom_call_target="tpu_custom_call" | custom-call | flops 3680000000 | tf_op jit(solution)/shard_map/pallas_call | solution.py:849
  32.3 3.6 %shard_map.144 = (bf16[2,2,64,384]{3,2,1,0:T(8,128)(2,1)S(1)}, bf16[2,2,64,384]{3,2,1,0:T(8,128)(2,1)S(1)}, bf16[2,128,384]{2,1,0:T(8,128)(2,1)S(1)}, bf16[2,256...) custom-call(s32[2]{0:T(128)S(1)} %copy-done.4, ...), custom_call_target="tpu_custom_call" | custom-call | flops 5980000256 | tf_op jit(solution)/shard_map/pallas_call | solution.py:883
  38.9 1.5 %collective-permute-start.15 = (bf16[256,384]{1,0:T(8,128)(2,1)S(1)}, bf16[256,384]{1,0:T(8,128)(2,1)S(1)}, u32[]{:S(2)}, u32[]{:S(2)}) collective-permute-start(bf16[256,384]{1,0:T(8,128)(2,1)S(1)} %shard_map.146.refs_4_.awaited_ref.refs_1_), channel_id=1, source_target_pairs={{0,2},{1,3},{2,0},{3,1},{4,6},{5,7},{6,4},{7,5},{8,10},{9,11},{10,... | collective-permute-start | bytes 589832 | tf_op jit(solution)/shard_map/ppermute | solution.py:783
  40.4 2.1 %shard_map.148 = (f32[16,384]{1,0:T(8,128)S(1)}, f32[16,384]{1,0:T(8,128)S(1)}) custom-call(f32[6,288,128]{2,1,0:T(8,128)S(1)} %get-tuple-element.66.masked_ref, f32[6,288,128]{2,1,0:T(8,128)S(1)} %get-tuple-element.67.cotangent_ref, bf16[256,384]{1,0:T(8,128)(2,1)S(1)} %shard_map.146.refs_4_.awaited_ref.refs_1_), custom_call_target="tpu_custom_call" | custom-call | flops 1150000000 | tf_op jit(solution)/shard_map/pallas_call | solution.py:915
  44.1 1.3 %shard_map.147.weight_ref = bf16[6,256,256]{2,1,0:T(8,128)(2,1)S(1)} custom-call(s32[2]{0:T(128)S(1)} %copy-done.4, bf16[3,64,384]{2,1,0:T(8,128)(2,1)S(1)} %copy-done.5, bf16[3,64,384]{2,1,0:T(8,128)(2,1)S(1)} %collective-permute-done.awaited_ref.refs_1_, bf16[3,64,384]{2,1,0:T(8,128)(2,1)S(1)} %collective-permute-done.1.refs_2_.awaited_ref, ...), custom_call_target="tpu_custom_call" | custom-call | flops 1150000000 | tf_op jit(solution)/shard_map/pallas_call | solution.py:923
  46.3 2.0 %shard_map.149 = (bf16[3,64,384]{2,1,0:T(8,128)(2,1)S(1)}, bf16[3,64,384]{2,1,0:T(8,128)(2,1)S(1)}, bf16[3,64,384]{2,1,0:T(8,128)(2,1)S(1)}, bf16[3,64,384]{2,1,0:T(8,128)(2,1)S(1)}) custom-call(bf16[6,256,256]{2,1,0:T(8,128)(2,1)S(1)} %shard_map.147.weight_ref, bf16[2,256,384]{2,1,0:T(8,128)(2,1)S(1)} %get-tuple-element.63.keep_ref, ...), custom_call_target="tpu_custom_call" | custom-call | flops 2529999872 | tf_op jit(solution)/shard_map/pallas_call | solution.py:928
  50.2 1.8 %collective-permute-start.18 = (bf16[3,64,384]{2,1,0:T(8,128)(2,1)S(1)}, bf16[3,64,384]{2,1,0:T(8,128)(2,1)S(1)}, u32[]{:S(2)}, u32[]{:S(2)}) collective-permute-start(bf16[3,64,384]{2,1,0:T(8,128)(2,1)S(1)} %shard_map.151), channel_id=1, source_target_pairs={{0,2},{1,3},{2,0},{3,1},{4,6},{5,7},{6,4},{7,5},{8,10},{9,11},{10,... | collective-permute-start | bytes 442376 | tf_op jit(solution)/shard_map/ppermute | solution.py:783
  52.5 1.4 %collective-permute-done.23 = bf16[2,112,384]{2,1,0:T(8,128)(2,1)S(1)} collective-permute-done((bf16[2,112,384]{2,1,0:T(8,128)(2,1)S(1)}, bf16[2,112,384]{2,1,0:T(8,128)(2,1)S(1)}, u32[]{:S(2)}, u32[]{:S(2)}) %collective-permute-start.23) | collective-permute-done | bytes 172064 | tf_op jit(solution)/shard_map/ppermute | solution.py:775
  53.9 3.7 %collective-permute-start.24 = (bf16[16,384]{1,0:T(8,128)(2,1)S(1)}, bf16[16,384]{1,0:T(8,128)(2,1)S(1)}, u32[]{:S(2)}, u32[]{:S(2)}) collective-permute-start(bf16[16,384]{1,0:T(8,128)(2,1)S(1)} %slice_bitcast_fusion.2), channel_id=1, source_target_pairs={{0,16},{4,20},{8,24},{12,28},{16,0},{20,4},{24,8},{28,12},{1,17},{... | collective-permute-start | bytes 36872 | tf_op jit(solution)/shard_map/ppermute | solution.py:775
  57.7 1.7 %collective-permute-done.19.refs_1_.refs_3_ = bf16[3,64,384]{2,1,0:T(8,128)(2,1)S(1)} collective-permute-done((bf16[3,64,384]{2,1,0:T(8,128)(2,1)S(1)}, bf16[3,64,384]{2,1,0:T(8,128)(2,1)S(1)}, u32[]{:S(2)}, u32[]{:S(2)}) %collective-permute-start.19) | collective-permute-done | bytes 147488 | tf_op jit(solution)/shard_map/ppermute | solution.py:783
  59.4 1.6 %collective-permute-start.27 = (f32[16,384]{1,0:T(8,128)S(1)}, f32[16,384]{1,0:T(8,128)S(1)}, u32[]{:S(2)}, u32[]{:S(2)}) collective-permute-start(f32[16,384]{1,0:T(8,128)S(1)} %shard_map.156.refs_8_), channel_id=1, source_target_pairs={{0,3},{1,2},{2,1},{3,0},{4,7},{5,6},{6,5},{7,4},{8,11},{9,10},{10,... | collective-permute-start | bytes 73736 | tf_op jit(solution)/shard_map/ppermute | solution.py:783
  61.4 1.5 %collective-permute-done.28 = bf16[96,384]{1,0:T(8,128)(2,1)S(1)} collective-permute-done((bf16[96,384]{1,0:T(8,128)(2,1)S(1)}, bf16[96,384]{1,0:T(8,128)(2,1)S(1)}, u32[]{:S(2)}, u32[]{:S(2)}) %collective-permute-start.28) | collective-permute-done | bytes 73760 | tf_op jit(solution)/shard_map/ppermute | solution.py:775
  64.9 1.3 %shard_map.157 = (bf16[2,64,768]{2,1,0:T(8,128)(2,1)}, bf16[2,64,768]{2,1,0:T(8,128)(2,1)}, bf16[2,64,768]{2,1,0:T(8,128)(2,1)}, bf16[2,64,1536]{2,1,0:T(8,128)(...) custom-call(bf16[3,64,384]{2,1,0:T(8,128)(2,1)S(1)} %get-tuple-element.69.awaited_ref.refs_0_, ...), custom_call_target="tpu_custom_call" | custom-call | flops 1150000000 | tf_op jit(solution)/shard_map/pallas_call | solution.py:961
  (75 shorter events, 15.7 us)
Async XLA Ops:
  3.2 7.5 %collective-permute-start.1 = (bf16[3,64,384]{2,1,0:T(8,128)(2,1)}, bf16[3,64,384]{2,1,0:T(8,128)(2,1)S(1)}, u32[]{:S(2)}, u32[]{:S(2)}) collective-permute-start(bf16[3,64,384]{2,1,0:T(8,128)(2,1)} %get-tuple-element.49), channel_id=1, source_target_pairs={{0,2},{1,3},{2,0},{3,1},{4,6},{5,7},{6,4},{7,5},{8,10},{9,11},{10,... | collective-permute-start | bytes 442376 | tf_op jit(solution)/shard_map/ppermute | solution.py:783
  5.8 8.9 %collective-permute-start.2 = (bf16[3,64,384]{2,1,0:T(8,128)(2,1)}, bf16[3,64,384]{2,1,0:T(8,128)(2,1)S(1)}, u32[]{:S(2)}, u32[]{:S(2)}) collective-permute-start(bf16[3,64,384]{2,1,0:T(8,128)(2,1)} %get-tuple-element.50), channel_id=1, source_target_pairs={{0,3},{1,2},{2,1},{3,0},{4,7},{5,6},{6,5},{7,4},{8,11},{9,10},{10,... | collective-permute-start | bytes 442376 | tf_op jit(solution)/shard_map/ppermute | solution.py:783
  5.9 7.7 %collective-permute-start.3 = (bf16[1,112,384]{2,1,0:T(8,128)(2,1)S(1)}, bf16[1,112,384]{2,1,0:T(8,128)(2,1)S(1)}, u32[]{:S(2)}, u32[]{:S(2)}) collective-permute-start(bf16[1,112,384]{2,1,0:T(8,128)(2,1)S(1)} %shard_map.136), channel_id=1, source_target_pairs={{0,16},{4,20},{8,24},{12,28},{16,0},{20,4},{24,8},{28,12},{1,17},{... | collective-permute-start | bytes 258056 | tf_op jit(solution)/shard_map/ppermute | solution.py:775
  11.0 6.8 %collective-permute-start.6 = (bf16[2,128,384]{2,1,0:T(8,128)(2,1)S(1)}, bf16[2,128,384]{2,1,0:T(8,128)(2,1)S(1)}, u32[]{:S(2)}, u32[]{:S(2)}) collective-permute-start(bf16[2,128,384]{2,1,0:T(8,128)(2,1)S(1)} %get-tuple-element.51), channel_id=1, source_target_pairs={{0,2},{1,3},{2,0},{3,1},{4,6},{5,7},{6,4},{7,5},{8,10},{9,11},{10,... | collective-permute-start | bytes 589832 | tf_op jit(solution)/shard_map/ppermute | solution.py:783
  13.7 6.1 %collective-permute-start.4 = (bf16[2,112,384]{2,1,0:T(8,128)(2,1)S(1)}, bf16[2,112,384]{2,1,0:T(8,128)(2,1)S(1)}, u32[]{:S(2)}, u32[]{:S(2)}) collective-permute-start(bf16[2,112,384]{2,1,0:T(8,128)(2,1)S(1)} %pad_maximum_fusion.held_ref), channel_id=1, source_target_pairs={{0,8},{4,12},{8,0},{12,4},{16,24},{20,28},{24,16},{28,20},{1,9},{5... | collective-permute-start | bytes 516104 | tf_op jit(solution)/shard_map/ppermute | solution.py:775
  17.8 6.1 %collective-permute-start.8 = (bf16[4,64,384]{2,1,0:T(8,128)(2,1)S(1)}, bf16[4,64,384]{2,1,0:T(8,128)(2,1)S(1)}, u32[]{:S(2)}, u32[]{:S(2)}) collective-permute-start(bf16[4,64,384]{2,1,0:T(8,128)(2,1)S(1)} %shard_map.140.refs_0_), channel_id=1, source_target_pairs={{0,2},{1,3},{2,0},{3,1},{4,6},{5,7},{6,4},{7,5},{8,10},{9,11},{10,... | collective-permute-start | bytes 589832 | tf_op jit(solution)/shard_map/ppermute | solution.py:783
  19.8 8.1 %collective-permute-start.5 = (bf16[400,384]{1,0:T(8,128)(2,1)S(1)}, bf16[400,384]{1,0:T(8,128)(2,1)S(1)}, u32[]{:S(2)}, u32[]{:S(2)}) collective-permute-start(bf16[400,384]{1,0:T(8,128)(2,1)S(1)} %shard_map.137.near_ref), channel_id=1, source_target_pairs={{0,4},{4,0},{8,12},{12,8},{16,20},{20,16},{24,28},{28,24},{1,5},{5... | collective-permute-start | bytes 921608 | tf_op jit(solution)/shard_map/ppermute | solution.py:775
  21.3 4.5 %collective-permute-start.10 = (bf16[3,128,384]{2,1,0:T(8,128)(2,1)S(1)}, bf16[3,128,384]{2,1,0:T(8,128)(2,1)S(1)}, u32[]{:S(2)}, u32[]{:S(2)}) collective-permute-start(bf16[3,128,384]{2,1,0:T(8,128)(2,1)S(1)} %shard_map.141), channel_id=1, source_target_pairs={{0,1},{1,0},{2,3},{3,2},{4,5},{5,4},{6,7},{7,6},{8,9},{9,8},{10,11... | collective-permute-start | bytes 884744 | tf_op jit(solution)/shard_map/ppermute | solution.py:783
  21.4 4.1 %collective-permute-start.7 = (bf16[4,64,384]{2,1,0:T(8,128)(2,1)S(1)}, bf16[4,64,384]{2,1,0:T(8,128)(2,1)S(1)}, u32[]{:S(2)}, u32[]{:S(2)}) collective-permute-start(bf16[4,64,384]{2,1,0:T(8,128)(2,1)S(1)} %shard_map.140.refs_0_), channel_id=1, source_target_pairs={{0,1},{1,0},{2,3},{3,2},{4,5},{5,4},{6,7},{7,6},{8,9},{9,8},{10,11... | collective-permute-start | bytes 589832 | tf_op jit(solution)/shard_map/ppermute | solution.py:783
  23.9 4.0 %collective-permute-start.9 = (bf16[4,64,384]{2,1,0:T(8,128)(2,1)S(1)}, bf16[4,64,384]{2,1,0:T(8,128)(2,1)S(1)}, u32[]{:S(2)}, u32[]{:S(2)}) collective-permute-start(bf16[4,64,384]{2,1,0:T(8,128)(2,1)S(1)} %collective-permute-done.8.refs_2_), channel_id=1, source_target_pairs={{0,1},{1,0},{2,3},{3,2},{4,5},{5,4},{6,7},{7,6},{8,9},{9,8},{10,11... | collective-permute-start | bytes 589832 | tf_op jit(solution)/shard_map/ppermute | solution.py:783
  23.9 8.4 %collective-permute-start.11 = (bf16[128,384]{1,0:T(8,128)(2,1)S(1)}, bf16[128,384]{1,0:T(8,128)(2,1)S(1)}, u32[]{:S(2)}, u32[]{:S(2)}) collective-permute-start(bf16[128,384]{1,0:T(8,128)(2,1)S(1)} %get-tuple-element.59), channel_id=1, source_target_pairs={{0,2},{1,3},{2,0},{3,1},{4,6},{5,7},{6,4},{7,5},{8,10},{9,11},{10,... | collective-permute-start | bytes 294920 | tf_op jit(solution)/shard_map/ppermute | solution.py:783
  25.4 6.9 %collective-permute-start.12 = (bf16[128,384]{1,0:T(8,128)(2,1)S(1)}, bf16[128,384]{1,0:T(8,128)(2,1)S(1)}, u32[]{:S(2)}, u32[]{:S(2)}) collective-permute-start(bf16[128,384]{1,0:T(8,128)(2,1)S(1)} %get-tuple-element.60), channel_id=1, source_target_pairs={{0,3},{1,2},{2,1},{3,0},{4,7},{5,6},{6,5},{7,4},{8,11},{9,10},{10,... | collective-permute-start | bytes 294920 | tf_op jit(solution)/shard_map/ppermute | solution.py:783
  31.2 5.7 %collective-permute-start.13 = (bf16[2,128,384]{2,1,0:T(8,128)(2,1)S(1)}, bf16[2,128,384]{2,1,0:T(8,128)(2,1)S(1)}, u32[]{:S(2)}, u32[]{:S(2)}) collective-permute-start(bf16[2,128,384]{2,1,0:T(8,128)(2,1)S(1)} %get-tuple-element.65), channel_id=1, source_target_pairs={{0,2},{1,3},{2,0},{3,1},{4,6},{5,7},{6,4},{7,5},{8,10},{9,11},{10,... | collective-permute-start | bytes 589832 | tf_op jit(solution)/shard_map/ppermute | solution.py:783
  37.6 10.7 %collective-permute-start.21 = (bf16[4,96,384]{2,1,0:T(8,128)(2,1)S(1)}, bf16[4,96,384]{2,1,0:T(8,128)(2,1)S(1)}, u32[]{:S(2)}, u32[]{:S(2)}) collective-permute-start(bf16[4,96,384]{2,1,0:T(8,128)(2,1)S(1)} %get-tuple-element.87), channel_id=1, source_target_pairs={{0,4},{4,0},{8,12},{12,8},{16,20},{20,16},{24,28},{28,24},{1,5},{5... | collective-permute-start | bytes 884744 | tf_op jit(solution)/shard_map/ppermute | solution.py:775
  38.9 7.4 %collective-permute-start.15 = (bf16[256,384]{1,0:T(8,128)(2,1)S(1)}, bf16[256,384]{1,0:T(8,128)(2,1)S(1)}, u32[]{:S(2)}, u32[]{:S(2)}) collective-permute-start(bf16[256,384]{1,0:T(8,128)(2,1)S(1)} %shard_map.146.refs_4_.awaited_ref.refs_1_), channel_id=1, source_target_pairs={{0,2},{1,3},{2,0},{3,1},{4,6},{5,7},{6,4},{7,5},{8,10},{9,11},{10,... | collective-permute-start | bytes 589832 | tf_op jit(solution)/shard_map/ppermute | solution.py:783
  42.5 5.8 %collective-permute-start.22 = (f32[16,384]{1,0:T(8,128)S(1)}, f32[16,384]{1,0:T(8,128)S(1)}, u32[]{:S(2)}, u32[]{:S(2)}) collective-permute-start(f32[16,384]{1,0:T(8,128)S(1)} %get-tuple-element.78), channel_id=1, source_target_pairs={{0,4},{4,0},{8,12},{12,8},{16,20},{20,16},{24,28},{28,24},{1,5},{5... | collective-permute-start | bytes 73736 | tf_op jit(solution)/shard_map/ppermute | solution.py:775
  43.5 6.7 %collective-permute-start.17 = (bf16[2,128,384]{2,1,0:T(8,128)(2,1)S(1)}, bf16[2,128,384]{2,1,0:T(8,128)(2,1)S(1)}, u32[]{:S(2)}, u32[]{:S(2)}) collective-permute-start(bf16[2,128,384]{2,1,0:T(8,128)(2,1)S(1)} %shard_map.150), channel_id=1, source_target_pairs={{0,2},{1,3},{2,0},{3,1},{4,6},{5,7},{6,4},{7,5},{8,10},{9,11},{10,... | collective-permute-start | bytes 589832 | tf_op jit(solution)/shard_map/ppermute | solution.py:783
  48.4 5.5 %collective-permute-start.23 = (bf16[2,112,384]{2,1,0:T(8,128)(2,1)S(1)}, bf16[2,112,384]{2,1,0:T(8,128)(2,1)S(1)}, u32[]{:S(2)}, u32[]{:S(2)}) collective-permute-start(bf16[2,112,384]{2,1,0:T(8,128)(2,1)S(1)} %get-tuple-element.80), channel_id=1, source_target_pairs={{0,8},{4,12},{8,0},{12,4},{16,24},{20,28},{24,16},{28,20},{1,9},{5... | collective-permute-start | bytes 516104 | tf_op jit(solution)/shard_map/ppermute | solution.py:775
  50.2 7.5 %collective-permute-start.18 = (bf16[3,64,384]{2,1,0:T(8,128)(2,1)S(1)}, bf16[3,64,384]{2,1,0:T(8,128)(2,1)S(1)}, u32[]{:S(2)}, u32[]{:S(2)}) collective-permute-start(bf16[3,64,384]{2,1,0:T(8,128)(2,1)S(1)} %shard_map.151), channel_id=1, source_target_pairs={{0,2},{1,3},{2,0},{3,1},{4,6},{5,7},{6,4},{7,5},{8,10},{9,11},{10,... | collective-permute-start | bytes 442376 | tf_op jit(solution)/shard_map/ppermute | solution.py:783
  52.0 7.4 %collective-permute-start.19 = (bf16[3,64,384]{2,1,0:T(8,128)(2,1)S(1)}, bf16[3,64,384]{2,1,0:T(8,128)(2,1)S(1)}, u32[]{:S(2)}, u32[]{:S(2)}) collective-permute-start(bf16[3,64,384]{2,1,0:T(8,128)(2,1)S(1)} %get-tuple-element.73), channel_id=1, source_target_pairs={{0,3},{1,2},{2,1},{3,0},{4,7},{5,6},{6,5},{7,4},{8,11},{9,10},{10,... | collective-permute-start | bytes 442376 | tf_op jit(solution)/shard_map/ppermute | solution.py:783
  52.2 12.7 %collective-permute-start.20 = (bf16[4,128,384]{2,1,0:T(8,128)(2,1)S(1)}, bf16[4,128,384]{2,1,0:T(8,128)(2,1)S(1)}, u32[]{:S(2)}, u32[]{:S(2)}) collective-permute-start(bf16[4,128,384]{2,1,0:T(8,128)(2,1)S(1)} %shard_map.152), channel_id=1, source_target_pairs={{0,1},{1,0},{2,3},{3,2},{4,5},{5,4},{6,7},{7,6},{8,9},{9,8},{10,11... | collective-permute-start | bytes 1179656 | tf_op jit(solution)/shard_map/ppermute | solution.py:783
  53.9 5.5 %collective-permute-start.24 = (bf16[16,384]{1,0:T(8,128)(2,1)S(1)}, bf16[16,384]{1,0:T(8,128)(2,1)S(1)}, u32[]{:S(2)}, u32[]{:S(2)}) collective-permute-start(bf16[16,384]{1,0:T(8,128)(2,1)S(1)} %slice_bitcast_fusion.2), channel_id=1, source_target_pairs={{0,16},{4,20},{8,24},{12,28},{16,0},{20,4},{24,8},{28,12},{1,17},{... | collective-permute-start | bytes 36872 | tf_op jit(solution)/shard_map/ppermute | solution.py:775
  57.7 5.3 %collective-permute-start.28 = (bf16[96,384]{1,0:T(8,128)(2,1)S(1)}, bf16[96,384]{1,0:T(8,128)(2,1)S(1)}, u32[]{:S(2)}, u32[]{:S(2)}) collective-permute-start(bf16[96,384]{1,0:T(8,128)(2,1)S(1)} %slice_bitcast_fusion), channel_id=1, source_target_pairs={{0,16},{4,20},{8,24},{12,28},{16,0},{20,4},{24,8},{28,12},{1,17},{... | collective-permute-start | bytes 221192 | tf_op jit(solution)/shard_map/ppermute | solution.py:775
  59.4 4.2 %collective-permute-start.27 = (f32[16,384]{1,0:T(8,128)S(1)}, f32[16,384]{1,0:T(8,128)S(1)}, u32[]{:S(2)}, u32[]{:S(2)}) collective-permute-start(f32[16,384]{1,0:T(8,128)S(1)} %shard_map.156.refs_8_), channel_id=1, source_target_pairs={{0,3},{1,2},{2,1},{3,0},{4,7},{5,6},{6,5},{7,4},{8,11},{9,10},{10,... | collective-permute-start | bytes 73736 | tf_op jit(solution)/shard_map/ppermute | solution.py:783
  (11 other events, 39.7 us)
